TPU v7x, 32 devices: a whole 2x2x4 slice. The times are simulated.
32 devices in a mesh: fibre: 8 (over y, x, core), tm: 4 (over z).
Axes of the slice: x: 2, y: 2, z: 4, core: 2. Of those that a mesh axis runs over, the one named last changes fastest.
Arguments:
- samples: bfloat16 [1024, 32, 1024], P('fibre', 'tm'), may hold values from -24 to 24
- band_gain: float32 [512], replicated, may hold values from 0.1 to 1
- dead_flags: int32 [1024], P('fibre'), may hold values 0 or 1
- section_ids: int32 [1024], P('fibre'), may hold values from 0 to 1, never falling along the last dimension, each value on 1 to 768 neighbouring positions
Outputs:
- stack: float32 [1024, 128, 128], P('fibre', 'tm')
Inputs may be any that keep to these rules, and one draw needn't show every extreme that they name: `section_ids`: section numbers never fall along the channels; each section holds 1 to 768 channels.
All inputs are finite; a program needn't handle non-finite values. No bound on the sum of `dead_flags` on one device may be relied on, other than what follows from the above.
Results may differ from a plain program's by a relative error of at most 0.008.
Values may be sent and summed in bfloat16 or wider, within the bound.
No kernel may reach another device: no remote copies, remote signals or barrier semaphores. Data moves between devices by JAX's collectives and lax.ppermute only.
A program may use at most 64 MiB of HBM per device.

v0:
```python
import math

import jax
import jax.numpy as jnp
from jax import lax
from jax.sharding import PartitionSpec as P

OFFS = 128
LAGS = 128
OBLK = 8
NSEC = 2


def from_behind(value, axis, steps):
    count = lax.axis_size(axis)
    pairs = [(source, (source + steps) % count) for source in range(count)]
    return lax.ppermute(value, axis, pairs)


def tables(ns, nf, nlag):
    tick = jnp.arange(ns, dtype=jnp.int32)
    freq = jnp.arange(nf, dtype=jnp.int32)
    phase = (tick[:, None] * freq[None, :] % ns).astype(jnp.float32) * (2.0 * math.pi / ns)
    window = 0.5 - 0.5 * jnp.cos(tick.astype(jnp.float32) * (2.0 * math.pi / ns))
    forward = jnp.concatenate(
        [window[:, None] * jnp.cos(phase), -window[:, None] * jnp.sin(phase)], axis=1
    ).astype(jnp.bfloat16)
    shifts = jnp.arange(nlag, dtype=jnp.int32) - nlag // 2
    turn = (freq[:, None] * shifts[None, :] % ns).astype(jnp.float32) * (2.0 * math.pi / ns)
    inverse = jnp.concatenate([jnp.cos(turn), -jnp.sin(turn)], axis=0).astype(jnp.bfloat16)
    return (forward, inverse)


def shards(samples, band_gain, dead_flags, section_ids):
    chans, wins, ns = samples.shape
    nf = ns // 2
    live = (1 - dead_flags).astype(jnp.float32)
    member = (section_ids[:, None] == jnp.arange(NSEC, dtype=jnp.int32)[None, :]).astype(
        jnp.float32
    )
    weighted = (member * live[:, None]).astype(jnp.bfloat16)
    flat = samples.reshape(chans, wins * ns)
    sec_sum = lax.dot_general(
        weighted, flat, (((0,), (0,)), ((), ())), preferred_element_type=jnp.float32
    )
    sec_count = jnp.sum(member * live[:, None], axis=0)
    sec_sum, sec_count = lax.psum((sec_sum, sec_count), "fibre")
    common = sec_sum / jnp.maximum(sec_count, 1.0)[:, None]
    local_common = jnp.dot(member, common, precision=lax.Precision.HIGHEST)
    cleaned = (
        ((flat.astype(jnp.float32) - local_common) * live[:, None])
        .astype(jnp.bfloat16)
        .reshape(chans, wins, ns)
    )
    forward, inverse = tables(ns, nf, LAGS)
    gain_pair = jnp.concatenate([band_gain, band_gain])
    spec = jnp.dot(cleaned.reshape(-1, ns), forward, preferred_element_type=jnp.float32)
    power = jnp.mean(spec * spec, axis=-1, keepdims=True)
    white = (spec * gain_pair * lax.rsqrt(power + 1e-06)).astype(jnp.bfloat16)
    own = white.reshape(cleaned.shape[0], wins, 2 * nf)
    following = from_behind(own, "fibre", -1)
    near = jnp.concatenate([own, following], axis=0)
    scale = 1.0 / math.sqrt(nf * wins * lax.axis_size("tm"))

    def one_group(step, buffer):
        first = (step * OBLK).astype(jnp.int32)
        rows = []
        for inner in range(OBLK):
            partner = lax.dynamic_slice_in_dim(near, first + inner + 1, chans, 0)
            pr = own[..., :nf].astype(jnp.float32)
            pi = own[..., nf:].astype(jnp.float32)
            qr = partner[..., :nf].astype(jnp.float32)
            qi = partner[..., nf:].astype(jnp.float32)
            real = jnp.sum(pr * qr + pi * qi, axis=1)
            imag = jnp.sum(pi * qr - pr * qi, axis=1)
            rows.append(jnp.concatenate([real, imag], axis=-1))
        cross = jnp.stack(rows, axis=1).astype(jnp.bfloat16)
        lagged = (
            jnp.dot(
                cross.reshape(chans * OBLK, 2 * nf), inverse, preferred_element_type=jnp.float32
            )
            * scale
        )
        lagged = lagged.astype(jnp.bfloat16)
        lagged = lax.optimization_barrier(lagged).astype(jnp.float32).reshape(chans, OBLK, LAGS)
        return lax.dynamic_update_slice_in_dim(buffer, lagged, first, 1)

    partial_value = lax.fori_loop(
        0, OFFS // OBLK, one_group, jnp.zeros((chans, OFFS, LAGS), jnp.float32)
    )
    summed = lax.psum(partial_value.astype(jnp.bfloat16), "tm").astype(jnp.float32)
    share = OFFS // lax.axis_size("tm")
    return lax.dynamic_slice_in_dim(summed, lax.axis_index("tm") * share, share, 1)


def solution(mesh):
    in_specs = (P("fibre", "tm", None), P(), P("fibre"), P("fibre"))
    out_specs = P("fibre", "tm", None)
    return jax.shard_map(shards, mesh=mesh, in_specs=in_specs, out_specs=out_specs, check_vma=False)
```

profile of v0, /device:TPU:19, one launch (start us, length us, event | category | flops | bytes accessed | tf_op | source)
XLA Modules:
  0.0 597.3 jit_solution(13640709187362482184)
XLA Ops:
  11.5 11.3 %psum.22 = f32[2]{0:T(128)S(1)} all-reduce(f32[2]{0:T(128)S(1)} %select_reduce_fusion), channel_id=1, replica_groups=mesh['fibre'=8,'tm'=4] {'fibre'}, use_global_device_ids=true, to_apply=%region_2.0 | all-reduce | flops 2 | bytes 16 | tf_op jit(solution)/shard_map/psum | solution.py:47
  22.8 9.7 %multiply_convert_fusion.1 = (bf16[1024,512]{1,0:T(8,128)(2,1)S(1)}, bf16[1024,512]{1,0:T(8,128)(2,1)}) fusion(f32[1024]{0:T(1024)S(1)} %fusion.70, f32[1024]{0:T(1024)S(1)} %multiply_subtract_fusion), kind=kLoop, calls=%fused_computation.103 | loop fusion | flops 9437184 | bytes 2105344 | tf_op jit(solution)/shard_map/convert.36
  32.5 30.9 %all-reduce.3.cloned.1.call-done = f32[2,8192]{1,0:T(2,128)} async-done(((f32[2,8192]{1,0:T(2,128)}), f32[2,8192]{1,0:T(2,128)}) %all-reduce.3.cloned.1.call-update) | async-done | bytes 65552 | tf_op jit(solution)/shard_map/psum | solution.py:47
  63.3 4.4 fusion.50
  77.7 23.7 %collective-permute-done = bf16[128,8,1024]{2,1,0:T(8,128)(2,1)} collective-permute-done((bf16[128,8,1024]{2,1,0:T(8,128)(2,1)S(1)}, bf16[128,8,1024]{2,1,0:T(8,128)(2,1)}, u32[]{:S(2)}, u32[]{:S(2)}) %collective-permute-start) | collective-permute-done | bytes 2097184 | tf_op jit(solution)/shard_map/ppermute | solution.py:17
  101.4 3.9 pad_maximum_fusion
  108.3 325.0 %while.17 = (s32[]{:T(128)}, bf16[128,128,128]{2,1,0:T(8,128)(2,1)}, bf16[128,8,1024]{2,1,0:T(8,128)(2,1)S(1)}, bf16[256,8,1024]{2,1,0:T(8,128)(2,1)}, bf16[1024...) while((s32[]{:T(128)}, ...), condition=%wide.region_21.22_spmd, body=%wide.region_4.21_spmd.sunk | while | flops 314966048 | bytes 28574376 | solution.py:88
  108.3 17.9 %fusion.95 = (bf16[128,512]{1,0:T(8,128)(2,1)S(1)}, bf16[128,512]{1,0:T(8,128)(2,1)S(1)}, bf16[128,512]{1,0:T(8,128)(2,1)S(1)}, bf16[128,512]{1,0:T(8,128)(2,1)S...) fusion(bf16[256,8,1024]{2,1,0:T(8,128)(2,1)} %get-tuple-element, ...), kind=kLoop, calls=%fused_computation.61.clone.1 | loop fusion | flops 41943040 | bytes 20971556 | tf_op jit(solution)/shard_map/while/body/eval_jaxpr/reduce_sum | solution.py:74
  128.6 18.0 %fusion.95 = (bf16[128,512]{1,0:T(8,128)(2,1)S(1)}, bf16[128,512]{1,0:T(8,128)(2,1)S(1)}, bf16[128,512]{1,0:T(8,128)(2,1)S(1)}, bf16[128,512]{1,0:T(8,128)(2,1)S...) fusion(bf16[256,8,1024]{2,1,0:T(8,128)(2,1)} %get-tuple-element, ...), kind=kLoop, calls=%fused_computation.61.clone.1 | loop fusion | flops 41943040 | bytes 20971556 | tf_op jit(solution)/shard_map/while/body/eval_jaxpr/reduce_sum | solution.py:74
  148.9 18.1 %fusion.95 = (bf16[128,512]{1,0:T(8,128)(2,1)S(1)}, bf16[128,512]{1,0:T(8,128)(2,1)S(1)}, bf16[128,512]{1,0:T(8,128)(2,1)S(1)}, bf16[128,512]{1,0:T(8,128)(2,1)S...) fusion(bf16[256,8,1024]{2,1,0:T(8,128)(2,1)} %get-tuple-element, ...), kind=kLoop, calls=%fused_computation.61.clone.1 | loop fusion | flops 41943040 | bytes 20971556 | tf_op jit(solution)/shard_map/while/body/eval_jaxpr/reduce_sum | solution.py:74
  169.3 18.0 %fusion.95 = (bf16[128,512]{1,0:T(8,128)(2,1)S(1)}, bf16[128,512]{1,0:T(8,128)(2,1)S(1)}, bf16[128,512]{1,0:T(8,128)(2,1)S(1)}, bf16[128,512]{1,0:T(8,128)(2,1)S...) fusion(bf16[256,8,1024]{2,1,0:T(8,128)(2,1)} %get-tuple-element, ...), kind=kLoop, calls=%fused_computation.61.clone.1 | loop fusion | flops 41943040 | bytes 20971556 | tf_op jit(solution)/shard_map/while/body/eval_jaxpr/reduce_sum | solution.py:74
  189.6 18.2 %fusion.95 = (bf16[128,512]{1,0:T(8,128)(2,1)S(1)}, bf16[128,512]{1,0:T(8,128)(2,1)S(1)}, bf16[128,512]{1,0:T(8,128)(2,1)S(1)}, bf16[128,512]{1,0:T(8,128)(2,1)S...) fusion(bf16[256,8,1024]{2,1,0:T(8,128)(2,1)} %get-tuple-element, ...), kind=kLoop, calls=%fused_computation.61.clone.1 | loop fusion | flops 41943040 | bytes 20971556 | tf_op jit(solution)/shard_map/while/body/eval_jaxpr/reduce_sum | solution.py:74
  210.1 18.1 %fusion.95 = (bf16[128,512]{1,0:T(8,128)(2,1)S(1)}, bf16[128,512]{1,0:T(8,128)(2,1)S(1)}, bf16[128,512]{1,0:T(8,128)(2,1)S(1)}, bf16[128,512]{1,0:T(8,128)(2,1)S...) fusion(bf16[256,8,1024]{2,1,0:T(8,128)(2,1)} %get-tuple-element, ...), kind=kLoop, calls=%fused_computation.61.clone.1 | loop fusion | flops 41943040 | bytes 20971556 | tf_op jit(solution)/shard_map/while/body/eval_jaxpr/reduce_sum | solution.py:74
  230.5 17.9 %fusion.95 = (bf16[128,512]{1,0:T(8,128)(2,1)S(1)}, bf16[128,512]{1,0:T(8,128)(2,1)S(1)}, bf16[128,512]{1,0:T(8,128)(2,1)S(1)}, bf16[128,512]{1,0:T(8,128)(2,1)S...) fusion(bf16[256,8,1024]{2,1,0:T(8,128)(2,1)} %get-tuple-element, ...), kind=kLoop, calls=%fused_computation.61.clone.1 | loop fusion | flops 41943040 | bytes 20971556 | tf_op jit(solution)/shard_map/while/body/eval_jaxpr/reduce_sum | solution.py:74
  250.6 18.0 %fusion.95 = (bf16[128,512]{1,0:T(8,128)(2,1)S(1)}, bf16[128,512]{1,0:T(8,128)(2,1)S(1)}, bf16[128,512]{1,0:T(8,128)(2,1)S(1)}, bf16[128,512]{1,0:T(8,128)(2,1)S...) fusion(bf16[256,8,1024]{2,1,0:T(8,128)(2,1)} %get-tuple-element, ...), kind=kLoop, calls=%fused_computation.61.clone.1 | loop fusion | flops 41943040 | bytes 20971556 | tf_op jit(solution)/shard_map/while/body/eval_jaxpr/reduce_sum | solution.py:74
  270.9 18.3 %fusion.95 = (bf16[128,512]{1,0:T(8,128)(2,1)S(1)}, bf16[128,512]{1,0:T(8,128)(2,1)S(1)}, bf16[128,512]{1,0:T(8,128)(2,1)S(1)}, bf16[128,512]{1,0:T(8,128)(2,1)S...) fusion(bf16[256,8,1024]{2,1,0:T(8,128)(2,1)} %get-tuple-element, ...), kind=kLoop, calls=%fused_computation.61.clone.1 | loop fusion | flops 41943040 | bytes 20971556 | tf_op jit(solution)/shard_map/while/body/eval_jaxpr/reduce_sum | solution.py:74
  291.4 18.3 %fusion.95 = (bf16[128,512]{1,0:T(8,128)(2,1)S(1)}, bf16[128,512]{1,0:T(8,128)(2,1)S(1)}, bf16[128,512]{1,0:T(8,128)(2,1)S(1)}, bf16[128,512]{1,0:T(8,128)(2,1)S...) fusion(bf16[256,8,1024]{2,1,0:T(8,128)(2,1)} %get-tuple-element, ...), kind=kLoop, calls=%fused_computation.61.clone.1 | loop fusion | flops 41943040 | bytes 20971556 | tf_op jit(solution)/shard_map/while/body/eval_jaxpr/reduce_sum | solution.py:74
  312.0 18.1 %fusion.95 = (bf16[128,512]{1,0:T(8,128)(2,1)S(1)}, bf16[128,512]{1,0:T(8,128)(2,1)S(1)}, bf16[128,512]{1,0:T(8,128)(2,1)S(1)}, bf16[128,512]{1,0:T(8,128)(2,1)S...) fusion(bf16[256,8,1024]{2,1,0:T(8,128)(2,1)} %get-tuple-element, ...), kind=kLoop, calls=%fused_computation.61.clone.1 | loop fusion | flops 41943040 | bytes 20971556 | tf_op jit(solution)/shard_map/while/body/eval_jaxpr/reduce_sum | solution.py:74
  332.5 17.9 %fusion.95 = (bf16[128,512]{1,0:T(8,128)(2,1)S(1)}, bf16[128,512]{1,0:T(8,128)(2,1)S(1)}, bf16[128,512]{1,0:T(8,128)(2,1)S(1)}, bf16[128,512]{1,0:T(8,128)(2,1)S...) fusion(bf16[256,8,1024]{2,1,0:T(8,128)(2,1)} %get-tuple-element, ...), kind=kLoop, calls=%fused_computation.61.clone.1 | loop fusion | flops 41943040 | bytes 20971556 | tf_op jit(solution)/shard_map/while/body/eval_jaxpr/reduce_sum | solution.py:74
  352.6 17.9 %fusion.95 = (bf16[128,512]{1,0:T(8,128)(2,1)S(1)}, bf16[128,512]{1,0:T(8,128)(2,1)S(1)}, bf16[128,512]{1,0:T(8,128)(2,1)S(1)}, bf16[128,512]{1,0:T(8,128)(2,1)S...) fusion(bf16[256,8,1024]{2,1,0:T(8,128)(2,1)} %get-tuple-element, ...), kind=kLoop, calls=%fused_computation.61.clone.1 | loop fusion | flops 41943040 | bytes 20971556 | tf_op jit(solution)/shard_map/while/body/eval_jaxpr/reduce_sum | solution.py:74
  372.9 17.9 %fusion.95 = (bf16[128,512]{1,0:T(8,128)(2,1)S(1)}, bf16[128,512]{1,0:T(8,128)(2,1)S(1)}, bf16[128,512]{1,0:T(8,128)(2,1)S(1)}, bf16[128,512]{1,0:T(8,128)(2,1)S...) fusion(bf16[256,8,1024]{2,1,0:T(8,128)(2,1)} %get-tuple-element, ...), kind=kLoop, calls=%fused_computation.61.clone.1 | loop fusion | flops 41943040 | bytes 20971556 | tf_op jit(solution)/shard_map/while/body/eval_jaxpr/reduce_sum | solution.py:74
  393.1 17.8 %fusion.95 = (bf16[128,512]{1,0:T(8,128)(2,1)S(1)}, bf16[128,512]{1,0:T(8,128)(2,1)S(1)}, bf16[128,512]{1,0:T(8,128)(2,1)S(1)}, bf16[128,512]{1,0:T(8,128)(2,1)S...) fusion(bf16[256,8,1024]{2,1,0:T(8,128)(2,1)} %get-tuple-element, ...), kind=kLoop, calls=%fused_computation.61.clone.1 | loop fusion | flops 41943040 | bytes 20971556 | tf_op jit(solution)/shard_map/while/body/eval_jaxpr/reduce_sum | solution.py:74
  413.2 17.9 %fusion.95 = (bf16[128,512]{1,0:T(8,128)(2,1)S(1)}, bf16[128,512]{1,0:T(8,128)(2,1)S(1)}, bf16[128,512]{1,0:T(8,128)(2,1)S(1)}, bf16[128,512]{1,0:T(8,128)(2,1)S...) fusion(bf16[256,8,1024]{2,1,0:T(8,128)(2,1)} %get-tuple-element, ...), kind=kLoop, calls=%fused_computation.61.clone.1 | loop fusion | flops 41943040 | bytes 20971556 | tf_op jit(solution)/shard_map/while/body/eval_jaxpr/reduce_sum | solution.py:74
  433.4 154.3 %all-reduce.5.cloned.1.call-done = bf16[128,128,128]{2,1,0:T(8,128)(2,1)} async-done(((bf16[128,128,128]{2,1,0:T(8,128)(2,1)}), bf16[128,128,128]{2,1,0:T(8,128)(2,1)}) %all-reduce.5.cloned.1.call-update) | async-done | bytes 4194320 | tf_op jit(solution)/shard_map/psum | solution.py:91
  (186 shorter events, 56.2 us)
Async XLA Ops:
  6.5 56.8 %all-reduce.3.cloned.1.call-start = ((), (), s32[]{:S(2)}) async-start(), calls=%async_computation | async-start | bytes 131072 | tf_op jit(solution)/shard_map/psum | solution.py:47
  7.2 3.0 copy-start.1
  10.2 22.2 %copy-start = (f32[512]{0:T(512)S(1)}, f32[512]{0:T(512)}, u32[]{:S(2)}) copy-start(f32[512]{0:T(512)} %param.7) | copy-start | bytes 6148
  11.3 576.3 %all-reduce.5.cloned.1.call-start = ((), (), s32[]{:S(2)}) async-start(), calls=%async_computation.1 | async-start | bytes 8388608 | tf_op jit(solution)/shard_map/psum | solution.py:91
  74.6 26.8 %collective-permute-start = (bf16[128,8,1024]{2,1,0:T(8,128)(2,1)S(1)}, bf16[128,8,1024]{2,1,0:T(8,128)(2,1)}, u32[]{:S(2)}, u32[]{:S(2)}) collective-permute-start(bf16[128,8,1024]{2,1,0:T(8,128)(2,1)S(1)} %fusion.54), channel_id=1, source_target_pairs={{0,28},{4,0},{8,4},{12,8},{16,12},{20,16},{24,20},{28,24},{1,29},{... | collective-permute-start | bytes 6291464 | tf_op jit(solution)/shard_map/ppermute | solution.py:17
Sparse Core Ops, SparseCore 0:
  11.4 51.8 all-reduce.2
  433.5 154.0 all-reduce.4
where the time goes:
time: 600 us; the launch traced here: 597 us
  other arithmetic  322 us (54%)
  waiting for transfers between devices  209 us (35%)
  matrix products  29.5 us (5%)
  between operations  13.5 us (2%)
  blocking collectives  11.3 us (2%)
  local copies, waits for them, and re-layouts  8.91 us (1%)
    reduce_sum x16, other arithmetic, one_group(): real = jnp.sum(pr * qr + pi * qi, axis=1)  288 us
    psum x1, waiting for transfers between devices, shards(): lax.psum(partial_value.astype(jnp.bfloat16), 'tm').astype(jnp.float32)  154 us
    psum x1, waiting for transfers between devices, shards(): sec_sum, sec_count = lax.psum((sec_sum, sec_count), 'fibre')  30.9 us
    ppermute x1, waiting for transfers between devices, from_behind(): return lax.ppermute(value, axis, pairs)  23.7 us
    dot_general x16, matrix products, one_group(): jnp.dot(cross.reshape(chans * OBLK, 2 * nf), inverse, preferred_element_t...  20.5 us
    dynamic_update_slice x16, other arithmetic, one_group(): return lax.dynamic_update_slice_in_dim(buffer, lagged, first, 1)  12.3 us
  transfers between devices with their start and end apart: 3, of which 3 were waited for; matrix products, arithmetic and copies ran while one was open for 2% of the time, Pallas kernels for 0%

commit v1 on v0

v1 whole, which is shorter than its diff:
```python
import functools
import math

import jax
import jax.numpy as jnp
import ml_dtypes
import numpy as np
from jax import lax
from jax.experimental import pallas as pl
from jax.experimental.pallas import tpu as pltpu
from jax.sharding import PartitionSpec as P

OFFS = 128
LAGS = 128
NSEC = 2
LANE = 128
CHUNKS = 2
VMEM = 56 * 1024 * 1024
NT = (((1,), (1,)), ((), ()))
F32 = jnp.float32
BF16 = jnp.bfloat16


def tables(ns, nf):
    tick = np.arange(ns)
    freq = np.arange(nf)
    phase = (tick[:, None] * freq[None, :] % ns) * (2.0 * math.pi / ns)
    window = 0.5 - 0.5 * np.cos(tick * (2.0 * math.pi / ns))
    forward = np.concatenate(
        [window[:, None] * np.cos(phase), -window[:, None] * np.sin(phase)], axis=1
    )
    back = np.concatenate([np.cos(phase), -np.sin(phase)], axis=1)
    back[:, 0] *= math.sqrt(0.5)
    size = 2 * LAGS
    bins = np.arange(size // 2)
    turn = math.pi / size * ((2 * bins[:, None] + 1) * np.arange(size)[None, :] % (2 * size))
    segment = np.stack([np.cos(turn), -np.sin(turn)], axis=1).reshape(size, size)
    lag = np.stack([np.cos(turn), -np.sin(turn)], axis=1).reshape(size, size)[:, :LAGS]
    cast = lambda a: a.astype(np.float32).astype(ml_dtypes.bfloat16)
    return cast(forward.T), cast(back), cast(segment), cast(lag)


def section_sums(dead_ref, sec_ref, x_ref, out_ref):
    chans, wins, ns = x_ref.shape

    def body(c, carry):
        value = x_ref[c].astype(F32)
        live = 1 - dead_ref[c]
        sums, counts = carry
        weights = [jnp.where(sec_ref[c] == s, live, 0).astype(F32) for s in range(NSEC)]
        return (
            tuple(sums[s] + weights[s] * value for s in range(NSEC)),
            tuple(counts[s] + weights[s] for s in range(NSEC)),
        )

    zero = jnp.zeros((wins, ns), F32)
    sums, counts = lax.fori_loop(
        0, chans, body, ((zero,) * NSEC, (jnp.float32(0),) * NSEC), unroll=4
    )
    for s in range(NSEC):
        out_ref[s, :, :ns] = sums[s]
        out_ref[s, :, ns:] = jnp.zeros((wins, LANE), F32) + counts[s]


def segments_kernel(
    both, dead_ref, sec_ref, x_ref, tot_ref, gain_ref, fwd_ref, back_ref, seg_ref, *rest
):
    if both:
        a_ref, b_ref, common, clean, rows, spec, white, series, a_s, b_s = rest
    else:
        b_ref, common, clean, rows, spec, white, series, b_s = rest
    chans, wins, ns = x_ref.shape
    nfr = spec.shape[0]
    pitch = wins + 1
    size = seg_ref.shape[0]
    half = size // 2
    blocks = ns // half
    jw = blocks * wins
    jpitch = jw + 1
    for s in range(NSEC):
        common[s] = tot_ref[s, :, :ns] / jnp.maximum(tot_ref[s, :, ns : ns + 1], 1.0)

    def clean_channel(c, _):
        live = (1 - dead_ref[c]).astype(F32)
        value = (x_ref[c].astype(F32) - common[sec_ref[c]]) * live
        for t in range(ns // LANE):
            clean[t, pl.ds(c * pitch, wins), :] = value[:, t * LANE : (t + 1) * LANE]
        return 0

    lax.fori_loop(0, chans, clean_channel, 0, unroll=4)

    def pair(step, _):
        for i in range(2):
            w = step * 2 + i
            for t in range(ns // LANE):
                rows[i * chans : (i + 1) * chans, t * LANE : (t + 1) * LANE] = clean[
                    t, pl.ds(w, chans, stride=pitch), :
                ].astype(BF16)
        power = jnp.zeros((1, 2 * chans), F32)
        tile = 256
        for f in range(nfr // tile):
            s = lax.dot_general(
                fwd_ref[f * tile : (f + 1) * tile, :], rows[...], NT, preferred_element_type=F32
            )
            spec[f * tile : (f + 1) * tile, :] = s
            power = power + jnp.sum(s * s, axis=0, keepdims=True)
        level = lax.rsqrt(power / nfr + 1e-06)
        for i in range(2):
            white[:, i * chans : (i + 1) * chans] = (
                spec[:, i * chans : (i + 1) * chans]
                * gain_ref[...]
                * level[:, i * chans : (i + 1) * chans]
            ).astype(BF16)
        for t in range(ns // tile):
            p = jnp.dot(
                back_ref[t * tile : (t + 1) * tile, :], white[...], preferred_element_type=F32
            ).astype(BF16)
            series[half // 2 + t * tile : half // 2 + (t + 1) * tile, :] = p
        series[: half // 2, :] = series[ns : ns + half // 2, :]
        series[ns + half // 2 :, :] = series[half // 2 : half, :]
        for j in range(blocks):
            if both:
                a = jnp.dot(
                    seg_ref[...], series[j * half : j * half + size, :], preferred_element_type=F32
                )
            b = jnp.dot(
                seg_ref[:, :half],
                series[j * half + half // 2 : j * half + half // 2 + half, :],
                preferred_element_type=F32,
            )
            for i in range(2):
                at = j * wins + step * 2 + i
                if both:
                    a_s[pl.ds(at, size, stride=jpitch), :] = a[:, i * chans : (i + 1) * chans]
                b_s[pl.ds(at, size, stride=jpitch), :] = b[:, i * chans : (i + 1) * chans]
        return 0

    lax.fori_loop(0, wins // 2, pair, 0)

    def one_bin(k, _):
        def both_parts(ref):
            return jnp.concatenate(
                [
                    ref[pl.ds(2 * k * jpitch, jw), :],
                    ref[pl.ds((2 * k + 1) * jpitch, jw), :],
                ],
                axis=0,
            )

        if both:
            a_ref[k] = both_parts(a_s).T.astype(BF16)
        b_ref[k] = both_parts(b_s).astype(BF16)
        return 0

    lax.fori_loop(0, half, one_bin, 0, unroll=2)


def segments(both, flags, x, total, gain, fwd, back, seg):
    chans, wins, ns = x.shape
    nfr = fwd.shape[0]
    size = seg.shape[0]
    half = size // 2
    depth = ns // half * wins * 2
    smem = pl.BlockSpec(memory_space=pltpu.SMEM)
    vmem = pl.BlockSpec(memory_space=pltpu.VMEM)
    out = [jax.ShapeDtypeStruct((half, depth, chans), BF16)]
    stage = [pltpu.VMEM((size * (depth // 2 + 1), chans), F32)]
    if both:
        out = [jax.ShapeDtypeStruct((half, chans, depth), BF16)] + out
        stage = stage * 2
    return pl.pallas_call(
        functools.partial(segments_kernel, both),
        out_shape=out,
        in_specs=[smem, smem] + [vmem] * 6,
        out_specs=[vmem] * len(out),
        scratch_shapes=[
            pltpu.VMEM((NSEC, wins, ns), F32),
            pltpu.VMEM((ns // LANE, chans * (wins + 1), LANE), F32),
            pltpu.VMEM((2 * chans, ns), BF16),
            pltpu.VMEM((nfr, 2 * chans), F32),
            pltpu.VMEM((nfr, 2 * chans), BF16),
            pltpu.VMEM((ns + half, 2 * chans), BF16),
        ]
        + stage,
        compiler_params=pltpu.CompilerParams(vmem_limit_bytes=VMEM),
        cost_estimate=pl.CostEstimate(
            flops=2 * wins * chans * ns * (2 * nfr + 3 * size),
            bytes_accessed=16 * 1024 * 1024,
            transcendentals=0,
        ),
    )(flags[0], flags[1], x, total, gain, fwd, back, seg)


def stack_kernel(first, scale, a_ref, b_ref, h_ref, lag_ref, out_ref, cross, one):
    bins, count, depth = a_ref.shape
    chans = b_ref.shape[2]
    nfr = 2 * bins
    pitch = nfr + 1
    row = lax.broadcasted_iota(jnp.int32, one.shape[1:], 0)
    column = lax.broadcasted_iota(jnp.int32, one.shape[1:], 1)
    for t in range(2):
        one[t] = jnp.where(row == column + t * chans, 1.0, 0.0)

    def one_bin(k, _):
        left = a_ref[k]
        for t, ref in enumerate((b_ref, h_ref)):
            right = ref[k]
            turned = jnp.concatenate([-right[depth // 2 :], right[: depth // 2]], axis=0)
            cross[t, pl.ds(2 * k, count, stride=pitch), :] = jnp.dot(
                left, right, preferred_element_type=F32
            )
            cross[t, pl.ds(2 * k + 1, count, stride=pitch), :] = jnp.dot(
                left, turned, preferred_element_type=F32
            )
        return 0

    lax.fori_loop(0, bins, one_bin, 0, unroll=2)
    shares, _, share, nlag = out_ref.shape

    def one_channel(c, _):
        value = jnp.concatenate(
            [cross[t, pl.ds(c * pitch, nfr), :] for t in range(2)], axis=1
        ).astype(BF16)
        pick = jnp.concatenate(
            [one[t, pl.ds(first + c + 1, OFFS), :] for t in range(2)], axis=1
        ).astype(BF16)
        band = lax.dot_general(pick, value, NT, preferred_element_type=F32).astype(BF16)
        lagged = jnp.dot(band, lag_ref[...], preferred_element_type=F32) * scale
        lagged = lagged.astype(BF16)
        for s in range(shares):
            out_ref[s, c] = lagged[s * share : (s + 1) * share, :]
        return 0

    lax.fori_loop(0, count, one_channel, 0, unroll=2)


def stacks(index, count, shares, scale, a, b, h, lag):
    bins, chans, depth = a.shape
    nlag = lag.shape[1]
    whole = lambda arr: pl.BlockSpec(arr.shape, lambda i: (0,) * arr.ndim)
    return pl.pallas_call(
        functools.partial(stack_kernel, index * count, scale),
        grid=(1,),
        out_shape=jax.ShapeDtypeStruct((shares, count, OFFS // shares, nlag), BF16),
        in_specs=[
            pl.BlockSpec((bins, count, depth), lambda i: (0, index, 0)),
            whole(b),
            whole(h),
            whole(lag),
        ],
        out_specs=pl.BlockSpec(
            (shares, count, OFFS // shares, nlag), lambda i: (0, 0, 0, 0)
        ),
        scratch_shapes=[
            pltpu.VMEM((2, count * (2 * bins + 1), chans), F32),
            pltpu.VMEM((2, chans + OFFS, chans), F32),
        ],
        compiler_params=pltpu.CompilerParams(vmem_limit_bytes=VMEM),
        cost_estimate=pl.CostEstimate(
            flops=2 * count * bins * 2 * (2 * depth * chans + 2 * OFFS * chans + OFFS * nlag),
            bytes_accessed=12 * 1024 * 1024,
            transcendentals=0,
        ),
    )(a, b, h, lag)


def add_over(value, axis):
    count = lax.axis_size(axis)
    if count & (count - 1):
        return lax.psum(value, axis)
    bit = 1
    while bit < count:
        value = value + lax.ppermute(value, axis, [(i, i ^ bit) for i in range(count)])
        bit *= 2
    return value


def scatter_sum(parts, axis):
    count = lax.axis_size(axis)
    me = lax.axis_index(axis)

    def take(s):
        return lax.dynamic_index_in_dim(parts, s, 0, keepdims=False).astype(F32)

    total = take(me)
    for way in (1, -1):
        arrived = None
        place = me if way == 1 else count - 1 - me
        for step in range(count - 1):
            s = (count - 1 - step + place) % count
            s = s if way == 1 else count - 1 - s
            value = take(s)
            if arrived is not None:
                value = value + arrived.astype(F32)
            line = range(count) if way == 1 else range(count - 1, -1, -1)
            pairs = [(z, z + way) for z in list(line)[: step + 1]]
            arrived = lax.ppermute(value.astype(BF16), axis, pairs)
        total = total + arrived.astype(F32)
    return total


def shards(samples, band_gain, dead_flags, section_ids):
    chans, wins, ns = samples.shape
    nf = ns // 2
    blocks = lax.axis_size("fibre")
    groups = lax.axis_size("tm")
    fwd, back, seg, lag = [jnp.asarray(t) for t in tables(ns, nf)]
    flags = jnp.stack([dead_flags, section_ids])
    ahead = [((i + 1) % blocks, i) for i in range(blocks)]
    smem = pl.BlockSpec(memory_space=pltpu.SMEM)
    vmem = pl.BlockSpec(memory_space=pltpu.VMEM)
    sums = pl.pallas_call(
        section_sums,
        out_shape=jax.ShapeDtypeStruct((NSEC, wins, ns + LANE), F32),
        in_specs=[smem, smem, vmem],
        out_specs=vmem,
        compiler_params=pltpu.CompilerParams(vmem_limit_bytes=VMEM),
    )(dead_flags, section_ids, samples)
    total = add_over(sums, "fibre")
    next_flags = lax.ppermute(flags, "fibre", ahead)
    next_samples = lax.ppermute(samples, "fibre", ahead)
    gain = jnp.broadcast_to(jnp.concatenate([band_gain, band_gain])[:, None], (2 * nf, chans))
    a, b = segments(True, (dead_flags, section_ids), samples, total, gain, fwd, back, seg)
    (h,) = segments(False, next_flags, next_samples, total, gain, fwd, back, seg)
    scale = 2.0 / ns / LAGS / math.sqrt(nf * wins * groups)
    count = chans // CHUNKS
    out = []
    for index in range(CHUNKS):
        parts = stacks(index, count, groups, scale, a, b, h, lag)
        out.append(scatter_sum(parts, "tm"))
    return jnp.concatenate(out, axis=0)


def solution(mesh):
    in_specs = (P("fibre", "tm", None), P(), P("fibre"), P("fibre"))
    out_specs = P("fibre", "tm", None)
    return jax.shard_map(shards, mesh=mesh, in_specs=in_specs, out_specs=out_specs, check_vma=False)
```

time: 600 us -> 226 us (0.38)
  the two profiles are of different devices: /device:TPU:19 before, /device:TPU:10 now
where the time goes in v1:
time: 226 us
  Pallas kernels  111 us (49%)
  waiting for transfers between devices  63.3 us (28%)
  starting transfers between devices  29.7 us (13%)
  other arithmetic  15.5 us (7%)
  local copies, waits for them, and re-layouts  6.09 us (3%)
    pallas_call x2, Pallas kernels, stacks(): pl.pallas_call(functools.partial(stack_kernel, index * count, scale), gri...  70.7 us
    ppermute x12, waiting for transfers between devices, scatter_sum(): arrived = lax.ppermute(value.astype(BF16), axis, pairs)  39.9 us
    pallas_call x2, Pallas kernels, segments(): pl.pallas_call(functools.partial(segments_kernel, both), out_shape=out, i...  36.8 us
    ppermute x12, starting transfers between devices, scatter_sum(): arrived = lax.ppermute(value.astype(BF16), axis, pairs)  25.2 us
    ppermute x3, waiting for transfers between devices, add_over(): lax.ppermute(value, axis, [(i, i ^ bit) for i in range(count)])  23.4 us
    convert_element_type x6, other arithmetic, scatter_sum(): arrived = lax.ppermute(value.astype(BF16), axis, pairs)  9.69 us
  transfers between devices with their start and end apart: 17, of which 9 were waited for; matrix products, arithmetic and copies ran while one was open for 7% of the time, Pallas kernels for 27%

profile of v1, /device:TPU:10, one launch (start us, length us, event | category | flops | bytes accessed | tf_op | source)
XLA Modules:
  0.0 225.7 jit_solution(6345930395388374432)
XLA Ops:
  0.1 3.3 %shard_map.82 = f32[2,8,1152]{2,1,0:T(8,128)} custom-call(s32[128]{0:T(128)} %dead_ref.3, s32[128]{0:T(128)} %sec_ref.3, bf16[128,8,1024]{2,1,0:T(8,128)(2,1)} %x_ref.3), custom_call_target="tpu_custom_call" | custom-call | tf_op jit(solution)/shard_map/pallas_call | solution.py:312
  3.8 2.1 collective-permute-start.3
  8.2 20.1 %collective-permute-done.1 = f32[2,8,1152]{2,1,0:T(8,128)S(1)} collective-permute-done((f32[2,8,1152]{2,1,0:T(8,128)S(1)}, f32[2,8,1152]{2,1,0:T(8,128)S(1)}, u32[]{:S(2)}, u32[]{:S(2)}) %collective-permute-start.1) | collective-permute-done | bytes 73760 | tf_op jit(solution)/shard_map/ppermute | solution.py:273
  29.5 3.3 %collective-permute-done.2 = f32[2,8,1152]{2,1,0:T(8,128)S(1)} collective-permute-done((f32[2,8,1152]{2,1,0:T(8,128)S(1)}, f32[2,8,1152]{2,1,0:T(8,128)S(1)}, u32[]{:S(2)}, u32[]{:S(2)}) %collective-permute-start.2) | collective-permute-done | bytes 73760 | tf_op jit(solution)/shard_map/ppermute | solution.py:273
  34.4 22.9 %shard_map.83 = (bf16[128,128,128]{2,1,0:T(8,128)(2,1)}, bf16[128,128,128]{2,1,0:T(8,128)(2,1)}) custom-call(s32[128]{0:T(128)} %dead_ref.3, s32[128]{0:T(128)} %sec_ref.3, bf16[128,8,1024]{2,1,0:T(8,128)(2,1)} %x_ref.3, f32[2,8,1152]{2,1,0:T(8,128)} %add.131.tot_ref, f32[1024,128]{1,0:T(8,128)} %broadcast_in_dim.2.gain_ref, ...), custom_call_target="tpu_custom_call" | custom-call | flops 5905580032 | bytes 16777216 | tf_op jit(solution)/shard_map/pallas_call | solution.py:171
  57.3 14.0 %shard_map.84.h_ref = bf16[128,128,128]{2,1,0:T(8,128)(2,1)} custom-call(s32[128]{0:T(128)} %get-tuple-element.18.dead_ref, s32[128]{0:T(128)} %get-tuple-element.17.sec_ref, bf16[128,8,1024]{2,1,0:T(8,128)(2,1)} %collective-permute-done.4.x_ref, f32[2,8,1152]{2,1,0:T(8,128)} %add.131.tot_ref, f32[1024,128]{1,0:T(8,128)} %broadcast_in_dim.2.gain_ref, ...), custom_call_target="tpu_custom_call" | custom-call | flops 5905580032 | bytes 16777216 | tf_op jit(solution)/shard_map/pallas_call | solution.py:171
  71.2 35.3 %shard_map.85 = bf16[4,64,32,128]{3,2,1,0:T(8,128)(2,1)} custom-call(bf16[128,128,128]{2,1,0:T(8,128)(2,1)} %get-tuple-element.7.a_ref, bf16[128,128,128]{2,1,0:T(8,128)(2,1)} %get-tuple-element.8.b_ref, bf16[128,128,128]{2,1,0:T(8,128)(2,1)} %shard_map.84.h_ref, bf16[256,128]{1,0:T(8,128)(2,1)} %constant.104.clone.lag_ref), custom_call_target="tpu_custom_call" | custom-call | flops 2684354560 | bytes 12582912 | tf_op jit(solution)/shard_map/pallas_call | solution.py:241
  106.5 2.1 dynamic-slice_bitcast_fusion.3
  109.9 35.3 %shard_map.86 = bf16[4,64,32,128]{3,2,1,0:T(8,128)(2,1)} custom-call(bf16[128,128,128]{2,1,0:T(8,128)(2,1)} %get-tuple-element.7.a_ref, bf16[128,128,128]{2,1,0:T(8,128)(2,1)} %get-tuple-element.8.b_ref, bf16[128,128,128]{2,1,0:T(8,128)(2,1)} %shard_map.84.h_ref, bf16[256,128]{1,0:T(8,128)(2,1)} %constant.104.clone.lag_ref), custom_call_target="tpu_custom_call" | custom-call | flops 2684354560 | bytes 12582912 | tf_op jit(solution)/shard_map/pallas_call | solution.py:241
  145.2 2.4 %dynamic-slice_bitcast_fusion.1 = (bf16[64,32,128]{2,1,0:T(8,128)(2,1)}, bf16[64,32,128]{2,1,0:T(8,128)(2,1)}) fusion(bf16[4,64,32,128]{3,2,1,0:T(8,128)(2,1)} %shard_map.86, s32[]{:T(128)S(6)} %select_n.74, s32[]{:T(128)S(6)} %select_n.80), kind=kLoop, calls=%fused_computation.22 | loop fusion | bytes 2097160 | tf_op jit(solution)/shard_map/jit(dynamic_index_in_dim)/squeeze | solution.py:283
  151.6 2.9 %collective-permute-start.6 = (bf16[64,32,128]{2,1,0:T(8,128)(2,1)S(1)}, bf16[64,32,128]{2,1,0:T(8,128)(2,1)}, u32[]{:S(2)}, u32[]{:S(2)}) collective-permute-start(bf16[64,32,128]{2,1,0:T(8,128)(2,1)S(1)} %fusion.7), channel_id=1, source_target_pairs={{0,1},{1,2},{4,5},{5,6},{8,9},{9,10},{12,13},{13,14},{16,17},{17,1... | collective-permute-start | bytes 1572872 | tf_op jit(solution)/shard_map/ppermute | solution.py:297
  156.0 8.7 %collective-permute-done.11 = bf16[64,32,128]{2,1,0:T(8,128)(2,1)} collective-permute-done((bf16[64,32,128]{2,1,0:T(8,128)(2,1)}, bf16[64,32,128]{2,1,0:T(8,128)(2,1)}, u32[]{:S(2)}, u32[]{:S(2)}) %collective-permute-start.11) | collective-permute-done | bytes 524320 | tf_op jit(solution)/shard_map/ppermute | solution.py:297
  165.9 1.9 collective-permute-start.12
  167.9 8.1 %collective-permute-done.6 = bf16[64,32,128]{2,1,0:T(8,128)(2,1)} collective-permute-done((bf16[64,32,128]{2,1,0:T(8,128)(2,1)S(1)}, bf16[64,32,128]{2,1,0:T(8,128)(2,1)}, u32[]{:S(2)}, u32[]{:S(2)}) %collective-permute-start.6) | collective-permute-done | bytes 524320 | tf_op jit(solution)/shard_map/ppermute | solution.py:297
  176.0 2.8 %fusion.8 = (bf16[64,32,128]{2,1,0:T(8,128)(2,1)}, bf16[64,32,128]{2,1,0:T(8,128)(2,1)}) fusion(bf16[64,32,128]{2,1,0:T(8,128)(2,1)} %collective-permute-done.6, bf16[4,64,32,128]{3,2,1,0:T(8,128)(2,1)} %shard_map.85, s32[]{:T(128)S(6)} %select_n.70, bf16[64,32,128]{2,1,0:T(8,128)(2,1)} %collective-permute-done.8, s32[]{:T(128)S(6)} %select_n.78), kind=kLoop, calls=%fused_computation.18 | loop fusion | flops 2097152 | bytes 3145736 | tf_op jit(solution)/shard_map/convert_element_type | solution.py:297
  181.8 2.5 %fusion.3 = (bf16[64,32,128]{2,1,0:T(8,128)(2,1)}, bf16[64,32,128]{2,1,0:T(8,128)(2,1)}) fusion(bf16[64,32,128]{2,1,0:T(8,128)(2,1)} %collective-permute-done.12, bf16[4,64,32,128]{3,2,1,0:T(8,128)(2,1)S(1)} %copy-done, s32[]{:T(128)S(6)} %select_n.70, bf16[64,32,128]{2,1,0:T(8,128)(2,1)} %collective-permute-done.14, s32[]{:T(128)S(6)} %select_n.78), kind=kLoop, calls=%fused_computation.8 | loop fusion | flops 2097152 | bytes 3145736 | tf_op jit(solution)/shard_map/convert_element_type | solution.py:297
  185.5 4.6 %collective-permute-start.7 = (bf16[64,32,128]{2,1,0:T(8,128)(2,1)}, bf16[64,32,128]{2,1,0:T(8,128)(2,1)}, u32[]{:S(2)}, u32[]{:S(2)}) collective-permute-start(bf16[64,32,128]{2,1,0:T(8,128)(2,1)} %get-tuple-element.9), channel_id=1, source_target_pairs={{0,1},{1,2},{2,3},{4,5},{5,6},{6,7},{8,9},{9,10},{10,11},{12,13},{... | collective-permute-start | bytes 1572872 | tf_op jit(solution)/shard_map/ppermute | solution.py:297
  190.1 5.5 %collective-permute-done.9 = bf16[64,32,128]{2,1,0:T(8,128)(2,1)S(1)} collective-permute-done((bf16[64,32,128]{2,1,0:T(8,128)(2,1)}, bf16[64,32,128]{2,1,0:T(8,128)(2,1)S(1)}, u32[]{:S(2)}, u32[]{:S(2)}) %collective-permute-start.9) | collective-permute-done | bytes 524320 | tf_op jit(solution)/shard_map/ppermute | solution.py:297
  195.6 2.0 fusion.6
  199.5 3.9 %collective-permute-start.13 = (bf16[64,32,128]{2,1,0:T(8,128)(2,1)}, bf16[64,32,128]{2,1,0:T(8,128)(2,1)}, u32[]{:S(2)}, u32[]{:S(2)}) collective-permute-start(bf16[64,32,128]{2,1,0:T(8,128)(2,1)} %get-tuple-element.13), channel_id=1, source_target_pairs={{0,1},{1,2},{2,3},{4,5},{5,6},{6,7},{8,9},{9,10},{10,11},{12,13},{... | collective-permute-start | bytes 1572872 | tf_op jit(solution)/shard_map/ppermute | solution.py:297
  203.4 3.4 %collective-permute-done.15 = bf16[64,32,128]{2,1,0:T(8,128)(2,1)S(1)} collective-permute-done((bf16[64,32,128]{2,1,0:T(8,128)(2,1)}, bf16[64,32,128]{2,1,0:T(8,128)(2,1)S(1)}, u32[]{:S(2)}, u32[]{:S(2)}) %collective-permute-start.15) | collective-permute-done | bytes 524320 | tf_op jit(solution)/shard_map/ppermute | solution.py:297
  207.0 1.9 collective-permute-start.16
  208.9 8.5 %collective-permute-done.10 = bf16[64,32,128]{2,1,0:T(8,128)(2,1)} collective-permute-done((bf16[64,32,128]{2,1,0:T(8,128)(2,1)}, bf16[64,32,128]{2,1,0:T(8,128)(2,1)}, u32[]{:S(2)}, u32[]{:S(2)}) %collective-permute-start.10) | collective-permute-done | bytes 524320 | tf_op jit(solution)/shard_map/ppermute | solution.py:297
  219.0 3.9 %collective-permute-done.16 = bf16[64,32,128]{2,1,0:T(8,128)(2,1)S(1)} collective-permute-done((bf16[64,32,128]{2,1,0:T(8,128)(2,1)S(1)}, bf16[64,32,128]{2,1,0:T(8,128)(2,1)S(1)}, u32[]{:S(2)}, u32[]{:S(2)}) %collective-permute-start.16) | collective-permute-done | bytes 524320 | tf_op jit(solution)/shard_map/ppermute | solution.py:297
  (41 shorter events, 24.2 us)
Async XLA Ops:
  0.0 3.8 %copy-start.3 = (s32[128]{0:T(128)S(1)}, s32[128]{0:T(128)}, u32[]{:S(2)}) copy-start(s32[128]{0:T(128)} %sec_ref.3) | copy-start | bytes 1540
  0.0 3.8 %copy-start.2 = (s32[128]{0:T(128)S(1)}, s32[128]{0:T(128)}, u32[]{:S(2)}) copy-start(s32[128]{0:T(128)} %dead_ref.3) | copy-start | bytes 1540
  0.0 8.2 %copy-start.1 = (f32[512]{0:T(512)S(1)}, f32[512]{0:T(512)}, u32[]{:S(2)}) copy-start(f32[512]{0:T(512)} %param.9) | copy-start | bytes 6148
  0.0 57.3 %collective-permute-start.4 = (bf16[128,8,1024]{2,1,0:T(8,128)(2,1)}, bf16[128,8,1024]{2,1,0:T(8,128)(2,1)}, u32[]{:S(2)}, u32[]{:S(2)}) collective-permute-start(bf16[128,8,1024]{2,1,0:T(8,128)(2,1)} %x_ref.3), channel_id=1, source_target_pairs={{4,0},{8,4},{12,8},{16,12},{20,16},{24,20},{28,24},{0,28},{5,1},{9... | collective-permute-start | bytes 6291464 | tf_op jit(solution)/shard_map/ppermute | solution.py:321
  3.3 2.6 %collective-permute-start = (f32[2,8,1152]{2,1,0:T(8,128)}, f32[2,8,1152]{2,1,0:T(8,128)S(1)}, u32[]{:S(2)}, u32[]{:S(2)}) collective-permute-start(f32[2,8,1152]{2,1,0:T(8,128)} %shard_map.82), channel_id=1, source_target_pairs={{0,4},{4,0},{8,12},{12,8},{16,20},{20,16},{24,28},{28,24},{1,5},{5... | collective-permute-start | bytes 221192 | tf_op jit(solution)/shard_map/ppermute | solution.py:273
  3.8 25.1 %collective-permute-start.3 = (s32[2,128]{1,0:T(2,128)S(1)}, s32[2,128]{1,0:T(2,128)S(1)}, u32[]{:S(2)}, u32[]{:S(2)}) collective-permute-start(s32[2,128]{1,0:T(2,128)S(1)} %pad_add_fusion), channel_id=1, source_target_pairs={{4,0},{8,4},{12,8},{16,12},{20,16},{24,20},{28,24},{0,28},{5,1},{9... | collective-permute-start | bytes 3080 | tf_op jit(solution)/shard_map/ppermute | solution.py:320
  6.8 21.5 %collective-permute-start.1 = (f32[2,8,1152]{2,1,0:T(8,128)S(1)}, f32[2,8,1152]{2,1,0:T(8,128)S(1)}, u32[]{:S(2)}, u32[]{:S(2)}) collective-permute-start(f32[2,8,1152]{2,1,0:T(8,128)S(1)} %add.129), channel_id=1, source_target_pairs={{0,8},{4,12},{8,0},{12,4},{16,24},{20,28},{24,16},{28,20},{1,9},{5... | collective-permute-start | bytes 221192 | tf_op jit(solution)/shard_map/ppermute | solution.py:273
  28.3 4.4 %collective-permute-start.2 = (f32[2,8,1152]{2,1,0:T(8,128)S(1)}, f32[2,8,1152]{2,1,0:T(8,128)S(1)}, u32[]{:S(2)}, u32[]{:S(2)}) collective-permute-start(f32[2,8,1152]{2,1,0:T(8,128)S(1)} %add.130), channel_id=1, source_target_pairs={{0,16},{4,20},{8,24},{12,28},{16,0},{20,4},{24,8},{28,12},{1,17},{... | collective-permute-start | bytes 221192 | tf_op jit(solution)/shard_map/ppermute | solution.py:273
  108.6 41.8 %collective-permute-start.5 = (bf16[64,32,128]{2,1,0:T(8,128)(2,1)S(1)}, bf16[64,32,128]{2,1,0:T(8,128)(2,1)S(1)}, u32[]{:S(2)}, u32[]{:S(2)}) collective-permute-start(bf16[64,32,128]{2,1,0:T(8,128)(2,1)S(1)} %get-tuple-element.11), channel_id=1, source_target_pairs={{0,1},{4,5},{8,9},{12,13},{16,17},{20,21},{24,25},{28,29}} | collective-permute-start | bytes 1572872 | tf_op jit(solution)/shard_map/ppermute | solution.py:297
  145.2 19.5 %copy-start = (bf16[4,64,32,128]{3,2,1,0:T(8,128)(2,1)S(1)}, bf16[4,64,32,128]{3,2,1,0:T(8,128)(2,1)}, u32[]{:S(2)}) copy-start(bf16[4,64,32,128]{3,2,1,0:T(8,128)(2,1)} %shard_map.86) | copy-start | bytes 6291460
  147.7 17.1 %collective-permute-start.11 = (bf16[64,32,128]{2,1,0:T(8,128)(2,1)}, bf16[64,32,128]{2,1,0:T(8,128)(2,1)}, u32[]{:S(2)}, u32[]{:S(2)}) collective-permute-start(bf16[64,32,128]{2,1,0:T(8,128)(2,1)} %get-tuple-element.15), channel_id=1, source_target_pairs={{0,1},{4,5},{8,9},{12,13},{16,17},{20,21},{24,25},{28,29}} | collective-permute-start | bytes 1572872 | tf_op jit(solution)/shard_map/ppermute | solution.py:297
  149.0 18.9 %collective-permute-start.8 = (bf16[64,32,128]{2,1,0:T(8,128)(2,1)}, bf16[64,32,128]{2,1,0:T(8,128)(2,1)}, u32[]{:S(2)}, u32[]{:S(2)}) collective-permute-start(bf16[64,32,128]{2,1,0:T(8,128)(2,1)} %get-tuple-element.12), channel_id=1, source_target_pairs={{3,2},{7,6},{11,10},{15,14},{19,18},{23,22},{27,26},{31,30}} | collective-permute-start | bytes 1572872 | tf_op jit(solution)/shard_map/ppermute | solution.py:297
  151.6 24.4 %collective-permute-start.6 = (bf16[64,32,128]{2,1,0:T(8,128)(2,1)S(1)}, bf16[64,32,128]{2,1,0:T(8,128)(2,1)}, u32[]{:S(2)}, u32[]{:S(2)}) collective-permute-start(bf16[64,32,128]{2,1,0:T(8,128)(2,1)S(1)} %fusion.7), channel_id=1, source_target_pairs={{0,1},{1,2},{4,5},{5,6},{8,9},{9,10},{12,13},{13,14},{16,17},{17,1... | collective-permute-start | bytes 1572872 | tf_op jit(solution)/shard_map/ppermute | solution.py:297
  154.5 25.5 %collective-permute-start.14 = (bf16[64,32,128]{2,1,0:T(8,128)(2,1)}, bf16[64,32,128]{2,1,0:T(8,128)(2,1)}, u32[]{:S(2)}, u32[]{:S(2)}) collective-permute-start(bf16[64,32,128]{2,1,0:T(8,128)(2,1)} %get-tuple-element.16), channel_id=1, source_target_pairs={{3,2},{7,6},{11,10},{15,14},{19,18},{23,22},{27,26},{31,30}} | collective-permute-start | bytes 1572872 | tf_op jit(solution)/shard_map/ppermute | solution.py:297
  165.9 15.8 %collective-permute-start.12 = (bf16[64,32,128]{2,1,0:T(8,128)(2,1)S(1)}, bf16[64,32,128]{2,1,0:T(8,128)(2,1)}, u32[]{:S(2)}, u32[]{:S(2)}) collective-permute-start(bf16[64,32,128]{2,1,0:T(8,128)(2,1)S(1)} %fusion.2), channel_id=1, source_target_pairs={{0,1},{1,2},{4,5},{5,6},{8,9},{9,10},{12,13},{13,14},{16,17},{17,1... | collective-permute-start | bytes 1572872 | tf_op jit(solution)/shard_map/ppermute | solution.py:297
  178.7 16.9 %collective-permute-start.9 = (bf16[64,32,128]{2,1,0:T(8,128)(2,1)}, bf16[64,32,128]{2,1,0:T(8,128)(2,1)S(1)}, u32[]{:S(2)}, u32[]{:S(2)}) collective-permute-start(bf16[64,32,128]{2,1,0:T(8,128)(2,1)} %get-tuple-element.10), channel_id=1, source_target_pairs={{3,2},{2,1},{7,6},{6,5},{11,10},{10,9},{15,14},{14,13},{19,18},{18... | collective-permute-start | bytes 1572872 | tf_op jit(solution)/shard_map/ppermute | solution.py:297
  184.2 22.6 %collective-permute-start.15 = (bf16[64,32,128]{2,1,0:T(8,128)(2,1)}, bf16[64,32,128]{2,1,0:T(8,128)(2,1)S(1)}, u32[]{:S(2)}, u32[]{:S(2)}) collective-permute-start(bf16[64,32,128]{2,1,0:T(8,128)(2,1)} %get-tuple-element.14), channel_id=1, source_target_pairs={{3,2},{2,1},{7,6},{6,5},{11,10},{10,9},{15,14},{14,13},{19,18},{18... | collective-permute-start | bytes 1572872 | tf_op jit(solution)/shard_map/ppermute | solution.py:297
  185.5 23.4 %collective-permute-start.7 = (bf16[64,32,128]{2,1,0:T(8,128)(2,1)}, bf16[64,32,128]{2,1,0:T(8,128)(2,1)}, u32[]{:S(2)}, u32[]{:S(2)}) collective-permute-start(bf16[64,32,128]{2,1,0:T(8,128)(2,1)} %get-tuple-element.9), channel_id=1, source_target_pairs={{0,1},{1,2},{2,3},{4,5},{5,6},{6,7},{8,9},{9,10},{10,11},{12,13},{... | collective-permute-start | bytes 1572872 | tf_op jit(solution)/shard_map/ppermute | solution.py:297
  197.6 19.8 %collective-permute-start.10 = (bf16[64,32,128]{2,1,0:T(8,128)(2,1)}, bf16[64,32,128]{2,1,0:T(8,128)(2,1)}, u32[]{:S(2)}, u32[]{:S(2)}) collective-permute-start(bf16[64,32,128]{2,1,0:T(8,128)(2,1)} %fusion.6), channel_id=1, source_target_pairs={{3,2},{2,1},{1,0},{7,6},{6,5},{5,4},{11,10},{10,9},{9,8},{15,14},{... | collective-permute-start | bytes 1572872 | tf_op jit(solution)/shard_map/ppermute | solution.py:297
  199.5 19.5 %collective-permute-start.13 = (bf16[64,32,128]{2,1,0:T(8,128)(2,1)}, bf16[64,32,128]{2,1,0:T(8,128)(2,1)}, u32[]{:S(2)}, u32[]{:S(2)}) collective-permute-start(bf16[64,32,128]{2,1,0:T(8,128)(2,1)} %get-tuple-element.13), channel_id=1, source_target_pairs={{0,1},{1,2},{2,3},{4,5},{5,6},{6,7},{8,9},{9,10},{10,11},{12,13},{... | collective-permute-start | bytes 1572872 | tf_op jit(solution)/shard_map/ppermute | solution.py:297
  207.0 15.9 %collective-permute-start.16 = (bf16[64,32,128]{2,1,0:T(8,128)(2,1)S(1)}, bf16[64,32,128]{2,1,0:T(8,128)(2,1)S(1)}, u32[]{:S(2)}, u32[]{:S(2)}) collective-permute-start(bf16[64,32,128]{2,1,0:T(8,128)(2,1)S(1)} %fusion.1), channel_id=1, source_target_pairs={{3,2},{2,1},{1,0},{7,6},{6,5},{5,4},{11,10},{10,9},{9,8},{15,14},{... | collective-permute-start | bytes 1572872 | tf_op jit(solution)/shard_map/ppermute | solution.py:297

commit v2 on v1

--- a/solution.py
+++ b/solution.py
@@ -35,7 +35,7 @@
     bins = np.arange(size // 2)
     turn = math.pi / size * ((2 * bins[:, None] + 1) * np.arange(size)[None, :] % (2 * size))
     segment = np.stack([np.cos(turn), -np.sin(turn)], axis=1).reshape(size, size)
-    lag = np.stack([np.cos(turn), -np.sin(turn)], axis=1).reshape(size, size)[:, :LAGS]
+    lag = np.stack([np.cos(turn), -np.sin(turn)], axis=1).reshape(size, size)[:, :LAGS].T
     cast = lambda a: a.astype(np.float32).astype(ml_dtypes.bfloat16)
     return cast(forward.T), cast(back), cast(segment), cast(lag)
 
@@ -87,7 +87,7 @@
             clean[t, pl.ds(c * pitch, wins), :] = value[:, t * LANE : (t + 1) * LANE]
         return 0
 
-    lax.fori_loop(0, chans, clean_channel, 0, unroll=4)
+    lax.fori_loop(0, chans, clean_channel, 0, unroll=8)
 
     def pair(step, _):
         for i in range(2):
@@ -97,7 +97,7 @@
                     t, pl.ds(w, chans, stride=pitch), :
                 ].astype(BF16)
         power = jnp.zeros((1, 2 * chans), F32)
-        tile = 256
+        tile = ns
         for f in range(nfr // tile):
             s = lax.dot_general(
                 fwd_ref[f * tile : (f + 1) * tile, :], rows[...], NT, preferred_element_type=F32
@@ -141,18 +141,18 @@
         def both_parts(ref):
             return jnp.concatenate(
                 [
-                    ref[pl.ds(2 * k * jpitch, jw), :],
-                    ref[pl.ds((2 * k + 1) * jpitch, jw), :],
+                    ref[pl.ds(2 * k * jpitch, jw), :].astype(BF16),
+                    ref[pl.ds((2 * k + 1) * jpitch, jw), :].astype(BF16),
                 ],
                 axis=0,
             )
 
         if both:
-            a_ref[k] = both_parts(a_s).T.astype(BF16)
-        b_ref[k] = both_parts(b_s).astype(BF16)
-        return 0
-
-    lax.fori_loop(0, half, one_bin, 0, unroll=2)
+            a_ref[k] = both_parts(a_s).T
+        b_ref[k] = both_parts(b_s)
+        return 0
+
+    lax.fori_loop(0, half, one_bin, 0, unroll=8)
 
 
 def segments(both, flags, x, total, gain, fwd, back, seg):
@@ -203,18 +203,17 @@
 
     def one_bin(k, _):
         left = a_ref[k]
-        for t, ref in enumerate((b_ref, h_ref)):
-            right = ref[k]
-            turned = jnp.concatenate([-right[depth // 2 :], right[: depth // 2]], axis=0)
-            cross[t, pl.ds(2 * k, count, stride=pitch), :] = jnp.dot(
-                left, right, preferred_element_type=F32
-            )
-            cross[t, pl.ds(2 * k + 1, count, stride=pitch), :] = jnp.dot(
-                left, turned, preferred_element_type=F32
-            )
-        return 0
-
-    lax.fori_loop(0, bins, one_bin, 0, unroll=2)
+        right = jnp.concatenate([b_ref[k], h_ref[k]], axis=1)
+        turned = jnp.concatenate([-right[depth // 2 :], right[: depth // 2]], axis=0)
+        for part, operand in enumerate((right, turned)):
+            value = jnp.dot(left, operand, preferred_element_type=F32)
+            for t in range(2):
+                cross[t, pl.ds(2 * k + part, count, stride=pitch), :] = value[
+                    :, t * chans : (t + 1) * chans
+                ]
+        return 0
+
+    lax.fori_loop(0, bins, one_bin, 0, unroll=8)
     shares, _, share, nlag = out_ref.shape
 
     def one_channel(c, _):
@@ -224,19 +223,19 @@
         pick = jnp.concatenate(
             [one[t, pl.ds(first + c + 1, OFFS), :] for t in range(2)], axis=1
         ).astype(BF16)
-        band = lax.dot_general(pick, value, NT, preferred_element_type=F32).astype(BF16)
-        lagged = jnp.dot(band, lag_ref[...], preferred_element_type=F32) * scale
+        lagged = jnp.dot(lag_ref[...], value, preferred_element_type=F32) * scale
         lagged = lagged.astype(BF16)
+        band = lax.dot_general(pick, lagged, NT, preferred_element_type=F32).astype(BF16)
         for s in range(shares):
-            out_ref[s, c] = lagged[s * share : (s + 1) * share, :]
-        return 0
-
-    lax.fori_loop(0, count, one_channel, 0, unroll=2)
+            out_ref[s, c] = band[s * share : (s + 1) * share, :]
+        return 0
+
+    lax.fori_loop(0, count, one_channel, 0, unroll=4)
 
 
 def stacks(index, count, shares, scale, a, b, h, lag):
     bins, chans, depth = a.shape
-    nlag = lag.shape[1]
+    nlag = lag.shape[0]
     whole = lambda arr: pl.BlockSpec(arr.shape, lambda i: (0,) * arr.ndim)
     return pl.pallas_call(
         functools.partial(stack_kernel, index * count, scale),
@@ -275,30 +274,6 @@
     return value
 
 
-def scatter_sum(parts, axis):
-    count = lax.axis_size(axis)
-    me = lax.axis_index(axis)
-
-    def take(s):
-        return lax.dynamic_index_in_dim(parts, s, 0, keepdims=False).astype(F32)
-
-    total = take(me)
-    for way in (1, -1):
-        arrived = None
-        place = me if way == 1 else count - 1 - me
-        for step in range(count - 1):
-            s = (count - 1 - step + place) % count
-            s = s if way == 1 else count - 1 - s
-            value = take(s)
-            if arrived is not None:
-                value = value + arrived.astype(F32)
-            line = range(count) if way == 1 else range(count - 1, -1, -1)
-            pairs = [(z, z + way) for z in list(line)[: step + 1]]
-            arrived = lax.ppermute(value.astype(BF16), axis, pairs)
-        total = total + arrived.astype(F32)
-    return total
-
-
 def shards(samples, band_gain, dead_flags, section_ids):
     chans, wins, ns = samples.shape
     nf = ns // 2
@@ -318,7 +293,8 @@
     )(dead_flags, section_ids, samples)
     total = add_over(sums, "fibre")
     next_flags = lax.ppermute(flags, "fibre", ahead)
-    next_samples = lax.ppermute(samples, "fibre", ahead)
+    total, to_send = lax.optimization_barrier((total, samples))
+    next_samples = lax.ppermute(to_send, "fibre", ahead)
     gain = jnp.broadcast_to(jnp.concatenate([band_gain, band_gain])[:, None], (2 * nf, chans))
     a, b = segments(True, (dead_flags, section_ids), samples, total, gain, fwd, back, seg)
     (h,) = segments(False, next_flags, next_samples, total, gain, fwd, back, seg)
@@ -327,7 +303,7 @@
     out = []
     for index in range(CHUNKS):
         parts = stacks(index, count, groups, scale, a, b, h, lag)
-        out.append(scatter_sum(parts, "tm"))
+        out.append(lax.psum_scatter(parts, "tm", scatter_dimension=0).astype(F32))
     return jnp.concatenate(out, axis=0)
 
 

time: 226 us -> 208 us (0.920)
  the two profiles are of different devices: /device:TPU:10 before, /device:TPU:19 now
where the time goes in v2:
time: 208 us; the launch traced here: 206 us
  waiting for transfers between devices  102 us (49%)
  Pallas kernels  78.1 us (38%)
  between operations  13.4 us (6%)
  starting transfers between devices  5.1 us (2%)
  other arithmetic  4.21 us (2%)
  local copies, waits for them, and re-layouts  2.92 us (1%)
    reduce_scatter x2, waiting for transfers between devices, shards(): out.append(lax.psum_scatter(parts, 'tm', scatter_dimension=0).astype(F32))  71.3 us
    pallas_call x2, Pallas kernels, segments(): pl.pallas_call(functools.partial(segments_kernel, both), out_shape=out, i...  40.2 us
    pallas_call x2, Pallas kernels, stacks(): pl.pallas_call(functools.partial(stack_kernel, index * count, scale), gri...  34.5 us
    ppermute x1, waiting for transfers between devices, shards(): next_flags = lax.ppermute(flags, 'fibre', ahead)  24.8 us
    ppermute x3, waiting for transfers between devices, add_over(): lax.ppermute(value, axis, [(i, i ^ bit) for i in range(count)])  6.04 us
  transfers between devices with their start and end apart: 7, of which 6 were waited for; matrix products, arithmetic and copies ran while one was open for 1% of the time, Pallas kernels for 19%

profile of v2, /device:TPU:19, one launch (start us, length us, event | category | flops | bytes accessed | tf_op | source)
XLA Modules:
  0.0 205.9 jit_solution(16683262136525990702)
XLA Ops:
  6.5 0.0 reduce-scatter.3.cloned.1.call-start
  6.6 3.4 %shard_map.82 = f32[2,8,1152]{2,1,0:T(8,128)} custom-call(s32[128]{0:T(128)} %dead_ref.3, s32[128]{0:T(128)} %sec_ref.3, bf16[128,8,1024]{2,1,0:T(8,128)(2,1)} %x_ref.3), custom_call_target="tpu_custom_call" | custom-call | tf_op jit(solution)/shard_map/pallas_call | solution.py:287
  10.0 0.7 collective-permute-start
  10.7 1.1 collective-permute-done
  11.8 0.9 add.13
  12.7 0.3 collective-permute-start.1
  13.0 2.9 %collective-permute-done.1 = f32[2,8,1152]{2,1,0:T(8,128)S(1)} collective-permute-done((f32[2,8,1152]{2,1,0:T(8,128)S(1)}, f32[2,8,1152]{2,1,0:T(8,128)S(1)}, u32[]{:S(2)}, u32[]{:S(2)}) %collective-permute-start.1) | collective-permute-done | bytes 73760 | tf_op jit(solution)/shard_map/ppermute | solution.py:272
  16.0 1.3 collective-permute-start.2
  17.3 2.0 collective-permute-done.2
  19.2 0.6 add.15.tot_ref
  19.9 2.7 %collective-permute-start.4 = (bf16[128,8,1024]{2,1,0:T(8,128)(2,1)S(1)}, bf16[128,8,1024]{2,1,0:T(8,128)(2,1)S(1)}, u32[]{:S(2)}, u32[]{:S(2)}) collective-permute-start(bf16[128,8,1024]{2,1,0:T(8,128)(2,1)S(1)} %copy-done), channel_id=1, source_target_pairs={{4,0},{8,4},{12,8},{16,12},{20,16},{24,20},{28,24},{0,28},{5,1},{9... | collective-permute-start | bytes 6291464 | tf_op jit(solution)/shard_map/ppermute | solution.py:297
  22.5 0.1 collective-permute-start.3
  22.6 24.8 %collective-permute-done.3 = s32[2,128]{1,0:T(2,128)S(1)} collective-permute-done((s32[2,128]{1,0:T(2,128)S(1)}, s32[2,128]{1,0:T(2,128)S(1)}, u32[]{:S(2)}, u32[]{:S(2)}) %collective-permute-start.3) | collective-permute-done | bytes 1056 | tf_op jit(solution)/shard_map/ppermute | solution.py:295
  47.4 0.6 slice_bitcast_fusion
  48.0 1.0 broadcast_in_dim.2.gain_ref
  49.0 22.2 %shard_map.83 = (bf16[128,128,128]{2,1,0:T(8,128)(2,1)}, bf16[128,128,128]{2,1,0:T(8,128)(2,1)}) custom-call(s32[128]{0:T(128)} %dead_ref.3, s32[128]{0:T(128)} %sec_ref.3, bf16[128,8,1024]{2,1,0:T(8,128)(2,1)} %x_ref.3, f32[2,8,1152]{2,1,0:T(8,128)} %add.15.tot_ref, f32[1024,128]{1,0:T(8,128)} %broadcast_in_dim.2.gain_ref, ...), custom_call_target="tpu_custom_call" | custom-call | flops 5905580032 | bytes 16777216 | tf_op jit(solution)/shard_map/pallas_call | solution.py:171
  71.2 1.3 copy-done.4
  72.5 18.0 %shard_map.84.h_ref = bf16[128,128,128]{2,1,0:T(8,128)(2,1)} custom-call(s32[128]{0:T(128)} %get-tuple-element.14.dead_ref, s32[128]{0:T(128)} %get-tuple-element.13.sec_ref, bf16[128,8,1024]{2,1,0:T(8,128)(2,1)} %copy-done.4, f32[2,8,1152]{2,1,0:T(8,128)} %add.15.tot_ref, f32[1024,128]{1,0:T(8,128)} %broadcast_in_dim.2.gain_ref, ...), custom_call_target="tpu_custom_call" | custom-call | flops 5905580032 | bytes 16777216 | tf_op jit(solution)/shard_map/pallas_call | solution.py:171
  90.5 17.2 %shard_map.85 = bf16[4,64,32,128]{3,2,1,0:T(8,128)(2,1)} custom-call(bf16[128,128,128]{2,1,0:T(8,128)(2,1)} %get-tuple-element.10.a_ref, bf16[128,128,128]{2,1,0:T(8,128)(2,1)} %get-tuple-element.11.b_ref, bf16[128,128,128]{2,1,0:T(8,128)(2,1)} %shard_map.84.h_ref, bf16[128,256]{1,0:T(8,128)(2,1)} %constant.11.clone.lag_ref), custom_call_target="tpu_custom_call" | custom-call | flops 2684354560 | bytes 12582912 | tf_op jit(solution)/shard_map/pallas_call | solution.py:240
  107.8 0.0 reduce-scatter.5.cloned.1.call-start
  107.8 17.3 %shard_map.86 = bf16[4,64,32,128]{3,2,1,0:T(8,128)(2,1)} custom-call(bf16[128,128,128]{2,1,0:T(8,128)(2,1)} %get-tuple-element.10.a_ref, bf16[128,128,128]{2,1,0:T(8,128)(2,1)} %get-tuple-element.11.b_ref, bf16[128,128,128]{2,1,0:T(8,128)(2,1)} %shard_map.84.h_ref, bf16[128,256]{1,0:T(8,128)(2,1)} %constant.11.clone.lag_ref), custom_call_target="tpu_custom_call" | custom-call | flops 2684354560 | bytes 12582912 | tf_op jit(solution)/shard_map/pallas_call | solution.py:240
  125.1 25.7 %reduce-scatter.3.cloned.1.call-done = bf16[1,64,32,128]{3,2,1,0:T(8,128)(2,1)} async-done(((bf16[4,64,32,128]{3,2,1,0:T(8,128)(2,1)}), bf16[1,64,32,128]{3,2,1,0:T(8,128)(2,1)}) %reduce-scatter.3.cloned.1.call-update) | async-done | bytes 524304 | tf_op jit(solution)/shard_map/reduce_scatter | solution.py:306
  150.8 45.6 %reduce-scatter.5.cloned.1.call-done = bf16[1,64,32,128]{3,2,1,0:T(8,128)(2,1)} async-done(((bf16[4,64,32,128]{3,2,1,0:T(8,128)(2,1)}), bf16[1,64,32,128]{3,2,1,0:T(8,128)(2,1)}) %reduce-scatter.5.cloned.1.call-update) | async-done | bytes 524304 | tf_op jit(solution)/shard_map/reduce_scatter | solution.py:306
  196.4 2.7 %maximum_convert_fusion = f32[128,32,128]{2,1,0:T(8,128)} fusion(bf16[64,32,128]{2,1,0:T(8,128)(2,1)} %bitcast.9, bf16[64,32,128]{2,1,0:T(8,128)(2,1)} %bitcast.8), kind=kLoop, calls=%fused_computation | loop fusion | flops 1048576 | bytes 3145728 | tf_op jit(solution)/shard_map/concatenate | solution.py:307
  (15 shorter events, 0.1 us)
Async XLA Ops:
  6.5 16.0 %copy-start.2 = (s32[128]{0:T(128)S(1)}, s32[128]{0:T(128)}, u32[]{:S(2)}) copy-start(s32[128]{0:T(128)} %dead_ref.3) | copy-start | bytes 1540
  6.5 16.0 %copy-start.3 = (s32[128]{0:T(128)S(1)}, s32[128]{0:T(128)}, u32[]{:S(2)}) copy-start(s32[128]{0:T(128)} %sec_ref.3) | copy-start | bytes 1540
  6.5 13.3 %copy-start = (bf16[128,8,1024]{2,1,0:T(8,128)(2,1)S(1)}, bf16[128,8,1024]{2,1,0:T(8,128)(2,1)}, u32[]{:S(2)}) copy-start(bf16[128,8,1024]{2,1,0:T(8,128)(2,1)} %x_ref.3) | copy-start | bytes 6291460
  6.5 16.1 %copy-start.1 = (f32[512]{0:T(512)S(1)}, f32[512]{0:T(512)}, u32[]{:S(2)}) copy-start(f32[512]{0:T(512)} %param.9) | copy-start | bytes 6148
  6.5 144.2 %reduce-scatter.3.cloned.1.call-start = ((), (), s32[]{:S(2)}) async-start(), calls=%async_computation.2 | async-start | bytes 2621440 | tf_op jit(solution)/shard_map/reduce_scatter | solution.py:306
  10.0 1.8 collective-permute-start
  12.7 3.3 %collective-permute-start.1 = (f32[2,8,1152]{2,1,0:T(8,128)S(1)}, f32[2,8,1152]{2,1,0:T(8,128)S(1)}, u32[]{:S(2)}, u32[]{:S(2)}) collective-permute-start(f32[2,8,1152]{2,1,0:T(8,128)S(1)} %add.13), channel_id=1, source_target_pairs={{0,8},{4,12},{8,0},{12,4},{16,24},{20,28},{24,16},{28,20},{1,9},{5... | collective-permute-start | bytes 221192 | tf_op jit(solution)/shard_map/ppermute | solution.py:272
  16.0 3.3 %collective-permute-start.2 = (f32[2,8,1152]{2,1,0:T(8,128)S(1)}, f32[2,8,1152]{2,1,0:T(8,128)S(1)}, u32[]{:S(2)}, u32[]{:S(2)}) collective-permute-start(f32[2,8,1152]{2,1,0:T(8,128)S(1)} %add.14), channel_id=1, source_target_pairs={{0,16},{4,20},{8,24},{12,28},{16,0},{20,4},{24,8},{28,12},{1,17},{... | collective-permute-start | bytes 221192 | tf_op jit(solution)/shard_map/ppermute | solution.py:272
  19.9 51.3 %collective-permute-start.4 = (bf16[128,8,1024]{2,1,0:T(8,128)(2,1)S(1)}, bf16[128,8,1024]{2,1,0:T(8,128)(2,1)S(1)}, u32[]{:S(2)}, u32[]{:S(2)}) collective-permute-start(bf16[128,8,1024]{2,1,0:T(8,128)(2,1)S(1)} %copy-done), channel_id=1, source_target_pairs={{4,0},{8,4},{12,8},{16,12},{20,16},{24,20},{28,24},{0,28},{5,1},{9... | collective-permute-start | bytes 6291464 | tf_op jit(solution)/shard_map/ppermute | solution.py:297
  22.5 24.8 %collective-permute-start.3 = (s32[2,128]{1,0:T(2,128)S(1)}, s32[2,128]{1,0:T(2,128)S(1)}, u32[]{:S(2)}, u32[]{:S(2)}) collective-permute-start(s32[2,128]{1,0:T(2,128)S(1)} %pad_add_fusion), channel_id=1, source_target_pairs={{4,0},{8,4},{12,8},{16,12},{20,16},{24,20},{28,24},{0,28},{5,1},{9... | collective-permute-start | bytes 3080 | tf_op jit(solution)/shard_map/ppermute | solution.py:295
  71.2 1.3 copy-start.4
  107.8 88.6 %reduce-scatter.5.cloned.1.call-start = ((), (), s32[]{:S(2)}) async-start(), calls=%async_computation.3 | async-start | bytes 2621440 | tf_op jit(solution)/shard_map/reduce_scatter | solution.py:306
Sparse Core Ops, SparseCore 0:
  107.9 42.8 reduce-scatter.2
  153.2 43.1 reduce-scatter.4

commit v3 on v2

v3 whole, which is shorter than its diff:
```python
import functools
import math

import jax
import jax.numpy as jnp
import ml_dtypes
import numpy as np
from jax import lax
from jax.experimental import pallas as pl
from jax.experimental.pallas import tpu as pltpu
from jax.sharding import PartitionSpec as P

OFFS = 128
LAGS = 128
NSEC = 2
LANE = 128
VMEM = 56 * 1024 * 1024
NT = (((1,), (1,)), ((), ()))
F32 = jnp.float32
BF16 = jnp.bfloat16


def tables(ns, nf):
    tick = np.arange(ns)
    freq = np.arange(nf)
    phase = (tick[:, None] * freq[None, :] % ns) * (2.0 * math.pi / ns)
    window = 0.5 - 0.5 * np.cos(tick * (2.0 * math.pi / ns))
    forward = np.concatenate(
        [window[:, None] * np.cos(phase), -window[:, None] * np.sin(phase)], axis=1
    )
    back = np.concatenate([np.cos(phase), -np.sin(phase)], axis=1)
    back[:, 0] *= math.sqrt(0.5)
    size = 2 * LAGS
    bins = np.arange(size // 2)
    turn = math.pi / size * ((2 * bins[:, None] + 1) * np.arange(size)[None, :] % (2 * size))
    segment = np.stack([np.cos(turn), -np.sin(turn)], axis=1).reshape(size, size)
    lag = np.stack([np.cos(turn), -np.sin(turn)], axis=1).reshape(size, size)[:, :LAGS].T
    cast = lambda a: a.astype(np.float32).astype(ml_dtypes.bfloat16)
    return cast(forward.T), cast(back), cast(segment), cast(lag)


def section_sums(dead_ref, sec_ref, x_ref, out_ref):
    chans, wins, ns = x_ref.shape

    def body(c, carry):
        value = x_ref[c].astype(F32)
        live = 1 - dead_ref[c]
        sums, counts = carry
        weights = [jnp.where(sec_ref[c] == s, live, 0).astype(F32) for s in range(NSEC)]
        return (
            tuple(sums[s] + weights[s] * value for s in range(NSEC)),
            tuple(counts[s] + weights[s] for s in range(NSEC)),
        )

    zero = jnp.zeros((wins, ns), F32)
    sums, counts = lax.fori_loop(
        0, chans, body, ((zero,) * NSEC, (jnp.float32(0),) * NSEC), unroll=8
    )
    for s in range(NSEC):
        out_ref[s, :, :ns] = sums[s]
        out_ref[s, :, ns:] = jnp.zeros((wins, LANE), F32) + counts[s]


def segments_kernel(
    sets, info_ref, dead_ref, sec_ref, tot_ref, gain_ref, fwd_ref, back_ref, seg_ref, *rest
):
    pieces = rest[: len(sets)]
    a_ref, b_ref, common, clean, rows, spec, white, series, a_s, b_s = rest[len(sets) :]
    _, wins, ns = pieces[0].shape
    chans = b_ref.shape[2]
    nfr = spec.shape[0]
    pitch = wins + 1
    size = seg_ref.shape[0]
    half = size // 2
    blocks = ns // half
    jw = blocks * wins
    jpitch = jw + 1
    want = info_ref[0] != 0
    for g in range(tot_ref.shape[0]):
        for s in range(NSEC):
            count = jnp.maximum(tot_ref[g, s, :, ns : ns + 1], 1.0)
            common[g * NSEC + s] = tot_ref[g, s, :, :ns] / count

    for number, (group, x_ref) in enumerate(zip(sets, pieces)):
        base = info_ref[1 + number]

        def clean_channel(c, _):
            at = base + c
            live = (1 - dead_ref[at]).astype(F32)
            value = (x_ref[c].astype(F32) - common[group * NSEC + sec_ref[at]]) * live
            for t in range(ns // LANE):
                clean[t, pl.ds(at * pitch, wins), :] = value[:, t * LANE : (t + 1) * LANE]
            return 0

        lax.fori_loop(0, x_ref.shape[0], clean_channel, 0, unroll=8)

    def pair(step, _):
        for i in range(2):
            w = step * 2 + i
            for t in range(ns // LANE):
                rows[i * chans : (i + 1) * chans, t * LANE : (t + 1) * LANE] = clean[
                    t, pl.ds(w, chans, stride=pitch), :
                ].astype(BF16)
        s = lax.dot_general(fwd_ref[...], rows[...], NT, preferred_element_type=F32)
        spec[...] = s
        power = jnp.sum(s * s, axis=0, keepdims=True)
        level = lax.rsqrt(power / nfr + 1e-06)
        for i in range(2):
            white[:, i * chans : (i + 1) * chans] = (
                spec[:, i * chans : (i + 1) * chans]
                * gain_ref[...]
                * level[:, i * chans : (i + 1) * chans]
            ).astype(BF16)
        series[half // 2 : ns + half // 2, :] = jnp.dot(
            back_ref[...], white[...], preferred_element_type=F32
        ).astype(BF16)
        series[: half // 2, :] = series[ns : ns + half // 2, :]
        series[ns + half // 2 :, :] = series[half // 2 : half, :]
        for j in range(blocks):
            b = jnp.dot(
                seg_ref[:, :half],
                series[j * half + half // 2 : j * half + half // 2 + half, :],
                preferred_element_type=F32,
            )
            for i in range(2):
                at = j * wins + step * 2 + i
                b_s[pl.ds(at, size, stride=jpitch), :] = b[:, i * chans : (i + 1) * chans]

        @pl.when(want)
        def _():
            for j in range(blocks):
                a = jnp.dot(
                    seg_ref[...], series[j * half : j * half + size, :], preferred_element_type=F32
                )
                for i in range(2):
                    at = j * wins + step * 2 + i
                    a_s[pl.ds(at, size, stride=jpitch), :] = a[:, i * chans : (i + 1) * chans]

        return 0

    lax.fori_loop(0, wins // 2, pair, 0)

    def both_parts(ref, k):
        return jnp.concatenate(
            [ref[pl.ds((2 * k + part) * jpitch, jw), :].astype(BF16) for part in range(2)], axis=0
        )

    def second(k, _):
        b_ref[k] = both_parts(b_s, k)
        return 0

    lax.fori_loop(0, half, second, 0, unroll=8)

    @pl.when(want)
    def _():
        def first(k, _):
            a_ref[k] = both_parts(a_s, k).T
            return 0

        lax.fori_loop(0, half, first, 0, unroll=8)


def segments(sets, info, flags, pieces, total, gain, fwd, back, seg):
    chans = sum(x.shape[0] for x in pieces)
    _, wins, ns = pieces[0].shape
    nfr = fwd.shape[0]
    size = seg.shape[0]
    half = size // 2
    depth = ns // half * wins * 2
    smem = pl.BlockSpec(memory_space=pltpu.SMEM)
    vmem = pl.BlockSpec(memory_space=pltpu.VMEM)
    return pl.pallas_call(
        functools.partial(segments_kernel, sets),
        out_shape=[
            jax.ShapeDtypeStruct((half, chans, depth), BF16),
            jax.ShapeDtypeStruct((half, depth, chans), BF16),
        ],
        in_specs=[smem] * 3 + [vmem] * (5 + len(pieces)),
        out_specs=[vmem] * 2,
        scratch_shapes=[
            pltpu.VMEM((total.shape[0] * NSEC, wins, ns), F32),
            pltpu.VMEM((ns // LANE, chans * (wins + 1), LANE), F32),
            pltpu.VMEM((2 * chans, ns), BF16),
            pltpu.VMEM((nfr, 2 * chans), F32),
            pltpu.VMEM((nfr, 2 * chans), BF16),
            pltpu.VMEM((ns + half, 2 * chans), BF16),
            pltpu.VMEM((size * (depth // 2 + 1), chans), F32),
            pltpu.VMEM((size * (depth // 2 + 1), chans), F32),
        ],
        compiler_params=pltpu.CompilerParams(vmem_limit_bytes=VMEM),
        cost_estimate=pl.CostEstimate(
            flops=2 * wins * chans * ns * (2 * nfr + 3 * size),
            bytes_accessed=16 * 1024 * 1024,
            transcendentals=0,
        ),
    )(info, flags[0], flags[1], total, gain, fwd, back, seg, *pieces)


def stack_kernel(
    scale, odd_ref, a0_ref, a1_ref, ah_ref, b0_ref, b1_ref, bh_ref, lag_ref, out_ref, cross, one
):
    bins, count, depth = a0_ref.shape
    chans = b0_ref.shape[2]
    nfr = 2 * bins
    pitch = nfr + 1
    odd = odd_ref[0] != 0
    span = chans + count
    row = lax.broadcasted_iota(jnp.int32, one.shape[1:], 0)
    column = lax.broadcasted_iota(jnp.int32, one.shape[1:], 1)
    turned = jnp.where(row < count, row + chans, row - count)
    place = row + (turned - row) * odd_ref[0]
    for t in range(2):
        one[t] = jnp.where(place == column + t * chans, 1.0, 0.0)

    def bins_with(left_of):
        def one_bin(k, _):
            left = left_of(k)
            part = depth // 2
            swapped = jnp.concatenate(
                [left[:, part:depth], -left[:, :part], left[:, depth + part :], -left[:, depth : depth + part]],
                axis=1,
            )
            halo = bh_ref[k]
            other = jnp.concatenate([halo[:, count:], halo[:, :count]], axis=1)
            right = jnp.concatenate(
                [
                    jnp.concatenate([b0_ref[k], halo], axis=1),
                    jnp.concatenate([b1_ref[k], other], axis=1),
                ],
                axis=0,
            )
            value = jnp.dot(
                jnp.concatenate([left, swapped], axis=0), right, preferred_element_type=F32
            )
            for p in range(2):
                for t in range(2):
                    cross[t, pl.ds(2 * k + p, count, stride=pitch), :] = value[
                        p * count : (p + 1) * count, t * chans : (t + 1) * chans
                    ]
            return 0

        lax.fori_loop(0, bins, one_bin, 0, unroll=8)

    @pl.when(odd)
    def _():
        bins_with(lambda k: jnp.concatenate([ah_ref[k, :count], ah_ref[k, count:]], axis=1))

    @pl.when(jnp.logical_not(odd))
    def _():
        bins_with(lambda k: jnp.concatenate([a0_ref[k], a1_ref[k]], axis=1))

    shares, _, share, nlag = out_ref.shape

    def one_channel(c, _):
        value = jnp.concatenate(
            [cross[t, pl.ds(c * pitch, nfr), :] for t in range(2)], axis=1
        ).astype(BF16)
        pick = jnp.concatenate(
            [one[t, pl.ds(c + 1, OFFS), :] for t in range(2)], axis=1
        ).astype(BF16)
        lagged = jnp.dot(lag_ref[...], value, preferred_element_type=F32) * scale
        lagged = lagged.astype(BF16)
        band = lax.dot_general(pick, lagged, NT, preferred_element_type=F32).astype(BF16)
        for s in range(shares):
            out_ref[s, c] = band[s * share : (s + 1) * share, :]
        return 0

    lax.fori_loop(0, count, one_channel, 0, unroll=4)


def stacks(shares, scale, odd, a0, a1, ah, b0, b1, bh, lag):
    bins, chans, depth = a0.shape
    count = chans // 2
    nlag = lag.shape[0]
    whole = lambda arr: pl.BlockSpec(arr.shape, lambda i: (0,) * arr.ndim)
    lower = pl.BlockSpec((bins, count, depth), lambda i: (0, 0, 0))
    return pl.pallas_call(
        functools.partial(stack_kernel, scale),
        grid=(1,),
        out_shape=jax.ShapeDtypeStruct((shares, count, OFFS // shares, nlag), BF16),
        in_specs=[
            pl.BlockSpec(memory_space=pltpu.SMEM),
            lower,
            lower,
            whole(ah),
            whole(b0),
            whole(b1),
            whole(bh),
            whole(lag),
        ],
        out_specs=pl.BlockSpec((shares, count, OFFS // shares, nlag), lambda i: (0, 0, 0, 0)),
        scratch_shapes=[
            pltpu.VMEM((2, count * (2 * bins + 1), chans), F32),
            pltpu.VMEM((2, chans + count, chans), F32),
        ],
        compiler_params=pltpu.CompilerParams(vmem_limit_bytes=VMEM),
        cost_estimate=pl.CostEstimate(
            flops=2 * count * bins * 4 * (2 * depth * chans + 2 * OFFS * chans),
            bytes_accessed=20 * 1024 * 1024,
            transcendentals=0,
        ),
    )(odd, a0, a1, ah, b0, b1, bh, lag)


def add_over(value, axis):
    count = lax.axis_size(axis)
    if count & (count - 1):
        return lax.psum(value, axis)
    bit = 1
    while bit < count:
        value = value + lax.ppermute(value, axis, [(i, i ^ bit) for i in range(count)])
        bit *= 2
    return value


def shards(samples, band_gain, dead_flags, section_ids):
    chans, wins, ns = samples.shape
    nf = ns // 2
    count = chans // 2
    blocks = lax.axis_size("fibre")
    groups = lax.axis_size("tm")
    odd = lax.axis_index("tm") % 2
    fwd, back, seg, lag = [jnp.asarray(t) for t in tables(ns, nf)]
    gain = jnp.broadcast_to(jnp.concatenate([band_gain, band_gain])[:, None], (2 * nf, chans))
    swap = [(z, z ^ 1) for z in range(groups)]
    both = ("fibre", "tm")
    halo_pairs = [
        (b * groups + z, (b + (1 if z % 2 else -1)) % blocks * groups + z)
        for b in range(blocks)
        for z in range(groups)
    ]
    smem = pl.BlockSpec(memory_space=pltpu.SMEM)
    vmem = pl.BlockSpec(memory_space=pltpu.VMEM)

    def lower_or_upper(array, upper):
        return lax.dynamic_slice_in_dim(array, upper * count, count, array.ndim - 1 if array.ndim == 2 else 0)

    flags = jnp.stack([dead_flags, section_ids])
    halo_flags = lax.ppermute(lower_or_upper(flags, odd), both, halo_pairs)
    sums = pl.pallas_call(
        section_sums,
        out_shape=jax.ShapeDtypeStruct((NSEC, wins, ns + LANE), F32),
        in_specs=[smem, smem, vmem],
        out_specs=vmem,
        compiler_params=pltpu.CompilerParams(vmem_limit_bytes=VMEM),
    )(dead_flags, section_ids, samples)
    sums, first_half = lax.optimization_barrier((sums, lower_or_upper(samples, 1 - odd)))
    their_sums = lax.ppermute(sums, "tm", swap)
    their_first = lax.ppermute(first_half, "tm", swap)
    their_sums, halo_flags, second_half = lax.optimization_barrier(
        (their_sums, halo_flags, lower_or_upper(samples, odd))
    )
    their_second = lax.ppermute(second_half, "tm", swap)
    total = add_over(jnp.stack([sums, their_sums]), "fibre")
    total, own_half = lax.optimization_barrier((total, lower_or_upper(samples, odd)))
    halo = lax.ppermute(own_half, both, halo_pairs)
    their_halo = lax.ppermute(their_first, both, halo_pairs)

    even = 1 - odd
    zero = jnp.zeros((), jnp.int32)
    own_flags = (dead_flags, section_ids)
    twice = (jnp.tile(halo_flags[0], 2), jnp.tile(halo_flags[1], 2))
    parts = (total, gain, fwd, back, seg)
    a0, b0 = segments((0,), jnp.stack([even, zero]), own_flags, (samples,), *parts)
    ah, bh = segments(
        (0, 1), jnp.stack([odd, zero, zero + count]), twice, (halo, their_halo), *parts
    )
    a1, b1 = segments(
        (1, 1),
        jnp.stack([even, odd * count, even * count]),
        own_flags,
        (their_first, their_second),
        *parts,
    )
    scale = 2.0 / ns / LAGS / math.sqrt(nf * wins * groups)
    found = stacks(groups, scale, odd[None], a0, a1, ah, b0, b1, bh, lag)
    arrived = []
    for d in range(groups):
        pairs = [
            (b * groups + z, (b - z % 2) % blocks * groups + (z ^ d))
            for b in range(blocks)
            for z in range(groups)
        ]
        share = lax.dynamic_index_in_dim(found, lax.axis_index("tm") ^ d, 0, keepdims=False)
        arrived.append(lax.ppermute(share, both, pairs).astype(F32))
    same = sum(arrived[2::2], arrived[0])
    other = sum(arrived[3::2], arrived[1])
    return jnp.concatenate(
        [jnp.where(odd == 0, same, other), jnp.where(odd == 0, other, same)], axis=0
    )


def solution(mesh):
    in_specs = (P("fibre", "tm", None), P(), P("fibre"), P("fibre"))
    out_specs = P("fibre", "tm", None)
    return jax.shard_map(shards, mesh=mesh, in_specs=in_specs, out_specs=out_specs, check_vma=False)
```

time: 208 us -> 176 us (0.85)
  waiting for transfers between devices: 102 us -> 55.9 us
  between operations: 13.4 us -> 0.1 us
  Pallas kernels: 78.1 us -> 90.5 us
  starting transfers between devices: 5.1 us -> 13.1 us
  local copies, waits for them, and re-layouts: 2.92 us -> 8.94 us
  other arithmetic: 4.21 us -> 7.13 us
    reduce_scatter x2 -> x0, waiting for transfers between devices: 71.3 us -> none  [shards(): out.append(lax.psum_scatter(parts, 'tm', scatter_dimension=0).astype(F32))]
    ppermute x2 -> x10, waiting for transfers between devices: 24.8 us -> 50.8 us  [the longest x4 43.6 us: shards(): arrived.append(lax.ppermute(share, both, pairs).astype(F32))]
    pallas_call x4, Pallas kernels: 74.7 us -> 87.4 us  [the longest x3 65 us: segments(): pl.pallas_call(functools.partial(segments_kernel, sets), out_shape=[jax.S...]
    ppermute x2 -> x10, starting transfers between devices: 2.72 us -> 11.6 us  [the longest x4 3.5 us: shards(): arrived.append(lax.ppermute(share, both, pairs).astype(F32))]
    another operation x0 -> x4, other arithmetic: none -> 2.8 us  [the longest x1 0.9 us: shards(): total = add_over(jnp.stack([sums, their_sums]), 'fibre')]
    squeeze x1, local copies, waits for them, and re-layouts: 0.57 us -> 2.91 us  [shards(): lax.dynamic_index_in_dim(found, lax.axis_index('tm') ^ d, 0, keepdims=False)]
  transfers between devices with their start and end apart: 7 -> 13, of which waited for: 6 -> 8; matrix products, arithmetic and copies ran while one was open for 1% -> 4% of each run, Pallas kernels for 19% -> 26%
where the time goes in v3:
time: 176 us
  Pallas kernels  90.5 us (51%)
  waiting for transfers between devices  55.9 us (32%)
  starting transfers between devices  13.1 us (7%)
  local copies, waits for them, and re-layouts  8.94 us (5%)
  other arithmetic  7.13 us (4%)
    pallas_call x3, Pallas kernels, segments(): pl.pallas_call(functools.partial(segments_kernel, sets), out_shape=[jax.S...  65 us
    ppermute x4, waiting for transfers between devices, shards(): arrived.append(lax.ppermute(share, both, pairs).astype(F32))  43.6 us
    pallas_call x1, Pallas kernels, stacks(): pl.pallas_call(functools.partial(stack_kernel, scale), grid=(1,), out_sha...  22.3 us
    ppermute x1, waiting for transfers between devices, shards(): their_first = lax.ppermute(first_half, 'tm', swap)  5.5 us
    ppermute x3, waiting for transfers between devices, add_over(): lax.ppermute(value, axis, [(i, i ^ bit) for i in range(count)])  5.07 us
  transfers between devices with their start and end apart: 13, of which 8 were waited for; matrix products, arithmetic and copies ran while one was open for 4% of the time, Pallas kernels for 26%

profile of v3, /device:TPU:19, one launch (start us, length us, event | category | flops | bytes accessed | tf_op | source)
XLA Modules:
  0.0 175.6 jit_solution(12376676136923674042)
XLA Ops:
  0.0 1.7 constant_dynamic-slice_fusion
  1.8 3.1 %shard_map.82 = f32[2,8,1152]{2,1,0:T(8,128)} custom-call(s32[128]{0:T(128)} %dead_ref.5, s32[128]{0:T(128)} %sec_ref.5, bf16[128,8,1024]{2,1,0:T(8,128)(2,1)} %rest_0_.1), custom_call_target="tpu_custom_call" | custom-call | tf_op jit(solution)/shard_map/pallas_call | solution.py:340
  4.9 1.3 collective-permute-start
  7.2 1.3 collective-permute-start.5
  8.5 1.7 collective-permute-done.1
  14.2 1.3 collective-permute-start.6
  15.6 3.0 %collective-permute-done.3 = f32[2,2,8,1152]{3,2,1,0:T(8,128)S(1)} collective-permute-done((f32[2,2,8,1152]{3,2,1,0:T(8,128)S(1)}, f32[2,2,8,1152]{3,2,1,0:T(8,128)S(1)}, u32[]{:S(2)}, u32[]{:S(2)}) %collective-permute-start.3) | collective-permute-done | bytes 147488 | tf_op jit(solution)/shard_map/ppermute | solution.py:311
  19.5 1.3 collective-permute-start.4
  22.0 1.9 %collective-permute-done.4 = f32[2,2,8,1152]{3,2,1,0:T(8,128)S(1)} collective-permute-done((f32[2,2,8,1152]{3,2,1,0:T(8,128)S(1)}, f32[2,2,8,1152]{3,2,1,0:T(8,128)S(1)}, u32[]{:S(2)}, u32[]{:S(2)}) %collective-permute-start.4) | collective-permute-done | bytes 147488 | tf_op jit(solution)/shard_map/ppermute | solution.py:311
  24.7 1.9 %collective-permute-start.7 = (bf16[64,8,1024]{2,1,0:T(8,128)(2,1)S(1)}, bf16[64,8,1024]{2,1,0:T(8,128)(2,1)S(1)}, u32[]{:S(2)}, u32[]{:S(2)}) collective-permute-start(bf16[64,8,1024]{2,1,0:T(8,128)(2,1)S(1)} %get-tuple-element.26), channel_id=1, source_target_pairs={{0,28},{1,5},{2,30},{3,7},{4,0},{5,9},{6,2},{7,11},{8,4},{9,13},{1... | collective-permute-start | bytes 3145736 | tf_op jit(solution)/shard_map/ppermute | solution.py:356
  26.5 5.5 %collective-permute-done.5.rest_0_ = bf16[64,8,1024]{2,1,0:T(8,128)(2,1)} collective-permute-done((bf16[64,8,1024]{2,1,0:T(8,128)(2,1)S(1)}, bf16[64,8,1024]{2,1,0:T(8,128)(2,1)}, u32[]{:S(2)}, u32[]{:S(2)}) %collective-permute-start.5) | collective-permute-done | bytes 1048608 | tf_op jit(solution)/shard_map/ppermute | solution.py:349
  32.0 1.3 collective-permute-start.8
  33.4 1.0 broadcast_in_dim.10.gain_ref
  34.4 22.9 %shard_map.83 = (bf16[128,128,128]{2,1,0:T(8,128)(2,1)}, bf16[128,128,128]{2,1,0:T(8,128)(2,1)}) custom-call(s32[2]{0:T(128)} %pad_add_fusion.1.info_ref, s32[128]{0:T(128)} %dead_ref.5, s32[128]{0:T(128)} %sec_ref.5, f32[2,2,8,1152]{3,2,1,0:T(8,128)} %add.45.tot_ref, f32[1024,128]{1,0:T(8,128)} %broadcast_in_dim.10.gain_ref, ...), custom_call_target="tpu_custom_call" | custom-call | flops 5905580032 | bytes 16777216 | tf_op jit(solution)/shard_map/pallas_call | solution.py:172
  57.3 22.8 %shard_map.84 = (bf16[128,128,128]{2,1,0:T(8,128)(2,1)}, bf16[128,128,128]{2,1,0:T(8,128)(2,1)}) custom-call(s32[3]{0:T(128)} %pad_add_fusion.2.info_ref, s32[128]{0:T(128)} %dead_ref.5, s32[128]{0:T(128)} %sec_ref.5, f32[2,2,8,1152]{3,2,1,0:T(8,128)} %add.45.tot_ref, f32[1024,128]{1,0:T(8,128)} %broadcast_in_dim.10.gain_ref, ...), custom_call_target="tpu_custom_call" | custom-call | flops 5905580032 | bytes 16777216 | tf_op jit(solution)/shard_map/pallas_call | solution.py:172
  81.1 1.1 copy-done.4
  82.1 19.3 %shard_map.85 = (bf16[128,128,128]{2,1,0:T(8,128)(2,1)}, bf16[128,128,128]{2,1,0:T(8,128)(2,1)}) custom-call(s32[3]{0:T(128)} %pad_add_fusion.3.info_ref, s32[128]{0:T(128)} %tile.22.dead_ref, s32[128]{0:T(128)} %tile.25.sec_ref, f32[2,2,8,1152]{3,2,1,0:T(8,128)} %add.45.tot_ref, f32[1024,128]{1,0:T(8,128)} %broadcast_in_dim.10.gain_ref, ...), custom_call_target="tpu_custom_call" | custom-call | flops 5905580032 | bytes 16777216 | tf_op jit(solution)/shard_map/pallas_call | solution.py:172
  101.4 22.3 %shard_map.86 = bf16[4,64,32,128]{3,2,1,0:T(8,128)(2,1)} custom-call(s32[1]{0:T(128)} %bitcast.odd_ref, bf16[128,128,128]{2,1,0:T(8,128)(2,1)} %get-tuple-element.21.a0_ref, bf16[128,128,128]{2,1,0:T(8,128)(2,1)} %get-tuple-element.24.a1_ref, bf16[128,128,128]{2,1,0:T(8,128)(2,1)} %get-tuple-element.27.ah_ref, ...), custom_call_target="tpu_custom_call" | custom-call | flops 4294967296 | bytes 20971520 | tf_op jit(solution)/shard_map/pallas_call | solution.py:277
  123.8 2.9 %dynamic-slice_bitcast_fusion.1 = (bf16[64,32,128]{2,1,0:T(8,128)(2,1)}, bf16[64,32,128]{2,1,0:T(8,128)(2,1)S(1)}, bf16[64,32,128]{2,1,0:T(8,128)(2,1)}, bf16[64,32,128]{2,1,0:T(8,128)(2,1)S(1)}) fusion(bf16[4,64,32,128]{3,2,1,0:T(8,128)(2,1)} %shard_map.86, s32[]{:T(128)S(6)} %select_n.46, s32[]{:T(128)S(6)} %select_n.47, s32[]{:T(128)S(6)} %select_n.45, ...), kind=kLoop, calls=%fused_computation.6 | loop fusion | bytes 4194320 | tf_op jit(solution)/shard_map/jit(dynamic_index_in_dim)/squeeze | solution.py:384
  126.7 2.8 %collective-permute-start.12 = (bf16[64,32,128]{2,1,0:T(8,128)(2,1)S(1)}, bf16[64,32,128]{2,1,0:T(8,128)(2,1)S(1)}, u32[]{:S(2)}, u32[]{:S(2)}) collective-permute-start(bf16[64,32,128]{2,1,0:T(8,128)(2,1)S(1)} %get-tuple-element.34), channel_id=1, source_target_pairs={{0,3},{1,30},{2,1},{3,28},{4,7},{5,2},{6,5},{7,0},{8,11},{9,6},{10... | collective-permute-start | bytes 1572872 | tf_op jit(solution)/shard_map/ppermute | solution.py:385
  130.2 18.5 %collective-permute-done.10 = bf16[64,32,128]{2,1,0:T(8,128)(2,1)S(1)} collective-permute-done((bf16[64,32,128]{2,1,0:T(8,128)(2,1)}, bf16[64,32,128]{2,1,0:T(8,128)(2,1)S(1)}, u32[]{:S(2)}, u32[]{:S(2)}) %collective-permute-start.10) | collective-permute-done | bytes 524320 | tf_op jit(solution)/shard_map/ppermute | solution.py:385
  148.6 2.7 %collective-permute-done.11 = bf16[64,32,128]{2,1,0:T(8,128)(2,1)S(1)} collective-permute-done((bf16[64,32,128]{2,1,0:T(8,128)(2,1)}, bf16[64,32,128]{2,1,0:T(8,128)(2,1)S(1)}, u32[]{:S(2)}, u32[]{:S(2)}) %collective-permute-start.11) | collective-permute-done | bytes 524320 | tf_op jit(solution)/shard_map/ppermute | solution.py:385
  151.4 22.4 %collective-permute-done.12 = bf16[64,32,128]{2,1,0:T(8,128)(2,1)S(1)} collective-permute-done((bf16[64,32,128]{2,1,0:T(8,128)(2,1)S(1)}, bf16[64,32,128]{2,1,0:T(8,128)(2,1)S(1)}, u32[]{:S(2)}, u32[]{:S(2)}) %collective-permute-start.12) | collective-permute-done | bytes 524320 | tf_op jit(solution)/shard_map/ppermute | solution.py:385
  174.1 1.5 pad_maximum_fusion
  (37 shorter events, 10.0 us)
Async XLA Ops:
  1.7 4.5 %copy-start.1 = (s32[128]{0:T(128)S(1)}, s32[128]{0:T(128)}, u32[]{:S(2)}) copy-start(s32[128]{0:T(128)} %dead_ref.5) | copy-start | bytes 1540
  1.7 4.5 %copy-start.2 = (s32[128]{0:T(128)S(1)}, s32[128]{0:T(128)}, u32[]{:S(2)}) copy-start(s32[128]{0:T(128)} %sec_ref.5) | copy-start | bytes 1540
  1.7 12.5 %copy-start = (f32[512]{0:T(512)S(1)}, f32[512]{0:T(512)}, u32[]{:S(2)}) copy-start(f32[512]{0:T(512)} %param.9) | copy-start | bytes 6148
  4.9 5.3 %collective-permute-start = (f32[2,8,1152]{2,1,0:T(8,128)}, f32[2,8,1152]{2,1,0:T(8,128)S(1)}, u32[]{:S(2)}, u32[]{:S(2)}) collective-permute-start(f32[2,8,1152]{2,1,0:T(8,128)} %shard_map.82), channel_id=1, source_target_pairs={{0,1},{1,0},{2,3},{3,2},{4,5},{5,4},{6,7},{7,6},{8,9},{9,8},{10,11... | collective-permute-start | bytes 221192 | tf_op jit(solution)/shard_map/ppermute | solution.py:348
  6.3 3.9 %collective-permute-start.1 = (s32[2,64]{1,0:T(2,128)S(1)}, s32[2,64]{1,0:T(2,128)S(1)}, u32[]{:S(2)}, u32[]{:S(2)}) collective-permute-start(s32[2,64]{1,0:T(2,128)S(1)} %constant_dynamic-slice_fusion.1), channel_id=1, source_target_pairs={{0,28},{1,5},{2,30},{3,7},{4,0},{5,9},{6,2},{7,11},{8,4},{9,13},{1... | collective-permute-start | bytes 1544 | tf_op jit(solution)/shard_map/ppermute | solution.py:339
  7.2 24.8 %collective-permute-start.5 = (bf16[64,8,1024]{2,1,0:T(8,128)(2,1)S(1)}, bf16[64,8,1024]{2,1,0:T(8,128)(2,1)}, u32[]{:S(2)}, u32[]{:S(2)}) collective-permute-start(bf16[64,8,1024]{2,1,0:T(8,128)(2,1)S(1)} %get-tuple-element.22), channel_id=1, source_target_pairs={{0,1},{1,0},{2,3},{3,2},{4,5},{5,4},{6,7},{7,6},{8,9},{9,8},{10,11... | collective-permute-start | bytes 3145736 | tf_op jit(solution)/shard_map/ppermute | solution.py:349
  11.1 1.4 collective-permute-start.2
  13.4 5.2 %collective-permute-start.3 = (f32[2,2,8,1152]{3,2,1,0:T(8,128)S(1)}, f32[2,2,8,1152]{3,2,1,0:T(8,128)S(1)}, u32[]{:S(2)}, u32[]{:S(2)}) collective-permute-start(f32[2,2,8,1152]{3,2,1,0:T(8,128)S(1)} %fusion.2), channel_id=1, source_target_pairs={{0,8},{4,12},{8,0},{12,4},{16,24},{20,28},{24,16},{28,20},{1,9},{5... | collective-permute-start | bytes 442376 | tf_op jit(solution)/shard_map/ppermute | solution.py:311
  14.2 43.0 %collective-permute-start.6 = (bf16[64,8,1024]{2,1,0:T(8,128)(2,1)S(1)}, bf16[64,8,1024]{2,1,0:T(8,128)(2,1)}, u32[]{:S(2)}, u32[]{:S(2)}) collective-permute-start(bf16[64,8,1024]{2,1,0:T(8,128)(2,1)S(1)} %get-tuple-element.26), channel_id=1, source_target_pairs={{0,1},{1,0},{2,3},{3,2},{4,5},{5,4},{6,7},{7,6},{8,9},{9,8},{10,11... | collective-permute-start | bytes 3145736 | tf_op jit(solution)/shard_map/ppermute | solution.py:353
  19.5 4.5 %collective-permute-start.4 = (f32[2,2,8,1152]{3,2,1,0:T(8,128)S(1)}, f32[2,2,8,1152]{3,2,1,0:T(8,128)S(1)}, u32[]{:S(2)}, u32[]{:S(2)}) collective-permute-start(f32[2,2,8,1152]{3,2,1,0:T(8,128)S(1)} %fusion.3), channel_id=1, source_target_pairs={{0,16},{4,20},{8,24},{12,28},{16,0},{20,4},{24,8},{28,12},{1,17},{... | collective-permute-start | bytes 442376 | tf_op jit(solution)/shard_map/ppermute | solution.py:311
  24.7 55.4 %collective-permute-start.7 = (bf16[64,8,1024]{2,1,0:T(8,128)(2,1)S(1)}, bf16[64,8,1024]{2,1,0:T(8,128)(2,1)S(1)}, u32[]{:S(2)}, u32[]{:S(2)}) collective-permute-start(bf16[64,8,1024]{2,1,0:T(8,128)(2,1)S(1)} %get-tuple-element.26), channel_id=1, source_target_pairs={{0,28},{1,5},{2,30},{3,7},{4,0},{5,9},{6,2},{7,11},{8,4},{9,13},{1... | collective-permute-start | bytes 3145736 | tf_op jit(solution)/shard_map/ppermute | solution.py:356
  32.0 48.1 %collective-permute-start.8 = (bf16[64,8,1024]{2,1,0:T(8,128)(2,1)}, bf16[64,8,1024]{2,1,0:T(8,128)(2,1)S(1)}, u32[]{:S(2)}, u32[]{:S(2)}) collective-permute-start(bf16[64,8,1024]{2,1,0:T(8,128)(2,1)} %collective-permute-done.5.rest_0_), channel_id=1, source_target_pairs={{0,28},{1,5},{2,30},{3,7},{4,0},{5,9},{6,2},{7,11},{8,4},{9,13},{1... | collective-permute-start | bytes 3145736 | tf_op jit(solution)/shard_map/ppermute | solution.py:357
  80.1 1.0 copy-start.3
  81.1 1.1 copy-start.4
  126.7 22.0 %collective-permute-start.10 = (bf16[64,32,128]{2,1,0:T(8,128)(2,1)}, bf16[64,32,128]{2,1,0:T(8,128)(2,1)S(1)}, u32[]{:S(2)}, u32[]{:S(2)}) collective-permute-start(bf16[64,32,128]{2,1,0:T(8,128)(2,1)} %get-tuple-element.35), channel_id=1, source_target_pairs={{0,2},{1,31},{2,0},{3,29},{4,6},{5,3},{6,4},{7,1},{8,10},{9,7},{10... | collective-permute-start | bytes 1572872 | tf_op jit(solution)/shard_map/ppermute | solution.py:385
  126.7 24.7 %collective-permute-start.11 = (bf16[64,32,128]{2,1,0:T(8,128)(2,1)}, bf16[64,32,128]{2,1,0:T(8,128)(2,1)S(1)}, u32[]{:S(2)}, u32[]{:S(2)}) collective-permute-start(bf16[64,32,128]{2,1,0:T(8,128)(2,1)} %get-tuple-element.33), channel_id=1, source_target_pairs={{0,1},{1,28},{2,3},{3,30},{4,5},{5,0},{6,7},{7,2},{8,9},{9,4},{10,... | collective-permute-start | bytes 1572872 | tf_op jit(solution)/shard_map/ppermute | solution.py:385
  126.7 47.1 %collective-permute-start.12 = (bf16[64,32,128]{2,1,0:T(8,128)(2,1)S(1)}, bf16[64,32,128]{2,1,0:T(8,128)(2,1)S(1)}, u32[]{:S(2)}, u32[]{:S(2)}) collective-permute-start(bf16[64,32,128]{2,1,0:T(8,128)(2,1)S(1)} %get-tuple-element.34), channel_id=1, source_target_pairs={{0,3},{1,30},{2,1},{3,28},{4,7},{5,2},{6,5},{7,0},{8,11},{9,6},{10... | collective-permute-start | bytes 1572872 | tf_op jit(solution)/shard_map/ppermute | solution.py:385
  129.5 44.3 %collective-permute-start.9 = (bf16[64,32,128]{2,1,0:T(8,128)(2,1)S(1)}, bf16[64,32,128]{2,1,0:T(8,128)(2,1)S(1)}, u32[]{:S(2)}, u32[]{:S(2)}) collective-permute-start(bf16[64,32,128]{2,1,0:T(8,128)(2,1)S(1)} %get-tuple-element.36), channel_id=1, source_target_pairs={{0,0},{1,29},{2,2},{3,31},{4,4},{5,1},{6,6},{7,3},{8,8},{9,5},{10,... | collective-permute-start | bytes 1572872 | tf_op jit(solution)/shard_map/ppermute | solution.py:385

commit v4 on v3

v4 whole, which is shorter than its diff:
```python
import functools
import math

import jax
import jax.numpy as jnp
import ml_dtypes
import numpy as np
from jax import lax
from jax.experimental import pallas as pl
from jax.experimental.pallas import tpu as pltpu
from jax.sharding import PartitionSpec as P

OFFS = 128
LAGS = 128
NSEC = 2
LANE = 128
CHUNKS = 2
TILE = 256
STEPS = 4
VMEM = 56 * 1024 * 1024
NT = (((1,), (1,)), ((), ()))
F32 = jnp.float32
BF16 = jnp.bfloat16


def tables(ns, nf):
    tick = np.arange(ns)
    freq = np.arange(nf)
    phase = (tick[:, None] * freq[None, :] % ns) * (2.0 * math.pi / ns)
    window = 0.5 - 0.5 * np.cos(tick * (2.0 * math.pi / ns))
    forward = np.concatenate(
        [window[:, None] * np.cos(phase), -window[:, None] * np.sin(phase)], axis=1
    )
    back = np.concatenate([np.cos(phase), -np.sin(phase)], axis=1)
    back[:, 0] *= math.sqrt(0.5)
    size = 2 * LAGS
    bins = np.arange(size // 2)
    turn = math.pi / size * ((2 * bins[:, None] + 1) * np.arange(size)[None, :] % (2 * size))
    segment = np.stack([np.cos(turn), -np.sin(turn)], axis=1).reshape(size, size)
    lag = np.stack([np.cos(turn), -np.sin(turn)], axis=1).reshape(size, size)[:, :LAGS].T
    cast = lambda a: a.astype(np.float32).astype(ml_dtypes.bfloat16)
    return cast(forward.T), cast(back), cast(segment), cast(lag)


def section_sums(dead_ref, sec_ref, x_ref, out_ref):
    chans, wins, ns = x_ref.shape
    first = pl.program_id(0) * chans

    @pl.when(pl.program_id(0) == 0)
    def _():
        out_ref[...] = jnp.zeros_like(out_ref)

    def body(c, carry):
        value = x_ref[c].astype(F32)
        live = 1 - dead_ref[first + c]
        sums, counts = carry
        weights = [jnp.where(sec_ref[first + c] == s, live, 0).astype(F32) for s in range(NSEC)]
        return (
            tuple(sums[s] + weights[s] * value for s in range(NSEC)),
            tuple(counts[s] + weights[s] for s in range(NSEC)),
        )

    zero = jnp.zeros((wins, ns), F32)
    sums, counts = lax.fori_loop(
        0, chans, body, ((zero,) * NSEC, (jnp.float32(0),) * NSEC), unroll=8
    )
    for s in range(NSEC):
        out_ref[s, :, :ns] += sums[s]
        out_ref[s, :, ns:] += jnp.zeros((wins, LANE), F32) + counts[s]


def segments_kernel(kind, odd_ref, flag_ref, *rest):
    sets = {"own": (0,), "halo": (0, 1), "other": (0, 0)}[kind]
    groups = max(sets) + 1
    count = len(sets)
    tot_hbm, rest = rest[:groups], rest[groups:]
    x_hbm, rest = rest[:count], rest[count:]
    gain_hbm, fwd_hbm, back_hbm, seg_hbm, a_hbm, b_hbm = rest[:6]
    tot, rest = rest[6 : 6 + groups], rest[6 + groups :]
    x, rest = rest[:count], rest[count:]
    gain, fwd, back, seg, common, clean, rows, spec, white, series, a_s, b_s, a_out, b_out = rest[:14]
    in_sem, out_sem = rest[14:]
    sources = list(tot_hbm) + list(x_hbm) + [fwd_hbm, gain_hbm, back_hbm, seg_hbm]
    targets = list(tot) + list(x) + [fwd, gain, back, seg]
    copies = [
        pltpu.make_async_copy(source, target, in_sem.at[n])
        for n, (source, target) in enumerate(zip(sources, targets))
    ]
    for copy in copies:
        copy.start()

    _, wins, ns = x[0].shape
    chans = b_out.shape[2]
    nfr = spec.shape[0]
    pitch = wins + 1
    size = seg.shape[0]
    half = size // 2
    blocks = ns // half
    jw = blocks * wins
    jpitch = jw + 1
    odd = odd_ref[0]
    want = (odd == 1) if kind == "halo" else (odd == 0)
    held = flag_ref.shape[1]
    for g in range(groups):
        copies[g].wait()
        for s in range(NSEC):
            common[g * NSEC + s] = tot[g][s, :, :ns] / jnp.maximum(tot[g][s, :, ns : ns + 1], 1.0)

    for number, group in enumerate(sets):
        copies[groups + number].wait()
        piece = x[number]
        length = piece.shape[0]
        base = number * length
        if kind == "other":
            base = odd * length if number == 0 else length - odd * length

        def clean_channel(c, _):
            at = base + c
            flag = lax.rem(at, held)
            live = (1 - flag_ref[0, flag]).astype(F32)
            value = (piece[c].astype(F32) - common[group * NSEC + flag_ref[1, flag]]) * live
            for t in range(ns // LANE):
                clean[t, pl.ds(at * pitch, wins), :] = value[:, t * LANE : (t + 1) * LANE]
            return 0

        lax.fori_loop(0, length, clean_channel, 0, unroll=8)
    for copy in copies[groups + count :]:
        copy.wait()

    def pair(step, _):
        for i in range(2):
            w = step * 2 + i
            for t in range(ns // LANE):
                rows[i * chans : (i + 1) * chans, t * LANE : (t + 1) * LANE] = clean[
                    t, pl.ds(w, chans, stride=pitch), :
                ].astype(BF16)
        power = jnp.zeros((1, 2 * chans), F32)
        for f in range(0, nfr, TILE):
            s = lax.dot_general(
                fwd[f : f + TILE, :], rows[...], NT, preferred_element_type=F32
            )
            spec[f : f + TILE, :] = s
            power = power + jnp.sum(s * s, axis=0, keepdims=True)
        level = lax.rsqrt(power / nfr + 1e-06)
        for i in range(2):
            white[:, i * chans : (i + 1) * chans] = (
                spec[:, i * chans : (i + 1) * chans]
                * gain[...]
                * level[:, i * chans : (i + 1) * chans]
            ).astype(BF16)
        for t in range(0, ns, TILE):
            series[half // 2 + t : half // 2 + t + TILE, :] = jnp.dot(
                back[t : t + TILE, :], white[...], preferred_element_type=F32
            ).astype(BF16)
        series[: half // 2, :] = series[ns : ns + half // 2, :]
        series[ns + half // 2 :, :] = series[half // 2 : half, :]
        for j in range(blocks):
            b = jnp.dot(
                seg[:, :half],
                series[j * half + half // 2 : j * half + half // 2 + half, :],
                preferred_element_type=F32,
            )
            for i in range(2):
                at = j * wins + step * 2 + i
                b_s[pl.ds(at, size, stride=jpitch), :] = b[:, i * chans : (i + 1) * chans]

        @pl.when(want)
        def _():
            for j in range(blocks):
                a = jnp.dot(
                    seg[...], series[j * half : j * half + size, :], preferred_element_type=F32
                )
                for i in range(2):
                    at = j * wins + step * 2 + i
                    a_s[pl.ds(at, size, stride=jpitch), :] = a[:, i * chans : (i + 1) * chans]

        return 0

    lax.fori_loop(0, wins // 2, pair, 0)

    def both_parts(ref, k):
        return jnp.concatenate(
            [ref[pl.ds((2 * k + part) * jpitch, jw), :].astype(BF16) for part in range(2)], axis=0
        )

    def second(k, _):
        b_out[k] = both_parts(b_s, k)
        return 0

    def first(k, _):
        a_out[k] = both_parts(a_s, k).T[: a_out.shape[1]]
        return 0

    step = half // STEPS

    def sends(n, stage, target):
        part = pl.ds(n % STEPS * step, step)
        return pltpu.make_async_copy(stage.at[part], target.at[part], out_sem.at[n])

    @pl.when(want)
    def _():
        for n in range(STEPS):
            lax.fori_loop(n * step, (n + 1) * step, first, 0, unroll=8)
            sends(n, a_out, a_hbm).start()

    for n in range(STEPS):
        lax.fori_loop(n * step, (n + 1) * step, second, 0, unroll=8)
        sends(STEPS + n, b_out, b_hbm).start()

    @pl.when(want)
    def _():
        for n in range(STEPS):
            sends(n, a_out, a_hbm).wait()

    for n in range(STEPS):
        sends(STEPS + n, b_out, b_hbm).wait()


def segments(kind, odd, flags, totals, pieces, gain, fwd, back, seg):
    chans = sum(x.shape[0] for x in pieces)
    _, wins, ns = pieces[0].shape
    nfr = fwd.shape[0]
    size = seg.shape[0]
    half = size // 2
    depth = ns // half * wins * 2
    kept = chans if kind == "halo" else chans // 2
    smem = pl.BlockSpec(memory_space=pltpu.SMEM)
    anywhere = pl.BlockSpec(memory_space=pl.ANY)
    tables_in = [gain, fwd, back, seg]
    operands = list(totals) + list(pieces) + tables_in
    a_shape = jax.ShapeDtypeStruct((half, kept, depth), BF16)
    b_shape = jax.ShapeDtypeStruct((half, depth, chans), BF16)
    return pl.pallas_call(
        functools.partial(segments_kernel, kind),
        out_shape=[a_shape, b_shape],
        in_specs=[smem] * 2 + [anywhere] * len(operands),
        out_specs=[anywhere] * 2,
        scratch_shapes=[pltpu.VMEM(value.shape, value.dtype) for value in operands]
        + [
            pltpu.VMEM((len(totals) * NSEC, wins, ns), F32),
            pltpu.VMEM((ns // LANE, chans * (wins + 1), LANE), F32),
            pltpu.VMEM((2 * chans, ns), BF16),
            pltpu.VMEM((nfr, 2 * chans), F32),
            pltpu.VMEM((nfr, 2 * chans), BF16),
            pltpu.VMEM((ns + half, 2 * chans), BF16),
            pltpu.VMEM((size * (depth // 2 + 1), chans), F32),
            pltpu.VMEM((size * (depth // 2 + 1), chans), F32),
            pltpu.VMEM(a_shape.shape, BF16),
            pltpu.VMEM(b_shape.shape, BF16),
            pltpu.SemaphoreType.DMA((len(operands),)),
            pltpu.SemaphoreType.DMA((2 * STEPS,)),
        ],
        compiler_params=pltpu.CompilerParams(vmem_limit_bytes=VMEM),
        cost_estimate=pl.CostEstimate(
            flops=2 * wins * chans * ns * (2 * nfr + 3 * size),
            bytes_accessed=16 * 1024 * 1024,
            transcendentals=0,
        ),
    )(odd, flags, *operands)


def stack_kernel(
    first, scale, me_ref, a0_ref, a1_ref, ah_ref, b0_ref, b1_ref, bh_ref, lag_ref, *rest
):
    outs, (cross, one) = rest[:-2], rest[-2:]
    bins, count, depth = a0_ref.shape
    chans = b0_ref.shape[2]
    width = chans // 2
    nfr = lag_ref.shape[1]
    pitch = nfr + 1
    me = me_ref[0]
    odd = lax.rem(me, 2)
    step = pl.program_id(0)

    def bins_with(left_of):
        def one_bin(k, _):
            left = left_of(k)
            part = depth // 2
            swapped = jnp.concatenate(
                [
                    left[:, part:depth],
                    -left[:, :part],
                    left[:, depth + part :],
                    -left[:, depth : depth + part],
                ],
                axis=1,
            )
            halo = bh_ref[k]
            other = jnp.concatenate([halo[:, width:], halo[:, :width]], axis=1)
            right = jnp.concatenate(
                [
                    jnp.concatenate([b0_ref[k], halo], axis=1),
                    jnp.concatenate([b1_ref[k], other], axis=1),
                ],
                axis=0,
            )
            value = jnp.dot(
                jnp.concatenate([left, swapped], axis=0), right, preferred_element_type=F32
            )
            at = 2 * (step * bins + k)
            for p in range(2):
                for t in range(2):
                    cross[t, pl.ds(at + p, count, stride=pitch), :] = value[
                        p * count : (p + 1) * count, t * chans : (t + 1) * chans
                    ]
            return 0

        lax.fori_loop(0, bins, one_bin, 0, unroll=8)

    @pl.when(odd == 1)
    def _():
        bins_with(lambda k: jnp.concatenate([ah_ref[k, 0], ah_ref[k, 1]], axis=1))

    @pl.when(odd == 0)
    def _():
        bins_with(lambda k: jnp.concatenate([a0_ref[k], a1_ref[k]], axis=1))

    @pl.when(step == pl.num_programs(0) - 1)
    def _():
        row = lax.broadcasted_iota(jnp.int32, one.shape[1:], 0)
        column = lax.broadcasted_iota(jnp.int32, one.shape[1:], 1)
        turned = jnp.where(row < width, row + chans, row - width)
        place = row + (turned - row) * odd
        for t in range(2):
            one[t] = jnp.where(place == column + t * chans, 1.0, 0.0)
        share = OFFS // len(outs)

        def one_channel(c, _):
            value = jnp.concatenate(
                [cross[t, pl.ds(c * pitch, nfr), :] for t in range(2)], axis=1
            ).astype(BF16)
            starts = [first + c + 1 + share * (me ^ d) for d in range(len(outs))]
            pick = jnp.concatenate(
                [
                    jnp.concatenate([one[t, pl.ds(start, share), :] for start in starts], axis=0)
                    for t in range(2)
                ],
                axis=1,
            ).astype(BF16)
            lagged = jnp.dot(lag_ref[...], value, preferred_element_type=F32) * scale
            band = lax.dot_general(pick, lagged.astype(BF16), NT, preferred_element_type=F32)
            for d, out in enumerate(outs):
                out[c] = band[d * share : (d + 1) * share, :].astype(BF16)
            return 0

        lax.fori_loop(0, count, one_channel, 0, unroll=4)


def stacks(index, shares, scale, me, a0, a1, ah, b0, b1, bh, lag):
    bins, width, depth = a0.shape
    chans = b0.shape[2]
    count = width // CHUNKS
    nlag, nfr = lag.shape
    ah = ah.reshape(bins, 2, width, depth)
    block = bins // 8
    left = pl.BlockSpec((block, count, depth), lambda i: (i, index, 0))
    right = pl.BlockSpec((block, depth, chans), lambda i: (i, 0, 0))
    return pl.pallas_call(
        functools.partial(stack_kernel, index * count, scale),
        grid=(bins // block,),
        out_shape=[jax.ShapeDtypeStruct((count, OFFS // shares, nlag), BF16)] * shares,
        in_specs=[
            pl.BlockSpec(memory_space=pltpu.SMEM),
            left,
            left,
            pl.BlockSpec((block, 2, count, depth), lambda i: (i, 0, index, 0)),
            right,
            right,
            right,
            pl.BlockSpec(lag.shape, lambda i: (0, 0)),
        ],
        out_specs=[pl.BlockSpec((count, OFFS // shares, nlag), lambda i: (0, 0, 0))] * shares,
        scratch_shapes=[
            pltpu.VMEM((2, count * (nfr + 1), chans), F32),
            pltpu.VMEM((2, chans + width, chans), F32),
        ],
        compiler_params=pltpu.CompilerParams(vmem_limit_bytes=VMEM),
        cost_estimate=pl.CostEstimate(
            flops=2 * count * bins * 4 * (2 * depth * chans + 2 * OFFS * chans),
            bytes_accessed=20 * 1024 * 1024,
            transcendentals=0,
        ),
    )(me, a0, a1, ah, b0, b1, bh, lag)


def add_over(value, axis):
    count = lax.axis_size(axis)
    if count & (count - 1):
        return lax.psum(value, axis)
    bit = 1
    while bit < count:
        value = value + lax.ppermute(value, axis, [(i, i ^ bit) for i in range(count)])
        bit *= 2
    return value


def shards(samples, band_gain, dead_flags, section_ids):
    chans, wins, ns = samples.shape
    nf = ns // 2
    width = chans // 2
    blocks = lax.axis_size("fibre")
    groups = lax.axis_size("tm")
    me = lax.axis_index("tm")
    odd = me % 2
    fwd, back, seg, lag = [jnp.asarray(t) for t in tables(ns, nf)]
    gain = jnp.broadcast_to(jnp.concatenate([band_gain, band_gain])[:, None], (2 * nf, chans))
    swap = [(z, z ^ 1) for z in range(groups)]
    both = ("fibre", "tm")
    halo_pairs = [
        (b * groups + z, (b + (1 if z % 2 else -1)) % blocks * groups + z)
        for b in range(blocks)
        for z in range(groups)
    ]

    first_half = lax.dynamic_slice_in_dim(samples, (1 - odd) * width, width, 0)
    their_first = lax.ppermute(first_half, "tm", swap)
    flags = jnp.stack([dead_flags, section_ids])
    halo_flags = lax.ppermute(
        lax.dynamic_slice_in_dim(flags, odd * width, width, 1), both, halo_pairs
    )
    smem = pl.BlockSpec(memory_space=pltpu.SMEM)
    steps = 4
    sums = pl.pallas_call(
        section_sums,
        grid=(steps,),
        out_shape=jax.ShapeDtypeStruct((NSEC, wins, ns + LANE), F32),
        in_specs=[smem, smem, pl.BlockSpec((chans // steps, wins, ns), lambda i: (i, 0, 0))],
        out_specs=pl.BlockSpec((NSEC, wins, ns + LANE), lambda i: (0, 0, 0)),
        compiler_params=pltpu.CompilerParams(vmem_limit_bytes=VMEM),
    )(dead_flags, section_ids, samples)
    total = add_over(sums, "fibre")
    total, halo_flags, kept = lax.optimization_barrier((total, halo_flags, samples))
    their_total = lax.ppermute(total, "tm", swap)
    own_half = lax.dynamic_slice_in_dim(kept, odd * width, width, 0)
    their_second = lax.ppermute(own_half, "tm", swap)
    halo = lax.ppermute(own_half, both, halo_pairs)

    side = odd[None]
    parts = (gain, fwd, back, seg)
    a0, b0 = segments("own", side, flags, (total,), (samples,), *parts)
    b0, forward = lax.optimization_barrier((b0, their_first))
    their_halo = lax.ppermute(forward, both, halo_pairs)
    ah, bh = segments("halo", side, halo_flags, (total, their_total), (halo, their_halo), *parts)
    a1, b1 = segments("other", side, flags, (their_total,), (their_first, their_second), *parts)
    scale = 2.0 / ns / LAGS / math.sqrt(nf * wins * groups)
    same, other = [], []
    for index in range(CHUNKS):
        found = stacks(index, groups, scale, me[None], a0, a1, ah, b0, b1, bh, lag)
        arrived = []
        for d in range(groups):
            pairs = [
                (b * groups + z, (b - z % 2) % blocks * groups + (z ^ d))
                for b in range(blocks)
                for z in range(groups)
            ]
            arrived.append(lax.ppermute(found[d], both, pairs).astype(F32))
        same.append(sum(arrived[2::2], arrived[0]))
        other.append(sum(arrived[3::2], arrived[1]))
    lower = [jnp.where(odd == 0, s, o) for s, o in zip(same, other)]
    upper = [jnp.where(odd == 0, o, s) for s, o in zip(same, other)]
    return jnp.concatenate(lower + upper, axis=0)


def solution(mesh):
    in_specs = (P("fibre", "tm", None), P(), P("fibre"), P("fibre"))
    out_specs = P("fibre", "tm", None)
    return jax.shard_map(shards, mesh=mesh, in_specs=in_specs, out_specs=out_specs, check_vma=False)
```

time: 176 us -> 150 us (0.85)
  waiting for transfers between devices: 55.9 us -> 38.8 us
  Pallas kernels: 90.5 us -> 80.7 us
  starting transfers between devices: 13.1 us -> 20.4 us
  other arithmetic: 7.13 us -> 3.36 us
  local copies, waits for them, and re-layouts: 8.94 us -> 6.23 us
    ppermute x8 -> x12, waiting for transfers between devices: 45.3 us -> 32.7 us  [the longest x8 22.1 us: shards(): arrived.append(lax.ppermute(found[d], both, pairs).astype(F32))]
    pallas_call x5 -> x6, Pallas kernels: 90.5 us -> 80.7 us  [the longest x3 47.8 us: segments(): pl.pallas_call(functools.partial(segments_kernel, kind), out_shape=[a_sha...]
    ppermute x8 -> x12, starting transfers between devices: 8.42 us -> 14.5 us  [the longest x8 12.5 us: shards(): arrived.append(lax.ppermute(found[d], both, pairs).astype(F32))]
    ppermute x1, waiting for transfers between devices: 5.5 us -> 0.01 us  [shards(): their_first = lax.ppermute(first_half, 'tm', swap)]
    squeeze x1 -> x0, local copies, waits for them, and re-layouts: 2.91 us -> none  [shards(): lax.dynamic_index_in_dim(found, lax.axis_index('tm') ^ d, 0, keepdims=False)]
    another operation x4 -> x0, other arithmetic: 2.8 us -> none  [the longest x1 0.9 us: shards(): total = add_over(jnp.stack([sums, their_sums]), 'fibre')]
    unnamed x10 -> x22, local copies, waits for them, and re-layouts: 2.03 us -> 3.62 us
  transfers between devices with their start and end apart: 13 -> 17, of which waited for: 8 -> 8; matrix products, arithmetic and copies ran while one was open for 4% -> 2% of each run, Pallas kernels for 26% -> 35%
where the time goes in v4:
time: 150 us
  Pallas kernels  80.7 us (54%)
  waiting for transfers between devices  38.8 us (26%)
  starting transfers between devices  20.4 us (14%)
  local copies, waits for them, and re-layouts  6.23 us (4%)
  other arithmetic  3.36 us (2%)
    pallas_call x3, Pallas kernels, segments(): pl.pallas_call(functools.partial(segments_kernel, kind), out_shape=[a_sha...  47.8 us
    pallas_call x2, Pallas kernels, stacks(): pl.pallas_call(functools.partial(stack_kernel, index * count, scale), gri...  29.3 us
    ppermute x8, waiting for transfers between devices, shards(): arrived.append(lax.ppermute(found[d], both, pairs).astype(F32))  22.1 us
    ppermute x8, starting transfers between devices, shards(): arrived.append(lax.ppermute(found[d], both, pairs).astype(F32))  12.5 us
    ppermute x1, waiting for transfers between devices, shards(): their_total = lax.ppermute(total, 'tm', swap)  10.6 us
    ppermute x3, waiting for transfers between devices, add_over(): lax.ppermute(value, axis, [(i, i ^ bit) for i in range(count)])  6.09 us
    unnamed x22, local copies, waits for them, and re-layouts  3.62 us
    pallas_call x1, Pallas kernels, shards(): pl.pallas_call(section_sums, grid=(steps,), out_shape=jax.ShapeDtypeStruc...  3.54 us
  transfers between devices with their start and end apart: 17, of which 8 were waited for; matrix products, arithmetic and copies ran while one was open for 2% of the time, Pallas kernels for 35%

profile of v4, /device:TPU:19, one launch (start us, length us, event | category | flops | bytes accessed | tf_op | source)
XLA Modules:
  0.0 149.7 jit_solution(16837604555893170102)
XLA Ops:
  0.0 1.4 constant_dynamic-slice_fusion.1
  1.5 1.4 collective-permute-start.5
  2.8 3.5 %shard_map.82 = f32[2,8,1152]{2,1,0:T(8,128)} custom-call(s32[128]{0:T(128)} %dead_ref.1, s32[128]{0:T(128)} %sec_ref.1, bf16[128,8,1024]{2,1,0:T(8,128)(2,1)} %rest_1_.1), custom_call_target="tpu_custom_call" | custom-call | tf_op jit(solution)/shard_map/pallas_call | solution.py:423
  10.4 2.6 %collective-permute-done.1 = f32[2,8,1152]{2,1,0:T(8,128)S(1)} collective-permute-done((f32[2,8,1152]{2,1,0:T(8,128)S(1)}, f32[2,8,1152]{2,1,0:T(8,128)S(1)}, u32[]{:S(2)}, u32[]{:S(2)}) %collective-permute-start.1) | collective-permute-done | bytes 73760 | tf_op jit(solution)/shard_map/ppermute | solution.py:392
  13.0 1.3 collective-permute-start.2
  14.4 2.4 %collective-permute-done.2 = f32[2,8,1152]{2,1,0:T(8,128)S(1)} collective-permute-done((f32[2,8,1152]{2,1,0:T(8,128)S(1)}, f32[2,8,1152]{2,1,0:T(8,128)S(1)}, u32[]{:S(2)}, u32[]{:S(2)}) %collective-permute-start.2) | collective-permute-done | bytes 73760 | tf_op jit(solution)/shard_map/ppermute | solution.py:392
  17.4 1.9 %collective-permute-start.7 = (bf16[64,8,1024]{2,1,0:T(8,128)(2,1)S(1)}, bf16[64,8,1024]{2,1,0:T(8,128)(2,1)S(1)}, u32[]{:S(2)}, u32[]{:S(2)}) collective-permute-start(bf16[64,8,1024]{2,1,0:T(8,128)(2,1)S(1)} %constant_dynamic-slice_fusion), channel_id=1, source_target_pairs={{0,28},{1,5},{2,30},{3,7},{4,0},{5,9},{6,2},{7,11},{8,4},{9,13},{1... | collective-permute-start | bytes 3145736 | tf_op jit(solution)/shard_map/ppermute | solution.py:436
  19.3 1.3 collective-permute-start.6
  21.6 17.2 %shard_map.83 = (bf16[128,64,128]{2,1,0:T(8,128)(2,1)}, bf16[128,128,128]{2,1,0:T(8,128)(2,1)}) custom-call(s32[1]{0:T(128)} %bitcast.1.odd_ref, s32[2,128]{1,0:T(2,128)} %copy-done.2, f32[2,8,1152]{2,1,0:T(8,128)} %add.35.rest_0_, bf16[128,8,1024]{2,1,0:T(8,128)(2,1)} %rest_1_.1, f32[1024,128]{1,0:T(8,128)} %broadcast_in_dim.15.rest_2_.rest_3_.rest_4_, ...), custom_call_target="tpu_custom_call" | custom-call | flops 5905580032 | bytes 16777216 | tf_op jit(solution)/shard_map/pallas_call | solution.py:233
  39.0 10.6 %collective-permute-done.4.rest_0_.rest_1_ = f32[2,8,1152]{2,1,0:T(8,128)S(1)} collective-permute-done((f32[2,8,1152]{2,1,0:T(8,128)S(1)}, f32[2,8,1152]{2,1,0:T(8,128)S(1)}, u32[]{:S(2)}, u32[]{:S(2)}) %collective-permute-start.4) | collective-permute-done | bytes 73760 | tf_op jit(solution)/shard_map/ppermute | solution.py:433
  51.2 17.1 %shard_map.84 = (bf16[128,64,128]{2,1,0:T(8,128)(2,1)}, bf16[128,128,128]{2,1,0:T(8,128)(2,1)}) custom-call(s32[1]{0:T(128)} %bitcast.1.odd_ref, s32[2,128]{1,0:T(2,128)} %copy-done.2, f32[2,8,1152]{2,1,0:T(8,128)} %copy-done.9, bf16[64,8,1024]{2,1,0:T(8,128)(2,1)} %collective-permute-done.5.rest_1_, bf16[64,8,1024]{2,1,0:T(8,128)(2,1)} %copy-done.8, ...), custom_call_target="tpu_custom_call" | custom-call | flops 5905580032 | bytes 16777216 | tf_op jit(solution)/shard_map/pallas_call | solution.py:233
  70.3 13.5 %shard_map.85 = (bf16[128,128,128]{2,1,0:T(8,128)(2,1)}, bf16[128,128,128]{2,1,0:T(8,128)(2,1)}) custom-call(s32[1]{0:T(128)} %bitcast.1.odd_ref, s32[2,64]{1,0:T(2,128)} %copy-done.10, f32[2,8,1152]{2,1,0:T(8,128)} %add.35.rest_0_, f32[2,8,1152]{2,1,0:T(8,128)} %copy-done.9, bf16[64,8,1024]{2,1,0:T(8,128)(2,1)} %copy-done.6, ...), custom_call_target="tpu_custom_call" | custom-call | flops 5905580032 | bytes 16777216 | tf_op jit(solution)/shard_map/pallas_call | solution.py:233
  83.9 14.7 %shard_map.86 = (bf16[32,32,128]{2,1,0:T(8,128)(2,1)}, bf16[32,32,128]{2,1,0:T(8,128)(2,1)}, bf16[32,32,128]{2,1,0:T(8,128)(2,1)}, bf16[32,32,128]{2,1,0:T(8,128)(2,1)}) custom-call(s32[1]{0:T(128)} %bitcast.me_ref, bf16[128,64,128]{2,1,0:T(8,128)(2,1)} %get-tuple-element.25.a0_ref, bf16[128,64,128]{2,1,0:T(8,128)(2,1)} %get-tuple-element.27.a1_ref, ...), custom_call_target="tpu_custom_call" | custom-call | flops 2147483648 | bytes 20971520 | tf_op jit(solution)/shard_map/pallas_call | solution.py:358
  98.7 3.0 %collective-permute-start.11 = (bf16[32,32,128]{2,1,0:T(8,128)(2,1)}, bf16[32,32,128]{2,1,0:T(8,128)(2,1)S(1)}, u32[]{:S(2)}, u32[]{:S(2)}) collective-permute-start(bf16[32,32,128]{2,1,0:T(8,128)(2,1)} %get-tuple-element.37), channel_id=1, source_target_pairs={{0,1},{1,28},{2,3},{3,30},{4,5},{5,0},{6,7},{7,2},{8,9},{9,4},{10,... | collective-permute-start | bytes 786440 | tf_op jit(solution)/shard_map/ppermute | solution.py:456
  101.7 1.3 collective-permute-start.12
  103.0 1.6 %collective-permute-start.9 = (bf16[32,32,128]{2,1,0:T(8,128)(2,1)}, bf16[32,32,128]{2,1,0:T(8,128)(2,1)S(1)}, u32[]{:S(2)}, u32[]{:S(2)}) collective-permute-start(bf16[32,32,128]{2,1,0:T(8,128)(2,1)} %get-tuple-element.35), channel_id=1, source_target_pairs={{0,0},{1,29},{2,2},{3,31},{4,4},{5,1},{6,6},{7,3},{8,8},{9,5},{10,... | collective-permute-start | bytes 786440 | tf_op jit(solution)/shard_map/ppermute | solution.py:456
  104.6 14.6 %shard_map.87 = (bf16[32,32,128]{2,1,0:T(8,128)(2,1)}, bf16[32,32,128]{2,1,0:T(8,128)(2,1)}, bf16[32,32,128]{2,1,0:T(8,128)(2,1)}, bf16[32,32,128]{2,1,0:T(8,128)(2,1)}) custom-call(s32[1]{0:T(128)} %bitcast.me_ref, bf16[128,64,128]{2,1,0:T(8,128)(2,1)} %get-tuple-element.25.a0_ref, bf16[128,64,128]{2,1,0:T(8,128)(2,1)} %get-tuple-element.27.a1_ref, ...), custom_call_target="tpu_custom_call" | custom-call | flops 2147483648 | bytes 20971520 | tf_op jit(solution)/shard_map/pallas_call | solution.py:358
  119.2 1.6 %collective-permute-start.13 = (bf16[32,32,128]{2,1,0:T(8,128)(2,1)}, bf16[32,32,128]{2,1,0:T(8,128)(2,1)S(1)}, u32[]{:S(2)}, u32[]{:S(2)}) collective-permute-start(bf16[32,32,128]{2,1,0:T(8,128)(2,1)} %get-tuple-element.39), channel_id=1, source_target_pairs={{0,0},{1,29},{2,2},{3,31},{4,4},{5,1},{6,6},{7,3},{8,8},{9,5},{10,... | collective-permute-start | bytes 786440 | tf_op jit(solution)/shard_map/ppermute | solution.py:456
  121.9 3.9 %collective-permute-start.15 = (bf16[32,32,128]{2,1,0:T(8,128)(2,1)}, bf16[32,32,128]{2,1,0:T(8,128)(2,1)S(1)}, u32[]{:S(2)}, u32[]{:S(2)}) collective-permute-start(bf16[32,32,128]{2,1,0:T(8,128)(2,1)} %get-tuple-element.41), channel_id=1, source_target_pairs={{0,1},{1,28},{2,3},{3,30},{4,5},{5,0},{6,7},{7,2},{8,9},{9,4},{10,... | collective-permute-start | bytes 786440 | tf_op jit(solution)/shard_map/ppermute | solution.py:456
  125.8 5.2 %collective-permute-done.12 = bf16[32,32,128]{2,1,0:T(8,128)(2,1)S(1)} collective-permute-done((bf16[32,32,128]{2,1,0:T(8,128)(2,1)}, bf16[32,32,128]{2,1,0:T(8,128)(2,1)S(1)}, u32[]{:S(2)}, u32[]{:S(2)}) %collective-permute-start.12) | collective-permute-done | bytes 262176 | tf_op jit(solution)/shard_map/ppermute | solution.py:456
  131.2 1.8 %collective-permute-done.14 = bf16[32,32,128]{2,1,0:T(8,128)(2,1)S(1)} collective-permute-done((bf16[32,32,128]{2,1,0:T(8,128)(2,1)}, bf16[32,32,128]{2,1,0:T(8,128)(2,1)S(1)}, u32[]{:S(2)}, u32[]{:S(2)}) %collective-permute-start.14) | collective-permute-done | bytes 262176 | tf_op jit(solution)/shard_map/ppermute | solution.py:456
  133.0 8.9 %collective-permute-done.15 = bf16[32,32,128]{2,1,0:T(8,128)(2,1)S(1)} collective-permute-done((bf16[32,32,128]{2,1,0:T(8,128)(2,1)}, bf16[32,32,128]{2,1,0:T(8,128)(2,1)S(1)}, u32[]{:S(2)}, u32[]{:S(2)}) %collective-permute-start.15) | collective-permute-done | bytes 262176 | tf_op jit(solution)/shard_map/ppermute | solution.py:456
  141.9 6.2 %collective-permute-done.16 = bf16[32,32,128]{2,1,0:T(8,128)(2,1)S(1)} collective-permute-done((bf16[32,32,128]{2,1,0:T(8,128)(2,1)}, bf16[32,32,128]{2,1,0:T(8,128)(2,1)S(1)}, u32[]{:S(2)}, u32[]{:S(2)}) %collective-permute-start.16) | collective-permute-done | bytes 262176 | tf_op jit(solution)/shard_map/ppermute | solution.py:456
  148.2 1.5 pad_maximum_fusion
  (50 shorter events, 10.9 us)
Async XLA Ops:
  0.0 7.3 %copy-start.4 = (s32[128]{0:T(128)S(1)}, s32[128]{0:T(128)}, u32[]{:S(2)}) copy-start(s32[128]{0:T(128)} %sec_ref.1) | copy-start | bytes 1540
  0.0 7.3 %copy-start.5 = (s32[128]{0:T(128)S(1)}, s32[128]{0:T(128)}, u32[]{:S(2)}) copy-start(s32[128]{0:T(128)} %dead_ref.1) | copy-start | bytes 1540
  0.0 14.3 %copy-start.3 = (f32[512]{0:T(512)S(1)}, f32[512]{0:T(512)}, u32[]{:S(2)}) copy-start(f32[512]{0:T(512)} %param.9) | copy-start | bytes 6148
  0.0 17.3 %copy-start = (bf16[128,8,1024]{2,1,0:T(8,128)(2,1)S(1)}, bf16[128,8,1024]{2,1,0:T(8,128)(2,1)}, u32[]{:S(2)}) copy-start(bf16[128,8,1024]{2,1,0:T(8,128)(2,1)} %rest_1_.1) | copy-start | bytes 6291460
  1.5 37.4 %collective-permute-start.5 = (bf16[64,8,1024]{2,1,0:T(8,128)(2,1)S(1)}, bf16[64,8,1024]{2,1,0:T(8,128)(2,1)}, u32[]{:S(2)}, u32[]{:S(2)}) collective-permute-start(bf16[64,8,1024]{2,1,0:T(8,128)(2,1)S(1)} %constant_dynamic-slice_fusion.1), channel_id=1, source_target_pairs={{0,1},{1,0},{2,3},{3,2},{4,5},{5,4},{6,7},{7,6},{8,9},{9,8},{10,11... | collective-permute-start | bytes 3145736 | tf_op jit(solution)/shard_map/ppermute | solution.py:416
  6.4 2.1 %collective-permute-start = (f32[2,8,1152]{2,1,0:T(8,128)}, f32[2,8,1152]{2,1,0:T(8,128)S(1)}, u32[]{:S(2)}, u32[]{:S(2)}) collective-permute-start(f32[2,8,1152]{2,1,0:T(8,128)} %shard_map.82), channel_id=1, source_target_pairs={{0,4},{4,0},{8,12},{12,8},{16,20},{20,16},{24,28},{28,24},{1,5},{5... | collective-permute-start | bytes 221192 | tf_op jit(solution)/shard_map/ppermute | solution.py:392
  7.3 14.3 %copy-start.2 = (s32[2,128]{1,0:T(2,128)}, s32[2,128]{1,0:T(2,128)S(1)}, u32[]{:S(2)}) copy-start(s32[2,128]{1,0:T(2,128)S(1)} %pad_add_fusion.flag_ref) | copy-start | bytes 3076
  9.4 3.7 %collective-permute-start.1 = (f32[2,8,1152]{2,1,0:T(8,128)S(1)}, f32[2,8,1152]{2,1,0:T(8,128)S(1)}, u32[]{:S(2)}, u32[]{:S(2)}) collective-permute-start(f32[2,8,1152]{2,1,0:T(8,128)S(1)} %add.33), channel_id=1, source_target_pairs={{0,8},{4,12},{8,0},{12,4},{16,24},{20,28},{24,16},{28,20},{1,9},{5... | collective-permute-start | bytes 221192 | tf_op jit(solution)/shard_map/ppermute | solution.py:392
  9.7 7.6 %collective-permute-start.3 = (s32[2,64]{1,0:T(2,128)S(1)}, s32[2,64]{1,0:T(2,128)S(1)}, u32[]{:S(2)}, u32[]{:S(2)}) collective-permute-start(s32[2,64]{1,0:T(2,128)S(1)} %constant_dynamic-slice_fusion.2), channel_id=1, source_target_pairs={{0,28},{1,5},{2,30},{3,7},{4,0},{5,9},{6,2},{7,11},{8,4},{9,13},{1... | collective-permute-start | bytes 1544 | tf_op jit(solution)/shard_map/ppermute | solution.py:418
  13.0 3.7 %collective-permute-start.2 = (f32[2,8,1152]{2,1,0:T(8,128)S(1)}, f32[2,8,1152]{2,1,0:T(8,128)S(1)}, u32[]{:S(2)}, u32[]{:S(2)}) collective-permute-start(f32[2,8,1152]{2,1,0:T(8,128)S(1)} %add.34), channel_id=1, source_target_pairs={{0,16},{4,20},{8,24},{12,28},{16,0},{20,4},{24,8},{28,12},{1,17},{... | collective-permute-start | bytes 221192 | tf_op jit(solution)/shard_map/ppermute | solution.py:392
  17.3 21.5 %copy-start.10 = (s32[2,64]{1,0:T(2,128)}, s32[2,64]{1,0:T(2,128)S(1)}, u32[]{:S(2)}) copy-start(s32[2,64]{1,0:T(2,128)S(1)} %collective-permute-done.3.flag_ref) | copy-start | bytes 1540
  17.4 50.9 %collective-permute-start.7 = (bf16[64,8,1024]{2,1,0:T(8,128)(2,1)S(1)}, bf16[64,8,1024]{2,1,0:T(8,128)(2,1)S(1)}, u32[]{:S(2)}, u32[]{:S(2)}) collective-permute-start(bf16[64,8,1024]{2,1,0:T(8,128)(2,1)S(1)} %constant_dynamic-slice_fusion), channel_id=1, source_target_pairs={{0,28},{1,5},{2,30},{3,7},{4,0},{5,9},{6,2},{7,11},{8,4},{9,13},{1... | collective-permute-start | bytes 3145736 | tf_op jit(solution)/shard_map/ppermute | solution.py:436
  19.3 30.3 %collective-permute-start.6 = (bf16[64,8,1024]{2,1,0:T(8,128)(2,1)S(1)}, bf16[64,8,1024]{2,1,0:T(8,128)(2,1)S(1)}, u32[]{:S(2)}, u32[]{:S(2)}) collective-permute-start(bf16[64,8,1024]{2,1,0:T(8,128)(2,1)S(1)} %constant_dynamic-slice_fusion), channel_id=1, source_target_pairs={{0,1},{1,0},{2,3},{3,2},{4,5},{5,4},{6,7},{7,6},{8,9},{9,8},{10,11... | collective-permute-start | bytes 3145736 | tf_op jit(solution)/shard_map/ppermute | solution.py:435
  21.6 17.3 %copy-start.1 = (f32[2,8,1152]{2,1,0:T(8,128)S(1)}, f32[2,8,1152]{2,1,0:T(8,128)}, u32[]{:S(2)}) copy-start(f32[2,8,1152]{2,1,0:T(8,128)} %add.35.rest_0_) | copy-start | bytes 221188
  38.8 29.5 %collective-permute-start.8 = (bf16[64,8,1024]{2,1,0:T(8,128)(2,1)}, bf16[64,8,1024]{2,1,0:T(8,128)(2,1)S(1)}, u32[]{:S(2)}, u32[]{:S(2)}) collective-permute-start(bf16[64,8,1024]{2,1,0:T(8,128)(2,1)} %collective-permute-done.5.rest_1_), channel_id=1, source_target_pairs={{0,28},{1,5},{2,30},{3,7},{4,0},{5,9},{6,2},{7,11},{8,4},{9,13},{1... | collective-permute-start | bytes 3145736 | tf_op jit(solution)/shard_map/ppermute | solution.py:442
  38.9 10.7 %collective-permute-start.4 = (f32[2,8,1152]{2,1,0:T(8,128)S(1)}, f32[2,8,1152]{2,1,0:T(8,128)S(1)}, u32[]{:S(2)}, u32[]{:S(2)}) collective-permute-start(f32[2,8,1152]{2,1,0:T(8,128)S(1)} %copy-done.1), channel_id=1, source_target_pairs={{0,1},{1,0},{2,3},{3,2},{4,5},{5,4},{6,7},{7,6},{8,9},{9,8},{10,11... | collective-permute-start | bytes 221192 | tf_op jit(solution)/shard_map/ppermute | solution.py:433
  98.6 22.2 %collective-permute-start.10 = (bf16[32,32,128]{2,1,0:T(8,128)(2,1)}, bf16[32,32,128]{2,1,0:T(8,128)(2,1)S(1)}, u32[]{:S(2)}, u32[]{:S(2)}) collective-permute-start(bf16[32,32,128]{2,1,0:T(8,128)(2,1)} %get-tuple-element.36), channel_id=1, source_target_pairs={{0,2},{1,31},{2,0},{3,29},{4,6},{5,3},{6,4},{7,1},{8,10},{9,7},{10... | collective-permute-start | bytes 786440 | tf_op jit(solution)/shard_map/ppermute | solution.py:456
  98.7 23.2 %collective-permute-start.11 = (bf16[32,32,128]{2,1,0:T(8,128)(2,1)}, bf16[32,32,128]{2,1,0:T(8,128)(2,1)S(1)}, u32[]{:S(2)}, u32[]{:S(2)}) collective-permute-start(bf16[32,32,128]{2,1,0:T(8,128)(2,1)} %get-tuple-element.37), channel_id=1, source_target_pairs={{0,1},{1,28},{2,3},{3,30},{4,5},{5,0},{6,7},{7,2},{8,9},{9,4},{10,... | collective-permute-start | bytes 786440 | tf_op jit(solution)/shard_map/ppermute | solution.py:456
  101.7 29.3 %collective-permute-start.12 = (bf16[32,32,128]{2,1,0:T(8,128)(2,1)}, bf16[32,32,128]{2,1,0:T(8,128)(2,1)S(1)}, u32[]{:S(2)}, u32[]{:S(2)}) collective-permute-start(bf16[32,32,128]{2,1,0:T(8,128)(2,1)} %get-tuple-element.38), channel_id=1, source_target_pairs={{0,3},{1,30},{2,1},{3,28},{4,7},{5,2},{6,5},{7,0},{8,11},{9,6},{10... | collective-permute-start | bytes 786440 | tf_op jit(solution)/shard_map/ppermute | solution.py:456
  103.0 28.0 %collective-permute-start.9 = (bf16[32,32,128]{2,1,0:T(8,128)(2,1)}, bf16[32,32,128]{2,1,0:T(8,128)(2,1)S(1)}, u32[]{:S(2)}, u32[]{:S(2)}) collective-permute-start(bf16[32,32,128]{2,1,0:T(8,128)(2,1)} %get-tuple-element.35), channel_id=1, source_target_pairs={{0,0},{1,29},{2,2},{3,31},{4,4},{5,1},{6,6},{7,3},{8,8},{9,5},{10,... | collective-permute-start | bytes 786440 | tf_op jit(solution)/shard_map/ppermute | solution.py:456
  119.2 12.0 %collective-permute-start.13 = (bf16[32,32,128]{2,1,0:T(8,128)(2,1)}, bf16[32,32,128]{2,1,0:T(8,128)(2,1)S(1)}, u32[]{:S(2)}, u32[]{:S(2)}) collective-permute-start(bf16[32,32,128]{2,1,0:T(8,128)(2,1)} %get-tuple-element.39), channel_id=1, source_target_pairs={{0,0},{1,29},{2,2},{3,31},{4,4},{5,1},{6,6},{7,3},{8,8},{9,5},{10,... | collective-permute-start | bytes 786440 | tf_op jit(solution)/shard_map/ppermute | solution.py:456
  120.8 12.2 %collective-permute-start.14 = (bf16[32,32,128]{2,1,0:T(8,128)(2,1)}, bf16[32,32,128]{2,1,0:T(8,128)(2,1)S(1)}, u32[]{:S(2)}, u32[]{:S(2)}) collective-permute-start(bf16[32,32,128]{2,1,0:T(8,128)(2,1)} %get-tuple-element.40), channel_id=1, source_target_pairs={{0,2},{1,31},{2,0},{3,29},{4,6},{5,3},{6,4},{7,1},{8,10},{9,7},{10... | collective-permute-start | bytes 786440 | tf_op jit(solution)/shard_map/ppermute | solution.py:456
  121.9 20.0 %collective-permute-start.15 = (bf16[32,32,128]{2,1,0:T(8,128)(2,1)}, bf16[32,32,128]{2,1,0:T(8,128)(2,1)S(1)}, u32[]{:S(2)}, u32[]{:S(2)}) collective-permute-start(bf16[32,32,128]{2,1,0:T(8,128)(2,1)} %get-tuple-element.41), channel_id=1, source_target_pairs={{0,1},{1,28},{2,3},{3,30},{4,5},{5,0},{6,7},{7,2},{8,9},{9,4},{10,... | collective-permute-start | bytes 786440 | tf_op jit(solution)/shard_map/ppermute | solution.py:456
  131.0 17.0 %collective-permute-start.16 = (bf16[32,32,128]{2,1,0:T(8,128)(2,1)}, bf16[32,32,128]{2,1,0:T(8,128)(2,1)S(1)}, u32[]{:S(2)}, u32[]{:S(2)}) collective-permute-start(bf16[32,32,128]{2,1,0:T(8,128)(2,1)} %get-tuple-element.42), channel_id=1, source_target_pairs={{0,3},{1,30},{2,1},{3,28},{4,7},{5,2},{6,5},{7,0},{8,11},{9,6},{10... | collective-permute-start | bytes 786440 | tf_op jit(solution)/shard_map/ppermute | solution.py:456
  (4 other events, 3.6 us)

commit v5 on v4

--- a/solution.py
+++ b/solution.py
@@ -17,7 +17,7 @@
 CHUNKS = 2
 TILE = 256
 STEPS = 4
-VMEM = 56 * 1024 * 1024
+VMEM = 60 * 1024 * 1024
 NT = (((1,), (1,)), ((), ()))
 F32 = jnp.float32
 BF16 = jnp.bfloat16
@@ -26,20 +26,16 @@
 def tables(ns, nf):
     tick = np.arange(ns)
     freq = np.arange(nf)
-    phase = (tick[:, None] * freq[None, :] % ns) * (2.0 * math.pi / ns)
     window = 0.5 - 0.5 * np.cos(tick * (2.0 * math.pi / ns))
-    forward = np.concatenate(
-        [window[:, None] * np.cos(phase), -window[:, None] * np.sin(phase)], axis=1
-    )
-    back = np.concatenate([np.cos(phase), -np.sin(phase)], axis=1)
-    back[:, 0] *= math.sqrt(0.5)
+    waves = np.cos((freq[:, None] * tick[None, :] % ns) * (2.0 * math.pi / ns))
+    waves[0] *= math.sqrt(0.5)
     size = 2 * LAGS
     bins = np.arange(size // 2)
     turn = math.pi / size * ((2 * bins[:, None] + 1) * np.arange(size)[None, :] % (2 * size))
     segment = np.stack([np.cos(turn), -np.sin(turn)], axis=1).reshape(size, size)
     lag = np.stack([np.cos(turn), -np.sin(turn)], axis=1).reshape(size, size)[:, :LAGS].T
     cast = lambda a: a.astype(np.float32).astype(ml_dtypes.bfloat16)
-    return cast(forward.T), cast(back), cast(segment), cast(lag)
+    return window.astype(np.float32), waves.astype(np.float32), cast(segment), cast(lag)
 
 
 def section_sums(dead_ref, sec_ref, x_ref, out_ref):
@@ -69,19 +65,27 @@
         out_ref[s, :, ns:] += jnp.zeros((wins, LANE), F32) + counts[s]
 
 
+def circulant_kernel(filter_ref, out_ref):
+    ns = filter_ref.shape[1]
+    rows = 16
+    for t in range(0, ns, rows):
+        block = jnp.broadcast_to(filter_ref[...], (rows, ns))
+        out_ref[t : t + rows, :] = pltpu.roll(block, t, 1, stride=1, stride_axis=0).astype(BF16)
+
+
 def segments_kernel(kind, odd_ref, flag_ref, *rest):
     sets = {"own": (0,), "halo": (0, 1), "other": (0, 0)}[kind]
     groups = max(sets) + 1
     count = len(sets)
     tot_hbm, rest = rest[:groups], rest[groups:]
     x_hbm, rest = rest[:count], rest[count:]
-    gain_hbm, fwd_hbm, back_hbm, seg_hbm, a_hbm, b_hbm = rest[:6]
-    tot, rest = rest[6 : 6 + groups], rest[6 + groups :]
+    hann_hbm, conv_hbm, seg_hbm, a_hbm, b_hbm = rest[:5]
+    tot, rest = rest[5 : 5 + groups], rest[5 + groups :]
     x, rest = rest[:count], rest[count:]
-    gain, fwd, back, seg, common, clean, rows, spec, white, series, a_s, b_s, a_out, b_out = rest[:14]
-    in_sem, out_sem = rest[14:]
-    sources = list(tot_hbm) + list(x_hbm) + [fwd_hbm, gain_hbm, back_hbm, seg_hbm]
-    targets = list(tot) + list(x) + [fwd, gain, back, seg]
+    hann, conv, seg, common, clean, rows, series, a_s, b_s, a_out, b_out = rest[:11]
+    in_sem, out_sem = rest[11:]
+    sources = list(tot_hbm) + [hann_hbm] + list(x_hbm) + [conv_hbm, seg_hbm]
+    targets = list(tot) + [hann] + list(x) + [conv, seg]
     copies = [
         pltpu.make_async_copy(source, target, in_sem.at[n])
         for n, (source, target) in enumerate(zip(sources, targets))
@@ -91,7 +95,6 @@
 
     _, wins, ns = x[0].shape
     chans = b_out.shape[2]
-    nfr = spec.shape[0]
     pitch = wins + 1
     size = seg.shape[0]
     half = size // 2
@@ -106,8 +109,11 @@
         for s in range(NSEC):
             common[g * NSEC + s] = tot[g][s, :, :ns] / jnp.maximum(tot[g][s, :, ns : ns + 1], 1.0)
 
+    copies[groups].wait()
+    sign = 1.0 - 2.0 * (lax.broadcasted_iota(jnp.int32, (wins, LANE), 1) % 2).astype(F32)
+
     for number, group in enumerate(sets):
-        copies[groups + number].wait()
+        copies[groups + 1 + number].wait()
         piece = x[number]
         length = piece.shape[0]
         base = number * length
@@ -118,13 +124,21 @@
             at = base + c
             flag = lax.rem(at, held)
             live = (1 - flag_ref[0, flag]).astype(F32)
-            value = (piece[c].astype(F32) - common[group * NSEC + flag_ref[1, flag]]) * live
+            value = (piece[c].astype(F32) - common[group * NSEC + flag_ref[1, flag]]) * hann[...]
+            tiles = [value[:, t * LANE : (t + 1) * LANE] for t in range(ns // LANE)]
+            mass = sum(tiles[1:], tiles[0])
+            square = sum([tile * tile for tile in tiles[1:]], tiles[0] * tiles[0])
+            lowest = jnp.sum(mass, axis=1, keepdims=True)
+            highest = jnp.sum(mass * sign, axis=1, keepdims=True)
+            square = jnp.sum(square, axis=1, keepdims=True)
+            power = 0.5 * square + (lowest * lowest - highest * highest) * (0.5 / ns)
+            value = value * (lax.rsqrt(power + 1e-06) * live)
             for t in range(ns // LANE):
                 clean[t, pl.ds(at * pitch, wins), :] = value[:, t * LANE : (t + 1) * LANE]
             return 0
 
         lax.fori_loop(0, length, clean_channel, 0, unroll=8)
-    for copy in copies[groups + count :]:
+    for copy in copies[groups + 1 + count :]:
         copy.wait()
 
     def pair(step, _):
@@ -134,23 +148,9 @@
                 rows[i * chans : (i + 1) * chans, t * LANE : (t + 1) * LANE] = clean[
                     t, pl.ds(w, chans, stride=pitch), :
                 ].astype(BF16)
-        power = jnp.zeros((1, 2 * chans), F32)
-        for f in range(0, nfr, TILE):
-            s = lax.dot_general(
-                fwd[f : f + TILE, :], rows[...], NT, preferred_element_type=F32
-            )
-            spec[f : f + TILE, :] = s
-            power = power + jnp.sum(s * s, axis=0, keepdims=True)
-        level = lax.rsqrt(power / nfr + 1e-06)
-        for i in range(2):
-            white[:, i * chans : (i + 1) * chans] = (
-                spec[:, i * chans : (i + 1) * chans]
-                * gain[...]
-                * level[:, i * chans : (i + 1) * chans]
-            ).astype(BF16)
         for t in range(0, ns, TILE):
-            series[half // 2 + t : half // 2 + t + TILE, :] = jnp.dot(
-                back[t : t + TILE, :], white[...], preferred_element_type=F32
+            series[half // 2 + t : half // 2 + t + TILE, :] = lax.dot_general(
+                conv[t : t + TILE, :], rows[...], NT, preferred_element_type=F32
             ).astype(BF16)
         series[: half // 2, :] = series[ns : ns + half // 2, :]
         series[ns + half // 2 :, :] = series[half // 2 : half, :]
@@ -216,17 +216,16 @@
         sends(STEPS + n, b_out, b_hbm).wait()
 
 
-def segments(kind, odd, flags, totals, pieces, gain, fwd, back, seg):
+def segments(kind, odd, flags, totals, pieces, hann, conv, seg):
     chans = sum(x.shape[0] for x in pieces)
     _, wins, ns = pieces[0].shape
-    nfr = fwd.shape[0]
     size = seg.shape[0]
     half = size // 2
     depth = ns // half * wins * 2
     kept = chans if kind == "halo" else chans // 2
     smem = pl.BlockSpec(memory_space=pltpu.SMEM)
     anywhere = pl.BlockSpec(memory_space=pl.ANY)
-    tables_in = [gain, fwd, back, seg]
+    tables_in = [hann, conv, seg]
     operands = list(totals) + list(pieces) + tables_in
     a_shape = jax.ShapeDtypeStruct((half, kept, depth), BF16)
     b_shape = jax.ShapeDtypeStruct((half, depth, chans), BF16)
@@ -240,8 +239,6 @@
             pltpu.VMEM((len(totals) * NSEC, wins, ns), F32),
             pltpu.VMEM((ns // LANE, chans * (wins + 1), LANE), F32),
             pltpu.VMEM((2 * chans, ns), BF16),
-            pltpu.VMEM((nfr, 2 * chans), F32),
-            pltpu.VMEM((nfr, 2 * chans), BF16),
             pltpu.VMEM((ns + half, 2 * chans), BF16),
             pltpu.VMEM((size * (depth // 2 + 1), chans), F32),
             pltpu.VMEM((size * (depth // 2 + 1), chans), F32),
@@ -252,7 +249,7 @@
         ],
         compiler_params=pltpu.CompilerParams(vmem_limit_bytes=VMEM),
         cost_estimate=pl.CostEstimate(
-            flops=2 * wins * chans * ns * (2 * nfr + 3 * size),
+            flops=2 * wins * chans * ns * (ns + 3 * size),
             bytes_accessed=16 * 1024 * 1024,
             transcendentals=0,
         ),
@@ -389,8 +386,11 @@
         return lax.psum(value, axis)
     bit = 1
     while bit < count:
-        value = value + lax.ppermute(value, axis, [(i, i ^ bit) for i in range(count)])
-        bit *= 2
+        steps = [bit] if bit == 1 or 2 * bit == count else [bit, 2 * bit, 3 * bit]
+        value = sum(
+            [lax.ppermute(value, axis, [(i, i ^ s) for i in range(count)]) for s in steps], value
+        )
+        bit *= 1 + len(steps)
     return value
 
 
@@ -402,8 +402,14 @@
     groups = lax.axis_size("tm")
     me = lax.axis_index("tm")
     odd = me % 2
-    fwd, back, seg, lag = [jnp.asarray(t) for t in tables(ns, nf)]
-    gain = jnp.broadcast_to(jnp.concatenate([band_gain, band_gain])[:, None], (2 * nf, chans))
+    window, waves, seg, lag = [jnp.asarray(t) for t in tables(ns, nf)]
+    hann = jnp.broadcast_to(window[None, :], (wins, ns))
+    response = jnp.sum(band_gain[:, None] * waves, axis=0, keepdims=True)
+    conv = pl.pallas_call(
+        circulant_kernel,
+        out_shape=jax.ShapeDtypeStruct((ns, ns), BF16),
+        compiler_params=pltpu.CompilerParams(vmem_limit_bytes=VMEM),
+    )(response)
     swap = [(z, z ^ 1) for z in range(groups)]
     both = ("fibre", "tm")
     halo_pairs = [
@@ -413,7 +419,9 @@
     ]
 
     first_half = lax.dynamic_slice_in_dim(samples, (1 - odd) * width, width, 0)
+    own_half = lax.dynamic_slice_in_dim(samples, odd * width, width, 0)
     their_first = lax.ppermute(first_half, "tm", swap)
+    halo = lax.ppermute(own_half, both, halo_pairs)
     flags = jnp.stack([dead_flags, section_ids])
     halo_flags = lax.ppermute(
         lax.dynamic_slice_in_dim(flags, odd * width, width, 1), both, halo_pairs
@@ -429,18 +437,19 @@
         compiler_params=pltpu.CompilerParams(vmem_limit_bytes=VMEM),
     )(dead_flags, section_ids, samples)
     total = add_over(sums, "fibre")
-    total, halo_flags, kept = lax.optimization_barrier((total, halo_flags, samples))
+    total, halo, halo_flags = lax.optimization_barrier((total, halo, halo_flags))
     their_total = lax.ppermute(total, "tm", swap)
-    own_half = lax.dynamic_slice_in_dim(kept, odd * width, width, 0)
+    ready = (total, their_total, their_first, own_half, flags, hann, conv, seg, lag)
+    ready = lax.optimization_barrier(ready)
+    total, their_total, their_first, own_half, flags, hann, conv, seg, lag = ready
+    their_halo = lax.ppermute(their_first, both, halo_pairs)
     their_second = lax.ppermute(own_half, "tm", swap)
-    halo = lax.ppermute(own_half, both, halo_pairs)
 
     side = odd[None]
-    parts = (gain, fwd, back, seg)
+    parts = (hann, conv, seg)
     a0, b0 = segments("own", side, flags, (total,), (samples,), *parts)
-    b0, forward = lax.optimization_barrier((b0, their_first))
-    their_halo = lax.ppermute(forward, both, halo_pairs)
     ah, bh = segments("halo", side, halo_flags, (total, their_total), (halo, their_halo), *parts)
+    bh, their_second = lax.optimization_barrier((bh, their_second))
     a1, b1 = segments("other", side, flags, (their_total,), (their_first, their_second), *parts)
     scale = 2.0 / ns / LAGS / math.sqrt(nf * wins * groups)
     same, other = [], []

time: 150 us -> 142 us (0.947)
  waiting for transfers between devices: 38.8 us -> 33.7 us
  Pallas kernels: 80.7 us -> 75.8 us
  starting transfers between devices: 20.4 us -> 23.2 us
    ppermute x1, waiting for transfers between devices: 10.6 us -> 0.98 us  [shards(): their_total = lax.ppermute(total, 'tm', swap)]
    pallas_call x3, Pallas kernels: 47.8 us -> 40.2 us  [segments(): pl.pallas_call(functools.partial(segments_kernel, kind), out_shape=[a_sha...]
    ppermute x1, starting transfers between devices: 0.63 us -> 4.78 us  [shards(): lax.ppermute(lax.dynamic_slice_in_dim(flags, odd * width, width, 1), both...]
    ppermute x1, waiting for transfers between devices: 0.01 us -> 3.72 us  [shards(): their_first = lax.ppermute(first_half, 'tm', swap)]
    ppermute x4 -> x5, waiting for transfers between devices: 6.1 us -> 3.18 us  [the longest x4 3.18 us: add_over(): lax.ppermute(value, axis, [(i, i ^ s) for i in range(count)])]
    pallas_call x0 -> x1, Pallas kernels: none -> 2.6 us  [shards(): pl.pallas_call(circulant_kernel, out_shape=jax.ShapeDtypeStruct((ns, ns),...]
    ppermute x8, starting transfers between devices: 12.5 us -> 9.91 us  [shards(): arrived.append(lax.ppermute(found[d], both, pairs).astype(F32))]
    ppermute x8, waiting for transfers between devices: 22.1 us -> 24.4 us  [shards(): arrived.append(lax.ppermute(found[d], both, pairs).astype(F32))]
  transfers between devices with their start and end apart: 17 -> 18, of which waited for: 8 -> 9; matrix products, arithmetic and copies ran while one was open for 2% -> 2% of each run, Pallas kernels for 35% -> 33%
where the time goes in v5:
time: 142 us
  Pallas kernels  75.8 us (53%)
  waiting for transfers between devices  33.7 us (24%)
  starting transfers between devices  23.2 us (16%)
  local copies, waits for them, and re-layouts  5.36 us (4%)
  other arithmetic  3.54 us (2%)
    pallas_call x3, Pallas kernels, segments(): pl.pallas_call(functools.partial(segments_kernel, kind), out_shape=[a_sha...  40.2 us
    pallas_call x2, Pallas kernels, stacks(): pl.pallas_call(functools.partial(stack_kernel, index * count, scale), gri...  29.4 us
    ppermute x8, waiting for transfers between devices, shards(): arrived.append(lax.ppermute(found[d], both, pairs).astype(F32))  24.4 us
    ppermute x8, starting transfers between devices, shards(): arrived.append(lax.ppermute(found[d], both, pairs).astype(F32))  9.91 us
    ppermute x1, starting transfers between devices, shards(): lax.ppermute(lax.dynamic_slice_in_dim(flags, odd * width, width, 1), both...  4.78 us
    ppermute x1, waiting for transfers between devices, shards(): their_first = lax.ppermute(first_half, 'tm', swap)  3.72 us
    pallas_call x1, Pallas kernels, shards(): pl.pallas_call(section_sums, grid=(steps,), out_shape=jax.ShapeDtypeStruc...  3.54 us
    ppermute x4, waiting for transfers between devices, add_over(): lax.ppermute(value, axis, [(i, i ^ s) for i in range(count)])  3.18 us
  transfers between devices with their start and end apart: 18, of which 9 were waited for; matrix products, arithmetic and copies ran while one was open for 2% of the time, Pallas kernels for 33%

profile of v5, /device:TPU:19, one launch (start us, length us, event | category | flops | bytes accessed | tf_op | source)
XLA Modules:
  0.0 141.7 jit_solution(12946018295251497083)
XLA Ops:
  0.0 2.7 %constant_dynamic-slice_fusion = (bf16[64,8,1024]{2,1,0:T(8,128)(2,1)}, bf16[64,8,1024]{2,1,0:T(8,128)(2,1)S(1)}) fusion(bf16[128,8,1024]{2,1,0:T(8,128)(2,1)} %rest_1_.1, s32[]{:T(128)S(6)} %select_n.37, s32[]{:T(128)S(6)} %select_n.36), kind=kLoop, calls=%fused_computation.12 | loop fusion | bytes 4194312 | tf_op jit(solution)/shard_map/dynamic_slice | solution.py:421
  3.4 2.4 %collective-permute-start.7 = (bf16[64,8,1024]{2,1,0:T(8,128)(2,1)}, bf16[64,8,1024]{2,1,0:T(8,128)(2,1)}, u32[]{:S(2)}, u32[]{:S(2)}) collective-permute-start(bf16[64,8,1024]{2,1,0:T(8,128)(2,1)} %get-tuple-element.61), channel_id=1, source_target_pairs={{0,1},{1,0},{2,3},{3,2},{4,5},{5,4},{6,7},{7,6},{8,9},{9,8},{10,11... | collective-permute-start | bytes 3145736 | tf_op jit(solution)/shard_map/ppermute | solution.py:423
  5.8 3.5 %shard_map.82 = f32[2,8,1152]{2,1,0:T(8,128)} custom-call(s32[128]{0:T(128)} %dead_ref.1, s32[128]{0:T(128)} %sec_ref.1, bf16[128,8,1024]{2,1,0:T(8,128)(2,1)} %rest_1_.1), custom_call_target="tpu_custom_call" | custom-call | tf_op jit(solution)/shard_map/pallas_call | solution.py:431
  9.4 1.4 %collective-permute-done = f32[2,8,1152]{2,1,0:T(8,128)S(1)} collective-permute-done((f32[2,8,1152]{2,1,0:T(8,128)}, f32[2,8,1152]{2,1,0:T(8,128)S(1)}, u32[]{:S(2)}, u32[]{:S(2)}) %collective-permute-start) | collective-permute-done | bytes 73760 | tf_op jit(solution)/shard_map/ppermute | solution.py:391
  14.5 1.7 %collective-permute-done.1 = f32[2,8,1152]{2,1,0:T(8,128)S(1)} collective-permute-done((f32[2,8,1152]{2,1,0:T(8,128)S(1)}, f32[2,8,1152]{2,1,0:T(8,128)S(1)}, u32[]{:S(2)}, u32[]{:S(2)}) %collective-permute-start.1) | collective-permute-done | bytes 73760 | tf_op jit(solution)/shard_map/ppermute | solution.py:391
  16.3 4.8 %collective-permute-start.5 = (s32[2,64]{1,0:T(2,128)S(1)}, s32[2,64]{1,0:T(2,128)S(1)}, u32[]{:S(2)}, u32[]{:S(2)}) collective-permute-start(s32[2,64]{1,0:T(2,128)S(1)} %constant_dynamic-slice_fusion.1), channel_id=1, source_target_pairs={{0,28},{1,5},{2,30},{3,7},{4,0},{5,9},{6,2},{7,11},{8,4},{9,13},{1... | collective-permute-start | bytes 1544 | tf_op jit(solution)/shard_map/ppermute | solution.py:426
  21.1 1.3 collective-permute-done.5.flag_ref
  23.3 2.6 %shard_map.83.rest_3_.rest_5_.rest_4_ = bf16[1024,1024]{1,0:T(8,128)(2,1)} custom-call(f32[1,1024]{1,0:T(1,128)} %bitcast.8), custom_call_target="tpu_custom_call" | custom-call | tf_op jit(solution)/shard_map/pallas_call | solution.py:408
  25.9 3.7 %collective-permute-done.7.rest_1_ = bf16[64,8,1024]{2,1,0:T(8,128)(2,1)} collective-permute-done((bf16[64,8,1024]{2,1,0:T(8,128)(2,1)}, bf16[64,8,1024]{2,1,0:T(8,128)(2,1)}, u32[]{:S(2)}, u32[]{:S(2)}) %collective-permute-start.7) | collective-permute-done | bytes 1048608 | tf_op jit(solution)/shard_map/ppermute | solution.py:423
  31.0 2.2 %collective-permute-start.9 = (bf16[64,8,1024]{2,1,0:T(8,128)(2,1)S(1)}, bf16[64,8,1024]{2,1,0:T(8,128)(2,1)S(1)}, u32[]{:S(2)}, u32[]{:S(2)}) collective-permute-start(bf16[64,8,1024]{2,1,0:T(8,128)(2,1)S(1)} %get-tuple-element.45), channel_id=1, source_target_pairs={{0,1},{1,0},{2,3},{3,2},{4,5},{5,4},{6,7},{7,6},{8,9},{9,8},{10,11... | collective-permute-start | bytes 3145736 | tf_op jit(solution)/shard_map/ppermute | solution.py:446
  33.8 14.8 %shard_map.84 = (bf16[128,64,128]{2,1,0:T(8,128)(2,1)}, bf16[128,128,128]{2,1,0:T(8,128)(2,1)}) custom-call(s32[1]{0:T(128)} %bitcast.1.odd_ref, s32[2,128]{1,0:T(2,128)} %copy-done.3, f32[2,8,1152]{2,1,0:T(8,128)} %copy-done.1, bf16[128,8,1024]{2,1,0:T(8,128)(2,1)} %rest_1_.1, f32[8,1024]{1,0:T(8,128)} %broadcast_in_dim.19.rest_2_.rest_4_.rest_3_, ...), custom_call_target="tpu_custom_call" | custom-call | flops 3758096384 | bytes 16777216 | tf_op jit(solution)/shard_map/pallas_call | solution.py:232
  49.7 10.9 %shard_map.85 = (bf16[128,128,128]{2,1,0:T(8,128)(2,1)}, bf16[128,128,128]{2,1,0:T(8,128)(2,1)}) custom-call(s32[1]{0:T(128)} %bitcast.1.odd_ref, s32[2,64]{1,0:T(2,128)} %copy-done.10, f32[2,8,1152]{2,1,0:T(8,128)} %copy-done.1, f32[2,8,1152]{2,1,0:T(8,128)} %copy-done.9, bf16[64,8,1024]{2,1,0:T(8,128)(2,1)} %collective-permute-done.4.rest_2_, ...), custom_call_target="tpu_custom_call" | custom-call | flops 3758096384 | bytes 16777216 | tf_op jit(solution)/shard_map/pallas_call | solution.py:232
  61.6 14.5 %shard_map.86 = (bf16[128,64,128]{2,1,0:T(8,128)(2,1)}, bf16[128,128,128]{2,1,0:T(8,128)(2,1)}) custom-call(s32[1]{0:T(128)} %bitcast.1.odd_ref, s32[2,128]{1,0:T(2,128)} %copy-done.3, f32[2,8,1152]{2,1,0:T(8,128)} %copy-done.9, bf16[64,8,1024]{2,1,0:T(8,128)(2,1)} %collective-permute-done.7.rest_1_, bf16[64,8,1024]{2,1,0:T(8,128)(2,1)} %copy-done.7, ...), custom_call_target="tpu_custom_call" | custom-call | flops 3758096384 | bytes 16777216 | tf_op jit(solution)/shard_map/pallas_call | solution.py:232
  76.1 14.7 %shard_map.87 = (bf16[32,32,128]{2,1,0:T(8,128)(2,1)}, bf16[32,32,128]{2,1,0:T(8,128)(2,1)}, bf16[32,32,128]{2,1,0:T(8,128)(2,1)}, bf16[32,32,128]{2,1,0:T(8,128)(2,1)}) custom-call(s32[1]{0:T(128)} %bitcast.me_ref, bf16[128,64,128]{2,1,0:T(8,128)(2,1)} %get-tuple-element.39.a0_ref, bf16[128,64,128]{2,1,0:T(8,128)(2,1)} %get-tuple-element.47.a1_ref, ...), custom_call_target="tpu_custom_call" | custom-call | flops 2147483648 | bytes 20971520 | tf_op jit(solution)/shard_map/pallas_call | solution.py:355
  90.8 1.6 %collective-permute-start.10 = (bf16[32,32,128]{2,1,0:T(8,128)(2,1)}, bf16[32,32,128]{2,1,0:T(8,128)(2,1)S(1)}, u32[]{:S(2)}, u32[]{:S(2)}) collective-permute-start(bf16[32,32,128]{2,1,0:T(8,128)(2,1)} %get-tuple-element.53), channel_id=1, source_target_pairs={{0,0},{1,29},{2,2},{3,31},{4,4},{5,1},{6,6},{7,3},{8,8},{9,5},{10,... | collective-permute-start | bytes 786440 | tf_op jit(solution)/shard_map/ppermute | solution.py:465
  92.5 2.3 %collective-permute-start.13 = (bf16[32,32,128]{2,1,0:T(8,128)(2,1)}, bf16[32,32,128]{2,1,0:T(8,128)(2,1)S(1)}, u32[]{:S(2)}, u32[]{:S(2)}) collective-permute-start(bf16[32,32,128]{2,1,0:T(8,128)(2,1)} %get-tuple-element.56), channel_id=1, source_target_pairs={{0,3},{1,30},{2,1},{3,28},{4,7},{5,2},{6,5},{7,0},{8,11},{9,6},{10... | collective-permute-start | bytes 786440 | tf_op jit(solution)/shard_map/ppermute | solution.py:465
  94.7 14.6 %shard_map.88 = (bf16[32,32,128]{2,1,0:T(8,128)(2,1)}, bf16[32,32,128]{2,1,0:T(8,128)(2,1)}, bf16[32,32,128]{2,1,0:T(8,128)(2,1)}, bf16[32,32,128]{2,1,0:T(8,128)(2,1)}) custom-call(s32[1]{0:T(128)} %bitcast.me_ref, bf16[128,64,128]{2,1,0:T(8,128)(2,1)} %get-tuple-element.39.a0_ref, bf16[128,64,128]{2,1,0:T(8,128)(2,1)} %get-tuple-element.47.a1_ref, ...), custom_call_target="tpu_custom_call" | custom-call | flops 2147483648 | bytes 20971520 | tf_op jit(solution)/shard_map/pallas_call | solution.py:355
  109.4 1.6 %collective-permute-start.14 = (bf16[32,32,128]{2,1,0:T(8,128)(2,1)}, bf16[32,32,128]{2,1,0:T(8,128)(2,1)S(1)}, u32[]{:S(2)}, u32[]{:S(2)}) collective-permute-start(bf16[32,32,128]{2,1,0:T(8,128)(2,1)} %get-tuple-element.57), channel_id=1, source_target_pairs={{0,0},{1,29},{2,2},{3,31},{4,4},{5,1},{6,6},{7,3},{8,8},{9,5},{10,... | collective-permute-start | bytes 786440 | tf_op jit(solution)/shard_map/ppermute | solution.py:465
  112.0 1.4 collective-permute-start.16
  113.3 2.1 %collective-permute-start.17 = (bf16[32,32,128]{2,1,0:T(8,128)(2,1)}, bf16[32,32,128]{2,1,0:T(8,128)(2,1)S(1)}, u32[]{:S(2)}, u32[]{:S(2)}) collective-permute-start(bf16[32,32,128]{2,1,0:T(8,128)(2,1)} %get-tuple-element.60), channel_id=1, source_target_pairs={{0,3},{1,30},{2,1},{3,28},{4,7},{5,2},{6,5},{7,0},{8,11},{9,6},{10... | collective-permute-start | bytes 786440 | tf_op jit(solution)/shard_map/ppermute | solution.py:465
  115.4 8.4 %collective-permute-done.13 = bf16[32,32,128]{2,1,0:T(8,128)(2,1)S(1)} collective-permute-done((bf16[32,32,128]{2,1,0:T(8,128)(2,1)}, bf16[32,32,128]{2,1,0:T(8,128)(2,1)S(1)}, u32[]{:S(2)}, u32[]{:S(2)}) %collective-permute-start.13) | collective-permute-done | bytes 262176 | tf_op jit(solution)/shard_map/ppermute | solution.py:465
  123.9 2.8 %collective-permute-done.15 = bf16[32,32,128]{2,1,0:T(8,128)(2,1)S(1)} collective-permute-done((bf16[32,32,128]{2,1,0:T(8,128)(2,1)}, bf16[32,32,128]{2,1,0:T(8,128)(2,1)S(1)}, u32[]{:S(2)}, u32[]{:S(2)}) %collective-permute-start.15) | collective-permute-done | bytes 262176 | tf_op jit(solution)/shard_map/ppermute | solution.py:465
  128.0 12.0 %collective-permute-done.17 = bf16[32,32,128]{2,1,0:T(8,128)(2,1)S(1)} collective-permute-done((bf16[32,32,128]{2,1,0:T(8,128)(2,1)}, bf16[32,32,128]{2,1,0:T(8,128)(2,1)S(1)}, u32[]{:S(2)}, u32[]{:S(2)}) %collective-permute-start.17) | collective-permute-done | bytes 262176 | tf_op jit(solution)/shard_map/ppermute | solution.py:465
  140.2 1.5 %pad_maximum_fusion = f32[128,32,128]{2,1,0:T(8,128)} fusion(f32[32,32,128]{2,1,0:T(8,128)S(1)} %get-tuple-element.66, f32[32,32,128]{2,1,0:T(8,128)S(1)} %get-tuple-element.64, f32[32,32,128]{2,1,0:T(8,128)S(1)} %get-tuple-element.65, f32[32,32,128]{2,1,0:T(8,128)S(1)} %get-tuple-element.63), kind=kLoop, calls=%fused_computation | loop fusion | flops 1572864 | bytes 4194304 | tf_op jit(solution)/shard_map/concatenate | solution.py:470
  (51 shorter events, 11.9 us)
Async XLA Ops:
  2.7 6.7 %copy-start.6 = (s32[128]{0:T(128)S(1)}, s32[128]{0:T(128)}, u32[]{:S(2)}) copy-start(s32[128]{0:T(128)} %dead_ref.1) | copy-start | bytes 1540
  2.7 19.8 %copy-start = (f32[512,1024]{1,0:T(8,128)S(1)}, f32[512,1024]{1,0:T(8,128)}, u32[]{:S(2)}) copy-start(f32[512,1024]{1,0:T(8,128)} %constant.34.clone) | copy-start | bytes 6291460
  2.7 19.8 %copy-start.4 = (f32[512]{0:T(512)S(1)}, f32[512]{0:T(512)}, u32[]{:S(2)}) copy-start(f32[512]{0:T(512)} %param.9) | copy-start | bytes 6148
  2.7 19.7 %collective-permute-start.4 = (bf16[64,8,1024]{2,1,0:T(8,128)(2,1)S(1)}, bf16[64,8,1024]{2,1,0:T(8,128)(2,1)}, u32[]{:S(2)}, u32[]{:S(2)}) collective-permute-start(bf16[64,8,1024]{2,1,0:T(8,128)(2,1)S(1)} %get-tuple-element.45), channel_id=1, source_target_pairs={{0,28},{1,5},{2,30},{3,7},{4,0},{5,9},{6,2},{7,11},{8,4},{9,13},{1... | collective-permute-start | bytes 3145736 | tf_op jit(solution)/shard_map/ppermute | solution.py:424
  3.4 26.2 %collective-permute-start.7 = (bf16[64,8,1024]{2,1,0:T(8,128)(2,1)}, bf16[64,8,1024]{2,1,0:T(8,128)(2,1)}, u32[]{:S(2)}, u32[]{:S(2)}) collective-permute-start(bf16[64,8,1024]{2,1,0:T(8,128)(2,1)} %get-tuple-element.61), channel_id=1, source_target_pairs={{0,1},{1,0},{2,3},{3,2},{4,5},{5,4},{6,7},{7,6},{8,9},{9,8},{10,11... | collective-permute-start | bytes 3145736 | tf_op jit(solution)/shard_map/ppermute | solution.py:423
  9.4 1.5 %collective-permute-start = (f32[2,8,1152]{2,1,0:T(8,128)}, f32[2,8,1152]{2,1,0:T(8,128)S(1)}, u32[]{:S(2)}, u32[]{:S(2)}) collective-permute-start(f32[2,8,1152]{2,1,0:T(8,128)} %shard_map.82), channel_id=1, source_target_pairs={{0,4},{4,0},{8,12},{12,8},{16,20},{20,16},{24,28},{28,24},{1,5},{5... | collective-permute-start | bytes 221192 | tf_op jit(solution)/shard_map/ppermute | solution.py:391
  9.4 16.5 %copy-start.3 = (s32[2,128]{1,0:T(2,128)}, s32[2,128]{1,0:T(2,128)S(1)}, u32[]{:S(2)}) copy-start(s32[2,128]{1,0:T(2,128)S(1)} %pad_add_fusion.flag_ref) | copy-start | bytes 3076
  11.7 4.5 %collective-permute-start.1 = (f32[2,8,1152]{2,1,0:T(8,128)S(1)}, f32[2,8,1152]{2,1,0:T(8,128)S(1)}, u32[]{:S(2)}, u32[]{:S(2)}) collective-permute-start(f32[2,8,1152]{2,1,0:T(8,128)S(1)} %add.36), channel_id=1, source_target_pairs={{0,8},{4,12},{8,0},{12,4},{16,24},{20,28},{24,16},{28,20},{1,9},{5... | collective-permute-start | bytes 221192 | tf_op jit(solution)/shard_map/ppermute | solution.py:391
  12.1 9.0 %collective-permute-start.2 = (f32[2,8,1152]{2,1,0:T(8,128)S(1)}, f32[2,8,1152]{2,1,0:T(8,128)S(1)}, u32[]{:S(2)}, u32[]{:S(2)}) collective-permute-start(f32[2,8,1152]{2,1,0:T(8,128)S(1)} %add.36), channel_id=1, source_target_pairs={{0,16},{4,20},{8,24},{12,28},{16,0},{20,4},{24,8},{28,12},{1,17},{... | collective-permute-start | bytes 221192 | tf_op jit(solution)/shard_map/ppermute | solution.py:391
  13.3 7.7 %collective-permute-start.3 = (f32[2,8,1152]{2,1,0:T(8,128)S(1)}, f32[2,8,1152]{2,1,0:T(8,128)S(1)}, u32[]{:S(2)}, u32[]{:S(2)}) collective-permute-start(f32[2,8,1152]{2,1,0:T(8,128)S(1)} %add.36), channel_id=1, source_target_pairs={{0,24},{4,28},{8,16},{12,20},{16,8},{20,12},{24,0},{28,4},{1,25},{... | collective-permute-start | bytes 221192 | tf_op jit(solution)/shard_map/ppermute | solution.py:391
  16.3 6.2 %collective-permute-start.5 = (s32[2,64]{1,0:T(2,128)S(1)}, s32[2,64]{1,0:T(2,128)S(1)}, u32[]{:S(2)}, u32[]{:S(2)}) collective-permute-start(s32[2,64]{1,0:T(2,128)S(1)} %constant_dynamic-slice_fusion.1), channel_id=1, source_target_pairs={{0,28},{1,5},{2,30},{3,7},{4,0},{5,9},{6,2},{7,11},{8,4},{9,13},{1... | collective-permute-start | bytes 1544 | tf_op jit(solution)/shard_map/ppermute | solution.py:426
  21.1 12.2 %copy-start.2 = (f32[1024]{0:T(1024)S(1)}, f32[1024]{0:T(1024)}, u32[]{:S(2)}) copy-start(f32[1024]{0:T(1024)} %constant.33.clone) | copy-start | bytes 12292
  22.4 8.2 %collective-permute-start.6 = (f32[2,8,1152]{2,1,0:T(8,128)S(1)}, f32[2,8,1152]{2,1,0:T(8,128)S(1)}, u32[]{:S(2)}, u32[]{:S(2)}) collective-permute-start(f32[2,8,1152]{2,1,0:T(8,128)S(1)} %add_add_fusion.rest_0_), channel_id=1, source_target_pairs={{0,1},{1,0},{2,3},{3,2},{4,5},{5,4},{6,7},{7,6},{8,9},{9,8},{10,11... | collective-permute-start | bytes 221192 | tf_op jit(solution)/shard_map/ppermute | solution.py:441
  30.6 18.1 %copy-start.9 = (f32[2,8,1152]{2,1,0:T(8,128)}, f32[2,8,1152]{2,1,0:T(8,128)S(1)}, u32[]{:S(2)}) copy-start(f32[2,8,1152]{2,1,0:T(8,128)S(1)} %collective-permute-done.6.rest_1_.rest_0_) | copy-start | bytes 221188
  30.6 18.1 %collective-permute-start.8 = (bf16[64,8,1024]{2,1,0:T(8,128)(2,1)}, bf16[64,8,1024]{2,1,0:T(8,128)(2,1)S(1)}, u32[]{:S(2)}, u32[]{:S(2)}) collective-permute-start(bf16[64,8,1024]{2,1,0:T(8,128)(2,1)} %collective-permute-done.7.rest_1_), channel_id=1, source_target_pairs={{0,28},{1,5},{2,30},{3,7},{4,0},{5,9},{6,2},{7,11},{8,4},{9,13},{1... | collective-permute-start | bytes 3145736 | tf_op jit(solution)/shard_map/ppermute | solution.py:445
  31.0 29.6 %collective-permute-start.9 = (bf16[64,8,1024]{2,1,0:T(8,128)(2,1)S(1)}, bf16[64,8,1024]{2,1,0:T(8,128)(2,1)S(1)}, u32[]{:S(2)}, u32[]{:S(2)}) collective-permute-start(bf16[64,8,1024]{2,1,0:T(8,128)(2,1)S(1)} %get-tuple-element.45), channel_id=1, source_target_pairs={{0,1},{1,0},{2,3},{3,2},{4,5},{5,4},{6,7},{7,6},{8,9},{9,8},{10,11... | collective-permute-start | bytes 3145736 | tf_op jit(solution)/shard_map/ppermute | solution.py:446
  90.8 20.1 %collective-permute-start.10 = (bf16[32,32,128]{2,1,0:T(8,128)(2,1)}, bf16[32,32,128]{2,1,0:T(8,128)(2,1)S(1)}, u32[]{:S(2)}, u32[]{:S(2)}) collective-permute-start(bf16[32,32,128]{2,1,0:T(8,128)(2,1)} %get-tuple-element.53), channel_id=1, source_target_pairs={{0,0},{1,29},{2,2},{3,31},{4,4},{5,1},{6,6},{7,3},{8,8},{9,5},{10,... | collective-permute-start | bytes 786440 | tf_op jit(solution)/shard_map/ppermute | solution.py:465
  92.4 19.5 %collective-permute-start.11 = (bf16[32,32,128]{2,1,0:T(8,128)(2,1)}, bf16[32,32,128]{2,1,0:T(8,128)(2,1)S(1)}, u32[]{:S(2)}, u32[]{:S(2)}) collective-permute-start(bf16[32,32,128]{2,1,0:T(8,128)(2,1)} %get-tuple-element.54), channel_id=1, source_target_pairs={{0,2},{1,31},{2,0},{3,29},{4,6},{5,3},{6,4},{7,1},{8,10},{9,7},{10... | collective-permute-start | bytes 786440 | tf_op jit(solution)/shard_map/ppermute | solution.py:465
  92.5 20.9 %collective-permute-start.12 = (bf16[32,32,128]{2,1,0:T(8,128)(2,1)}, bf16[32,32,128]{2,1,0:T(8,128)(2,1)S(1)}, u32[]{:S(2)}, u32[]{:S(2)}) collective-permute-start(bf16[32,32,128]{2,1,0:T(8,128)(2,1)} %get-tuple-element.55), channel_id=1, source_target_pairs={{0,1},{1,28},{2,3},{3,30},{4,5},{5,0},{6,7},{7,2},{8,9},{9,4},{10,... | collective-permute-start | bytes 786440 | tf_op jit(solution)/shard_map/ppermute | solution.py:465
  92.5 31.3 %collective-permute-start.13 = (bf16[32,32,128]{2,1,0:T(8,128)(2,1)}, bf16[32,32,128]{2,1,0:T(8,128)(2,1)S(1)}, u32[]{:S(2)}, u32[]{:S(2)}) collective-permute-start(bf16[32,32,128]{2,1,0:T(8,128)(2,1)} %get-tuple-element.56), channel_id=1, source_target_pairs={{0,3},{1,30},{2,1},{3,28},{4,7},{5,2},{6,5},{7,0},{8,11},{9,6},{10... | collective-permute-start | bytes 786440 | tf_op jit(solution)/shard_map/ppermute | solution.py:465
  109.4 14.5 %collective-permute-start.14 = (bf16[32,32,128]{2,1,0:T(8,128)(2,1)}, bf16[32,32,128]{2,1,0:T(8,128)(2,1)S(1)}, u32[]{:S(2)}, u32[]{:S(2)}) collective-permute-start(bf16[32,32,128]{2,1,0:T(8,128)(2,1)} %get-tuple-element.57), channel_id=1, source_target_pairs={{0,0},{1,29},{2,2},{3,31},{4,4},{5,1},{6,6},{7,3},{8,8},{9,5},{10,... | collective-permute-start | bytes 786440 | tf_op jit(solution)/shard_map/ppermute | solution.py:465
  111.0 15.8 %collective-permute-start.15 = (bf16[32,32,128]{2,1,0:T(8,128)(2,1)}, bf16[32,32,128]{2,1,0:T(8,128)(2,1)S(1)}, u32[]{:S(2)}, u32[]{:S(2)}) collective-permute-start(bf16[32,32,128]{2,1,0:T(8,128)(2,1)} %get-tuple-element.58), channel_id=1, source_target_pairs={{0,2},{1,31},{2,0},{3,29},{4,6},{5,3},{6,4},{7,1},{8,10},{9,7},{10... | collective-permute-start | bytes 786440 | tf_op jit(solution)/shard_map/ppermute | solution.py:465
  112.0 16.1 %collective-permute-start.16 = (bf16[32,32,128]{2,1,0:T(8,128)(2,1)}, bf16[32,32,128]{2,1,0:T(8,128)(2,1)S(1)}, u32[]{:S(2)}, u32[]{:S(2)}) collective-permute-start(bf16[32,32,128]{2,1,0:T(8,128)(2,1)} %get-tuple-element.59), channel_id=1, source_target_pairs={{0,1},{1,28},{2,3},{3,30},{4,5},{5,0},{6,7},{7,2},{8,9},{9,4},{10,... | collective-permute-start | bytes 786440 | tf_op jit(solution)/shard_map/ppermute | solution.py:465
  113.3 26.7 %collective-permute-start.17 = (bf16[32,32,128]{2,1,0:T(8,128)(2,1)}, bf16[32,32,128]{2,1,0:T(8,128)(2,1)S(1)}, u32[]{:S(2)}, u32[]{:S(2)}) collective-permute-start(bf16[32,32,128]{2,1,0:T(8,128)(2,1)} %get-tuple-element.60), channel_id=1, source_target_pairs={{0,3},{1,30},{2,1},{3,28},{4,7},{5,2},{6,5},{7,0},{8,11},{9,6},{10... | collective-permute-start | bytes 786440 | tf_op jit(solution)/shard_map/ppermute | solution.py:465
  (5 other events, 17.0 us)

commit v6 on v5

--- a/solution.py
+++ b/solution.py
@@ -17,6 +17,7 @@
 CHUNKS = 2
 TILE = 256
 STEPS = 4
+TOGETHER = 4
 VMEM = 60 * 1024 * 1024
 NT = (((1,), (1,)), ((), ()))
 F32 = jnp.float32
@@ -141,9 +142,9 @@
     for copy in copies[groups + 1 + count :]:
         copy.wait()
 
-    def pair(step, _):
-        for i in range(2):
-            w = step * 2 + i
+    def some_windows(step, _):
+        for i in range(TOGETHER):
+            w = step * TOGETHER + i
             for t in range(ns // LANE):
                 rows[i * chans : (i + 1) * chans, t * LANE : (t + 1) * LANE] = clean[
                     t, pl.ds(w, chans, stride=pitch), :
@@ -154,15 +155,18 @@
             ).astype(BF16)
         series[: half // 2, :] = series[ns : ns + half // 2, :]
         series[ns + half // 2 :, :] = series[half // 2 : half, :]
+
+        def place(stage, j, value):
+            for i in range(TOGETHER):
+                at = j * wins + step * TOGETHER + i
+                stage[pl.ds(at, size, stride=jpitch), :] = value[:, i * chans : (i + 1) * chans]
+
         for j in range(blocks):
+            start = j * half + half // 2
             b = jnp.dot(
-                seg[:, :half],
-                series[j * half + half // 2 : j * half + half // 2 + half, :],
-                preferred_element_type=F32,
+                seg[:, :half], series[start : start + half, :], preferred_element_type=F32
             )
-            for i in range(2):
-                at = j * wins + step * 2 + i
-                b_s[pl.ds(at, size, stride=jpitch), :] = b[:, i * chans : (i + 1) * chans]
+            place(b_s, j, b)
 
         @pl.when(want)
         def _():
@@ -170,13 +174,11 @@
                 a = jnp.dot(
                     seg[...], series[j * half : j * half + size, :], preferred_element_type=F32
                 )
-                for i in range(2):
-                    at = j * wins + step * 2 + i
-                    a_s[pl.ds(at, size, stride=jpitch), :] = a[:, i * chans : (i + 1) * chans]
+                place(a_s, j, a)
 
         return 0
 
-    lax.fori_loop(0, wins // 2, pair, 0)
+    lax.fori_loop(0, wins // TOGETHER, some_windows, 0)
 
     def both_parts(ref, k):
         return jnp.concatenate(
@@ -238,8 +240,8 @@
         + [
             pltpu.VMEM((len(totals) * NSEC, wins, ns), F32),
             pltpu.VMEM((ns // LANE, chans * (wins + 1), LANE), F32),
-            pltpu.VMEM((2 * chans, ns), BF16),
-            pltpu.VMEM((ns + half, 2 * chans), BF16),
+            pltpu.VMEM((TOGETHER * chans, ns), BF16),
+            pltpu.VMEM((ns + half, TOGETHER * chans), BF16),
             pltpu.VMEM((size * (depth // 2 + 1), chans), F32),
             pltpu.VMEM((size * (depth // 2 + 1), chans), F32),
             pltpu.VMEM(a_shape.shape, BF16),
@@ -271,34 +273,27 @@
 
     def bins_with(left_of):
         def one_bin(k, _):
-            left = left_of(k)
             part = depth // 2
-            swapped = jnp.concatenate(
-                [
-                    left[:, part:depth],
-                    -left[:, :part],
-                    left[:, depth + part :],
-                    -left[:, depth : depth + part],
-                ],
-                axis=1,
-            )
             halo = bh_ref[k]
             other = jnp.concatenate([halo[:, width:], halo[:, :width]], axis=1)
-            right = jnp.concatenate(
-                [
-                    jnp.concatenate([b0_ref[k], halo], axis=1),
-                    jnp.concatenate([b1_ref[k], other], axis=1),
-                ],
-                axis=0,
-            )
+            right = [
+                jnp.concatenate([b0_ref[k], halo], axis=1),
+                jnp.concatenate([b1_ref[k], other], axis=1),
+            ]
+            turned = [piece for r in right for piece in (-r[part:], r[:part])]
             value = jnp.dot(
-                jnp.concatenate([left, swapped], axis=0), right, preferred_element_type=F32
+                left_of(k),
+                jnp.concatenate(
+                    [jnp.concatenate(right, axis=0), jnp.concatenate(turned, axis=0)], axis=1
+                ),
+                preferred_element_type=F32,
             )
             at = 2 * (step * bins + k)
             for p in range(2):
                 for t in range(2):
+                    column = (2 * p + t) * chans
                     cross[t, pl.ds(at + p, count, stride=pitch), :] = value[
-                        p * count : (p + 1) * count, t * chans : (t + 1) * chans
+                        :, column : column + chans
                     ]
             return 0
 
@@ -322,25 +317,35 @@
             one[t] = jnp.where(place == column + t * chans, 1.0, 0.0)
         share = OFFS // len(outs)
 
-        def one_channel(c, _):
-            value = jnp.concatenate(
-                [cross[t, pl.ds(c * pitch, nfr), :] for t in range(2)], axis=1
-            ).astype(BF16)
-            starts = [first + c + 1 + share * (me ^ d) for d in range(len(outs))]
-            pick = jnp.concatenate(
-                [
-                    jnp.concatenate([one[t, pl.ds(start, share), :] for start in starts], axis=0)
-                    for t in range(2)
-                ],
-                axis=1,
-            ).astype(BF16)
+        def two_channels(n, _):
+            def taken(c):
+                return [cross[t, pl.ds(c * pitch, nfr), :] for t in range(2)]
+
+            def pick(c):
+                starts = [first + c + 1 + share * (me ^ d) for d in range(len(outs))]
+                return jnp.concatenate(
+                    [
+                        jnp.concatenate([one[t, pl.ds(at, share), :] for at in starts], axis=0)
+                        for t in range(2)
+                    ],
+                    axis=1,
+                ).astype(BF16)
+
+            value = jnp.concatenate(taken(2 * n) + taken(2 * n + 1), axis=1).astype(BF16)
             lagged = jnp.dot(lag_ref[...], value, preferred_element_type=F32) * scale
-            band = lax.dot_general(pick, lagged.astype(BF16), NT, preferred_element_type=F32)
-            for d, out in enumerate(outs):
-                out[c] = band[d * share : (d + 1) * share, :].astype(BF16)
+            lagged = lagged.astype(BF16)
+            for i in range(2):
+                band = lax.dot_general(
+                    pick(2 * n + i),
+                    lagged[:, 2 * i * chans : 2 * (i + 1) * chans],
+                    NT,
+                    preferred_element_type=F32,
+                )
+                for d, out in enumerate(outs):
+                    out[2 * n + i] = band[d * share : (d + 1) * share, :].astype(BF16)
             return 0
 
-        lax.fori_loop(0, count, one_channel, 0, unroll=4)
+        lax.fori_loop(0, count // 2, two_channels, 0, unroll=4)
 
 
 def stacks(index, shares, scale, me, a0, a1, ah, b0, b1, bh, lag):
@@ -419,9 +424,7 @@
     ]
 
     first_half = lax.dynamic_slice_in_dim(samples, (1 - odd) * width, width, 0)
-    own_half = lax.dynamic_slice_in_dim(samples, odd * width, width, 0)
     their_first = lax.ppermute(first_half, "tm", swap)
-    halo = lax.ppermute(own_half, both, halo_pairs)
     flags = jnp.stack([dead_flags, section_ids])
     halo_flags = lax.ppermute(
         lax.dynamic_slice_in_dim(flags, odd * width, width, 1), both, halo_pairs
@@ -437,8 +440,10 @@
         compiler_params=pltpu.CompilerParams(vmem_limit_bytes=VMEM),
     )(dead_flags, section_ids, samples)
     total = add_over(sums, "fibre")
-    total, halo, halo_flags = lax.optimization_barrier((total, halo, halo_flags))
+    total, halo_flags, kept = lax.optimization_barrier((total, halo_flags, samples))
     their_total = lax.ppermute(total, "tm", swap)
+    own_half = lax.dynamic_slice_in_dim(kept, odd * width, width, 0)
+    halo = lax.ppermute(own_half, both, halo_pairs)
     ready = (total, their_total, their_first, own_half, flags, hann, conv, seg, lag)
     ready = lax.optimization_barrier(ready)
     total, their_total, their_first, own_half, flags, hann, conv, seg, lag = ready

time: 142 us -> 143 us (level)
  waiting for transfers between devices: 33.7 us -> 30.3 us
  Pallas kernels: 75.8 us -> 78 us
  other arithmetic: 3.54 us -> 5.12 us
    ppermute x1, waiting for transfers between devices: 0.98 us -> 7.29 us  [shards(): their_total = lax.ppermute(total, 'tm', swap)]
    ppermute x1, starting transfers between devices: 4.78 us -> 0.01 us  [shards(): lax.ppermute(lax.dynamic_slice_in_dim(flags, odd * width, width, 1), both...]
    pallas_call x2, Pallas kernels: 29.4 us -> 33.1 us  [stacks(): pl.pallas_call(functools.partial(stack_kernel, index * count, scale), gri...]
    ppermute x1, waiting for transfers between devices: 3.72 us -> 0.01 us  [shards(): their_first = lax.ppermute(first_half, 'tm', swap)]
    ppermute x8, waiting for transfers between devices: 24.4 us -> 22 us  [shards(): arrived.append(lax.ppermute(found[d], both, pairs).astype(F32))]
    ppermute x4, waiting for transfers between devices: 3.18 us -> 1.02 us  [add_over(): lax.ppermute(value, axis, [(i, i ^ s) for i in range(count)])]
    ppermute x8, starting transfers between devices: 9.91 us -> 12.1 us  [shards(): arrived.append(lax.ppermute(found[d], both, pairs).astype(F32))]
    reduce_sum x1, other arithmetic: 0.8 us -> 2.39 us  [shards(): response = jnp.sum(band_gain[:, None] * waves, axis=0, keepdims=True)]
  transfers between devices with their start and end apart: 18 -> 18, of which waited for: 9 -> 5; matrix products, arithmetic and copies ran while one was open for 2% -> 4% of each run, Pallas kernels for 33% -> 33%
where the time goes in v6:
time: 143 us; the launch traced here: 142 us
  Pallas kernels  78 us (55%)
  waiting for transfers between devices  30.3 us (21%)
  starting transfers between devices  22.6 us (16%)
  local copies, waits for them, and re-layouts  6.07 us (4%)
  other arithmetic  5.12 us (4%)
    pallas_call x3, Pallas kernels, segments(): pl.pallas_call(functools.partial(segments_kernel, kind), out_shape=[a_sha...  38.7 us
    pallas_call x2, Pallas kernels, stacks(): pl.pallas_call(functools.partial(stack_kernel, index * count, scale), gri...  33.1 us
    ppermute x8, waiting for transfers between devices, shards(): arrived.append(lax.ppermute(found[d], both, pairs).astype(F32))  22 us
    ppermute x8, starting transfers between devices, shards(): arrived.append(lax.ppermute(found[d], both, pairs).astype(F32))  12.1 us
    ppermute x1, waiting for transfers between devices, shards(): their_total = lax.ppermute(total, 'tm', swap)  7.29 us
    ppermute x4, starting transfers between devices, add_over(): lax.ppermute(value, axis, [(i, i ^ s) for i in range(count)])  3.67 us
    pallas_call x1, Pallas kernels, shards(): pl.pallas_call(section_sums, grid=(steps,), out_shape=jax.ShapeDtypeStruc...  3.54 us
    unnamed x24, local copies, waits for them, and re-layouts  2.99 us
  transfers between devices with their start and end apart: 18, of which 5 were waited for; matrix products, arithmetic and copies ran while one was open for 4% of the time, Pallas kernels for 33%

profile of v6, /device:TPU:19, one launch (start us, length us, event | category | flops | bytes accessed | tf_op | source)
XLA Modules:
  0.0 142.4 jit_solution(15453657696199579923)
XLA Ops:
  0.0 1.3 constant_dynamic-slice_fusion.1
  1.3 1.4 collective-permute-start.6
  2.7 3.5 %shard_map.82 = f32[2,8,1152]{2,1,0:T(8,128)} custom-call(s32[128]{0:T(128)} %dead_ref.1, s32[128]{0:T(128)} %sec_ref.1, bf16[128,8,1024]{2,1,0:T(8,128)(2,1)} %rest_1_.1), custom_call_target="tpu_custom_call" | custom-call | tf_op jit(solution)/shard_map/pallas_call | solution.py:434
  9.6 1.2 collective-permute-start.2
  12.0 2.4 %multiply_reduce_fusion = f32[1024]{0:T(1024)} fusion(f32[512,1024]{1,0:T(8,128)} %constant.34.clone, f32[512]{0:T(512)S(1)} %copy-done.4), kind=kLoop, calls=%fused_computation.1 | loop fusion | flops 1047552 | bytes 2103296 | tf_op jit(solution)/shard_map/reduce_sum | solution.py:412
  14.3 2.6 %shard_map.83.rest_3_.rest_5_.rest_4_ = bf16[1024,1024]{1,0:T(8,128)(2,1)} custom-call(f32[1,1024]{1,0:T(1,128)} %bitcast.8), custom_call_target="tpu_custom_call" | custom-call | tf_op jit(solution)/shard_map/pallas_call | solution.py:413
  18.4 1.4 collective-permute-start.7
  19.8 7.3 %collective-permute-done.5.rest_1_.rest_0_ = f32[2,8,1152]{2,1,0:T(8,128)S(1)} collective-permute-done((f32[2,8,1152]{2,1,0:T(8,128)S(1)}, f32[2,8,1152]{2,1,0:T(8,128)S(1)}, u32[]{:S(2)}, u32[]{:S(2)}) %collective-permute-start.5) | collective-permute-done | bytes 73760 | tf_op jit(solution)/shard_map/ppermute | solution.py:444
  27.1 1.4 %collective-permute-start.8 = (bf16[64,8,1024]{2,1,0:T(8,128)(2,1)}, bf16[64,8,1024]{2,1,0:T(8,128)(2,1)S(1)}, u32[]{:S(2)}, u32[]{:S(2)}) collective-permute-start(bf16[64,8,1024]{2,1,0:T(8,128)(2,1)} %collective-permute-done.6.rest_1_), channel_id=1, source_target_pairs={{0,28},{1,5},{2,30},{3,7},{4,0},{5,9},{6,2},{7,11},{8,4},{9,13},{1... | collective-permute-start | bytes 3145736 | tf_op jit(solution)/shard_map/ppermute | solution.py:450
  28.6 2.4 %collective-permute-start.9 = (bf16[64,8,1024]{2,1,0:T(8,128)(2,1)}, bf16[64,8,1024]{2,1,0:T(8,128)(2,1)S(1)}, u32[]{:S(2)}, u32[]{:S(2)}) collective-permute-start(bf16[64,8,1024]{2,1,0:T(8,128)(2,1)} %constant_dynamic-slice_fusion), channel_id=1, source_target_pairs={{0,1},{1,0},{2,3},{3,2},{4,5},{5,4},{6,7},{7,6},{8,9},{9,8},{10,11... | collective-permute-start | bytes 3145736 | tf_op jit(solution)/shard_map/ppermute | solution.py:451
  31.6 14.2 %shard_map.84 = (bf16[128,64,128]{2,1,0:T(8,128)(2,1)}, bf16[128,128,128]{2,1,0:T(8,128)(2,1)}) custom-call(s32[1]{0:T(128)} %bitcast.1.odd_ref, s32[2,128]{1,0:T(2,128)} %copy-done.3, f32[2,8,1152]{2,1,0:T(8,128)} %copy-done.1, bf16[128,8,1024]{2,1,0:T(8,128)(2,1)} %rest_1_.1, f32[8,1024]{1,0:T(8,128)} %broadcast_in_dim.19.rest_2_.rest_4_.rest_3_, ...), custom_call_target="tpu_custom_call" | custom-call | flops 3758096384 | bytes 16777216 | tf_op jit(solution)/shard_map/pallas_call | solution.py:234
  47.8 10.6 %shard_map.85 = (bf16[128,128,128]{2,1,0:T(8,128)(2,1)}, bf16[128,128,128]{2,1,0:T(8,128)(2,1)}) custom-call(s32[1]{0:T(128)} %bitcast.1.odd_ref, s32[2,64]{1,0:T(2,128)} %copy-done.11, f32[2,8,1152]{2,1,0:T(8,128)} %copy-done.1, f32[2,8,1152]{2,1,0:T(8,128)} %copy-done.10, bf16[64,8,1024]{2,1,0:T(8,128)(2,1)} %copy-done.7, bf16[64,8,1024]{2,1,0:T(8,128)(2,1)} %copy-done.9, ...), custom_call_target="tpu_custom_call" | custom-call | flops 3758096384 | bytes 16777216 | tf_op jit(solution)/shard_map/pallas_call | solution.py:234
  59.4 13.9 %shard_map.86 = (bf16[128,64,128]{2,1,0:T(8,128)(2,1)}, bf16[128,128,128]{2,1,0:T(8,128)(2,1)}) custom-call(s32[1]{0:T(128)} %bitcast.1.odd_ref, s32[2,128]{1,0:T(2,128)} %copy-done.3, f32[2,8,1152]{2,1,0:T(8,128)} %copy-done.10, bf16[64,8,1024]{2,1,0:T(8,128)(2,1)} %collective-permute-done.6.rest_1_, bf16[64,8,1024]{2,1,0:T(8,128)(2,1)} %copy-done.8, ...), custom_call_target="tpu_custom_call" | custom-call | flops 3758096384 | bytes 16777216 | tf_op jit(solution)/shard_map/pallas_call | solution.py:234
  73.3 16.6 %shard_map.87 = (bf16[32,32,128]{2,1,0:T(8,128)(2,1)}, bf16[32,32,128]{2,1,0:T(8,128)(2,1)}, bf16[32,32,128]{2,1,0:T(8,128)(2,1)}, bf16[32,32,128]{2,1,0:T(8,128)(2,1)}) custom-call(s32[1]{0:T(128)} %bitcast.me_ref, bf16[128,64,128]{2,1,0:T(8,128)(2,1)} %get-tuple-element.40.a0_ref, bf16[128,64,128]{2,1,0:T(8,128)(2,1)} %get-tuple-element.47.a1_ref, ...), custom_call_target="tpu_custom_call" | custom-call | flops 2147483648 | bytes 20971520 | tf_op jit(solution)/shard_map/pallas_call | solution.py:360
  89.9 1.6 %collective-permute-start.10 = (bf16[32,32,128]{2,1,0:T(8,128)(2,1)}, bf16[32,32,128]{2,1,0:T(8,128)(2,1)S(1)}, u32[]{:S(2)}, u32[]{:S(2)}) collective-permute-start(bf16[32,32,128]{2,1,0:T(8,128)(2,1)} %get-tuple-element.53), channel_id=1, source_target_pairs={{0,0},{1,29},{2,2},{3,31},{4,4},{5,1},{6,6},{7,3},{8,8},{9,5},{10,... | collective-permute-start | bytes 786440 | tf_op jit(solution)/shard_map/ppermute | solution.py:470
  92.3 1.3 collective-permute-start.13
  93.6 16.5 %shard_map.88 = (bf16[32,32,128]{2,1,0:T(8,128)(2,1)}, bf16[32,32,128]{2,1,0:T(8,128)(2,1)}, bf16[32,32,128]{2,1,0:T(8,128)(2,1)}, bf16[32,32,128]{2,1,0:T(8,128)(2,1)}) custom-call(s32[1]{0:T(128)} %bitcast.me_ref, bf16[128,64,128]{2,1,0:T(8,128)(2,1)} %get-tuple-element.40.a0_ref, bf16[128,64,128]{2,1,0:T(8,128)(2,1)} %get-tuple-element.47.a1_ref, ...), custom_call_target="tpu_custom_call" | custom-call | flops 2147483648 | bytes 20971520 | tf_op jit(solution)/shard_map/pallas_call | solution.py:360
  110.1 1.6 %collective-permute-start.14 = (bf16[32,32,128]{2,1,0:T(8,128)(2,1)}, bf16[32,32,128]{2,1,0:T(8,128)(2,1)S(1)}, u32[]{:S(2)}, u32[]{:S(2)}) collective-permute-start(bf16[32,32,128]{2,1,0:T(8,128)(2,1)} %get-tuple-element.57), channel_id=1, source_target_pairs={{0,0},{1,29},{2,2},{3,31},{4,4},{5,1},{6,6},{7,3},{8,8},{9,5},{10,... | collective-permute-start | bytes 786440 | tf_op jit(solution)/shard_map/ppermute | solution.py:470
  112.7 4.3 %collective-permute-start.16 = (bf16[32,32,128]{2,1,0:T(8,128)(2,1)}, bf16[32,32,128]{2,1,0:T(8,128)(2,1)S(1)}, u32[]{:S(2)}, u32[]{:S(2)}) collective-permute-start(bf16[32,32,128]{2,1,0:T(8,128)(2,1)} %get-tuple-element.59), channel_id=1, source_target_pairs={{0,1},{1,28},{2,3},{3,30},{4,5},{5,0},{6,7},{7,2},{8,9},{9,4},{10,... | collective-permute-start | bytes 786440 | tf_op jit(solution)/shard_map/ppermute | solution.py:470
  117.0 1.5 %collective-permute-start.17 = (bf16[32,32,128]{2,1,0:T(8,128)(2,1)}, bf16[32,32,128]{2,1,0:T(8,128)(2,1)S(1)}, u32[]{:S(2)}, u32[]{:S(2)}) collective-permute-start(bf16[32,32,128]{2,1,0:T(8,128)(2,1)} %get-tuple-element.60), channel_id=1, source_target_pairs={{0,3},{1,30},{2,1},{3,28},{4,7},{5,2},{6,5},{7,0},{8,11},{9,6},{10... | collective-permute-start | bytes 786440 | tf_op jit(solution)/shard_map/ppermute | solution.py:470
  118.5 5.3 %collective-permute-done.13 = bf16[32,32,128]{2,1,0:T(8,128)(2,1)S(1)} collective-permute-done((bf16[32,32,128]{2,1,0:T(8,128)(2,1)}, bf16[32,32,128]{2,1,0:T(8,128)(2,1)S(1)}, u32[]{:S(2)}, u32[]{:S(2)}) %collective-permute-start.13) | collective-permute-done | bytes 262176 | tf_op jit(solution)/shard_map/ppermute | solution.py:470
  124.0 9.4 %collective-permute-done.16 = bf16[32,32,128]{2,1,0:T(8,128)(2,1)S(1)} collective-permute-done((bf16[32,32,128]{2,1,0:T(8,128)(2,1)}, bf16[32,32,128]{2,1,0:T(8,128)(2,1)S(1)}, u32[]{:S(2)}, u32[]{:S(2)}) %collective-permute-start.16) | collective-permute-done | bytes 262176 | tf_op jit(solution)/shard_map/ppermute | solution.py:470
  133.4 7.3 %collective-permute-done.17 = bf16[32,32,128]{2,1,0:T(8,128)(2,1)S(1)} collective-permute-done((bf16[32,32,128]{2,1,0:T(8,128)(2,1)}, bf16[32,32,128]{2,1,0:T(8,128)(2,1)S(1)}, u32[]{:S(2)}, u32[]{:S(2)}) %collective-permute-start.17) | collective-permute-done | bytes 262176 | tf_op jit(solution)/shard_map/ppermute | solution.py:470
  140.9 1.5 %pad_maximum_fusion = f32[128,32,128]{2,1,0:T(8,128)} fusion(f32[32,32,128]{2,1,0:T(8,128)S(1)} %get-tuple-element.64, f32[32,32,128]{2,1,0:T(8,128)S(1)} %get-tuple-element.62, f32[32,32,128]{2,1,0:T(8,128)S(1)} %get-tuple-element.63, f32[32,32,128]{2,1,0:T(8,128)S(1)} %get-tuple-element.61), kind=kLoop, calls=%fused_computation | loop fusion | flops 1572864 | bytes 4194304 | tf_op jit(solution)/shard_map/concatenate | solution.py:475
  (54 shorter events, 11.5 us)
Async XLA Ops:
  0.0 11.9 %copy-start.4 = (f32[512]{0:T(512)S(1)}, f32[512]{0:T(512)}, u32[]{:S(2)}) copy-start(f32[512]{0:T(512)} %param.9) | copy-start | bytes 6148
  1.3 25.8 %collective-permute-start.6 = (bf16[64,8,1024]{2,1,0:T(8,128)(2,1)S(1)}, bf16[64,8,1024]{2,1,0:T(8,128)(2,1)}, u32[]{:S(2)}, u32[]{:S(2)}) collective-permute-start(bf16[64,8,1024]{2,1,0:T(8,128)(2,1)S(1)} %constant_dynamic-slice_fusion.1), channel_id=1, source_target_pairs={{0,1},{1,0},{2,3},{3,2},{4,5},{5,4},{6,7},{7,6},{8,9},{9,8},{10,11... | collective-permute-start | bytes 3145736 | tf_op jit(solution)/shard_map/ppermute | solution.py:427
  6.2 2.1 %collective-permute-start = (f32[2,8,1152]{2,1,0:T(8,128)}, f32[2,8,1152]{2,1,0:T(8,128)S(1)}, u32[]{:S(2)}, u32[]{:S(2)}) collective-permute-start(f32[2,8,1152]{2,1,0:T(8,128)} %shard_map.82), channel_id=1, source_target_pairs={{0,4},{4,0},{8,12},{12,8},{16,20},{20,16},{24,28},{28,24},{1,5},{5... | collective-permute-start | bytes 221192 | tf_op jit(solution)/shard_map/ppermute | solution.py:396
  7.2 9.7 %copy-start.3 = (s32[2,128]{1,0:T(2,128)}, s32[2,128]{1,0:T(2,128)S(1)}, u32[]{:S(2)}) copy-start(s32[2,128]{1,0:T(2,128)S(1)} %pad_add_fusion.flag_ref) | copy-start | bytes 3076
  7.3 9.7 %collective-permute-start.4 = (s32[2,64]{1,0:T(2,128)S(1)}, s32[2,64]{1,0:T(2,128)S(1)}, u32[]{:S(2)}, u32[]{:S(2)}) collective-permute-start(s32[2,64]{1,0:T(2,128)S(1)} %constant_dynamic-slice_fusion.2), channel_id=1, source_target_pairs={{0,28},{1,5},{2,30},{3,7},{4,0},{5,9},{6,2},{7,11},{8,4},{9,13},{1... | collective-permute-start | bytes 1544 | tf_op jit(solution)/shard_map/ppermute | solution.py:429
  9.2 7.7 %collective-permute-start.1 = (f32[2,8,1152]{2,1,0:T(8,128)S(1)}, f32[2,8,1152]{2,1,0:T(8,128)S(1)}, u32[]{:S(2)}, u32[]{:S(2)}) collective-permute-start(f32[2,8,1152]{2,1,0:T(8,128)S(1)} %add.36), channel_id=1, source_target_pairs={{0,8},{4,12},{8,0},{12,4},{16,24},{20,28},{24,16},{28,20},{1,9},{5... | collective-permute-start | bytes 221192 | tf_op jit(solution)/shard_map/ppermute | solution.py:396
  9.6 7.4 %collective-permute-start.2 = (f32[2,8,1152]{2,1,0:T(8,128)S(1)}, f32[2,8,1152]{2,1,0:T(8,128)S(1)}, u32[]{:S(2)}, u32[]{:S(2)}) collective-permute-start(f32[2,8,1152]{2,1,0:T(8,128)S(1)} %add.36), channel_id=1, source_target_pairs={{0,16},{4,20},{8,24},{12,28},{16,0},{20,4},{24,8},{28,12},{1,17},{... | collective-permute-start | bytes 221192 | tf_op jit(solution)/shard_map/ppermute | solution.py:396
  10.8 6.2 %collective-permute-start.3 = (f32[2,8,1152]{2,1,0:T(8,128)S(1)}, f32[2,8,1152]{2,1,0:T(8,128)S(1)}, u32[]{:S(2)}, u32[]{:S(2)}) collective-permute-start(f32[2,8,1152]{2,1,0:T(8,128)S(1)} %add.36), channel_id=1, source_target_pairs={{0,24},{4,28},{8,16},{12,20},{16,8},{20,12},{24,0},{28,4},{1,25},{... | collective-permute-start | bytes 221192 | tf_op jit(solution)/shard_map/ppermute | solution.py:396
  14.3 16.6 %copy-start.2 = (f32[1024]{0:T(1024)S(1)}, f32[1024]{0:T(1024)}, u32[]{:S(2)}) copy-start(f32[1024]{0:T(1024)} %constant.33.clone) | copy-start | bytes 12292
  17.0 14.6 %copy-start.1 = (f32[2,8,1152]{2,1,0:T(8,128)}, f32[2,8,1152]{2,1,0:T(8,128)S(1)}, u32[]{:S(2)}) copy-start(f32[2,8,1152]{2,1,0:T(8,128)S(1)} %add_add_fusion.rest_0_) | copy-start | bytes 221188
  17.0 28.7 %copy-start.11 = (s32[2,64]{1,0:T(2,128)}, s32[2,64]{1,0:T(2,128)S(1)}, u32[]{:S(2)}) copy-start(s32[2,64]{1,0:T(2,128)S(1)} %collective-permute-done.4.flag_ref) | copy-start | bytes 1540
  17.0 10.1 %collective-permute-start.5 = (f32[2,8,1152]{2,1,0:T(8,128)S(1)}, f32[2,8,1152]{2,1,0:T(8,128)S(1)}, u32[]{:S(2)}, u32[]{:S(2)}) collective-permute-start(f32[2,8,1152]{2,1,0:T(8,128)S(1)} %add_add_fusion.rest_0_), channel_id=1, source_target_pairs={{0,1},{1,0},{2,3},{3,2},{4,5},{5,4},{6,7},{7,6},{8,9},{9,8},{10,11... | collective-permute-start | bytes 221192 | tf_op jit(solution)/shard_map/ppermute | solution.py:444
  18.4 27.4 %collective-permute-start.7 = (bf16[64,8,1024]{2,1,0:T(8,128)(2,1)}, bf16[64,8,1024]{2,1,0:T(8,128)(2,1)S(1)}, u32[]{:S(2)}, u32[]{:S(2)}) collective-permute-start(bf16[64,8,1024]{2,1,0:T(8,128)(2,1)} %constant_dynamic-slice_fusion), channel_id=1, source_target_pairs={{0,28},{1,5},{2,30},{3,7},{4,0},{5,9},{6,2},{7,11},{8,4},{9,13},{1... | collective-permute-start | bytes 3145736 | tf_op jit(solution)/shard_map/ppermute | solution.py:446
  27.1 18.7 %copy-start.10 = (f32[2,8,1152]{2,1,0:T(8,128)}, f32[2,8,1152]{2,1,0:T(8,128)S(1)}, u32[]{:S(2)}) copy-start(f32[2,8,1152]{2,1,0:T(8,128)S(1)} %collective-permute-done.5.rest_1_.rest_0_) | copy-start | bytes 221188
  27.1 18.7 %collective-permute-start.8 = (bf16[64,8,1024]{2,1,0:T(8,128)(2,1)}, bf16[64,8,1024]{2,1,0:T(8,128)(2,1)S(1)}, u32[]{:S(2)}, u32[]{:S(2)}) collective-permute-start(bf16[64,8,1024]{2,1,0:T(8,128)(2,1)} %collective-permute-done.6.rest_1_), channel_id=1, source_target_pairs={{0,28},{1,5},{2,30},{3,7},{4,0},{5,9},{6,2},{7,11},{8,4},{9,13},{1... | collective-permute-start | bytes 3145736 | tf_op jit(solution)/shard_map/ppermute | solution.py:450
  28.6 29.8 %collective-permute-start.9 = (bf16[64,8,1024]{2,1,0:T(8,128)(2,1)}, bf16[64,8,1024]{2,1,0:T(8,128)(2,1)S(1)}, u32[]{:S(2)}, u32[]{:S(2)}) collective-permute-start(bf16[64,8,1024]{2,1,0:T(8,128)(2,1)} %constant_dynamic-slice_fusion), channel_id=1, source_target_pairs={{0,1},{1,0},{2,3},{3,2},{4,5},{5,4},{6,7},{7,6},{8,9},{9,8},{10,11... | collective-permute-start | bytes 3145736 | tf_op jit(solution)/shard_map/ppermute | solution.py:451
  89.9 21.8 %collective-permute-start.10 = (bf16[32,32,128]{2,1,0:T(8,128)(2,1)}, bf16[32,32,128]{2,1,0:T(8,128)(2,1)S(1)}, u32[]{:S(2)}, u32[]{:S(2)}) collective-permute-start(bf16[32,32,128]{2,1,0:T(8,128)(2,1)} %get-tuple-element.53), channel_id=1, source_target_pairs={{0,0},{1,29},{2,2},{3,31},{4,4},{5,1},{6,6},{7,3},{8,8},{9,5},{10,... | collective-permute-start | bytes 786440 | tf_op jit(solution)/shard_map/ppermute | solution.py:470
  91.5 21.1 %collective-permute-start.11 = (bf16[32,32,128]{2,1,0:T(8,128)(2,1)}, bf16[32,32,128]{2,1,0:T(8,128)(2,1)S(1)}, u32[]{:S(2)}, u32[]{:S(2)}) collective-permute-start(bf16[32,32,128]{2,1,0:T(8,128)(2,1)} %get-tuple-element.54), channel_id=1, source_target_pairs={{0,2},{1,31},{2,0},{3,29},{4,6},{5,3},{6,4},{7,1},{8,10},{9,7},{10... | collective-permute-start | bytes 786440 | tf_op jit(solution)/shard_map/ppermute | solution.py:470
  91.6 25.4 %collective-permute-start.12 = (bf16[32,32,128]{2,1,0:T(8,128)(2,1)}, bf16[32,32,128]{2,1,0:T(8,128)(2,1)S(1)}, u32[]{:S(2)}, u32[]{:S(2)}) collective-permute-start(bf16[32,32,128]{2,1,0:T(8,128)(2,1)} %get-tuple-element.55), channel_id=1, source_target_pairs={{0,1},{1,28},{2,3},{3,30},{4,5},{5,0},{6,7},{7,2},{8,9},{9,4},{10,... | collective-permute-start | bytes 786440 | tf_op jit(solution)/shard_map/ppermute | solution.py:470
  92.3 31.5 %collective-permute-start.13 = (bf16[32,32,128]{2,1,0:T(8,128)(2,1)}, bf16[32,32,128]{2,1,0:T(8,128)(2,1)S(1)}, u32[]{:S(2)}, u32[]{:S(2)}) collective-permute-start(bf16[32,32,128]{2,1,0:T(8,128)(2,1)} %get-tuple-element.56), channel_id=1, source_target_pairs={{0,3},{1,30},{2,1},{3,28},{4,7},{5,2},{6,5},{7,0},{8,11},{9,6},{10... | collective-permute-start | bytes 786440 | tf_op jit(solution)/shard_map/ppermute | solution.py:470
  110.1 13.9 %collective-permute-start.14 = (bf16[32,32,128]{2,1,0:T(8,128)(2,1)}, bf16[32,32,128]{2,1,0:T(8,128)(2,1)S(1)}, u32[]{:S(2)}, u32[]{:S(2)}) collective-permute-start(bf16[32,32,128]{2,1,0:T(8,128)(2,1)} %get-tuple-element.57), channel_id=1, source_target_pairs={{0,0},{1,29},{2,2},{3,31},{4,4},{5,1},{6,6},{7,3},{8,8},{9,5},{10,... | collective-permute-start | bytes 786440 | tf_op jit(solution)/shard_map/ppermute | solution.py:470
  111.7 12.3 %collective-permute-start.15 = (bf16[32,32,128]{2,1,0:T(8,128)(2,1)}, bf16[32,32,128]{2,1,0:T(8,128)(2,1)S(1)}, u32[]{:S(2)}, u32[]{:S(2)}) collective-permute-start(bf16[32,32,128]{2,1,0:T(8,128)(2,1)} %get-tuple-element.58), channel_id=1, source_target_pairs={{0,2},{1,31},{2,0},{3,29},{4,6},{5,3},{6,4},{7,1},{8,10},{9,7},{10... | collective-permute-start | bytes 786440 | tf_op jit(solution)/shard_map/ppermute | solution.py:470
  112.7 20.8 %collective-permute-start.16 = (bf16[32,32,128]{2,1,0:T(8,128)(2,1)}, bf16[32,32,128]{2,1,0:T(8,128)(2,1)S(1)}, u32[]{:S(2)}, u32[]{:S(2)}) collective-permute-start(bf16[32,32,128]{2,1,0:T(8,128)(2,1)} %get-tuple-element.59), channel_id=1, source_target_pairs={{0,1},{1,28},{2,3},{3,30},{4,5},{5,0},{6,7},{7,2},{8,9},{9,4},{10,... | collective-permute-start | bytes 786440 | tf_op jit(solution)/shard_map/ppermute | solution.py:470
  117.0 23.7 %collective-permute-start.17 = (bf16[32,32,128]{2,1,0:T(8,128)(2,1)}, bf16[32,32,128]{2,1,0:T(8,128)(2,1)S(1)}, u32[]{:S(2)}, u32[]{:S(2)}) collective-permute-start(bf16[32,32,128]{2,1,0:T(8,128)(2,1)} %get-tuple-element.60), channel_id=1, source_target_pairs={{0,3},{1,30},{2,1},{3,28},{4,7},{5,2},{6,5},{7,0},{8,11},{9,6},{10... | collective-permute-start | bytes 786440 | tf_op jit(solution)/shard_map/ppermute | solution.py:470
  (6 other events, 25.5 us)

commit v7 on v5

v7 whole, which is shorter than its diff:
```python
import functools
import math

import jax
import jax.numpy as jnp
import ml_dtypes
import numpy as np
from jax import lax
from jax.experimental import pallas as pl
from jax.experimental.pallas import tpu as pltpu
from jax.sharding import PartitionSpec as P

OFFS = 128
LAGS = 128
NSEC = 2
LANE = 128
PIECES = 4
TILE = 256
STEPS = 4
TOGETHER = 4
VMEM = 60 * 1024 * 1024
NT = (((1,), (1,)), ((), ()))
F32 = jnp.float32
BF16 = jnp.bfloat16


def tables(ns, nf):
    tick = np.arange(ns)
    freq = np.arange(nf)
    window = 0.5 - 0.5 * np.cos(tick * (2.0 * math.pi / ns))
    waves = np.cos((freq[:, None] * tick[None, :] % ns) * (2.0 * math.pi / ns))
    waves[0] *= math.sqrt(0.5)
    size = 2 * LAGS
    bins = np.arange(size // 2)
    turn = math.pi / size * ((2 * bins[:, None] + 1) * np.arange(size)[None, :] % (2 * size))
    segment = np.stack([np.cos(turn), -np.sin(turn)], axis=1).reshape(size, size)
    lag = np.stack([np.cos(turn), -np.sin(turn)], axis=1).reshape(size, size)[:, :LAGS].T
    cast = lambda a: a.astype(np.float32).astype(ml_dtypes.bfloat16)
    return window.astype(np.float32), waves.astype(np.float32), cast(segment), cast(lag)


def section_sums(dead_ref, sec_ref, x_ref, out_ref):
    chans, wins, ns = x_ref.shape
    first = pl.program_id(0) * chans

    @pl.when(pl.program_id(0) == 0)
    def _():
        out_ref[...] = jnp.zeros_like(out_ref)

    def body(c, carry):
        value = x_ref[c].astype(F32)
        live = 1 - dead_ref[first + c]
        sums, counts = carry
        weights = [jnp.where(sec_ref[first + c] == s, live, 0).astype(F32) for s in range(NSEC)]
        return (
            tuple(sums[s] + weights[s] * value for s in range(NSEC)),
            tuple(counts[s] + weights[s] for s in range(NSEC)),
        )

    zero = jnp.zeros((wins, ns), F32)
    sums, counts = lax.fori_loop(
        0, chans, body, ((zero,) * NSEC, (jnp.float32(0),) * NSEC), unroll=8
    )
    for s in range(NSEC):
        out_ref[s, :, :ns] += sums[s]
        out_ref[s, :, ns:] += jnp.zeros((wins, LANE), F32) + counts[s]


def circulant_kernel(filter_ref, out_ref):
    ns = filter_ref.shape[1]
    rows = 16
    for t in range(0, ns, rows):
        block = jnp.broadcast_to(filter_ref[...], (rows, ns))
        out_ref[t : t + rows, :] = pltpu.roll(block, t, 1, stride=1, stride_axis=0).astype(BF16)


def segment_factors(kind, odd, flag_ref, tot, x, hann, conv, seg, work, copied, emit):
    common, clean, rows, series, stage = work
    sets = {"own": (0,), "halo": (0, 1), "other": (0, 0)}[kind]
    _, wins, ns = x[0].shape
    chans = sum(piece.shape[0] for piece in x)
    pitch = wins + 1
    size = seg.shape[0]
    half = size // 2
    blocks = ns // half
    jw = blocks * wins
    jpitch = jw + 1
    held = flag_ref.shape[1]
    for copy in copied["first"]:
        copy.wait()
    for g in range(len(tot)):
        for s in range(NSEC):
            common[g * NSEC + s] = tot[g][s, :, :ns] / jnp.maximum(tot[g][s, :, ns : ns + 1], 1.0)
    sign = 1.0 - 2.0 * (lax.broadcasted_iota(jnp.int32, (wins, LANE), 1) % 2).astype(F32)

    for number, group in enumerate(sets):
        piece = x[number]
        length = piece.shape[0]
        base = number * length
        if kind == "other":
            base = odd * length if number == 0 else length - odd * length

        def clean_channel(c, _):
            at = base + c
            flag = lax.rem(at, held)
            live = (1 - flag_ref[0, flag]).astype(F32)
            value = (piece[c].astype(F32) - common[group * NSEC + flag_ref[1, flag]]) * hann[...]
            tiles = [value[:, t * LANE : (t + 1) * LANE] for t in range(ns // LANE)]
            mass = sum(tiles[1:], tiles[0])
            square = sum([tile * tile for tile in tiles[1:]], tiles[0] * tiles[0])
            lowest = jnp.sum(mass, axis=1, keepdims=True)
            highest = jnp.sum(mass * sign, axis=1, keepdims=True)
            square = jnp.sum(square, axis=1, keepdims=True)
            power = 0.5 * square + (lowest * lowest - highest * highest) * (0.5 / ns)
            value = value * (lax.rsqrt(power + 1e-06) * live)
            for t in range(ns // LANE):
                clean[t, pl.ds(at * pitch, wins), :] = value[:, t * LANE : (t + 1) * LANE]
            return 0

        parts = copied["x"][number]
        part = length // len(parts)
        for n, copy in enumerate(parts):
            copy.wait()
            lax.fori_loop(n * part, (n + 1) * part, clean_channel, 0, unroll=8)
    for copy in copied["tables"]:
        copy.wait()
    want = (odd == 1) if kind == "halo" else (odd == 0)

    def some_windows(step, _):
        for i in range(TOGETHER):
            w = step * TOGETHER + i
            for t in range(ns // LANE):
                rows[i * chans : (i + 1) * chans, t * LANE : (t + 1) * LANE] = clean[
                    t, pl.ds(w, chans, stride=pitch), :
                ].astype(BF16)
        for t in range(0, ns, TILE):
            series[half // 2 + t : half // 2 + t + TILE, :] = lax.dot_general(
                conv[t : t + TILE, :], rows[...], NT, preferred_element_type=F32
            ).astype(BF16)
        series[: half // 2, :] = series[ns : ns + half // 2, :]
        series[ns + half // 2 :, :] = series[half // 2 : half, :]

        def place(which, j, value):
            for i in range(TOGETHER):
                at = j * wins + step * TOGETHER + i
                stage[which, pl.ds(at, size, stride=jpitch), :] = value[
                    :, i * chans : (i + 1) * chans
                ]

        for j in range(blocks):
            start = j * half + half // 2
            b = jnp.dot(
                seg[:, :half], series[start : start + half, :], preferred_element_type=F32
            )
            place(1, j, b)

        @pl.when(want)
        def _():
            for j in range(blocks):
                a = jnp.dot(
                    seg[...], series[j * half : j * half + size, :], preferred_element_type=F32
                )
                place(0, j, a)

        return 0

    lax.fori_loop(0, wins // TOGETHER, some_windows, 0)

    def factor(which, k):
        return jnp.concatenate(
            [
                stage[which, pl.ds((2 * k + part) * jpitch, jw), :].astype(BF16)
                for part in range(2)
            ],
            axis=0,
        )

    emit(want, factor)


def work_shapes(groups, chans, wins, ns):
    half = LAGS
    rows = 2 * half * (ns // half * wins + 1)
    return [
        pltpu.VMEM((groups * NSEC, wins, ns), F32),
        pltpu.VMEM((ns // LANE, chans * (wins + 1), LANE), F32),
        pltpu.VMEM((TOGETHER * chans, ns), BF16),
        pltpu.VMEM((ns + half, TOGETHER * chans), BF16),
        pltpu.VMEM((2, rows, chans), F32),
    ]


def input_copies(first, x, tables_in, sem):
    copied = {"first": [], "x": [], "tables": []}
    used = 0

    def copy(source, target):
        nonlocal used
        made = pltpu.make_async_copy(source, target, sem.at[used])
        made.start()
        used += 1
        return made

    copied["first"] = [copy(*pair) for pair in first]
    for source, target in x:
        part = target.shape[0] // PIECES
        copied["x"].append(
            [
                copy(source.at[pl.ds(n * part, part)], target.at[pl.ds(n * part, part)])
                for n in range(PIECES)
            ]
        )
    copied["tables"] = [copy(*pair) for pair in tables_in]
    return copied


def segments_kernel(kind, groups, count, odd_ref, flag_ref, *rest):
    tot_hbm, rest = rest[:groups], rest[groups:]
    x_hbm, rest = rest[:count], rest[count:]
    hann_hbm, conv_hbm, seg_hbm, a_hbm, b_hbm = rest[:5]
    tot, rest = rest[5 : 5 + groups], rest[5 + groups :]
    x, rest = rest[:count], rest[count:]
    hann, conv, seg = rest[:3]
    work, (a_out, b_out, in_sem, out_sem) = rest[3:-4], rest[-4:]
    copied = input_copies(
        list(zip(tot_hbm, tot)) + [(hann_hbm, hann)],
        list(zip(x_hbm, x)),
        [(conv_hbm, conv), (seg_hbm, seg)],
        in_sem,
    )
    bins = b_out.shape[0]
    step = bins // STEPS

    def emit(want, factor):
        def first(k, _):
            a_out[k] = factor(0, k).T[: a_out.shape[1]]
            return 0

        def second(k, _):
            b_out[k] = factor(1, k)
            return 0

        def send(n, source, target):
            part = pl.ds(n % STEPS * step, step)
            return pltpu.make_async_copy(source.at[part], target.at[part], out_sem.at[n])

        @pl.when(want)
        def _():
            for n in range(STEPS):
                lax.fori_loop(n * step, (n + 1) * step, first, 0, unroll=8)
                send(n, a_out, a_hbm).start()

        for n in range(STEPS):
            lax.fori_loop(n * step, (n + 1) * step, second, 0, unroll=8)
            send(STEPS + n, b_out, b_hbm).start()

        @pl.when(want)
        def _():
            for n in range(STEPS):
                send(n, a_out, a_hbm).wait()

        for n in range(STEPS):
            send(STEPS + n, b_out, b_hbm).wait()

    segment_factors(
        kind, odd_ref[0], flag_ref, tot, x, hann, conv, seg, work, copied, emit
    )


def segments(kind, odd, flags, totals, pieces, hann, conv, seg):
    chans = sum(x.shape[0] for x in pieces)
    _, wins, ns = pieces[0].shape
    size = seg.shape[0]
    half = size // 2
    depth = ns // half * wins * 2
    kept = chans if kind == "halo" else chans // 2
    smem = pl.BlockSpec(memory_space=pltpu.SMEM)
    anywhere = pl.BlockSpec(memory_space=pl.ANY)
    operands = list(totals) + list(pieces) + [hann, conv, seg]
    a_shape = jax.ShapeDtypeStruct((half, kept, depth), BF16)
    b_shape = jax.ShapeDtypeStruct((half, depth, chans), BF16)
    return pl.pallas_call(
        functools.partial(segments_kernel, kind, len(totals), len(pieces)),
        out_shape=[a_shape, b_shape],
        in_specs=[smem] * 2 + [anywhere] * len(operands),
        out_specs=[anywhere] * 2,
        scratch_shapes=[pltpu.VMEM(value.shape, value.dtype) for value in operands]
        + work_shapes(len(totals), chans, wins, ns)
        + [
            pltpu.VMEM(a_shape.shape, BF16),
            pltpu.VMEM(b_shape.shape, BF16),
            pltpu.SemaphoreType.DMA((len(operands) + len(pieces) * PIECES,)),
            pltpu.SemaphoreType.DMA((2 * STEPS,)),
        ],
        compiler_params=pltpu.CompilerParams(vmem_limit_bytes=VMEM),
        cost_estimate=pl.CostEstimate(
            flops=2 * wins * chans * ns * (ns + 3 * size),
            bytes_accessed=16 * 1024 * 1024,
            transcendentals=0,
        ),
    )(odd, flags, *operands)


def stack_kernel(scale, shares, me_ref, flag_ref, *rest):
    tot_hbm, x0_hbm, x1_hbm, hann_hbm, conv_hbm, seg_hbm, lag_hbm = rest[:7]
    left_hbm, rest = rest[7:11], rest[11:]
    outs, rest = rest[:shares], rest[shares:]
    tot, x0, x1, hann, conv, seg, lag = rest[:7]
    (a0, ah, b0, bh), rest = rest[7:11], rest[11:]
    work, (a1, b1, one, in_sem, late_sem) = rest[:-5], rest[-5:]
    me = me_ref[0]
    odd = lax.rem(me, 2)
    copied = input_copies(
        [(tot_hbm, tot), (hann_hbm, hann)],
        [(x0_hbm, x0), (x1_hbm, x1)],
        [(conv_hbm, conv), (seg_hbm, seg), (lag_hbm, lag)],
        in_sem,
    )
    late = [
        pltpu.make_async_copy(source, target, late_sem.at[n])
        for n, (source, target) in enumerate(zip(left_hbm, (a0, ah, b0, bh)))
    ]
    for copy in late:
        copy.start()
    bins, width, depth = a0.shape
    chans = b0.shape[2]
    nfr = lag.shape[1]
    pitch = nfr + 1
    cross = work[-1]

    def emit(want, factor):
        def first(k, _):
            a1[k] = factor(0, k).T[:width]
            return 0

        def second(k, _):
            b1[k] = factor(1, k)
            return 0

        @pl.when(want)
        def _():
            lax.fori_loop(0, bins, first, 0, unroll=8)

        lax.fori_loop(0, bins, second, 0, unroll=8)

    segment_factors(
        "other", odd, flag_ref, [tot], [x0, x1], hann, conv, seg, work, copied, emit
    )
    for copy in late:
        copy.wait()

    def bins_with(left_of):
        def one_bin(k, _):
            left = left_of(k)
            part = depth // 2
            swapped = jnp.concatenate(
                [
                    left[:, part:depth],
                    -left[:, :part],
                    left[:, depth + part :],
                    -left[:, depth : depth + part],
                ],
                axis=1,
            )
            halo = bh[k]
            other = jnp.concatenate([halo[:, width:], halo[:, :width]], axis=1)
            right = jnp.concatenate(
                [
                    jnp.concatenate([b0[k], halo], axis=1),
                    jnp.concatenate([b1[k], other], axis=1),
                ],
                axis=0,
            )
            value = jnp.dot(
                jnp.concatenate([left, swapped], axis=0), right, preferred_element_type=F32
            )
            for p in range(2):
                for t in range(2):
                    cross[t, pl.ds(2 * k + p, width, stride=pitch), :] = value[
                        p * width : (p + 1) * width, t * chans : (t + 1) * chans
                    ]
            return 0

        lax.fori_loop(0, bins, one_bin, 0, unroll=8)

    @pl.when(odd == 1)
    def _():
        bins_with(lambda k: jnp.concatenate([ah[k, :width], ah[k, width:]], axis=1))

    @pl.when(odd == 0)
    def _():
        bins_with(lambda k: jnp.concatenate([a0[k], a1[k]], axis=1))

    row = lax.broadcasted_iota(jnp.int32, one.shape[1:], 0)
    column = lax.broadcasted_iota(jnp.int32, one.shape[1:], 1)
    turned = jnp.where(row < width, row + chans, row - width)
    place = row + (turned - row) * odd
    for t in range(2):
        one[t] = jnp.where(place == column + t * chans, 1.0, 0.0)
    share = OFFS // shares

    def one_channel(c, _):
        value = jnp.concatenate(
            [cross[t, pl.ds(c * pitch, nfr), :] for t in range(2)], axis=1
        ).astype(BF16)
        starts = [c + 1 + share * (me ^ d) for d in range(shares)]
        pick = jnp.concatenate(
            [
                jnp.concatenate([one[t, pl.ds(start, share), :] for start in starts], axis=0)
                for t in range(2)
            ],
            axis=1,
        ).astype(BF16)
        lagged = jnp.dot(lag[...], value, preferred_element_type=F32) * scale
        band = lax.dot_general(pick, lagged.astype(BF16), NT, preferred_element_type=F32)
        for d, out in enumerate(outs):
            out[c] = band[d * share : (d + 1) * share, :].astype(BF16)
        return 0

    lax.fori_loop(0, width, one_channel, 0, unroll=4)


def stacks(shares, scale, me, flags, total, pieces, hann, conv, seg, lag, a0, ah, b0, bh):
    bins, width, depth = a0.shape
    chans = b0.shape[2]
    _, wins, ns = pieces[0].shape
    nlag, nfr = lag.shape
    smem = pl.BlockSpec(memory_space=pltpu.SMEM)
    vmem = pl.BlockSpec(memory_space=pltpu.VMEM)
    anywhere = pl.BlockSpec(memory_space=pl.ANY)
    operands = [total, *pieces, hann, conv, seg, lag, a0, ah, b0, bh]
    return pl.pallas_call(
        functools.partial(stack_kernel, scale, shares),
        out_shape=[jax.ShapeDtypeStruct((width, OFFS // shares, nlag), BF16)] * shares,
        in_specs=[smem] * 2 + [anywhere] * len(operands),
        out_specs=[vmem] * shares,
        scratch_shapes=[pltpu.VMEM(value.shape, value.dtype) for value in operands]
        + work_shapes(1, chans, wins, ns)
        + [
            pltpu.VMEM(a0.shape, BF16),
            pltpu.VMEM(b0.shape, BF16),
            pltpu.VMEM((2, chans + width, chans), F32),
            pltpu.SemaphoreType.DMA((8 + len(pieces) * PIECES,)),
            pltpu.SemaphoreType.DMA((4,)),
        ],
        compiler_params=pltpu.CompilerParams(vmem_limit_bytes=VMEM),
        cost_estimate=pl.CostEstimate(
            flops=2 * width * bins * 4 * (2 * depth * chans + 2 * OFFS * chans),
            bytes_accessed=20 * 1024 * 1024,
            transcendentals=0,
        ),
    )(me, flags, *operands)


def add_over(value, axis):
    count = lax.axis_size(axis)
    if count & (count - 1):
        return lax.psum(value, axis)
    bit = 1
    while bit < count:
        steps = [bit] if bit == 1 or 2 * bit == count else [bit, 2 * bit, 3 * bit]
        value = sum(
            [lax.ppermute(value, axis, [(i, i ^ s) for i in range(count)]) for s in steps], value
        )
        bit *= 1 + len(steps)
    return value


def shards(samples, band_gain, dead_flags, section_ids):
    chans, wins, ns = samples.shape
    nf = ns // 2
    width = chans // 2
    blocks = lax.axis_size("fibre")
    groups = lax.axis_size("tm")
    me = lax.axis_index("tm")
    odd = me % 2
    window, waves, seg, lag = [jnp.asarray(t) for t in tables(ns, nf)]
    hann = jnp.broadcast_to(window[None, :], (wins, ns))
    response = jnp.sum(band_gain[:, None] * waves, axis=0, keepdims=True)
    conv = pl.pallas_call(
        circulant_kernel,
        out_shape=jax.ShapeDtypeStruct((ns, ns), BF16),
        compiler_params=pltpu.CompilerParams(vmem_limit_bytes=VMEM),
    )(response)
    swap = [(z, z ^ 1) for z in range(groups)]
    both = ("fibre", "tm")
    halo_pairs = [
        (b * groups + z, (b + (1 if z % 2 else -1)) % blocks * groups + z)
        for b in range(blocks)
        for z in range(groups)
    ]

    first_half = lax.dynamic_slice_in_dim(samples, (1 - odd) * width, width, 0)
    their_first = lax.ppermute(first_half, "tm", swap)
    flags = jnp.stack([dead_flags, section_ids])
    halo_flags = lax.ppermute(
        lax.dynamic_slice_in_dim(flags, odd * width, width, 1), both, halo_pairs
    )
    smem = pl.BlockSpec(memory_space=pltpu.SMEM)
    steps = 4
    sums = pl.pallas_call(
        section_sums,
        grid=(steps,),
        out_shape=jax.ShapeDtypeStruct((NSEC, wins, ns + LANE), F32),
        in_specs=[smem, smem, pl.BlockSpec((chans // steps, wins, ns), lambda i: (i, 0, 0))],
        out_specs=pl.BlockSpec((NSEC, wins, ns + LANE), lambda i: (0, 0, 0)),
        compiler_params=pltpu.CompilerParams(vmem_limit_bytes=VMEM),
    )(dead_flags, section_ids, samples)
    total = add_over(sums, "fibre")
    total, halo_flags, kept = lax.optimization_barrier((total, halo_flags, samples))
    their_total = lax.ppermute(total, "tm", swap)
    own_half = lax.dynamic_slice_in_dim(kept, odd * width, width, 0)
    halo = lax.ppermute(own_half, both, halo_pairs)
    ready = (total, their_total, their_first, own_half, flags, hann, conv, seg, lag)
    ready = lax.optimization_barrier(ready)
    total, their_total, their_first, own_half, flags, hann, conv, seg, lag = ready
    their_halo = lax.ppermute(their_first, both, halo_pairs)
    their_second = lax.ppermute(own_half, "tm", swap)

    side = odd[None]
    parts = (hann, conv, seg)
    a0, b0 = segments("own", side, flags, (total,), (samples,), *parts)
    ah, bh = segments("halo", side, halo_flags, (total, their_total), (halo, their_halo), *parts)
    scale = 2.0 / ns / LAGS / math.sqrt(nf * wins * groups)
    found = stacks(
        groups,
        scale,
        me[None],
        flags,
        their_total,
        (their_first, their_second),
        *(hann, conv, seg, lag),
        *(a0, ah, b0, bh),
    )
    arrived = []
    for d in range(groups):
        pairs = [
            (b * groups + z, (b - z % 2) % blocks * groups + (z ^ d))
            for b in range(blocks)
            for z in range(groups)
        ]
        arrived.append(lax.ppermute(found[d], both, pairs).astype(F32))
    same = sum(arrived[2::2], arrived[0])
    other = sum(arrived[3::2], arrived[1])
    return jnp.concatenate(
        [jnp.where(odd == 0, same, other), jnp.where(odd == 0, other, same)], axis=0
    )


def solution(mesh):
    in_specs = (P("fibre", "tm", None), P(), P("fibre"), P("fibre"))
    out_specs = P("fibre", "tm", None)
    return jax.shard_map(shards, mesh=mesh, in_specs=in_specs, out_specs=out_specs, check_vma=False)
```

time: 142 us -> 141 us (level)
  waiting for transfers between devices: 33.7 us -> 55.4 us
  Pallas kernels: 75.8 us -> 59 us
  starting transfers between devices: 23.2 us -> 14.3 us
  other arithmetic: 3.54 us -> 5.12 us
    ppermute x8 -> x4, waiting for transfers between devices: 24.4 us -> 47.1 us  [shards(): arrived.append(lax.ppermute(found[d], both, pairs).astype(F32))]
    pallas_call x5 -> x3, Pallas kernels: 69.6 us -> 52.9 us  [the longest x1 28.7 us: stacks(): pl.pallas_call(functools.partial(stack_kernel, scale, shares), out_shape=...]
    ppermute x1, waiting for transfers between devices: 0.98 us -> 7.33 us  [shards(): their_total = lax.ppermute(total, 'tm', swap)]
    ppermute x8 -> x4, starting transfers between devices: 9.91 us -> 3.76 us  [shards(): arrived.append(lax.ppermute(found[d], both, pairs).astype(F32))]
    ppermute x1, starting transfers between devices: 4.78 us -> 0.01 us  [shards(): lax.ppermute(lax.dynamic_slice_in_dim(flags, odd * width, width, 1), both...]
    ppermute x1, waiting for transfers between devices: 3.72 us -> 0.01 us  [shards(): their_first = lax.ppermute(first_half, 'tm', swap)]
    ppermute x4, waiting for transfers between devices: 3.18 us -> 1.02 us  [add_over(): lax.ppermute(value, axis, [(i, i ^ s) for i in range(count)])]
    reduce_sum x1, other arithmetic: 0.8 us -> 2.38 us  [shards(): response = jnp.sum(band_gain[:, None] * waves, axis=0, keepdims=True)]
  transfers between devices with their start and end apart: 18 -> 14, of which waited for: 9 -> 5; matrix products, arithmetic and copies ran while one was open for 2% -> 4% of each run, Pallas kernels for 33% -> 22%
where the time goes in v7:
time: 141 us; the launch traced here: 140 us
  Pallas kernels  59 us (42%)
  waiting for transfers between devices  55.4 us (39%)
  starting transfers between devices  14.3 us (10%)
  local copies, waits for them, and re-layouts  6.01 us (4%)
  other arithmetic  5.12 us (4%)
    ppermute x4, waiting for transfers between devices, shards(): arrived.append(lax.ppermute(found[d], both, pairs).astype(F32))  47.1 us
    pallas_call x1, Pallas kernels, stacks(): pl.pallas_call(functools.partial(stack_kernel, scale, shares), out_shape=...  28.7 us
    pallas_call x2, Pallas kernels, segments(): pl.pallas_call(functools.partial(segments_kernel, kind, len(totals), len(...  24.2 us
    ppermute x1, waiting for transfers between devices, shards(): their_total = lax.ppermute(total, 'tm', swap)  7.33 us
    ppermute x4, starting transfers between devices, shards(): arrived.append(lax.ppermute(found[d], both, pairs).astype(F32))  3.76 us
    ppermute x4, starting transfers between devices, add_over(): lax.ppermute(value, axis, [(i, i ^ s) for i in range(count)])  3.67 us
    pallas_call x1, Pallas kernels, shards(): pl.pallas_call(section_sums, grid=(steps,), out_shape=jax.ShapeDtypeStruc...  3.54 us
    unnamed x24, local copies, waits for them, and re-layouts  2.95 us
  transfers between devices with their start and end apart: 14, of which 5 were waited for; matrix products, arithmetic and copies ran while one was open for 4% of the time, Pallas kernels for 22%

profile of v7, /device:TPU:19, one launch (start us, length us, event | category | flops | bytes accessed | tf_op | source)
XLA Modules:
  0.0 140.1 jit_solution(2718112313546272587)
XLA Ops:
  0.0 1.3 constant_dynamic-slice_fusion.1
  1.3 1.4 collective-permute-start.6
  2.7 3.5 %shard_map.82 = f32[2,8,1152]{2,1,0:T(8,128)} custom-call(s32[128]{0:T(128)} %dead_ref.1, s32[128]{0:T(128)} %sec_ref.1, bf16[128,8,1024]{2,1,0:T(8,128)(2,1)} %rest_1_.1), custom_call_target="tpu_custom_call" | custom-call | tf_op jit(solution)/shard_map/pallas_call | solution.py:501
  7.3 1.0 collective-permute-done
  9.2 1.3 collective-permute-start.3
  10.7 1.2 collective-permute-start.1
  12.0 2.4 %multiply_reduce_fusion = f32[1024]{0:T(1024)} fusion(f32[512,1024]{1,0:T(8,128)} %constant.34.clone, f32[512]{0:T(512)S(1)} %copy-done.6), kind=kLoop, calls=%fused_computation.1 | loop fusion | flops 1047552 | bytes 2103296 | tf_op jit(solution)/shard_map/reduce_sum | solution.py:479
  14.3 2.6 %shard_map.83.rest_3_.rest_5_.rest_4_ = bf16[1024,1024]{1,0:T(8,128)(2,1)} custom-call(f32[1,1024]{1,0:T(1,128)} %bitcast.5), custom_call_target="tpu_custom_call" | custom-call | tf_op jit(solution)/shard_map/pallas_call | solution.py:480
  17.4 1.0 constant_dynamic-slice_fusion
  18.4 1.4 collective-permute-start.8
  19.8 7.3 %collective-permute-done.5.rest_1_.rest_0_ = f32[2,8,1152]{2,1,0:T(8,128)S(1)} collective-permute-done((f32[2,8,1152]{2,1,0:T(8,128)S(1)}, f32[2,8,1152]{2,1,0:T(8,128)S(1)}, u32[]{:S(2)}, u32[]{:S(2)}) %collective-permute-start.5) | collective-permute-done | bytes 73760 | tf_op jit(solution)/shard_map/ppermute | solution.py:511
  27.1 1.4 %collective-permute-start.9 = (bf16[64,8,1024]{2,1,0:T(8,128)(2,1)}, bf16[64,8,1024]{2,1,0:T(8,128)(2,1)S(1)}, u32[]{:S(2)}, u32[]{:S(2)}) collective-permute-start(bf16[64,8,1024]{2,1,0:T(8,128)(2,1)} %collective-permute-done.6.rest_1_), channel_id=1, source_target_pairs={{0,28},{1,5},{2,30},{3,7},{4,0},{5,9},{6,2},{7,11},{8,4},{9,13},{1... | collective-permute-start | bytes 3145736 | tf_op jit(solution)/shard_map/ppermute | solution.py:517
  28.6 2.4 %collective-permute-start.7 = (bf16[64,8,1024]{2,1,0:T(8,128)(2,1)}, bf16[64,8,1024]{2,1,0:T(8,128)(2,1)S(1)}, u32[]{:S(2)}, u32[]{:S(2)}) collective-permute-start(bf16[64,8,1024]{2,1,0:T(8,128)(2,1)} %constant_dynamic-slice_fusion), channel_id=1, source_target_pairs={{0,1},{1,0},{2,3},{3,2},{4,5},{5,4},{6,7},{7,6},{8,9},{9,8},{10,11... | collective-permute-start | bytes 3145736 | tf_op jit(solution)/shard_map/ppermute | solution.py:518
  31.6 13.7 %shard_map.84 = (bf16[128,64,128]{2,1,0:T(8,128)(2,1)}, bf16[128,128,128]{2,1,0:T(8,128)(2,1)}) custom-call(s32[1]{0:T(128)} %bitcast.4.odd_ref, s32[2,128]{1,0:T(2,128)} %copy-done.4, f32[2,8,1152]{2,1,0:T(8,128)} %copy-done.3, bf16[128,8,1024]{2,1,0:T(8,128)(2,1)} %rest_1_.1, f32[8,1024]{1,0:T(8,128)} %broadcast_in_dim.17.rest_2_.rest_4_.rest_3_, ...), custom_call_target="tpu_custom_call" | custom-call | flops 3758096384 | bytes 16777216 | tf_op jit(solution)/shard_map/pallas_call | solution.py:282
  45.3 1.0 copy-done.9
  47.3 10.5 %shard_map.85 = (bf16[128,128,128]{2,1,0:T(8,128)(2,1)}, bf16[128,128,128]{2,1,0:T(8,128)(2,1)}) custom-call(s32[1]{0:T(128)} %bitcast.4.odd_ref, s32[2,64]{1,0:T(2,128)} %copy-done.11, f32[2,8,1152]{2,1,0:T(8,128)} %copy-done.3, f32[2,8,1152]{2,1,0:T(8,128)} %copy-done.2, bf16[64,8,1024]{2,1,0:T(8,128)(2,1)} %copy-done.9, bf16[64,8,1024]{2,1,0:T(8,128)(2,1)} %copy-done.10, ...), custom_call_target="tpu_custom_call" | custom-call | flops 3758096384 | bytes 16777216 | tf_op jit(solution)/shard_map/pallas_call | solution.py:282
  57.8 1.0 copy-done.1
  58.8 28.7 %shard_map.86 = (bf16[64,32,128]{2,1,0:T(8,128)(2,1)}, bf16[64,32,128]{2,1,0:T(8,128)(2,1)}, bf16[64,32,128]{2,1,0:T(8,128)(2,1)}, bf16[64,32,128]{2,1,0:T(8,128)(2,1)}) custom-call(s32[1]{0:T(128)} %bitcast.me_ref, s32[2,128]{1,0:T(2,128)} %copy-done.4, f32[2,8,1152]{2,1,0:T(8,128)} %copy-done.2, bf16[64,8,1024]{2,1,0:T(8,128)(2,1)} %collective-permute-done.6.rest_1_, ...), custom_call_target="tpu_custom_call" | custom-call | flops 4294967296 | bytes 20971520 | tf_op jit(solution)/shard_map/pallas_call | solution.py:432
  87.5 1.7 %collective-permute-start.10 = (bf16[64,32,128]{2,1,0:T(8,128)(2,1)}, bf16[64,32,128]{2,1,0:T(8,128)(2,1)S(1)}, u32[]{:S(2)}, u32[]{:S(2)}) collective-permute-start(bf16[64,32,128]{2,1,0:T(8,128)(2,1)} %get-tuple-element.41), channel_id=1, source_target_pairs={{0,0},{1,29},{2,2},{3,31},{4,4},{5,1},{6,6},{7,3},{8,8},{9,5},{10,... | collective-permute-start | bytes 1572872 | tf_op jit(solution)/shard_map/ppermute | solution.py:542
  90.1 1.1 collective-permute-start.13
  91.2 23.0 %collective-permute-done.11 = bf16[64,32,128]{2,1,0:T(8,128)(2,1)S(1)} collective-permute-done((bf16[64,32,128]{2,1,0:T(8,128)(2,1)}, bf16[64,32,128]{2,1,0:T(8,128)(2,1)S(1)}, u32[]{:S(2)}, u32[]{:S(2)}) %collective-permute-start.11) | collective-permute-done | bytes 524320 | tf_op jit(solution)/shard_map/ppermute | solution.py:542
  114.2 1.9 %collective-permute-done.12 = bf16[64,32,128]{2,1,0:T(8,128)(2,1)S(1)} collective-permute-done((bf16[64,32,128]{2,1,0:T(8,128)(2,1)}, bf16[64,32,128]{2,1,0:T(8,128)(2,1)S(1)}, u32[]{:S(2)}, u32[]{:S(2)}) %collective-permute-start.12) | collective-permute-done | bytes 524320 | tf_op jit(solution)/shard_map/ppermute | solution.py:542
  116.1 22.2 %collective-permute-done.13 = bf16[64,32,128]{2,1,0:T(8,128)(2,1)S(1)} collective-permute-done((bf16[64,32,128]{2,1,0:T(8,128)(2,1)}, bf16[64,32,128]{2,1,0:T(8,128)(2,1)S(1)}, u32[]{:S(2)}, u32[]{:S(2)}) %collective-permute-start.13) | collective-permute-done | bytes 524320 | tf_op jit(solution)/shard_map/ppermute | solution.py:542
  138.6 1.5 %pad_maximum_fusion = f32[128,32,128]{2,1,0:T(8,128)} fusion(f32[64,32,128]{2,1,0:T(8,128)S(1)} %get-tuple-element.46, f32[64,32,128]{2,1,0:T(8,128)S(1)} %get-tuple-element.45), kind=kLoop, calls=%fused_computation | loop fusion | flops 524288 | bytes 4194304 | tf_op jit(solution)/shard_map/concatenate | solution.py:545
  (43 shorter events, 5.4 us)
Async XLA Ops:
  0.0 7.2 %copy-start.7 = (s32[128]{0:T(128)S(1)}, s32[128]{0:T(128)}, u32[]{:S(2)}) copy-start(s32[128]{0:T(128)} %sec_ref.1) | copy-start | bytes 1540
  0.0 7.2 %copy-start.8 = (s32[128]{0:T(128)S(1)}, s32[128]{0:T(128)}, u32[]{:S(2)}) copy-start(s32[128]{0:T(128)} %dead_ref.1) | copy-start | bytes 1540
  0.0 11.9 %copy-start.6 = (f32[512]{0:T(512)S(1)}, f32[512]{0:T(512)}, u32[]{:S(2)}) copy-start(f32[512]{0:T(512)} %param.9) | copy-start | bytes 6148
  1.3 25.8 %collective-permute-start.6 = (bf16[64,8,1024]{2,1,0:T(8,128)(2,1)S(1)}, bf16[64,8,1024]{2,1,0:T(8,128)(2,1)}, u32[]{:S(2)}, u32[]{:S(2)}) collective-permute-start(bf16[64,8,1024]{2,1,0:T(8,128)(2,1)S(1)} %constant_dynamic-slice_fusion.1), channel_id=1, source_target_pairs={{0,1},{1,0},{2,3},{3,2},{4,5},{5,4},{6,7},{7,6},{8,9},{9,8},{10,11... | collective-permute-start | bytes 3145736 | tf_op jit(solution)/shard_map/ppermute | solution.py:494
  6.2 2.1 %collective-permute-start = (f32[2,8,1152]{2,1,0:T(8,128)}, f32[2,8,1152]{2,1,0:T(8,128)S(1)}, u32[]{:S(2)}, u32[]{:S(2)}) collective-permute-start(f32[2,8,1152]{2,1,0:T(8,128)} %shard_map.82), channel_id=1, source_target_pairs={{0,4},{4,0},{8,12},{12,8},{16,20},{20,16},{24,28},{28,24},{1,5},{5... | collective-permute-start | bytes 221192 | tf_op jit(solution)/shard_map/ppermute | solution.py:463
  7.2 9.7 %copy-start.4 = (s32[2,128]{1,0:T(2,128)}, s32[2,128]{1,0:T(2,128)S(1)}, u32[]{:S(2)}) copy-start(s32[2,128]{1,0:T(2,128)S(1)} %pad_add_fusion.flag_ref) | copy-start | bytes 3076
  7.3 9.7 %collective-permute-start.4 = (s32[2,64]{1,0:T(2,128)S(1)}, s32[2,64]{1,0:T(2,128)S(1)}, u32[]{:S(2)}, u32[]{:S(2)}) collective-permute-start(s32[2,64]{1,0:T(2,128)S(1)} %constant_dynamic-slice_fusion.2), channel_id=1, source_target_pairs={{0,28},{1,5},{2,30},{3,7},{4,0},{5,9},{6,2},{7,11},{8,4},{9,13},{1... | collective-permute-start | bytes 1544 | tf_op jit(solution)/shard_map/ppermute | solution.py:496
  9.2 8.1 %copy-start = (bf16[128,8,1024]{2,1,0:T(8,128)(2,1)S(1)}, bf16[128,8,1024]{2,1,0:T(8,128)(2,1)}, u32[]{:S(2)}) copy-start(bf16[128,8,1024]{2,1,0:T(8,128)(2,1)} %rest_1_.1) | copy-start | bytes 6291460
  9.2 7.7 %collective-permute-start.3 = (f32[2,8,1152]{2,1,0:T(8,128)S(1)}, f32[2,8,1152]{2,1,0:T(8,128)S(1)}, u32[]{:S(2)}, u32[]{:S(2)}) collective-permute-start(f32[2,8,1152]{2,1,0:T(8,128)S(1)} %add.30), channel_id=1, source_target_pairs={{0,24},{4,28},{8,16},{12,20},{16,8},{20,12},{24,0},{28,4},{1,25},{... | collective-permute-start | bytes 221192 | tf_op jit(solution)/shard_map/ppermute | solution.py:463
  10.5 6.5 %collective-permute-start.2 = (f32[2,8,1152]{2,1,0:T(8,128)S(1)}, f32[2,8,1152]{2,1,0:T(8,128)S(1)}, u32[]{:S(2)}, u32[]{:S(2)}) collective-permute-start(f32[2,8,1152]{2,1,0:T(8,128)S(1)} %add.30), channel_id=1, source_target_pairs={{0,16},{4,20},{8,24},{12,28},{16,0},{20,4},{24,8},{28,12},{1,17},{... | collective-permute-start | bytes 221192 | tf_op jit(solution)/shard_map/ppermute | solution.py:463
  10.7 6.2 %collective-permute-start.1 = (f32[2,8,1152]{2,1,0:T(8,128)S(1)}, f32[2,8,1152]{2,1,0:T(8,128)S(1)}, u32[]{:S(2)}, u32[]{:S(2)}) collective-permute-start(f32[2,8,1152]{2,1,0:T(8,128)S(1)} %add.30), channel_id=1, source_target_pairs={{0,8},{4,12},{8,0},{12,4},{16,24},{20,28},{24,16},{28,20},{1,9},{5... | collective-permute-start | bytes 221192 | tf_op jit(solution)/shard_map/ppermute | solution.py:463
  14.3 16.6 %copy-start.5 = (f32[1024]{0:T(1024)S(1)}, f32[1024]{0:T(1024)}, u32[]{:S(2)}) copy-start(f32[1024]{0:T(1024)} %constant.33.clone) | copy-start | bytes 12292
  17.0 14.6 %copy-start.3 = (f32[2,8,1152]{2,1,0:T(8,128)}, f32[2,8,1152]{2,1,0:T(8,128)S(1)}, u32[]{:S(2)}) copy-start(f32[2,8,1152]{2,1,0:T(8,128)S(1)} %add_add_fusion.rest_0_) | copy-start | bytes 221188
  17.0 28.2 %copy-start.11 = (s32[2,64]{1,0:T(2,128)}, s32[2,64]{1,0:T(2,128)S(1)}, u32[]{:S(2)}) copy-start(s32[2,64]{1,0:T(2,128)S(1)} %collective-permute-done.4.flag_ref) | copy-start | bytes 1540
  17.0 10.1 %collective-permute-start.5 = (f32[2,8,1152]{2,1,0:T(8,128)S(1)}, f32[2,8,1152]{2,1,0:T(8,128)S(1)}, u32[]{:S(2)}, u32[]{:S(2)}) collective-permute-start(f32[2,8,1152]{2,1,0:T(8,128)S(1)} %add_add_fusion.rest_0_), channel_id=1, source_target_pairs={{0,1},{1,0},{2,3},{3,2},{4,5},{5,4},{6,7},{7,6},{8,9},{9,8},{10,11... | collective-permute-start | bytes 221192 | tf_op jit(solution)/shard_map/ppermute | solution.py:511
  18.4 26.9 %collective-permute-start.8 = (bf16[64,8,1024]{2,1,0:T(8,128)(2,1)}, bf16[64,8,1024]{2,1,0:T(8,128)(2,1)S(1)}, u32[]{:S(2)}, u32[]{:S(2)}) collective-permute-start(bf16[64,8,1024]{2,1,0:T(8,128)(2,1)} %constant_dynamic-slice_fusion), channel_id=1, source_target_pairs={{0,28},{1,5},{2,30},{3,7},{4,0},{5,9},{6,2},{7,11},{8,4},{9,13},{1... | collective-permute-start | bytes 3145736 | tf_op jit(solution)/shard_map/ppermute | solution.py:513
  27.1 18.2 %copy-start.2 = (f32[2,8,1152]{2,1,0:T(8,128)}, f32[2,8,1152]{2,1,0:T(8,128)S(1)}, u32[]{:S(2)}) copy-start(f32[2,8,1152]{2,1,0:T(8,128)S(1)} %collective-permute-done.5.rest_1_.rest_0_) | copy-start | bytes 221188
  27.1 18.2 %collective-permute-start.9 = (bf16[64,8,1024]{2,1,0:T(8,128)(2,1)}, bf16[64,8,1024]{2,1,0:T(8,128)(2,1)S(1)}, u32[]{:S(2)}, u32[]{:S(2)}) collective-permute-start(bf16[64,8,1024]{2,1,0:T(8,128)(2,1)} %collective-permute-done.6.rest_1_), channel_id=1, source_target_pairs={{0,28},{1,5},{2,30},{3,7},{4,0},{5,9},{6,2},{7,11},{8,4},{9,13},{1... | collective-permute-start | bytes 3145736 | tf_op jit(solution)/shard_map/ppermute | solution.py:517
  28.6 29.2 %collective-permute-start.7 = (bf16[64,8,1024]{2,1,0:T(8,128)(2,1)}, bf16[64,8,1024]{2,1,0:T(8,128)(2,1)S(1)}, u32[]{:S(2)}, u32[]{:S(2)}) collective-permute-start(bf16[64,8,1024]{2,1,0:T(8,128)(2,1)} %constant_dynamic-slice_fusion), channel_id=1, source_target_pairs={{0,1},{1,0},{2,3},{3,2},{4,5},{5,4},{6,7},{7,6},{8,9},{9,8},{10,11... | collective-permute-start | bytes 3145736 | tf_op jit(solution)/shard_map/ppermute | solution.py:518
  45.3 1.0 copy-start.9
  87.5 3.8 %collective-permute-start.10 = (bf16[64,32,128]{2,1,0:T(8,128)(2,1)}, bf16[64,32,128]{2,1,0:T(8,128)(2,1)S(1)}, u32[]{:S(2)}, u32[]{:S(2)}) collective-permute-start(bf16[64,32,128]{2,1,0:T(8,128)(2,1)} %get-tuple-element.41), channel_id=1, source_target_pairs={{0,0},{1,29},{2,2},{3,31},{4,4},{5,1},{6,6},{7,3},{8,8},{9,5},{10,... | collective-permute-start | bytes 1572872 | tf_op jit(solution)/shard_map/ppermute | solution.py:542
  89.2 25.0 %collective-permute-start.11 = (bf16[64,32,128]{2,1,0:T(8,128)(2,1)}, bf16[64,32,128]{2,1,0:T(8,128)(2,1)S(1)}, u32[]{:S(2)}, u32[]{:S(2)}) collective-permute-start(bf16[64,32,128]{2,1,0:T(8,128)(2,1)} %get-tuple-element.42), channel_id=1, source_target_pairs={{0,2},{1,31},{2,0},{3,29},{4,6},{5,3},{6,4},{7,1},{8,10},{9,7},{10... | collective-permute-start | bytes 1572872 | tf_op jit(solution)/shard_map/ppermute | solution.py:542
  89.2 26.9 %collective-permute-start.12 = (bf16[64,32,128]{2,1,0:T(8,128)(2,1)}, bf16[64,32,128]{2,1,0:T(8,128)(2,1)S(1)}, u32[]{:S(2)}, u32[]{:S(2)}) collective-permute-start(bf16[64,32,128]{2,1,0:T(8,128)(2,1)} %get-tuple-element.43), channel_id=1, source_target_pairs={{0,1},{1,28},{2,3},{3,30},{4,5},{5,0},{6,7},{7,2},{8,9},{9,4},{10,... | collective-permute-start | bytes 1572872 | tf_op jit(solution)/shard_map/ppermute | solution.py:542
  90.1 48.2 %collective-permute-start.13 = (bf16[64,32,128]{2,1,0:T(8,128)(2,1)}, bf16[64,32,128]{2,1,0:T(8,128)(2,1)S(1)}, u32[]{:S(2)}, u32[]{:S(2)}) collective-permute-start(bf16[64,32,128]{2,1,0:T(8,128)(2,1)} %get-tuple-element.44), channel_id=1, source_target_pairs={{0,3},{1,30},{2,1},{3,28},{4,7},{5,2},{6,5},{7,0},{8,11},{9,6},{10... | collective-permute-start | bytes 1572872 | tf_op jit(solution)/shard_map/ppermute | solution.py:542
  (2 other events, 1.9 us)

commit v8 on v7

--- a/solution.py
+++ b/solution.py
@@ -14,11 +14,11 @@
 LAGS = 128
 NSEC = 2
 LANE = 128
-PIECES = 4
+PART = 16
 TILE = 256
 STEPS = 4
 TOGETHER = 4
-VMEM = 60 * 1024 * 1024
+VMEM = 63 * 1024 * 1024
 NT = (((1,), (1,)), ((), ()))
 F32 = jnp.float32
 BF16 = jnp.bfloat16
@@ -66,17 +66,16 @@
         out_ref[s, :, ns:] += jnp.zeros((wins, LANE), F32) + counts[s]
 
 
-def circulant_kernel(filter_ref, out_ref):
+def circulant(filter_ref, out_ref):
     ns = filter_ref.shape[1]
-    rows = 16
-    for t in range(0, ns, rows):
-        block = jnp.broadcast_to(filter_ref[...], (rows, ns))
-        out_ref[t : t + rows, :] = pltpu.roll(block, t, 1, stride=1, stride_axis=0).astype(BF16)
-
-
-def segment_factors(kind, odd, flag_ref, tot, x, hann, conv, seg, work, copied, emit):
-    common, clean, rows, series, stage = work
-    sets = {"own": (0,), "halo": (0, 1), "other": (0, 0)}[kind]
+
+    for t in range(0, ns, 16):
+        block = jnp.broadcast_to(filter_ref[...], (16, ns))
+        out_ref[t : t + 16, :] = pltpu.roll(block, t, 1, stride=1, stride_axis=0).astype(BF16)
+
+
+def segment_factors(places, want, odd, flag_ref, tot, x, hann, response, seg, work, copied, emit):
+    common, clean, rows, series, conv, stage = work
     _, wins, ns = x[0].shape
     chans = sum(piece.shape[0] for piece in x)
     pitch = wins + 1
@@ -88,17 +87,16 @@
     held = flag_ref.shape[1]
     for copy in copied["first"]:
         copy.wait()
+    circulant(response, conv)
     for g in range(len(tot)):
         for s in range(NSEC):
             common[g * NSEC + s] = tot[g][s, :, :ns] / jnp.maximum(tot[g][s, :, ns : ns + 1], 1.0)
     sign = 1.0 - 2.0 * (lax.broadcasted_iota(jnp.int32, (wins, LANE), 1) % 2).astype(F32)
 
-    for number, group in enumerate(sets):
+    for number, (group, even_base, odd_base) in enumerate(places):
         piece = x[number]
         length = piece.shape[0]
-        base = number * length
-        if kind == "other":
-            base = odd * length if number == 0 else length - odd * length
+        base = even_base + odd * (odd_base - even_base)
 
         def clean_channel(c, _):
             at = base + c
@@ -121,10 +119,9 @@
         part = length // len(parts)
         for n, copy in enumerate(parts):
             copy.wait()
-            lax.fori_loop(n * part, (n + 1) * part, clean_channel, 0, unroll=8)
+            lax.fori_loop(n * part, (n + 1) * part, clean_channel, 0, unroll=4)
     for copy in copied["tables"]:
         copy.wait()
-    want = (odd == 1) if kind == "halo" else (odd == 0)
 
     def some_windows(step, _):
         for i in range(TOGETHER):
@@ -186,6 +183,7 @@
         pltpu.VMEM((ns // LANE, chans * (wins + 1), LANE), F32),
         pltpu.VMEM((TOGETHER * chans, ns), BF16),
         pltpu.VMEM((ns + half, TOGETHER * chans), BF16),
+        pltpu.VMEM((ns, ns), BF16),
         pltpu.VMEM((2, rows, chans), F32),
     ]
 
@@ -203,29 +201,31 @@
 
     copied["first"] = [copy(*pair) for pair in first]
     for source, target in x:
-        part = target.shape[0] // PIECES
+        parts = max(target.shape[0] // PART, 1)
+        part = target.shape[0] // parts
         copied["x"].append(
             [
                 copy(source.at[pl.ds(n * part, part)], target.at[pl.ds(n * part, part)])
-                for n in range(PIECES)
+                for n in range(parts)
             ]
         )
     copied["tables"] = [copy(*pair) for pair in tables_in]
     return copied
 
 
-def segments_kernel(kind, groups, count, odd_ref, flag_ref, *rest):
+def segments_kernel(places, wanted, groups, odd_ref, flag_ref, *rest):
+    count = len(places)
     tot_hbm, rest = rest[:groups], rest[groups:]
     x_hbm, rest = rest[:count], rest[count:]
-    hann_hbm, conv_hbm, seg_hbm, a_hbm, b_hbm = rest[:5]
+    hann_hbm, response_hbm, seg_hbm, a_hbm, b_hbm = rest[:5]
     tot, rest = rest[5 : 5 + groups], rest[5 + groups :]
     x, rest = rest[:count], rest[count:]
-    hann, conv, seg = rest[:3]
+    hann, response, seg = rest[:3]
     work, (a_out, b_out, in_sem, out_sem) = rest[3:-4], rest[-4:]
     copied = input_copies(
-        list(zip(tot_hbm, tot)) + [(hann_hbm, hann)],
+        list(zip(tot_hbm, tot)) + [(hann_hbm, hann), (response_hbm, response)],
         list(zip(x_hbm, x)),
-        [(conv_hbm, conv), (seg_hbm, seg)],
+        [(seg_hbm, seg)],
         in_sem,
     )
     bins = b_out.shape[0]
@@ -262,25 +262,26 @@
         for n in range(STEPS):
             send(STEPS + n, b_out, b_hbm).wait()
 
+    odd = odd_ref[0]
     segment_factors(
-        kind, odd_ref[0], flag_ref, tot, x, hann, conv, seg, work, copied, emit
-    )
-
-
-def segments(kind, odd, flags, totals, pieces, hann, conv, seg):
+        places, odd == wanted, odd, flag_ref, tot, x, hann, response, seg, work, copied, emit
+    )
+
+
+def segments(places, wanted, odd, flags, totals, pieces, hann, response, seg):
     chans = sum(x.shape[0] for x in pieces)
     _, wins, ns = pieces[0].shape
     size = seg.shape[0]
     half = size // 2
     depth = ns // half * wins * 2
-    kept = chans if kind == "halo" else chans // 2
+    kept = chans if wanted else chans // 2
     smem = pl.BlockSpec(memory_space=pltpu.SMEM)
     anywhere = pl.BlockSpec(memory_space=pl.ANY)
-    operands = list(totals) + list(pieces) + [hann, conv, seg]
+    operands = list(totals) + list(pieces) + [hann, response, seg]
     a_shape = jax.ShapeDtypeStruct((half, kept, depth), BF16)
     b_shape = jax.ShapeDtypeStruct((half, depth, chans), BF16)
     return pl.pallas_call(
-        functools.partial(segments_kernel, kind, len(totals), len(pieces)),
+        functools.partial(segments_kernel, places, wanted, len(totals)),
         out_shape=[a_shape, b_shape],
         in_specs=[smem] * 2 + [anywhere] * len(operands),
         out_specs=[anywhere] * 2,
@@ -289,7 +290,7 @@
         + [
             pltpu.VMEM(a_shape.shape, BF16),
             pltpu.VMEM(b_shape.shape, BF16),
-            pltpu.SemaphoreType.DMA((len(operands) + len(pieces) * PIECES,)),
+            pltpu.SemaphoreType.DMA((len(operands) + chans // PART,)),
             pltpu.SemaphoreType.DMA((2 * STEPS,)),
         ],
         compiler_params=pltpu.CompilerParams(vmem_limit_bytes=VMEM),
@@ -301,19 +302,22 @@
     )(odd, flags, *operands)
 
 
-def stack_kernel(scale, shares, me_ref, flag_ref, *rest):
-    tot_hbm, x0_hbm, x1_hbm, hann_hbm, conv_hbm, seg_hbm, lag_hbm = rest[:7]
-    left_hbm, rest = rest[7:11], rest[11:]
+def stack_kernel(places, scale, shares, me_ref, flag_ref, *rest):
+    count = len(places)
+    x_hbm, rest = rest[:count], rest[count:]
+    tot_hbm, hann_hbm, response_hbm, seg_hbm, lag_hbm = rest[:5]
+    left_hbm, rest = rest[5:9], rest[9:]
     outs, rest = rest[:shares], rest[shares:]
-    tot, x0, x1, hann, conv, seg, lag = rest[:7]
-    (a0, ah, b0, bh), rest = rest[7:11], rest[11:]
+    x, rest = rest[:count], rest[count:]
+    tot, hann, response, seg, lag = rest[:5]
+    (a0, ah, b0, bh), rest = rest[5:9], rest[9:]
     work, (a1, b1, one, in_sem, late_sem) = rest[:-5], rest[-5:]
     me = me_ref[0]
     odd = lax.rem(me, 2)
     copied = input_copies(
-        [(tot_hbm, tot), (hann_hbm, hann)],
-        [(x0_hbm, x0), (x1_hbm, x1)],
-        [(conv_hbm, conv), (seg_hbm, seg), (lag_hbm, lag)],
+        [(tot_hbm, tot), (hann_hbm, hann), (response_hbm, response)],
+        list(zip(x_hbm, x)),
+        [(seg_hbm, seg), (lag_hbm, lag)],
         in_sem,
     )
     late = [
@@ -344,7 +348,7 @@
         lax.fori_loop(0, bins, second, 0, unroll=8)
 
     segment_factors(
-        "other", odd, flag_ref, [tot], [x0, x1], hann, conv, seg, work, copied, emit
+        places, odd == 0, odd, flag_ref, [tot], x, hann, response, seg, work, copied, emit
     )
     for copy in late:
         copy.wait()
@@ -420,7 +424,7 @@
     lax.fori_loop(0, width, one_channel, 0, unroll=4)
 
 
-def stacks(shares, scale, me, flags, total, pieces, hann, conv, seg, lag, a0, ah, b0, bh):
+def stacks(places, shares, scale, me, flags, total, pieces, hann, response, seg, lag, a0, ah, b0, bh):
     bins, width, depth = a0.shape
     chans = b0.shape[2]
     _, wins, ns = pieces[0].shape
@@ -428,9 +432,9 @@
     smem = pl.BlockSpec(memory_space=pltpu.SMEM)
     vmem = pl.BlockSpec(memory_space=pltpu.VMEM)
     anywhere = pl.BlockSpec(memory_space=pl.ANY)
-    operands = [total, *pieces, hann, conv, seg, lag, a0, ah, b0, bh]
+    operands = [*pieces, total, hann, response, seg, lag, a0, ah, b0, bh]
     return pl.pallas_call(
-        functools.partial(stack_kernel, scale, shares),
+        functools.partial(stack_kernel, places, scale, shares),
         out_shape=[jax.ShapeDtypeStruct((width, OFFS // shares, nlag), BF16)] * shares,
         in_specs=[smem] * 2 + [anywhere] * len(operands),
         out_specs=[vmem] * shares,
@@ -440,7 +444,7 @@
             pltpu.VMEM(a0.shape, BF16),
             pltpu.VMEM(b0.shape, BF16),
             pltpu.VMEM((2, chans + width, chans), F32),
-            pltpu.SemaphoreType.DMA((8 + len(pieces) * PIECES,)),
+            pltpu.SemaphoreType.DMA((8 + chans // PART,)),
             pltpu.SemaphoreType.DMA((4,)),
         ],
         compiler_params=pltpu.CompilerParams(vmem_limit_bytes=VMEM),
@@ -477,11 +481,6 @@
     window, waves, seg, lag = [jnp.asarray(t) for t in tables(ns, nf)]
     hann = jnp.broadcast_to(window[None, :], (wins, ns))
     response = jnp.sum(band_gain[:, None] * waves, axis=0, keepdims=True)
-    conv = pl.pallas_call(
-        circulant_kernel,
-        out_shape=jax.ShapeDtypeStruct((ns, ns), BF16),
-        compiler_params=pltpu.CompilerParams(vmem_limit_bytes=VMEM),
-    )(response)
     swap = [(z, z ^ 1) for z in range(groups)]
     both = ("fibre", "tm")
     halo_pairs = [
@@ -490,8 +489,12 @@
         for z in range(groups)
     ]
 
-    first_half = lax.dynamic_slice_in_dim(samples, (1 - odd) * width, width, 0)
-    their_first = lax.ppermute(first_half, "tm", swap)
+    head = width * 5 // 8
+
+    def part_of(array, upper, start, length):
+        return lax.dynamic_slice_in_dim(array, upper * width + start, length, 0)
+
+    their_head = lax.ppermute(part_of(samples, 1 - odd, 0, head), "tm", swap)
     flags = jnp.stack([dead_flags, section_ids])
     halo_flags = lax.ppermute(
         lax.dynamic_slice_in_dim(flags, odd * width, width, 1), both, halo_pairs
@@ -507,29 +510,44 @@
         compiler_params=pltpu.CompilerParams(vmem_limit_bytes=VMEM),
     )(dead_flags, section_ids, samples)
     total = add_over(sums, "fibre")
-    total, halo_flags, kept = lax.optimization_barrier((total, halo_flags, samples))
+    total, halo_flags, kept, their_head, response = lax.optimization_barrier(
+        (total, halo_flags, samples, their_head, response)
+    )
     their_total = lax.ppermute(total, "tm", swap)
-    own_half = lax.dynamic_slice_in_dim(kept, odd * width, width, 0)
+    own_half = part_of(kept, odd, 0, width)
+    tail = part_of(kept, 1 - odd, head, width - head)
     halo = lax.ppermute(own_half, both, halo_pairs)
-    ready = (total, their_total, their_first, own_half, flags, hann, conv, seg, lag)
+    ready = (total, their_total, their_head, own_half, tail, flags, hann, response, seg, lag)
     ready = lax.optimization_barrier(ready)
-    total, their_total, their_first, own_half, flags, hann, conv, seg, lag = ready
-    their_halo = lax.ppermute(their_first, both, halo_pairs)
+    total, their_total, their_head, own_half, tail, flags, hann, response, seg, lag = ready
+    their_tail = lax.ppermute(tail, "tm", swap)
     their_second = lax.ppermute(own_half, "tm", swap)
+    halo_head = lax.ppermute(their_head, both, halo_pairs)
 
     side = odd[None]
-    parts = (hann, conv, seg)
-    a0, b0 = segments("own", side, flags, (total,), (samples,), *parts)
-    ah, bh = segments("halo", side, halo_flags, (total, their_total), (halo, their_halo), *parts)
+    parts = (hann, response, seg)
+    a0, b0 = segments(((0, 0, 0),), 0, side, flags, (total,), (samples,), *parts)
+    b0, forward = lax.optimization_barrier((b0, their_tail))
+    halo_tail = lax.ppermute(forward, both, halo_pairs)
+    ah, bh = segments(
+        ((0, 0, 0), (1, width, width), (1, width + head, width + head)),
+        1,
+        side,
+        halo_flags,
+        (total, their_total),
+        (halo, halo_head, halo_tail),
+        *parts,
+    )
     scale = 2.0 / ns / LAGS / math.sqrt(nf * wins * groups)
     found = stacks(
+        ((0, 0, width), (0, head, width + head), (0, width, 0)),
         groups,
         scale,
         me[None],
         flags,
         their_total,
-        (their_first, their_second),
-        *(hann, conv, seg, lag),
+        (their_head, their_tail, their_second),
+        *(hann, response, seg, lag),
         *(a0, ah, b0, bh),
     )
     arrived = []

time: 141 us -> 146 us (1.035)
  waiting for transfers between devices: 55.4 us -> 60.3 us
  local copies, waits for them, and re-layouts: 6.01 us -> 3.75 us
  Pallas kernels: 59 us -> 60.8 us
    ppermute x2 -> x4, waiting for transfers between devices: 0.01 us -> 15.7 us  [the longest x1 8.27 us: shards(): halo_tail = lax.ppermute(forward, both, halo_pairs)]
    ppermute x1, waiting for transfers between devices: 7.33 us -> 1.35 us  [shards(): their_total = lax.ppermute(total, 'tm', swap)]
    ppermute x4, waiting for transfers between devices: 47.1 us -> 41.6 us  [shards(): arrived.append(lax.ppermute(found[d], both, pairs).astype(F32))]
    unnamed x24 -> x20, local copies, waits for them, and re-layouts: 2.95 us -> 0.04 us
    ppermute x1, starting transfers between devices: 2.39 us -> 0.03 us  [shards(): their_second = lax.ppermute(own_half, 'tm', swap)]
    ppermute x2 -> x4, starting transfers between devices: 2.8 us -> 5.01 us  [the longest x1 2.45 us: shards(): their_head = lax.ppermute(part_of(samples, 1 - odd, 0, head), 'tm', swap)]
    ppermute x1, starting transfers between devices: 0.32 us -> 2.33 us  [shards(): their_total = lax.ppermute(total, 'tm', swap)]
    pallas_call x4 -> x3, Pallas kernels: 55.5 us -> 57.2 us  [the longest x1 29.2 us: stacks(): pl.pallas_call(functools.partial(stack_kernel, places, scale, shares), ou...]
  transfers between devices with their start and end apart: 14 -> 16, of which waited for: 5 -> 6; matrix products, arithmetic and copies ran while one was open for 4% -> 4% of each run, Pallas kernels for 22% -> 19%
where the time goes in v8:
time: 146 us; the launch traced here: 145 us
  Pallas kernels  60.8 us (42%)
  waiting for transfers between devices  60.3 us (41%)
  starting transfers between devices  14.8 us (10%)
  other arithmetic  5.13 us (4%)
  local copies, waits for them, and re-layouts  3.75 us (3%)
    ppermute x4, waiting for transfers between devices, shards(): arrived.append(lax.ppermute(found[d], both, pairs).astype(F32))  41.6 us
    pallas_call x1, Pallas kernels, stacks(): pl.pallas_call(functools.partial(stack_kernel, places, scale, shares), ou...  29.2 us
    pallas_call x2, Pallas kernels, segments(): pl.pallas_call(functools.partial(segments_kernel, places, wanted, len(tot...  28.1 us
    ppermute x1, waiting for transfers between devices, shards(): halo_tail = lax.ppermute(forward, both, halo_pairs)  8.27 us
    ppermute x1, waiting for transfers between devices, shards(): their_head = lax.ppermute(part_of(samples, 1 - odd, 0, head), 'tm', swap)  7.39 us
    pallas_call x1, Pallas kernels, shards(): pl.pallas_call(section_sums, grid=(steps,), out_shape=jax.ShapeDtypeStruc...  3.58 us
    ppermute x4, starting transfers between devices, shards(): arrived.append(lax.ppermute(found[d], both, pairs).astype(F32))  3.49 us
    ppermute x4, starting transfers between devices, add_over(): lax.ppermute(value, axis, [(i, i ^ s) for i in range(count)])  3.39 us
  transfers between devices with their start and end apart: 16, of which 6 were waited for; matrix products, arithmetic and copies ran while one was open for 4% of the time, Pallas kernels for 19%

profile of v8, /device:TPU:19, one launch (start us, length us, event | category | flops | bytes accessed | tf_op | source)
XLA Modules:
  0.0 145.0 jit_solution(4023407259329557860)
XLA Ops:
  0.0 3.6 %shard_map.82 = f32[2,8,1152]{2,1,0:T(8,128)} custom-call(s32[128]{0:T(128)} %dead_ref.1, s32[128]{0:T(128)} %sec_ref.1, bf16[128,8,1024]{2,1,0:T(8,128)(2,1)} %rest_1_.1), custom_call_target="tpu_custom_call" | custom-call | tf_op jit(solution)/shard_map/pallas_call | solution.py:504
  3.6 0.7 collective-permute-start
  4.4 1.1 constant_dynamic-slice_fusion.2
  5.5 2.5 %collective-permute-start.5 = (bf16[40,8,1024]{2,1,0:T(8,128)(2,1)S(1)}, bf16[40,8,1024]{2,1,0:T(8,128)(2,1)S(1)}, u32[]{:S(2)}, u32[]{:S(2)}) collective-permute-start(bf16[40,8,1024]{2,1,0:T(8,128)(2,1)S(1)} %constant_dynamic-slice_fusion.2), channel_id=1, source_target_pairs={{0,1},{1,0},{2,3},{3,2},{4,5},{5,4},{6,7},{7,6},{8,9},{9,8},{10,11... | collective-permute-start | bytes 1966088 | tf_op jit(solution)/shard_map/ppermute | solution.py:497
  8.0 0.9 add.38
  8.9 1.3 collective-permute-start.3
  10.4 1.2 collective-permute-start.1
  11.6 2.4 %multiply_reduce_fusion = f32[1024]{0:T(1024)} fusion(f32[512,1024]{1,0:T(8,128)} %constant.38.clone, f32[512]{0:T(512)S(1)} %copy-done.6), kind=kLoop, calls=%fused_computation.1 | loop fusion | flops 1047552 | bytes 2103296 | tf_op jit(solution)/shard_map/reduce_sum | solution.py:483
  14.0 1.7 %collective-permute-done.2 = f32[2,8,1152]{2,1,0:T(8,128)S(1)} collective-permute-done((f32[2,8,1152]{2,1,0:T(8,128)S(1)}, f32[2,8,1152]{2,1,0:T(8,128)S(1)}, u32[]{:S(2)}, u32[]{:S(2)}) %collective-permute-start.2) | collective-permute-done | bytes 73760 | tf_op jit(solution)/shard_map/ppermute | solution.py:467
  15.7 7.4 %collective-permute-done.5.rest_0_ = bf16[40,8,1024]{2,1,0:T(8,128)(2,1)S(1)} collective-permute-done((bf16[40,8,1024]{2,1,0:T(8,128)(2,1)S(1)}, bf16[40,8,1024]{2,1,0:T(8,128)(2,1)S(1)}, u32[]{:S(2)}, u32[]{:S(2)}) %collective-permute-start.5) | collective-permute-done | bytes 655392 | tf_op jit(solution)/shard_map/ppermute | solution.py:497
  23.1 1.1 constant_dynamic-slice_fusion.1
  24.8 2.3 %collective-permute-start.6 = (f32[2,8,1152]{2,1,0:T(8,128)S(1)}, f32[2,8,1152]{2,1,0:T(8,128)S(1)}, u32[]{:S(2)}, u32[]{:S(2)}) collective-permute-start(f32[2,8,1152]{2,1,0:T(8,128)S(1)} %add_add_fusion.rest_0_), channel_id=1, source_target_pairs={{0,1},{1,0},{2,3},{3,2},{4,5},{5,4},{6,7},{7,6},{8,9},{9,8},{10,11... | collective-permute-start | bytes 221192 | tf_op jit(solution)/shard_map/ppermute | solution.py:516
  27.1 0.8 constant_dynamic-slice_fusion
  27.9 1.4 collective-permute-done.6.rest_1_.rest_3_
  29.3 1.7 %collective-permute-start.7 = (bf16[24,8,1024]{2,1,0:T(8,128)(2,1)}, bf16[24,8,1024]{2,1,0:T(8,128)(2,1)}, u32[]{:S(2)}, u32[]{:S(2)}) collective-permute-start(bf16[24,8,1024]{2,1,0:T(8,128)(2,1)} %constant_dynamic-slice_fusion), channel_id=1, source_target_pairs={{0,1},{1,0},{2,3},{3,2},{4,5},{5,4},{6,7},{7,6},{8,9},{9,8},{10,11... | collective-permute-start | bytes 1179656 | tf_op jit(solution)/shard_map/ppermute | solution.py:523
  32.3 15.5 %shard_map.83 = (bf16[128,64,128]{2,1,0:T(8,128)(2,1)}, bf16[128,128,128]{2,1,0:T(8,128)(2,1)}) custom-call(s32[1]{0:T(128)} %bitcast.4.odd_ref, s32[2,128]{1,0:T(2,128)} %copy-done.4, f32[2,8,1152]{2,1,0:T(8,128)} %copy-done.3, bf16[128,8,1024]{2,1,0:T(8,128)(2,1)} %rest_1_.1, f32[8,1024]{1,0:T(8,128)} %broadcast_in_dim.18.rest_2_.rest_5_.rest_4_, ...), custom_call_target="tpu_custom_call" | custom-call | flops 3758096384 | bytes 16777216 | tf_op jit(solution)/shard_map/pallas_call | solution.py:283
  48.1 8.3 %collective-permute-done.11.rest_4_ = bf16[24,8,1024]{2,1,0:T(8,128)(2,1)} collective-permute-done((bf16[24,8,1024]{2,1,0:T(8,128)(2,1)}, bf16[24,8,1024]{2,1,0:T(8,128)(2,1)}, u32[]{:S(2)}, u32[]{:S(2)}) %collective-permute-start.11) | collective-permute-done | bytes 393248 | tf_op jit(solution)/shard_map/ppermute | solution.py:531
  56.3 12.5 %shard_map.84 = (bf16[128,128,128]{2,1,0:T(8,128)(2,1)}, bf16[128,128,128]{2,1,0:T(8,128)(2,1)}) custom-call(s32[1]{0:T(128)} %bitcast.4.odd_ref, s32[2,64]{1,0:T(2,128)} %copy-done.9, f32[2,8,1152]{2,1,0:T(8,128)} %copy-done.3, f32[2,8,1152]{2,1,0:T(8,128)} %copy-done.2, bf16[64,8,1024]{2,1,0:T(8,128)(2,1)} %collective-permute-done.9.rest_2_, ...), custom_call_target="tpu_custom_call" | custom-call | flops 3758096384 | bytes 16777216 | tf_op jit(solution)/shard_map/pallas_call | solution.py:283
  68.9 29.2 %shard_map.85 = (bf16[64,32,128]{2,1,0:T(8,128)(2,1)}, bf16[64,32,128]{2,1,0:T(8,128)(2,1)}, bf16[64,32,128]{2,1,0:T(8,128)(2,1)}, bf16[64,32,128]{2,1,0:T(8,128)(2,1)}) custom-call(s32[1]{0:T(128)} %bitcast.me_ref, s32[2,128]{1,0:T(2,128)} %copy-done.4, bf16[40,8,1024]{2,1,0:T(8,128)(2,1)} %copy-done.1, ...), custom_call_target="tpu_custom_call" | custom-call | flops 4294967296 | bytes 20971520 | tf_op jit(solution)/shard_map/pallas_call | solution.py:436
  98.1 1.7 %collective-permute-start.12 = (bf16[64,32,128]{2,1,0:T(8,128)(2,1)}, bf16[64,32,128]{2,1,0:T(8,128)(2,1)S(1)}, u32[]{:S(2)}, u32[]{:S(2)}) collective-permute-start(bf16[64,32,128]{2,1,0:T(8,128)(2,1)} %get-tuple-element.51), channel_id=1, source_target_pairs={{0,0},{1,29},{2,2},{3,31},{4,4},{5,1},{6,6},{7,3},{8,8},{9,5},{10,... | collective-permute-start | bytes 1572872 | tf_op jit(solution)/shard_map/ppermute | solution.py:560
  99.8 1.7 %collective-permute-start.14 = (bf16[64,32,128]{2,1,0:T(8,128)(2,1)}, bf16[64,32,128]{2,1,0:T(8,128)(2,1)S(1)}, u32[]{:S(2)}, u32[]{:S(2)}) collective-permute-start(bf16[64,32,128]{2,1,0:T(8,128)(2,1)} %get-tuple-element.53), channel_id=1, source_target_pairs={{0,1},{1,28},{2,3},{3,30},{4,5},{5,0},{6,7},{7,2},{8,9},{9,4},{10,... | collective-permute-start | bytes 1572872 | tf_op jit(solution)/shard_map/ppermute | solution.py:560
  101.6 28.2 %collective-permute-done.13 = bf16[64,32,128]{2,1,0:T(8,128)(2,1)S(1)} collective-permute-done((bf16[64,32,128]{2,1,0:T(8,128)(2,1)}, bf16[64,32,128]{2,1,0:T(8,128)(2,1)S(1)}, u32[]{:S(2)}, u32[]{:S(2)}) %collective-permute-start.13) | collective-permute-done | bytes 524320 | tf_op jit(solution)/shard_map/ppermute | solution.py:560
  129.8 13.4 %collective-permute-done.15 = bf16[64,32,128]{2,1,0:T(8,128)(2,1)S(1)} collective-permute-done((bf16[64,32,128]{2,1,0:T(8,128)(2,1)}, bf16[64,32,128]{2,1,0:T(8,128)(2,1)S(1)}, u32[]{:S(2)}, u32[]{:S(2)}) %collective-permute-start.15) | collective-permute-done | bytes 524320 | tf_op jit(solution)/shard_map/ppermute | solution.py:560
  143.5 1.5 %pad_maximum_fusion = f32[128,32,128]{2,1,0:T(8,128)} fusion(f32[64,32,128]{2,1,0:T(8,128)S(1)} %get-tuple-element.56, f32[64,32,128]{2,1,0:T(8,128)S(1)} %get-tuple-element.55), kind=kLoop, calls=%fused_computation | loop fusion | flops 524288 | bytes 4194304 | tf_op jit(solution)/shard_map/concatenate | solution.py:563
  (43 shorter events, 2.8 us)
Async XLA Ops:
  0.0 11.6 %copy-start.6 = (f32[512]{0:T(512)S(1)}, f32[512]{0:T(512)}, u32[]{:S(2)}) copy-start(f32[512]{0:T(512)} %param.9) | copy-start | bytes 6148
  3.6 19.5 %copy-start = (bf16[128,8,1024]{2,1,0:T(8,128)(2,1)S(1)}, bf16[128,8,1024]{2,1,0:T(8,128)(2,1)}, u32[]{:S(2)}) copy-start(bf16[128,8,1024]{2,1,0:T(8,128)(2,1)} %rest_1_.1) | copy-start | bytes 6291460
  3.6 4.4 %collective-permute-start = (f32[2,8,1152]{2,1,0:T(8,128)}, f32[2,8,1152]{2,1,0:T(8,128)S(1)}, u32[]{:S(2)}, u32[]{:S(2)}) collective-permute-start(f32[2,8,1152]{2,1,0:T(8,128)} %shard_map.82), channel_id=1, source_target_pairs={{0,4},{4,0},{8,12},{12,8},{16,20},{20,16},{24,28},{28,24},{1,5},{5... | collective-permute-start | bytes 221192 | tf_op jit(solution)/shard_map/ppermute | solution.py:467
  4.3 20.0 %copy-start.4 = (s32[2,128]{1,0:T(2,128)}, s32[2,128]{1,0:T(2,128)S(1)}, u32[]{:S(2)}) copy-start(s32[2,128]{1,0:T(2,128)S(1)} %pad_add_fusion.flag_ref) | copy-start | bytes 3076
  4.4 11.3 %collective-permute-start.4 = (s32[2,64]{1,0:T(2,128)S(1)}, s32[2,64]{1,0:T(2,128)S(1)}, u32[]{:S(2)}, u32[]{:S(2)}) collective-permute-start(s32[2,64]{1,0:T(2,128)S(1)} %constant_dynamic-slice_fusion.3), channel_id=1, source_target_pairs={{0,28},{1,5},{2,30},{3,7},{4,0},{5,9},{6,2},{7,11},{8,4},{9,13},{1... | collective-permute-start | bytes 1544 | tf_op jit(solution)/shard_map/ppermute | solution.py:499
  5.5 17.6 %collective-permute-start.5 = (bf16[40,8,1024]{2,1,0:T(8,128)(2,1)S(1)}, bf16[40,8,1024]{2,1,0:T(8,128)(2,1)S(1)}, u32[]{:S(2)}, u32[]{:S(2)}) collective-permute-start(bf16[40,8,1024]{2,1,0:T(8,128)(2,1)S(1)} %constant_dynamic-slice_fusion.2), channel_id=1, source_target_pairs={{0,1},{1,0},{2,3},{3,2},{4,5},{5,4},{6,7},{7,6},{8,9},{9,8},{10,11... | collective-permute-start | bytes 1966088 | tf_op jit(solution)/shard_map/ppermute | solution.py:497
  8.9 5.1 %collective-permute-start.3 = (f32[2,8,1152]{2,1,0:T(8,128)S(1)}, f32[2,8,1152]{2,1,0:T(8,128)S(1)}, u32[]{:S(2)}, u32[]{:S(2)}) collective-permute-start(f32[2,8,1152]{2,1,0:T(8,128)S(1)} %add.38), channel_id=1, source_target_pairs={{0,24},{4,28},{8,16},{12,20},{16,8},{20,12},{24,0},{28,4},{1,25},{... | collective-permute-start | bytes 221192 | tf_op jit(solution)/shard_map/ppermute | solution.py:467
  10.2 5.5 %collective-permute-start.2 = (f32[2,8,1152]{2,1,0:T(8,128)S(1)}, f32[2,8,1152]{2,1,0:T(8,128)S(1)}, u32[]{:S(2)}, u32[]{:S(2)}) collective-permute-start(f32[2,8,1152]{2,1,0:T(8,128)S(1)} %add.38), channel_id=1, source_target_pairs={{0,16},{4,20},{8,24},{12,28},{16,0},{20,4},{24,8},{28,12},{1,17},{... | collective-permute-start | bytes 221192 | tf_op jit(solution)/shard_map/ppermute | solution.py:467
  10.4 5.3 %collective-permute-start.1 = (f32[2,8,1152]{2,1,0:T(8,128)S(1)}, f32[2,8,1152]{2,1,0:T(8,128)S(1)}, u32[]{:S(2)}, u32[]{:S(2)}) collective-permute-start(f32[2,8,1152]{2,1,0:T(8,128)S(1)} %add.38), channel_id=1, source_target_pairs={{0,8},{4,12},{8,0},{12,4},{16,24},{20,28},{24,16},{28,20},{1,9},{5... | collective-permute-start | bytes 221192 | tf_op jit(solution)/shard_map/ppermute | solution.py:467
  14.0 17.7 %copy-start.5 = (f32[1024]{0:T(1024)S(1)}, f32[1024]{0:T(1024)}, u32[]{:S(2)}) copy-start(f32[1024]{0:T(1024)} %constant.37.clone) | copy-start | bytes 12292
  15.7 16.6 %copy-start.3 = (f32[2,8,1152]{2,1,0:T(8,128)}, f32[2,8,1152]{2,1,0:T(8,128)S(1)}, u32[]{:S(2)}) copy-start(f32[2,8,1152]{2,1,0:T(8,128)S(1)} %add_add_fusion.rest_0_) | copy-start | bytes 221188
  15.7 32.1 %copy-start.9 = (s32[2,64]{1,0:T(2,128)}, s32[2,64]{1,0:T(2,128)S(1)}, u32[]{:S(2)}) copy-start(s32[2,64]{1,0:T(2,128)S(1)} %collective-permute-done.4.flag_ref) | copy-start | bytes 1540
  23.1 24.7 %copy-start.1 = (bf16[40,8,1024]{2,1,0:T(8,128)(2,1)}, bf16[40,8,1024]{2,1,0:T(8,128)(2,1)S(1)}, u32[]{:S(2)}) copy-start(bf16[40,8,1024]{2,1,0:T(8,128)(2,1)S(1)} %collective-permute-done.5.rest_0_) | copy-start | bytes 1966084
  24.2 32.1 %collective-permute-start.9 = (bf16[64,8,1024]{2,1,0:T(8,128)(2,1)}, bf16[64,8,1024]{2,1,0:T(8,128)(2,1)}, u32[]{:S(2)}, u32[]{:S(2)}) collective-permute-start(bf16[64,8,1024]{2,1,0:T(8,128)(2,1)} %constant_dynamic-slice_fusion.1), channel_id=1, source_target_pairs={{0,28},{1,5},{2,30},{3,7},{4,0},{5,9},{6,2},{7,11},{8,4},{9,13},{1... | collective-permute-start | bytes 3145736 | tf_op jit(solution)/shard_map/ppermute | solution.py:519
  24.8 4.5 %collective-permute-start.6 = (f32[2,8,1152]{2,1,0:T(8,128)S(1)}, f32[2,8,1152]{2,1,0:T(8,128)S(1)}, u32[]{:S(2)}, u32[]{:S(2)}) collective-permute-start(f32[2,8,1152]{2,1,0:T(8,128)S(1)} %add_add_fusion.rest_0_), channel_id=1, source_target_pairs={{0,1},{1,0},{2,3},{3,2},{4,5},{5,4},{6,7},{7,6},{8,9},{9,8},{10,11... | collective-permute-start | bytes 221192 | tf_op jit(solution)/shard_map/ppermute | solution.py:516
  29.3 18.6 %copy-start.2 = (f32[2,8,1152]{2,1,0:T(8,128)}, f32[2,8,1152]{2,1,0:T(8,128)S(1)}, u32[]{:S(2)}) copy-start(f32[2,8,1152]{2,1,0:T(8,128)S(1)} %collective-permute-done.6.rest_1_.rest_3_) | copy-start | bytes 221188
  29.3 18.6 %collective-permute-start.7 = (bf16[24,8,1024]{2,1,0:T(8,128)(2,1)}, bf16[24,8,1024]{2,1,0:T(8,128)(2,1)}, u32[]{:S(2)}, u32[]{:S(2)}) collective-permute-start(bf16[24,8,1024]{2,1,0:T(8,128)(2,1)} %constant_dynamic-slice_fusion), channel_id=1, source_target_pairs={{0,1},{1,0},{2,3},{3,2},{4,5},{5,4},{6,7},{7,6},{8,9},{9,8},{10,11... | collective-permute-start | bytes 1179656 | tf_op jit(solution)/shard_map/ppermute | solution.py:523
  31.0 37.9 %collective-permute-start.8 = (bf16[64,8,1024]{2,1,0:T(8,128)(2,1)}, bf16[64,8,1024]{2,1,0:T(8,128)(2,1)}, u32[]{:S(2)}, u32[]{:S(2)}) collective-permute-start(bf16[64,8,1024]{2,1,0:T(8,128)(2,1)} %constant_dynamic-slice_fusion.1), channel_id=1, source_target_pairs={{0,1},{1,0},{2,3},{3,2},{4,5},{5,4},{6,7},{7,6},{8,9},{9,8},{10,11... | collective-permute-start | bytes 3145736 | tf_op jit(solution)/shard_map/ppermute | solution.py:524
  31.0 17.0 %collective-permute-start.10 = (bf16[40,8,1024]{2,1,0:T(8,128)(2,1)S(1)}, bf16[40,8,1024]{2,1,0:T(8,128)(2,1)}, u32[]{:S(2)}, u32[]{:S(2)}) collective-permute-start(bf16[40,8,1024]{2,1,0:T(8,128)(2,1)S(1)} %collective-permute-done.5.rest_0_), channel_id=1, source_target_pairs={{0,28},{1,5},{2,30},{3,7},{4,0},{5,9},{6,2},{7,11},{8,4},{9,13},{1... | collective-permute-start | bytes 1966088 | tf_op jit(solution)/shard_map/ppermute | solution.py:525
  47.9 8.5 %collective-permute-start.11 = (bf16[24,8,1024]{2,1,0:T(8,128)(2,1)}, bf16[24,8,1024]{2,1,0:T(8,128)(2,1)}, u32[]{:S(2)}, u32[]{:S(2)}) collective-permute-start(bf16[24,8,1024]{2,1,0:T(8,128)(2,1)} %collective-permute-done.7.rest_1_), channel_id=1, source_target_pairs={{0,28},{1,5},{2,30},{3,7},{4,0},{5,9},{6,2},{7,11},{8,4},{9,13},{1... | collective-permute-start | bytes 1179656 | tf_op jit(solution)/shard_map/ppermute | solution.py:531
  98.1 31.7 %collective-permute-start.13 = (bf16[64,32,128]{2,1,0:T(8,128)(2,1)}, bf16[64,32,128]{2,1,0:T(8,128)(2,1)S(1)}, u32[]{:S(2)}, u32[]{:S(2)}) collective-permute-start(bf16[64,32,128]{2,1,0:T(8,128)(2,1)} %get-tuple-element.52), channel_id=1, source_target_pairs={{0,2},{1,31},{2,0},{3,29},{4,6},{5,3},{6,4},{7,1},{8,10},{9,7},{10... | collective-permute-start | bytes 1572872 | tf_op jit(solution)/shard_map/ppermute | solution.py:560
  98.1 31.6 %collective-permute-start.12 = (bf16[64,32,128]{2,1,0:T(8,128)(2,1)}, bf16[64,32,128]{2,1,0:T(8,128)(2,1)S(1)}, u32[]{:S(2)}, u32[]{:S(2)}) collective-permute-start(bf16[64,32,128]{2,1,0:T(8,128)(2,1)} %get-tuple-element.51), channel_id=1, source_target_pairs={{0,0},{1,29},{2,2},{3,31},{4,4},{5,1},{6,6},{7,3},{8,8},{9,5},{10,... | collective-permute-start | bytes 1572872 | tf_op jit(solution)/shard_map/ppermute | solution.py:560
  99.8 43.3 %collective-permute-start.15 = (bf16[64,32,128]{2,1,0:T(8,128)(2,1)}, bf16[64,32,128]{2,1,0:T(8,128)(2,1)S(1)}, u32[]{:S(2)}, u32[]{:S(2)}) collective-permute-start(bf16[64,32,128]{2,1,0:T(8,128)(2,1)} %get-tuple-element.54), channel_id=1, source_target_pairs={{0,3},{1,30},{2,1},{3,28},{4,7},{5,2},{6,5},{7,0},{8,11},{9,6},{10... | collective-permute-start | bytes 1572872 | tf_op jit(solution)/shard_map/ppermute | solution.py:560
  99.8 43.3 %collective-permute-start.14 = (bf16[64,32,128]{2,1,0:T(8,128)(2,1)}, bf16[64,32,128]{2,1,0:T(8,128)(2,1)S(1)}, u32[]{:S(2)}, u32[]{:S(2)}) collective-permute-start(bf16[64,32,128]{2,1,0:T(8,128)(2,1)} %get-tuple-element.53), channel_id=1, source_target_pairs={{0,1},{1,28},{2,3},{3,30},{4,5},{5,0},{6,7},{7,2},{8,9},{9,4},{10,... | collective-permute-start | bytes 1572872 | tf_op jit(solution)/shard_map/ppermute | solution.py:560
  (2 other events, 8.5 us)

commit v9 on v8

--- a/solution.py
+++ b/solution.py
@@ -66,16 +66,15 @@
         out_ref[s, :, ns:] += jnp.zeros((wins, LANE), F32) + counts[s]
 
 
-def circulant(filter_ref, out_ref):
+def circulant_kernel(filter_ref, out_ref):
     ns = filter_ref.shape[1]
-
     for t in range(0, ns, 16):
         block = jnp.broadcast_to(filter_ref[...], (16, ns))
         out_ref[t : t + 16, :] = pltpu.roll(block, t, 1, stride=1, stride_axis=0).astype(BF16)
 
 
-def segment_factors(places, want, odd, flag_ref, tot, x, hann, response, seg, work, copied, emit):
-    common, clean, rows, series, conv, stage = work
+def segment_factors(places, want, odd, flag_ref, tot, x, hann, conv, seg, work, copied, emit):
+    common, clean, rows, series, stage = work
     _, wins, ns = x[0].shape
     chans = sum(piece.shape[0] for piece in x)
     pitch = wins + 1
@@ -87,7 +86,6 @@
     held = flag_ref.shape[1]
     for copy in copied["first"]:
         copy.wait()
-    circulant(response, conv)
     for g in range(len(tot)):
         for s in range(NSEC):
             common[g * NSEC + s] = tot[g][s, :, :ns] / jnp.maximum(tot[g][s, :, ns : ns + 1], 1.0)
@@ -183,7 +181,6 @@
         pltpu.VMEM((ns // LANE, chans * (wins + 1), LANE), F32),
         pltpu.VMEM((TOGETHER * chans, ns), BF16),
         pltpu.VMEM((ns + half, TOGETHER * chans), BF16),
-        pltpu.VMEM((ns, ns), BF16),
         pltpu.VMEM((2, rows, chans), F32),
     ]
 
@@ -217,15 +214,15 @@
     count = len(places)
     tot_hbm, rest = rest[:groups], rest[groups:]
     x_hbm, rest = rest[:count], rest[count:]
-    hann_hbm, response_hbm, seg_hbm, a_hbm, b_hbm = rest[:5]
+    hann_hbm, conv_hbm, seg_hbm, a_hbm, b_hbm = rest[:5]
     tot, rest = rest[5 : 5 + groups], rest[5 + groups :]
     x, rest = rest[:count], rest[count:]
-    hann, response, seg = rest[:3]
+    hann, conv, seg = rest[:3]
     work, (a_out, b_out, in_sem, out_sem) = rest[3:-4], rest[-4:]
     copied = input_copies(
-        list(zip(tot_hbm, tot)) + [(hann_hbm, hann), (response_hbm, response)],
+        list(zip(tot_hbm, tot)) + [(hann_hbm, hann)],
         list(zip(x_hbm, x)),
-        [(seg_hbm, seg)],
+        [(conv_hbm, conv), (seg_hbm, seg)],
         in_sem,
     )
     bins = b_out.shape[0]
@@ -264,11 +261,11 @@
 
     odd = odd_ref[0]
     segment_factors(
-        places, odd == wanted, odd, flag_ref, tot, x, hann, response, seg, work, copied, emit
-    )
-
-
-def segments(places, wanted, odd, flags, totals, pieces, hann, response, seg):
+        places, odd == wanted, odd, flag_ref, tot, x, hann, conv, seg, work, copied, emit
+    )
+
+
+def segments(places, wanted, odd, flags, totals, pieces, hann, conv, seg):
     chans = sum(x.shape[0] for x in pieces)
     _, wins, ns = pieces[0].shape
     size = seg.shape[0]
@@ -277,7 +274,7 @@
     kept = chans if wanted else chans // 2
     smem = pl.BlockSpec(memory_space=pltpu.SMEM)
     anywhere = pl.BlockSpec(memory_space=pl.ANY)
-    operands = list(totals) + list(pieces) + [hann, response, seg]
+    operands = list(totals) + list(pieces) + [hann, conv, seg]
     a_shape = jax.ShapeDtypeStruct((half, kept, depth), BF16)
     b_shape = jax.ShapeDtypeStruct((half, depth, chans), BF16)
     return pl.pallas_call(
@@ -305,19 +302,19 @@
 def stack_kernel(places, scale, shares, me_ref, flag_ref, *rest):
     count = len(places)
     x_hbm, rest = rest[:count], rest[count:]
-    tot_hbm, hann_hbm, response_hbm, seg_hbm, lag_hbm = rest[:5]
+    tot_hbm, hann_hbm, conv_hbm, seg_hbm, lag_hbm = rest[:5]
     left_hbm, rest = rest[5:9], rest[9:]
     outs, rest = rest[:shares], rest[shares:]
     x, rest = rest[:count], rest[count:]
-    tot, hann, response, seg, lag = rest[:5]
+    tot, hann, conv, seg, lag = rest[:5]
     (a0, ah, b0, bh), rest = rest[5:9], rest[9:]
     work, (a1, b1, one, in_sem, late_sem) = rest[:-5], rest[-5:]
     me = me_ref[0]
     odd = lax.rem(me, 2)
     copied = input_copies(
-        [(tot_hbm, tot), (hann_hbm, hann), (response_hbm, response)],
+        [(tot_hbm, tot), (hann_hbm, hann)],
         list(zip(x_hbm, x)),
-        [(seg_hbm, seg), (lag_hbm, lag)],
+        [(conv_hbm, conv), (seg_hbm, seg), (lag_hbm, lag)],
         in_sem,
     )
     late = [
@@ -348,7 +345,7 @@
         lax.fori_loop(0, bins, second, 0, unroll=8)
 
     segment_factors(
-        places, odd == 0, odd, flag_ref, [tot], x, hann, response, seg, work, copied, emit
+        places, odd == 0, odd, flag_ref, [tot], x, hann, conv, seg, work, copied, emit
     )
     for copy in late:
         copy.wait()
@@ -424,7 +421,7 @@
     lax.fori_loop(0, width, one_channel, 0, unroll=4)
 
 
-def stacks(places, shares, scale, me, flags, total, pieces, hann, response, seg, lag, a0, ah, b0, bh):
+def stacks(places, shares, scale, me, flags, total, pieces, hann, conv, seg, lag, a0, ah, b0, bh):
     bins, width, depth = a0.shape
     chans = b0.shape[2]
     _, wins, ns = pieces[0].shape
@@ -432,7 +429,7 @@
     smem = pl.BlockSpec(memory_space=pltpu.SMEM)
     vmem = pl.BlockSpec(memory_space=pltpu.VMEM)
     anywhere = pl.BlockSpec(memory_space=pl.ANY)
-    operands = [*pieces, total, hann, response, seg, lag, a0, ah, b0, bh]
+    operands = [*pieces, total, hann, conv, seg, lag, a0, ah, b0, bh]
     return pl.pallas_call(
         functools.partial(stack_kernel, places, scale, shares),
         out_shape=[jax.ShapeDtypeStruct((width, OFFS // shares, nlag), BF16)] * shares,
@@ -456,18 +453,19 @@
     )(me, flags, *operands)
 
 
-def add_over(value, axis):
+def add_over(value, axis, beside):
     count = lax.axis_size(axis)
     if count & (count - 1):
-        return lax.psum(value, axis)
+        return lax.psum(value, axis), beside
     bit = 1
     while bit < count:
         steps = [bit] if bit == 1 or 2 * bit == count else [bit, 2 * bit, 3 * bit]
-        value = sum(
-            [lax.ppermute(value, axis, [(i, i ^ s) for i in range(count)]) for s in steps], value
-        )
+        arrived = [lax.ppermute(value, axis, [(i, i ^ s) for i in range(count)]) for s in steps]
         bit *= 1 + len(steps)
-    return value
+        if bit == count:
+            arrived, beside = lax.optimization_barrier((arrived, beside))
+        value = sum(arrived, value)
+    return value, beside
 
 
 def shards(samples, band_gain, dead_flags, section_ids):
@@ -481,6 +479,12 @@
     window, waves, seg, lag = [jnp.asarray(t) for t in tables(ns, nf)]
     hann = jnp.broadcast_to(window[None, :], (wins, ns))
     response = jnp.sum(band_gain[:, None] * waves, axis=0, keepdims=True)
+    conv = pl.pallas_call(
+        circulant_kernel,
+        out_shape=jax.ShapeDtypeStruct((ns, ns), BF16),
+        compiler_params=pltpu.CompilerParams(vmem_limit_bytes=VMEM),
+        cost_estimate=pl.CostEstimate(flops=1, bytes_accessed=1, transcendentals=0),
+    )(response)
     swap = [(z, z ^ 1) for z in range(groups)]
     both = ("fibre", "tm")
     halo_pairs = [
@@ -508,24 +512,25 @@
         in_specs=[smem, smem, pl.BlockSpec((chans // steps, wins, ns), lambda i: (i, 0, 0))],
         out_specs=pl.BlockSpec((NSEC, wins, ns + LANE), lambda i: (0, 0, 0)),
         compiler_params=pltpu.CompilerParams(vmem_limit_bytes=VMEM),
+        cost_estimate=pl.CostEstimate(flops=1, bytes_accessed=1, transcendentals=0),
     )(dead_flags, section_ids, samples)
-    total = add_over(sums, "fibre")
-    total, halo_flags, kept, their_head, response = lax.optimization_barrier(
-        (total, halo_flags, samples, their_head, response)
+    total, their_head = add_over(sums, "fibre", their_head)
+    total, halo_flags, kept, conv = lax.optimization_barrier(
+        (total, halo_flags, samples, conv)
     )
     their_total = lax.ppermute(total, "tm", swap)
     own_half = part_of(kept, odd, 0, width)
     tail = part_of(kept, 1 - odd, head, width - head)
     halo = lax.ppermute(own_half, both, halo_pairs)
-    ready = (total, their_total, their_head, own_half, tail, flags, hann, response, seg, lag)
+    ready = (total, their_total, their_head, own_half, tail, flags, hann, conv, seg, lag)
     ready = lax.optimization_barrier(ready)
-    total, their_total, their_head, own_half, tail, flags, hann, response, seg, lag = ready
+    total, their_total, their_head, own_half, tail, flags, hann, conv, seg, lag = ready
     their_tail = lax.ppermute(tail, "tm", swap)
     their_second = lax.ppermute(own_half, "tm", swap)
     halo_head = lax.ppermute(their_head, both, halo_pairs)
 
     side = odd[None]
-    parts = (hann, response, seg)
+    parts = (hann, conv, seg)
     a0, b0 = segments(((0, 0, 0),), 0, side, flags, (total,), (samples,), *parts)
     b0, forward = lax.optimization_barrier((b0, their_tail))
     halo_tail = lax.ppermute(forward, both, halo_pairs)
@@ -547,7 +552,7 @@
         flags,
         their_total,
         (their_head, their_tail, their_second),
-        *(hann, response, seg, lag),
+        *(hann, conv, seg, lag),
         *(a0, ah, b0, bh),
     )
     arrived = []

time: 146 us -> 141 us (0.966)
  waiting for transfers between devices: 60.3 us -> 51.2 us
  local copies, waits for them, and re-layouts: 3.75 us -> 5.91 us
    ppermute x1, waiting for transfers between devices: 7.39 us -> 0.16 us  [shards(): their_head = lax.ppermute(part_of(samples, 1 - odd, 0, head), 'tm', swap)]
    pallas_call x0 -> x1, Pallas kernels: none -> 2.6 us  [shards(): pl.pallas_call(circulant_kernel, out_shape=jax.ShapeDtypeStruct((ns, ns),...]
  transfers between devices with their start and end apart: 16 -> 16, of which waited for: 6 -> 6; matrix products, arithmetic and copies ran while one was open for 4% -> 4% of each run, Pallas kernels for 19% -> 24%
where the time goes in v9:
time: 141 us; the launch traced here: 140 us
  Pallas kernels  61.9 us (44%)
  waiting for transfers between devices  51.2 us (36%)
  starting transfers between devices  15.6 us (11%)
  local copies, waits for them, and re-layouts  5.91 us (4%)
  other arithmetic  5.12 us (4%)
    ppermute x4, waiting for transfers between devices, shards(): arrived.append(lax.ppermute(found[d], both, pairs).astype(F32))  40.9 us
    pallas_call x1, Pallas kernels, stacks(): pl.pallas_call(functools.partial(stack_kernel, places, scale, shares), ou...  28.7 us
    pallas_call x2, Pallas kernels, segments(): pl.pallas_call(functools.partial(segments_kernel, places, wanted, len(tot...  27.1 us
    ppermute x1, waiting for transfers between devices, shards(): halo_tail = lax.ppermute(forward, both, halo_pairs)  8.02 us
    dynamic_slice x3, local copies, waits for them, and re-layouts, part_of(): return lax.dynamic_slice_in_dim(array, upper * width + start, length, 0)  4.46 us
    ppermute x4, starting transfers between devices, shards(): arrived.append(lax.ppermute(found[d], both, pairs).astype(F32))  4.15 us
    ppermute x4, starting transfers between devices, add_over(): lax.ppermute(value, axis, [(i, i ^ s) for i in range(count)])  3.67 us
    pallas_call x1, Pallas kernels, shards(): pl.pallas_call(section_sums, grid=(steps,), out_shape=jax.ShapeDtypeStruc...  3.54 us
  transfers between devices with their start and end apart: 16, of which 6 were waited for; matrix products, arithmetic and copies ran while one was open for 4% of the time, Pallas kernels for 24%

profile of v9, /device:TPU:19, one launch (start us, length us, event | category | flops | bytes accessed | tf_op | source)
XLA Modules:
  0.0 139.9 jit_solution(3891210197767913281)
XLA Ops:
  0.0 1.1 constant_dynamic-slice_fusion.3
  1.2 1.4 collective-permute-start.4
  2.5 3.5 %shard_map.82 = f32[2,8,1152]{2,1,0:T(8,128)} custom-call(s32[128]{0:T(128)} %dead_ref.1, s32[128]{0:T(128)} %sec_ref.1, bf16[128,8,1024]{2,1,0:T(8,128)(2,1)} %rest_1_.1), custom_call_target="tpu_custom_call" | custom-call | flops 1 | bytes 1 | tf_op jit(solution)/shard_map/pallas_call | solution.py:508
  6.1 1.0 collective-permute-start
  7.2 1.0 collective-permute-done
  9.4 1.2 collective-permute-start.2
  10.6 1.2 collective-permute-start.3
  11.8 2.4 %multiply_reduce_fusion = f32[1024]{0:T(1024)} fusion(f32[512,1024]{1,0:T(8,128)} %constant.38.clone, f32[512]{0:T(512)S(1)} %copy-done.5), kind=kLoop, calls=%fused_computation.1 | loop fusion | flops 1047552 | bytes 2103296 | tf_op jit(solution)/shard_map/reduce_sum | solution.py:481
  14.2 2.6 %shard_map.83.rest_3_.rest_6_.rest_5_ = bf16[1024,1024]{1,0:T(8,128)(2,1)} custom-call(f32[1,1024]{1,0:T(1,128)} %bitcast.5), custom_call_target="tpu_custom_call" | custom-call | flops 1 | bytes 1 | tf_op jit(solution)/shard_map/pallas_call | solution.py:482
  17.0 2.3 %constant_dynamic-slice_fusion.1 = bf16[64,8,1024]{2,1,0:T(8,128)(2,1)} fusion(bf16[128,8,1024]{2,1,0:T(8,128)(2,1)} %rest_1_.1, s32[]{:T(128)S(6)} %select_n.32), kind=kLoop, calls=%fused_computation.9 | loop fusion | bytes 2097156 | tf_op jit(solution)/shard_map/dynamic_slice | solution.py:499
  19.3 1.5 %collective-permute-start.9 = (bf16[64,8,1024]{2,1,0:T(8,128)(2,1)}, bf16[64,8,1024]{2,1,0:T(8,128)(2,1)}, u32[]{:S(2)}, u32[]{:S(2)}) collective-permute-start(bf16[64,8,1024]{2,1,0:T(8,128)(2,1)} %constant_dynamic-slice_fusion.1), channel_id=1, source_target_pairs={{0,28},{1,5},{2,30},{3,7},{4,0},{5,9},{6,2},{7,11},{8,4},{9,13},{1... | collective-permute-start | bytes 3145736 | tf_op jit(solution)/shard_map/ppermute | solution.py:524
  20.8 2.4 %collective-permute-start.6 = (f32[2,8,1152]{2,1,0:T(8,128)S(1)}, f32[2,8,1152]{2,1,0:T(8,128)S(1)}, u32[]{:S(2)}, u32[]{:S(2)}) collective-permute-start(f32[2,8,1152]{2,1,0:T(8,128)S(1)} %add_add_fusion.rest_0_), channel_id=1, source_target_pairs={{0,1},{1,0},{2,3},{3,2},{4,5},{5,4},{6,7},{7,6},{8,9},{9,8},{10,11... | collective-permute-start | bytes 221192 | tf_op jit(solution)/shard_map/ppermute | solution.py:521
  23.2 1.0 constant_dynamic-slice_fusion
  24.3 1.0 collective-permute-done.6.rest_1_.rest_3_
  25.3 1.7 %collective-permute-start.7 = (bf16[24,8,1024]{2,1,0:T(8,128)(2,1)S(1)}, bf16[24,8,1024]{2,1,0:T(8,128)(2,1)S(1)}, u32[]{:S(2)}, u32[]{:S(2)}) collective-permute-start(bf16[24,8,1024]{2,1,0:T(8,128)(2,1)S(1)} %constant_dynamic-slice_fusion), channel_id=1, source_target_pairs={{0,1},{1,0},{2,3},{3,2},{4,5},{5,4},{6,7},{7,6},{8,9},{9,8},{10,11... | collective-permute-start | bytes 1179656 | tf_op jit(solution)/shard_map/ppermute | solution.py:528
  28.2 15.0 %shard_map.84 = (bf16[128,64,128]{2,1,0:T(8,128)(2,1)}, bf16[128,128,128]{2,1,0:T(8,128)(2,1)}) custom-call(s32[1]{0:T(128)} %bitcast.4.odd_ref, s32[2,128]{1,0:T(2,128)} %copy-done.3, f32[2,8,1152]{2,1,0:T(8,128)} %copy-done.2, bf16[128,8,1024]{2,1,0:T(8,128)(2,1)} %rest_1_.1, f32[8,1024]{1,0:T(8,128)} %broadcast_in_dim.18.rest_2_.rest_5_.rest_4_, ...), custom_call_target="tpu_custom_call" | custom-call | flops 3758096384 | bytes 16777216 | tf_op jit(solution)/shard_map/pallas_call | solution.py:280
  43.4 8.0 %collective-permute-done.11.rest_4_ = bf16[24,8,1024]{2,1,0:T(8,128)(2,1)S(1)} collective-permute-done((bf16[24,8,1024]{2,1,0:T(8,128)(2,1)S(1)}, bf16[24,8,1024]{2,1,0:T(8,128)(2,1)S(1)}, u32[]{:S(2)}, u32[]{:S(2)}) %collective-permute-start.11) | collective-permute-done | bytes 393248 | tf_op jit(solution)/shard_map/ppermute | solution.py:536
  52.2 12.0 %shard_map.85 = (bf16[128,128,128]{2,1,0:T(8,128)(2,1)}, bf16[128,128,128]{2,1,0:T(8,128)(2,1)}) custom-call(s32[1]{0:T(128)} %bitcast.4.odd_ref, s32[2,64]{1,0:T(2,128)} %copy-done.9, f32[2,8,1152]{2,1,0:T(8,128)} %copy-done.2, f32[2,8,1152]{2,1,0:T(8,128)} %copy-done.1, bf16[64,8,1024]{2,1,0:T(8,128)(2,1)} %collective-permute-done.9.rest_2_, ...), custom_call_target="tpu_custom_call" | custom-call | flops 3758096384 | bytes 16777216 | tf_op jit(solution)/shard_map/pallas_call | solution.py:280
  64.3 28.7 %shard_map.86 = (bf16[64,32,128]{2,1,0:T(8,128)(2,1)}, bf16[64,32,128]{2,1,0:T(8,128)(2,1)}, bf16[64,32,128]{2,1,0:T(8,128)(2,1)}, bf16[64,32,128]{2,1,0:T(8,128)(2,1)}) custom-call(s32[1]{0:T(128)} %bitcast.me_ref, s32[2,128]{1,0:T(2,128)} %copy-done.3, bf16[40,8,1024]{2,1,0:T(8,128)(2,1)} %collective-permute-done.4.rest_0_, bf16[24,8,1024]{2,1,0:T(8,128)(2,1)} %copy-done, ...), custom_call_target="tpu_custom_call" | custom-call | flops 4294967296 | bytes 20971520 | tf_op jit(solution)/shard_map/pallas_call | solution.py:433
  93.1 1.7 %collective-permute-start.12 = (bf16[64,32,128]{2,1,0:T(8,128)(2,1)}, bf16[64,32,128]{2,1,0:T(8,128)(2,1)S(1)}, u32[]{:S(2)}, u32[]{:S(2)}) collective-permute-start(bf16[64,32,128]{2,1,0:T(8,128)(2,1)} %get-tuple-element.57), channel_id=1, source_target_pairs={{0,0},{1,29},{2,2},{3,31},{4,4},{5,1},{6,6},{7,3},{8,8},{9,5},{10,... | collective-permute-start | bytes 1572872 | tf_op jit(solution)/shard_map/ppermute | solution.py:565
  94.8 2.4 %collective-permute-start.14 = (bf16[64,32,128]{2,1,0:T(8,128)(2,1)}, bf16[64,32,128]{2,1,0:T(8,128)(2,1)S(1)}, u32[]{:S(2)}, u32[]{:S(2)}) collective-permute-start(bf16[64,32,128]{2,1,0:T(8,128)(2,1)} %get-tuple-element.59), channel_id=1, source_target_pairs={{0,1},{1,28},{2,3},{3,30},{4,5},{5,0},{6,7},{7,2},{8,9},{9,4},{10,... | collective-permute-start | bytes 1572872 | tf_op jit(solution)/shard_map/ppermute | solution.py:565
  97.1 27.6 %collective-permute-done.13 = bf16[64,32,128]{2,1,0:T(8,128)(2,1)S(1)} collective-permute-done((bf16[64,32,128]{2,1,0:T(8,128)(2,1)}, bf16[64,32,128]{2,1,0:T(8,128)(2,1)S(1)}, u32[]{:S(2)}, u32[]{:S(2)}) %collective-permute-start.13) | collective-permute-done | bytes 524320 | tf_op jit(solution)/shard_map/ppermute | solution.py:565
  124.7 13.3 %collective-permute-done.15 = bf16[64,32,128]{2,1,0:T(8,128)(2,1)S(1)} collective-permute-done((bf16[64,32,128]{2,1,0:T(8,128)(2,1)}, bf16[64,32,128]{2,1,0:T(8,128)(2,1)S(1)}, u32[]{:S(2)}, u32[]{:S(2)}) %collective-permute-start.15) | collective-permute-done | bytes 524320 | tf_op jit(solution)/shard_map/ppermute | solution.py:565
  138.4 1.5 %pad_maximum_fusion = f32[128,32,128]{2,1,0:T(8,128)} fusion(f32[64,32,128]{2,1,0:T(8,128)S(1)} %get-tuple-element.62, f32[64,32,128]{2,1,0:T(8,128)S(1)} %get-tuple-element.61), kind=kLoop, calls=%fused_computation | loop fusion | flops 524288 | bytes 4194304 | tf_op jit(solution)/shard_map/concatenate | solution.py:568
  (44 shorter events, 4.1 us)
Async XLA Ops:
  0.0 7.0 %copy-start.6 = (s32[128]{0:T(128)S(1)}, s32[128]{0:T(128)}, u32[]{:S(2)}) copy-start(s32[128]{0:T(128)} %sec_ref.1) | copy-start | bytes 1540
  0.0 11.8 %copy-start.5 = (f32[512]{0:T(512)S(1)}, f32[512]{0:T(512)}, u32[]{:S(2)}) copy-start(f32[512]{0:T(512)} %param.9) | copy-start | bytes 6148
  1.2 15.8 %collective-permute-start.4 = (bf16[40,8,1024]{2,1,0:T(8,128)(2,1)S(1)}, bf16[40,8,1024]{2,1,0:T(8,128)(2,1)}, u32[]{:S(2)}, u32[]{:S(2)}) collective-permute-start(bf16[40,8,1024]{2,1,0:T(8,128)(2,1)S(1)} %constant_dynamic-slice_fusion.3), channel_id=1, source_target_pairs={{0,1},{1,0},{2,3},{3,2},{4,5},{5,4},{6,7},{7,6},{8,9},{9,8},{10,11... | collective-permute-start | bytes 1966088 | tf_op jit(solution)/shard_map/ppermute | solution.py:501
  6.1 2.1 %collective-permute-start = (f32[2,8,1152]{2,1,0:T(8,128)}, f32[2,8,1152]{2,1,0:T(8,128)S(1)}, u32[]{:S(2)}, u32[]{:S(2)}) collective-permute-start(f32[2,8,1152]{2,1,0:T(8,128)} %shard_map.82), channel_id=1, source_target_pairs={{0,4},{4,0},{8,12},{12,8},{16,20},{20,16},{24,28},{28,24},{1,5},{5... | collective-permute-start | bytes 221192 | tf_op jit(solution)/shard_map/ppermute | solution.py:463
  7.1 9.7 %copy-start.3 = (s32[2,128]{1,0:T(2,128)}, s32[2,128]{1,0:T(2,128)S(1)}, u32[]{:S(2)}) copy-start(s32[2,128]{1,0:T(2,128)S(1)} %pad_add_fusion.flag_ref) | copy-start | bytes 3076
  7.1 9.8 %collective-permute-start.5 = (s32[2,64]{1,0:T(2,128)S(1)}, s32[2,64]{1,0:T(2,128)S(1)}, u32[]{:S(2)}, u32[]{:S(2)}) collective-permute-start(s32[2,64]{1,0:T(2,128)S(1)} %constant_dynamic-slice_fusion.2), channel_id=1, source_target_pairs={{0,28},{1,5},{2,30},{3,7},{4,0},{5,9},{6,2},{7,11},{8,4},{9,13},{1... | collective-permute-start | bytes 1544 | tf_op jit(solution)/shard_map/ppermute | solution.py:503
  9.1 7.7 %collective-permute-start.1 = (f32[2,8,1152]{2,1,0:T(8,128)S(1)}, f32[2,8,1152]{2,1,0:T(8,128)S(1)}, u32[]{:S(2)}, u32[]{:S(2)}) collective-permute-start(f32[2,8,1152]{2,1,0:T(8,128)S(1)} %add.38), channel_id=1, source_target_pairs={{0,8},{4,12},{8,0},{12,4},{16,24},{20,28},{24,16},{28,20},{1,9},{5... | collective-permute-start | bytes 221192 | tf_op jit(solution)/shard_map/ppermute | solution.py:463
  9.4 7.4 %collective-permute-start.2 = (f32[2,8,1152]{2,1,0:T(8,128)S(1)}, f32[2,8,1152]{2,1,0:T(8,128)S(1)}, u32[]{:S(2)}, u32[]{:S(2)}) collective-permute-start(f32[2,8,1152]{2,1,0:T(8,128)S(1)} %add.38), channel_id=1, source_target_pairs={{0,16},{4,20},{8,24},{12,28},{16,0},{20,4},{24,8},{28,12},{1,17},{... | collective-permute-start | bytes 221192 | tf_op jit(solution)/shard_map/ppermute | solution.py:463
  10.6 6.2 %collective-permute-start.3 = (f32[2,8,1152]{2,1,0:T(8,128)S(1)}, f32[2,8,1152]{2,1,0:T(8,128)S(1)}, u32[]{:S(2)}, u32[]{:S(2)}) collective-permute-start(f32[2,8,1152]{2,1,0:T(8,128)S(1)} %add.38), channel_id=1, source_target_pairs={{0,24},{4,28},{8,16},{12,20},{16,8},{20,12},{24,0},{28,4},{1,25},{... | collective-permute-start | bytes 221192 | tf_op jit(solution)/shard_map/ppermute | solution.py:463
  16.8 10.9 %copy-start.4 = (f32[1024]{0:T(1024)S(1)}, f32[1024]{0:T(1024)}, u32[]{:S(2)}) copy-start(f32[1024]{0:T(1024)} %constant.37.clone) | copy-start | bytes 12292
  17.0 11.3 %copy-start.2 = (f32[2,8,1152]{2,1,0:T(8,128)}, f32[2,8,1152]{2,1,0:T(8,128)S(1)}, u32[]{:S(2)}) copy-start(f32[2,8,1152]{2,1,0:T(8,128)S(1)} %add_add_fusion.rest_0_) | copy-start | bytes 221188
  17.0 26.3 %copy-start.9 = (s32[2,64]{1,0:T(2,128)}, s32[2,64]{1,0:T(2,128)S(1)}, u32[]{:S(2)}) copy-start(s32[2,64]{1,0:T(2,128)S(1)} %collective-permute-done.5.flag_ref) | copy-start | bytes 1540
  19.3 32.2 %collective-permute-start.9 = (bf16[64,8,1024]{2,1,0:T(8,128)(2,1)}, bf16[64,8,1024]{2,1,0:T(8,128)(2,1)}, u32[]{:S(2)}, u32[]{:S(2)}) collective-permute-start(bf16[64,8,1024]{2,1,0:T(8,128)(2,1)} %constant_dynamic-slice_fusion.1), channel_id=1, source_target_pairs={{0,28},{1,5},{2,30},{3,7},{4,0},{5,9},{6,2},{7,11},{8,4},{9,13},{1... | collective-permute-start | bytes 3145736 | tf_op jit(solution)/shard_map/ppermute | solution.py:524
  20.8 4.5 %collective-permute-start.6 = (f32[2,8,1152]{2,1,0:T(8,128)S(1)}, f32[2,8,1152]{2,1,0:T(8,128)S(1)}, u32[]{:S(2)}, u32[]{:S(2)}) collective-permute-start(f32[2,8,1152]{2,1,0:T(8,128)S(1)} %add_add_fusion.rest_0_), channel_id=1, source_target_pairs={{0,1},{1,0},{2,3},{3,2},{4,5},{5,4},{6,7},{7,6},{8,9},{9,8},{10,11... | collective-permute-start | bytes 221192 | tf_op jit(solution)/shard_map/ppermute | solution.py:521
  25.3 18.0 %copy-start.1 = (f32[2,8,1152]{2,1,0:T(8,128)}, f32[2,8,1152]{2,1,0:T(8,128)S(1)}, u32[]{:S(2)}) copy-start(f32[2,8,1152]{2,1,0:T(8,128)S(1)} %collective-permute-done.6.rest_1_.rest_3_) | copy-start | bytes 221188
  25.3 18.0 %collective-permute-start.7 = (bf16[24,8,1024]{2,1,0:T(8,128)(2,1)S(1)}, bf16[24,8,1024]{2,1,0:T(8,128)(2,1)S(1)}, u32[]{:S(2)}, u32[]{:S(2)}) collective-permute-start(bf16[24,8,1024]{2,1,0:T(8,128)(2,1)S(1)} %constant_dynamic-slice_fusion), channel_id=1, source_target_pairs={{0,1},{1,0},{2,3},{3,2},{4,5},{5,4},{6,7},{7,6},{8,9},{9,8},{10,11... | collective-permute-start | bytes 1179656 | tf_op jit(solution)/shard_map/ppermute | solution.py:528
  27.0 37.3 %collective-permute-start.8 = (bf16[64,8,1024]{2,1,0:T(8,128)(2,1)}, bf16[64,8,1024]{2,1,0:T(8,128)(2,1)}, u32[]{:S(2)}, u32[]{:S(2)}) collective-permute-start(bf16[64,8,1024]{2,1,0:T(8,128)(2,1)} %constant_dynamic-slice_fusion.1), channel_id=1, source_target_pairs={{0,1},{1,0},{2,3},{3,2},{4,5},{5,4},{6,7},{7,6},{8,9},{9,8},{10,11... | collective-permute-start | bytes 3145736 | tf_op jit(solution)/shard_map/ppermute | solution.py:529
  27.0 16.4 %collective-permute-start.10 = (bf16[40,8,1024]{2,1,0:T(8,128)(2,1)}, bf16[40,8,1024]{2,1,0:T(8,128)(2,1)}, u32[]{:S(2)}, u32[]{:S(2)}) collective-permute-start(bf16[40,8,1024]{2,1,0:T(8,128)(2,1)} %collective-permute-done.4.rest_0_), channel_id=1, source_target_pairs={{0,28},{1,5},{2,30},{3,7},{4,0},{5,9},{6,2},{7,11},{8,4},{9,13},{1... | collective-permute-start | bytes 1966088 | tf_op jit(solution)/shard_map/ppermute | solution.py:530
  43.3 21.0 %copy-start = (bf16[24,8,1024]{2,1,0:T(8,128)(2,1)}, bf16[24,8,1024]{2,1,0:T(8,128)(2,1)S(1)}, u32[]{:S(2)}) copy-start(bf16[24,8,1024]{2,1,0:T(8,128)(2,1)S(1)} %collective-permute-done.7.rest_1_) | copy-start | bytes 1179652
  43.3 8.2 %collective-permute-start.11 = (bf16[24,8,1024]{2,1,0:T(8,128)(2,1)S(1)}, bf16[24,8,1024]{2,1,0:T(8,128)(2,1)S(1)}, u32[]{:S(2)}, u32[]{:S(2)}) collective-permute-start(bf16[24,8,1024]{2,1,0:T(8,128)(2,1)S(1)} %collective-permute-done.7.rest_1_), channel_id=1, source_target_pairs={{0,28},{1,5},{2,30},{3,7},{4,0},{5,9},{6,2},{7,11},{8,4},{9,13},{1... | collective-permute-start | bytes 1179656 | tf_op jit(solution)/shard_map/ppermute | solution.py:536
  93.0 31.7 %collective-permute-start.13 = (bf16[64,32,128]{2,1,0:T(8,128)(2,1)}, bf16[64,32,128]{2,1,0:T(8,128)(2,1)S(1)}, u32[]{:S(2)}, u32[]{:S(2)}) collective-permute-start(bf16[64,32,128]{2,1,0:T(8,128)(2,1)} %get-tuple-element.58), channel_id=1, source_target_pairs={{0,2},{1,31},{2,0},{3,29},{4,6},{5,3},{6,4},{7,1},{8,10},{9,7},{10... | collective-permute-start | bytes 1572872 | tf_op jit(solution)/shard_map/ppermute | solution.py:565
  93.1 31.6 %collective-permute-start.12 = (bf16[64,32,128]{2,1,0:T(8,128)(2,1)}, bf16[64,32,128]{2,1,0:T(8,128)(2,1)S(1)}, u32[]{:S(2)}, u32[]{:S(2)}) collective-permute-start(bf16[64,32,128]{2,1,0:T(8,128)(2,1)} %get-tuple-element.57), channel_id=1, source_target_pairs={{0,0},{1,29},{2,2},{3,31},{4,4},{5,1},{6,6},{7,3},{8,8},{9,5},{10,... | collective-permute-start | bytes 1572872 | tf_op jit(solution)/shard_map/ppermute | solution.py:565
  94.8 43.3 %collective-permute-start.15 = (bf16[64,32,128]{2,1,0:T(8,128)(2,1)}, bf16[64,32,128]{2,1,0:T(8,128)(2,1)S(1)}, u32[]{:S(2)}, u32[]{:S(2)}) collective-permute-start(bf16[64,32,128]{2,1,0:T(8,128)(2,1)} %get-tuple-element.60), channel_id=1, source_target_pairs={{0,3},{1,30},{2,1},{3,28},{4,7},{5,2},{6,5},{7,0},{8,11},{9,6},{10... | collective-permute-start | bytes 1572872 | tf_op jit(solution)/shard_map/ppermute | solution.py:565
  94.8 43.3 %collective-permute-start.14 = (bf16[64,32,128]{2,1,0:T(8,128)(2,1)}, bf16[64,32,128]{2,1,0:T(8,128)(2,1)S(1)}, u32[]{:S(2)}, u32[]{:S(2)}) collective-permute-start(bf16[64,32,128]{2,1,0:T(8,128)(2,1)} %get-tuple-element.59), channel_id=1, source_target_pairs={{0,1},{1,28},{2,3},{3,30},{4,5},{5,0},{6,7},{7,2},{8,9},{9,4},{10,... | collective-permute-start | bytes 1572872 | tf_op jit(solution)/shard_map/ppermute | solution.py:565
  (2 other events, 7.8 us)

commit v10 on v9

--- a/solution.py
+++ b/solution.py
@@ -39,13 +39,23 @@
     return window.astype(np.float32), waves.astype(np.float32), cast(segment), cast(lag)
 
 
-def section_sums(dead_ref, sec_ref, x_ref, out_ref):
+def section_sums(odd_ref, dead_ref, sec_ref, x_ref, whole_ref, out_ref, half_ref, tail_ref, sem):
     chans, wins, ns = x_ref.shape
     first = pl.program_id(0) * chans
+    width, length = half_ref.shape[0], tail_ref.shape[0]
+    odd = odd_ref[0]
+    copies = [
+        pltpu.make_async_copy(whole_ref.at[pl.ds(odd * width, width)], half_ref, sem.at[0]),
+        pltpu.make_async_copy(
+            whole_ref.at[pl.ds((2 - odd) * width - length, length)], tail_ref, sem.at[1]
+        ),
+    ]
 
     @pl.when(pl.program_id(0) == 0)
     def _():
         out_ref[...] = jnp.zeros_like(out_ref)
+        for copy in copies:
+            copy.start()
 
     def body(c, carry):
         value = x_ref[c].astype(F32)
@@ -65,6 +75,11 @@
         out_ref[s, :, :ns] += sums[s]
         out_ref[s, :, ns:] += jnp.zeros((wins, LANE), F32) + counts[s]
 
+    @pl.when(pl.program_id(0) == pl.num_programs(0) - 1)
+    def _():
+        for copy in copies:
+            copy.wait()
+
 
 def circulant_kernel(filter_ref, out_ref):
     ns = filter_ref.shape[1]
@@ -73,8 +88,8 @@
         out_ref[t : t + 16, :] = pltpu.roll(block, t, 1, stride=1, stride_axis=0).astype(BF16)
 
 
-def segment_factors(places, want, odd, flag_ref, tot, x, hann, conv, seg, work, copied, emit):
-    common, clean, rows, series, stage = work
+def segment_factors(places, want, repeat, odd, flag_ref, tot, x, hann, conv, seg, work, copied, emit):
+    common, clean, mass, square, rows, series, series_a, stage = work
     _, wins, ns = x[0].shape
     chans = sum(piece.shape[0] for piece in x)
     pitch = wins + 1
@@ -89,7 +104,8 @@
     for g in range(len(tot)):
         for s in range(NSEC):
             common[g * NSEC + s] = tot[g][s, :, :ns] / jnp.maximum(tot[g][s, :, ns : ns + 1], 1.0)
-    sign = 1.0 - 2.0 * (lax.broadcasted_iota(jnp.int32, (wins, LANE), 1) % 2).astype(F32)
+    sign = 1.0 - 2.0 * (lax.broadcasted_iota(jnp.int32, (chans, LANE), 1) % 2).astype(F32)
+    lower = lax.broadcasted_iota(jnp.int32, (1, LANE), 1) < LANE // 2
 
     for number, (group, even_base, odd_base) in enumerate(places):
         piece = x[number]
@@ -100,34 +116,38 @@
             at = base + c
             flag = lax.rem(at, held)
             live = (1 - flag_ref[0, flag]).astype(F32)
-            value = (piece[c].astype(F32) - common[group * NSEC + flag_ref[1, flag]]) * hann[...]
+            value = (piece[c].astype(F32) - common[group * NSEC + flag_ref[1, flag]]) * (
+                hann[...] * live
+            )
             tiles = [value[:, t * LANE : (t + 1) * LANE] for t in range(ns // LANE)]
-            mass = sum(tiles[1:], tiles[0])
-            square = sum([tile * tile for tile in tiles[1:]], tiles[0] * tiles[0])
-            lowest = jnp.sum(mass, axis=1, keepdims=True)
-            highest = jnp.sum(mass * sign, axis=1, keepdims=True)
-            square = jnp.sum(square, axis=1, keepdims=True)
-            power = 0.5 * square + (lowest * lowest - highest * highest) * (0.5 / ns)
-            value = value * (lax.rsqrt(power + 1e-06) * live)
-            for t in range(ns // LANE):
-                clean[t, pl.ds(at * pitch, wins), :] = value[:, t * LANE : (t + 1) * LANE]
+            row = pl.ds(at * pitch, wins)
+            mass[row, :] = sum(tiles[1:], tiles[0])
+            square[row, :] = sum([tile * tile for tile in tiles[1:]], tiles[0] * tiles[0])
+            for t, tile in enumerate(tiles):
+                clean[t, row, :] = tile
             return 0
 
         parts = copied["x"][number]
         part = length // len(parts)
         for n, copy in enumerate(parts):
             copy.wait()
-            lax.fori_loop(n * part, (n + 1) * part, clean_channel, 0, unroll=4)
+            lax.fori_loop(n * part, (n + 1) * part, clean_channel, 0, unroll=8)
     for copy in copied["tables"]:
         copy.wait()
 
     def some_windows(step, _):
         for i in range(TOGETHER):
-            w = step * TOGETHER + i
+            window = pl.ds(step * TOGETHER + i, chans, stride=pitch)
+            total = mass[window, :]
+            lowest = jnp.sum(total, axis=1, keepdims=True)
+            highest = jnp.sum(total * sign, axis=1, keepdims=True)
+            power = 0.5 * jnp.sum(square[window, :], axis=1, keepdims=True)
+            power = power + (lowest * lowest - highest * highest) * (0.5 / ns)
+            level = lax.rsqrt(power + 1e-06)
             for t in range(ns // LANE):
-                rows[i * chans : (i + 1) * chans, t * LANE : (t + 1) * LANE] = clean[
-                    t, pl.ds(w, chans, stride=pitch), :
-                ].astype(BF16)
+                rows[i * chans : (i + 1) * chans, t * LANE : (t + 1) * LANE] = (
+                    clean[t, window, :] * level
+                ).astype(BF16)
         for t in range(0, ns, TILE):
             series[half // 2 + t : half // 2 + t + TILE, :] = lax.dot_general(
                 conv[t : t + TILE, :], rows[...], NT, preferred_element_type=F32
@@ -151,9 +171,18 @@
 
         @pl.when(want)
         def _():
+            source = series
+            if repeat:
+                source = series_a
+                for i in range(TOGETHER):
+                    value = series[:, i * chans : (i + 1) * chans]
+                    turned = jnp.concatenate(
+                        [value[:, chans // 2 :], value[:, : chans // 2]], axis=1
+                    )
+                    series_a[:, i * chans : (i + 1) * chans] = jnp.where(lower, value, turned)
             for j in range(blocks):
                 a = jnp.dot(
-                    seg[...], series[j * half : j * half + size, :], preferred_element_type=F32
+                    seg[...], source[j * half : j * half + size, :], preferred_element_type=F32
                 )
                 place(0, j, a)
 
@@ -161,16 +190,29 @@
 
     lax.fori_loop(0, wins // TOGETHER, some_windows, 0)
 
-    def factor(which, k):
-        return jnp.concatenate(
-            [
-                stage[which, pl.ds((2 * k + part) * jpitch, jw), :].astype(BF16)
-                for part in range(2)
-            ],
-            axis=0,
-        )
-
-    emit(want, factor)
+    def factor(which, k, turn=False):
+        real, imag = [
+            stage[which, pl.ds((2 * k + part) * jpitch, jw), :] for part in range(2)
+        ]
+        if turn:
+            real, imag = imag, -real
+        return jnp.concatenate([real.astype(BF16), imag.astype(BF16)], axis=0)
+
+    def first_factor(k, put):
+        if repeat:
+            put(0, slice(None), jnp.where(lower, factor(0, k), factor(0, k, True)).T)
+        else:
+            width = chans // 2
+            for part in range(2):
+                value = factor(0, k, part == 1).T
+                for group in range(2):
+                    put(
+                        group,
+                        slice(part * width, (part + 1) * width),
+                        value[group * width : (group + 1) * width],
+                    )
+
+    emit(want, first_factor, lambda k: factor(1, k))
 
 
 def work_shapes(groups, chans, wins, ns):
@@ -179,7 +221,10 @@
     return [
         pltpu.VMEM((groups * NSEC, wins, ns), F32),
         pltpu.VMEM((ns // LANE, chans * (wins + 1), LANE), F32),
+        pltpu.VMEM((chans * (wins + 1), LANE), F32),
+        pltpu.VMEM((chans * (wins + 1), LANE), F32),
         pltpu.VMEM((TOGETHER * chans, ns), BF16),
+        pltpu.VMEM((ns + half, TOGETHER * chans), BF16),
         pltpu.VMEM((ns + half, TOGETHER * chans), BF16),
         pltpu.VMEM((2, rows, chans), F32),
     ]
@@ -228,13 +273,16 @@
     bins = b_out.shape[0]
     step = bins // STEPS
 
-    def emit(want, factor):
+    def emit(want, first_factor, second_factor):
         def first(k, _):
-            a_out[k] = factor(0, k).T[: a_out.shape[1]]
+            def put(group, rows, value):
+                a_out[k, group, rows] = value
+
+            first_factor(k, put)
             return 0
 
         def second(k, _):
-            b_out[k] = factor(1, k)
+            b_out[k] = second_factor(k)
             return 0
 
         def send(n, source, target):
@@ -261,7 +309,8 @@
 
     odd = odd_ref[0]
     segment_factors(
-        places, odd == wanted, odd, flag_ref, tot, x, hann, conv, seg, work, copied, emit
+        *(places, odd == wanted, wanted == 0, odd, flag_ref),
+        *(tot, x, hann, conv, seg, work, copied, emit),
     )
 
 
@@ -271,11 +320,10 @@
     size = seg.shape[0]
     half = size // 2
     depth = ns // half * wins * 2
-    kept = chans if wanted else chans // 2
     smem = pl.BlockSpec(memory_space=pltpu.SMEM)
     anywhere = pl.BlockSpec(memory_space=pl.ANY)
     operands = list(totals) + list(pieces) + [hann, conv, seg]
-    a_shape = jax.ShapeDtypeStruct((half, kept, depth), BF16)
+    a_shape = jax.ShapeDtypeStruct((half, 2 if wanted else 1, chans, depth), BF16)
     b_shape = jax.ShapeDtypeStruct((half, depth, chans), BF16)
     return pl.pallas_call(
         functools.partial(segments_kernel, places, wanted, len(totals)),
@@ -307,8 +355,8 @@
     outs, rest = rest[:shares], rest[shares:]
     x, rest = rest[:count], rest[count:]
     tot, hann, conv, seg, lag = rest[:5]
-    (a0, ah, b0, bh), rest = rest[5:9], rest[9:]
-    work, (a1, b1, one, in_sem, late_sem) = rest[:-5], rest[-5:]
+    (a, b0, bh), rest = rest[5:8], rest[8:]
+    work, (b1, one, in_sem, late_sem) = rest[:-4], rest[-4:]
     me = me_ref[0]
     odd = lax.rem(me, 2)
     copied = input_copies(
@@ -317,25 +365,40 @@
         [(conv_hbm, conv), (seg_hbm, seg), (lag_hbm, lag)],
         in_sem,
     )
+    a0_hbm, ah_hbm, b0_hbm, bh_hbm = left_hbm
+    own_a = pltpu.make_async_copy(a0_hbm.at[:, 0], a.at[:, 0], late_sem.at[0])
+    halo_a = pltpu.make_async_copy(ah_hbm, a, late_sem.at[0])
     late = [
-        pltpu.make_async_copy(source, target, late_sem.at[n])
-        for n, (source, target) in enumerate(zip(left_hbm, (a0, ah, b0, bh)))
+        pltpu.make_async_copy(b0_hbm, b0, late_sem.at[1]),
+        pltpu.make_async_copy(bh_hbm, bh, late_sem.at[2]),
     ]
     for copy in late:
         copy.start()
-    bins, width, depth = a0.shape
-    chans = b0.shape[2]
+
+    @pl.when(odd == 0)
+    def _():
+        own_a.start()
+
+    @pl.when(odd == 1)
+    def _():
+        halo_a.start()
+
+    bins, depth, chans = b0.shape
+    width = chans // 2
     nfr = lag.shape[1]
     pitch = nfr + 1
     cross = work[-1]
 
-    def emit(want, factor):
+    def emit(want, first_factor, second_factor):
         def first(k, _):
-            a1[k] = factor(0, k).T[:width]
+            def put(group, rows, value):
+                a[k, 1, rows] = value
+
+            first_factor(k, put)
             return 0
 
         def second(k, _):
-            b1[k] = factor(1, k)
+            b1[k] = second_factor(k)
             return 0
 
         @pl.when(want)
@@ -345,59 +408,51 @@
         lax.fori_loop(0, bins, second, 0, unroll=8)
 
     segment_factors(
-        places, odd == 0, odd, flag_ref, [tot], x, hann, conv, seg, work, copied, emit
+        *(places, odd == 0, True, odd, flag_ref),
+        *([tot], x, hann, conv, seg, work, copied, emit),
     )
     for copy in late:
         copy.wait()
 
-    def bins_with(left_of):
-        def one_bin(k, _):
-            left = left_of(k)
-            part = depth // 2
-            swapped = jnp.concatenate(
-                [
-                    left[:, part:depth],
-                    -left[:, :part],
-                    left[:, depth + part :],
-                    -left[:, depth : depth + part],
-                ],
-                axis=1,
-            )
-            halo = bh[k]
-            other = jnp.concatenate([halo[:, width:], halo[:, :width]], axis=1)
-            right = jnp.concatenate(
-                [
-                    jnp.concatenate([b0[k], halo], axis=1),
-                    jnp.concatenate([b1[k], other], axis=1),
-                ],
-                axis=0,
-            )
-            value = jnp.dot(
-                jnp.concatenate([left, swapped], axis=0), right, preferred_element_type=F32
-            )
-            for p in range(2):
-                for t in range(2):
-                    cross[t, pl.ds(2 * k + p, width, stride=pitch), :] = value[
-                        p * width : (p + 1) * width, t * chans : (t + 1) * chans
-                    ]
-            return 0
-
-        lax.fori_loop(0, bins, one_bin, 0, unroll=8)
+    @pl.when(odd == 0)
+    def _():
+        own_a.wait()
 
     @pl.when(odd == 1)
     def _():
-        bins_with(lambda k: jnp.concatenate([ah[k, :width], ah[k, width:]], axis=1))
-
-    @pl.when(odd == 0)
-    def _():
-        bins_with(lambda k: jnp.concatenate([a0[k], a1[k]], axis=1))
+        halo_a.wait()
+
+    lane = lax.broadcasted_iota(jnp.int32, (1, chans), 1)
+    keep = [jnp.where((lane < width) == (g == 0), 1.0, 0.0).astype(BF16) for g in range(2)]
+
+    def one_bin(k, _):
+        halo = bh[k]
+        right = jnp.concatenate(
+            [
+                jnp.concatenate([b0[k], halo * keep[0]], axis=1),
+                jnp.concatenate([b1[k], halo * keep[1]], axis=1),
+            ],
+            axis=0,
+        )
+        left = jnp.concatenate([a[k, 0], a[k, 1]], axis=1)
+        value = jnp.dot(left, right, preferred_element_type=F32)
+        for p in range(2):
+            for t in range(2):
+                cross[t, pl.ds(2 * k + p, width, stride=pitch), :] = value[
+                    p * width : (p + 1) * width, t * chans : (t + 1) * chans
+                ]
+        return 0
+
+    lax.fori_loop(0, bins, one_bin, 0, unroll=8)
 
     row = lax.broadcasted_iota(jnp.int32, one.shape[1:], 0)
     column = lax.broadcasted_iota(jnp.int32, one.shape[1:], 1)
     turned = jnp.where(row < width, row + chans, row - width)
     place = row + (turned - row) * odd
     for t in range(2):
-        one[t] = jnp.where(place == column + t * chans, 1.0, 0.0)
+        here = column + t * chans
+        found = (place == here) | ((here >= chans + width) & (place == here - width))
+        one[t] = jnp.where(found, 1.0, 0.0)
     share = OFFS // shares
 
     def one_channel(c, _):
@@ -422,8 +477,8 @@
 
 
 def stacks(places, shares, scale, me, flags, total, pieces, hann, conv, seg, lag, a0, ah, b0, bh):
-    bins, width, depth = a0.shape
-    chans = b0.shape[2]
+    bins, depth, chans = b0.shape
+    width = chans // 2
     _, wins, ns = pieces[0].shape
     nlag, nfr = lag.shape
     smem = pl.BlockSpec(memory_space=pltpu.SMEM)
@@ -435,14 +490,15 @@
         out_shape=[jax.ShapeDtypeStruct((width, OFFS // shares, nlag), BF16)] * shares,
         in_specs=[smem] * 2 + [anywhere] * len(operands),
         out_specs=[vmem] * shares,
-        scratch_shapes=[pltpu.VMEM(value.shape, value.dtype) for value in operands]
+        scratch_shapes=[
+            pltpu.VMEM(value.shape, value.dtype) for value in operands if value is not a0
+        ]
         + work_shapes(1, chans, wins, ns)
         + [
-            pltpu.VMEM(a0.shape, BF16),
             pltpu.VMEM(b0.shape, BF16),
             pltpu.VMEM((2, chans + width, chans), F32),
             pltpu.SemaphoreType.DMA((8 + chans // PART,)),
-            pltpu.SemaphoreType.DMA((4,)),
+            pltpu.SemaphoreType.DMA((3,)),
         ],
         compiler_params=pltpu.CompilerParams(vmem_limit_bytes=VMEM),
         cost_estimate=pl.CostEstimate(
@@ -476,8 +532,9 @@
     groups = lax.axis_size("tm")
     me = lax.axis_index("tm")
     odd = me % 2
-    window, waves, seg, lag = [jnp.asarray(t) for t in tables(ns, nf)]
-    hann = jnp.broadcast_to(window[None, :], (wins, ns))
+    window, waves, seg, lag = tables(ns, nf)
+    waves, seg, lag = jnp.asarray(waves), jnp.asarray(seg), jnp.asarray(lag)
+    hann = jnp.asarray(np.broadcast_to(window[None, :], (wins, ns)))
     response = jnp.sum(band_gain[:, None] * waves, axis=0, keepdims=True)
     conv = pl.pallas_call(
         circulant_kernel,
@@ -495,32 +552,36 @@
 
     head = width * 5 // 8
 
-    def part_of(array, upper, start, length):
-        return lax.dynamic_slice_in_dim(array, upper * width + start, length, 0)
-
-    their_head = lax.ppermute(part_of(samples, 1 - odd, 0, head), "tm", swap)
+    their_head = lax.ppermute(
+        lax.dynamic_slice_in_dim(samples, (1 - odd) * width, head, 0), "tm", swap
+    )
     flags = jnp.stack([dead_flags, section_ids])
     halo_flags = lax.ppermute(
         lax.dynamic_slice_in_dim(flags, odd * width, width, 1), both, halo_pairs
     )
     smem = pl.BlockSpec(memory_space=pltpu.SMEM)
     steps = 4
-    sums = pl.pallas_call(
+    anywhere = pl.BlockSpec(memory_space=pl.ANY)
+    sums, own_half, tail = pl.pallas_call(
         section_sums,
         grid=(steps,),
-        out_shape=jax.ShapeDtypeStruct((NSEC, wins, ns + LANE), F32),
-        in_specs=[smem, smem, pl.BlockSpec((chans // steps, wins, ns), lambda i: (i, 0, 0))],
-        out_specs=pl.BlockSpec((NSEC, wins, ns + LANE), lambda i: (0, 0, 0)),
+        out_shape=[
+            jax.ShapeDtypeStruct((NSEC, wins, ns + LANE), F32),
+            jax.ShapeDtypeStruct((width, wins, ns), BF16),
+            jax.ShapeDtypeStruct((width - head, wins, ns), BF16),
+        ],
+        in_specs=[smem] * 3
+        + [pl.BlockSpec((chans // steps, wins, ns), lambda i: (i, 0, 0)), anywhere],
+        out_specs=[pl.BlockSpec((NSEC, wins, ns + LANE), lambda i: (0, 0, 0)), anywhere, anywhere],
+        scratch_shapes=[pltpu.SemaphoreType.DMA((2,))],
         compiler_params=pltpu.CompilerParams(vmem_limit_bytes=VMEM),
         cost_estimate=pl.CostEstimate(flops=1, bytes_accessed=1, transcendentals=0),
-    )(dead_flags, section_ids, samples)
+    )(odd[None], dead_flags, section_ids, samples, samples)
     total, their_head = add_over(sums, "fibre", their_head)
-    total, halo_flags, kept, conv = lax.optimization_barrier(
-        (total, halo_flags, samples, conv)
+    total, halo_flags, own_half, conv = lax.optimization_barrier(
+        (total, halo_flags, own_half, conv)
     )
     their_total = lax.ppermute(total, "tm", swap)
-    own_half = part_of(kept, odd, 0, width)
-    tail = part_of(kept, 1 - odd, head, width - head)
     halo = lax.ppermute(own_half, both, halo_pairs)
     ready = (total, their_total, their_head, own_half, tail, flags, hann, conv, seg, lag)
     ready = lax.optimization_barrier(ready)

time: 141 us -> 176 us (1.25)
  Pallas kernels: 61.9 us -> 101 us
  local copies, waits for them, and re-layouts: 5.91 us -> 2.6 us
    pallas_call x1, Pallas kernels: 3.54 us -> 46.5 us  [shards(): pl.pallas_call(section_sums, grid=(steps,), out_shape=[jax.ShapeDtypeStru...]
    pallas_call x2, Pallas kernels: 27.1 us -> 23.2 us  [segments(): pl.pallas_call(functools.partial(segments_kernel, places, wanted, len(tot...]
    dynamic_slice x3 -> x1, local copies, waits for them, and re-layouts: 4.46 us -> 1.13 us  [shards(): lax.dynamic_slice_in_dim(samples, (1 - odd) * width, head, 0)]
  transfers between devices with their start and end apart: 16 -> 16, of which waited for: 6 -> 6; matrix products, arithmetic and copies ran while one was open for 4% -> 2% of each run, Pallas kernels for 24% -> 41%
where the time goes in v10:
time: 176 us; the launch traced here: 175 us
  Pallas kernels  101 us (57%)
  waiting for transfers between devices  51.3 us (29%)
  starting transfers between devices  15.3 us (9%)
  other arithmetic  5.13 us (3%)
  local copies, waits for them, and re-layouts  2.6 us (1%)
    pallas_call x1, Pallas kernels, shards(): pl.pallas_call(section_sums, grid=(steps,), out_shape=[jax.ShapeDtypeStru...  46.5 us
    ppermute x4, waiting for transfers between devices, shards(): arrived.append(lax.ppermute(found[d], both, pairs).astype(F32))  39.8 us
    pallas_call x1, Pallas kernels, stacks(): pl.pallas_call(functools.partial(stack_kernel, places, scale, shares), ou...  28.5 us
    pallas_call x2, Pallas kernels, segments(): pl.pallas_call(functools.partial(segments_kernel, places, wanted, len(tot...  23.2 us
    ppermute x1, waiting for transfers between devices, shards(): halo_tail = lax.ppermute(forward, both, halo_pairs)  7.76 us
    ppermute x4, starting transfers between devices, shards(): arrived.append(lax.ppermute(found[d], both, pairs).astype(F32))  4.45 us
    ppermute x4, starting transfers between devices, add_over(): lax.ppermute(value, axis, [(i, i ^ s) for i in range(count)])  3.73 us
  transfers between devices with their start and end apart: 16, of which 6 were waited for; matrix products, arithmetic and copies ran while one was open for 2% of the time, Pallas kernels for 41%

profile of v10, /device:TPU:19, one launch (start us, length us, event | category | flops | bytes accessed | tf_op | source)
XLA Modules:
  0.0 175.3 jit_solution(3385949355481959150)
XLA Ops:
  0.0 1.1 constant_dynamic-slice_fusion.1
  1.1 1.4 collective-permute-start.4
  2.5 46.5 %shard_map.82 = (f32[2,8,1152]{2,1,0:T(8,128)}, bf16[64,8,1024]{2,1,0:T(8,128)(2,1)}, bf16[24,8,1024]{2,1,0:T(8,128)(2,1)}) custom-call(s32[1]{0:T(128)} %bitcast.1.odd_ref, s32[128]{0:T(128)} %dead_ref.1, s32[128]{0:T(128)} %sec_ref.1, bf16[128,8,1024]{2,1,0:T(8,128)(2,1)} %rest_1_.1, bf16[128,8,1024]{2,1,0:T(8,128)(2,1)} %rest_1_.1), custom_call_target="tpu_custom_call" | custom-call | flops 1 | bytes 1 | tf_op jit(solution)/shard_map/pallas_call | solution.py:565
  49.0 1.0 collective-permute-start
  50.2 1.0 collective-permute-done
  51.2 0.9 add.29
  52.4 1.2 collective-permute-start.2
  53.6 1.2 collective-permute-start.3
  54.8 2.4 %multiply_reduce_fusion = f32[1024]{0:T(1024)} fusion(f32[512,1024]{1,0:T(8,128)} %constant.33.clone, f32[512]{0:T(512)S(1)} %copy-done.5), kind=kLoop, calls=%fused_computation.1 | loop fusion | flops 1047552 | bytes 2103296 | tf_op jit(solution)/shard_map/reduce_sum | solution.py:538
  57.2 2.6 %shard_map.83.rest_3_.rest_6_.rest_5_ = bf16[1024,1024]{1,0:T(8,128)(2,1)} custom-call(f32[1,1024]{1,0:T(1,128)} %bitcast.5), custom_call_target="tpu_custom_call" | custom-call | flops 1 | bytes 1 | tf_op jit(solution)/shard_map/pallas_call | solution.py:539
  59.9 1.2 collective-permute-start.9
  61.1 1.3 collective-permute-start.6
  62.4 2.6 %collective-permute-done.6.rest_1_.rest_3_ = f32[2,8,1152]{2,1,0:T(8,128)S(1)} collective-permute-done((f32[2,8,1152]{2,1,0:T(8,128)S(1)}, f32[2,8,1152]{2,1,0:T(8,128)S(1)}, u32[]{:S(2)}, u32[]{:S(2)}) %collective-permute-start.6) | collective-permute-done | bytes 73760 | tf_op jit(solution)/shard_map/ppermute | solution.py:584
  65.0 1.3 collective-permute-start.7
  66.5 1.4 collective-permute-start.10
  68.5 13.5 %shard_map.84 = (bf16[128,1,128,128]{3,2,1,0:T(8,128)(2,1)}, bf16[128,128,128]{2,1,0:T(8,128)(2,1)}) custom-call(s32[1]{0:T(128)} %bitcast.1.odd_ref, s32[2,128]{1,0:T(2,128)} %copy-done.3, f32[2,8,1152]{2,1,0:T(8,128)} %copy-done.2, bf16[128,8,1024]{2,1,0:T(8,128)(2,1)} %rest_1_.1, f32[8,1024]{1,0:T(8,128)} %jit_solution_.3.rest_2_.rest_5_.rest_4_, ...), custom_call_target="tpu_custom_call" | custom-call | flops 3758096384 | bytes 16777216 | tf_op jit(solution)/shard_map/pallas_call | solution.py:328
  82.4 7.8 %collective-permute-done.11.rest_4_ = bf16[24,8,1024]{2,1,0:T(8,128)(2,1)S(1)} collective-permute-done((bf16[24,8,1024]{2,1,0:T(8,128)(2,1)S(1)}, bf16[24,8,1024]{2,1,0:T(8,128)(2,1)S(1)}, u32[]{:S(2)}, u32[]{:S(2)}) %collective-permute-start.11) | collective-permute-done | bytes 393248 | tf_op jit(solution)/shard_map/ppermute | solution.py:597
  90.9 9.7 %shard_map.85 = (bf16[128,2,128,128]{3,2,1,0:T(8,128)(2,1)}, bf16[128,128,128]{2,1,0:T(8,128)(2,1)}) custom-call(s32[1]{0:T(128)} %bitcast.1.odd_ref, s32[2,64]{1,0:T(2,128)} %copy-done.9, f32[2,8,1152]{2,1,0:T(8,128)} %copy-done.2, f32[2,8,1152]{2,1,0:T(8,128)} %copy-done.1, bf16[64,8,1024]{2,1,0:T(8,128)(2,1)} %collective-permute-done.9.rest_2_, ...), custom_call_target="tpu_custom_call" | custom-call | flops 3758096384 | bytes 16777216 | tf_op jit(solution)/shard_map/pallas_call | solution.py:328
  100.6 28.5 %shard_map.86 = (bf16[64,32,128]{2,1,0:T(8,128)(2,1)}, bf16[64,32,128]{2,1,0:T(8,128)(2,1)}, bf16[64,32,128]{2,1,0:T(8,128)(2,1)}, bf16[64,32,128]{2,1,0:T(8,128)(2,1)}) custom-call(s32[1]{0:T(128)} %bitcast.me_ref, s32[2,128]{1,0:T(2,128)} %copy-done.3, bf16[40,8,1024]{2,1,0:T(8,128)(2,1)} %collective-permute-done.4.rest_0_, bf16[24,8,1024]{2,1,0:T(8,128)(2,1)} %copy-done, ...), custom_call_target="tpu_custom_call" | custom-call | flops 4294967296 | bytes 20971520 | tf_op jit(solution)/shard_map/pallas_call | solution.py:488
  129.2 1.7 collective-permute-start.12
  130.9 2.7 %collective-permute-start.14 = (bf16[64,32,128]{2,1,0:T(8,128)(2,1)}, bf16[64,32,128]{2,1,0:T(8,128)(2,1)S(1)}, u32[]{:S(2)}, u32[]{:S(2)}) collective-permute-start(bf16[64,32,128]{2,1,0:T(8,128)(2,1)} %get-tuple-element.65), channel_id=1, source_target_pairs={{0,1},{1,28},{2,3},{3,30},{4,5},{5,0},{6,7},{7,2},{8,9},{9,4},{10,... | collective-permute-start | bytes 1572872 | tf_op jit(solution)/shard_map/ppermute | solution.py:626
  133.6 26.5 %collective-permute-done.13 = bf16[64,32,128]{2,1,0:T(8,128)(2,1)S(1)} collective-permute-done((bf16[64,32,128]{2,1,0:T(8,128)(2,1)}, bf16[64,32,128]{2,1,0:T(8,128)(2,1)S(1)}, u32[]{:S(2)}, u32[]{:S(2)}) %collective-permute-start.13) | collective-permute-done | bytes 524320 | tf_op jit(solution)/shard_map/ppermute | solution.py:626
  160.1 13.4 %collective-permute-done.15 = bf16[64,32,128]{2,1,0:T(8,128)(2,1)S(1)} collective-permute-done((bf16[64,32,128]{2,1,0:T(8,128)(2,1)}, bf16[64,32,128]{2,1,0:T(8,128)(2,1)S(1)}, u32[]{:S(2)}, u32[]{:S(2)}) %collective-permute-start.15) | collective-permute-done | bytes 524320 | tf_op jit(solution)/shard_map/ppermute | solution.py:626
  173.8 1.5 pad_maximum_fusion
  (42 shorter events, 2.9 us)
Async XLA Ops:
  1.1 58.7 %collective-permute-start.4 = (bf16[40,8,1024]{2,1,0:T(8,128)(2,1)S(1)}, bf16[40,8,1024]{2,1,0:T(8,128)(2,1)}, u32[]{:S(2)}, u32[]{:S(2)}) collective-permute-start(bf16[40,8,1024]{2,1,0:T(8,128)(2,1)S(1)} %constant_dynamic-slice_fusion.1), channel_id=1, source_target_pairs={{0,1},{1,0},{2,3},{3,2},{4,5},{5,4},{6,7},{7,6},{8,9},{9,8},{10,11... | collective-permute-start | bytes 1966088 | tf_op jit(solution)/shard_map/ppermute | solution.py:555
  2.5 47.6 %copy-start.6 = (s32[128]{0:T(128)S(1)}, s32[128]{0:T(128)}, u32[]{:S(2)}) copy-start(s32[128]{0:T(128)} %sec_ref.1) | copy-start | bytes 1540
  2.5 47.6 %copy-start.7 = (s32[128]{0:T(128)S(1)}, s32[128]{0:T(128)}, u32[]{:S(2)}) copy-start(s32[128]{0:T(128)} %dead_ref.1) | copy-start | bytes 1540
  2.5 52.3 %copy-start.5 = (f32[512]{0:T(512)S(1)}, f32[512]{0:T(512)}, u32[]{:S(2)}) copy-start(f32[512]{0:T(512)} %param.9) | copy-start | bytes 6148
  49.0 2.1 %collective-permute-start = (f32[2,8,1152]{2,1,0:T(8,128)}, f32[2,8,1152]{2,1,0:T(8,128)S(1)}, u32[]{:S(2)}, u32[]{:S(2)}) collective-permute-start(f32[2,8,1152]{2,1,0:T(8,128)} %get-tuple-element.36), channel_id=1, source_target_pairs={{0,4},{4,0},{8,12},{12,8},{16,20},{20,16},{24,28},{28,24},{1,5},{5... | collective-permute-start | bytes 221192 | tf_op jit(solution)/shard_map/ppermute | solution.py:519
  50.1 9.7 %copy-start.3 = (s32[2,128]{1,0:T(2,128)}, s32[2,128]{1,0:T(2,128)S(1)}, u32[]{:S(2)}) copy-start(s32[2,128]{1,0:T(2,128)S(1)} %pad_add_fusion.flag_ref) | copy-start | bytes 3076
  50.2 9.7 %collective-permute-start.5 = (s32[2,64]{1,0:T(2,128)S(1)}, s32[2,64]{1,0:T(2,128)S(1)}, u32[]{:S(2)}, u32[]{:S(2)}) collective-permute-start(s32[2,64]{1,0:T(2,128)S(1)} %constant_dynamic-slice_fusion), channel_id=1, source_target_pairs={{0,28},{1,5},{2,30},{3,7},{4,0},{5,9},{6,2},{7,11},{8,4},{9,13},{1... | collective-permute-start | bytes 1544 | tf_op jit(solution)/shard_map/ppermute | solution.py:559
  52.1 15.8 %copy-start.4 = (f32[1024]{0:T(1024)S(1)}, f32[1024]{0:T(1024)}, u32[]{:S(2)}) copy-start(f32[1024]{0:T(1024)} %constant.36.clone) | copy-start | bytes 12292
  52.1 7.7 %collective-permute-start.1 = (f32[2,8,1152]{2,1,0:T(8,128)S(1)}, f32[2,8,1152]{2,1,0:T(8,128)S(1)}, u32[]{:S(2)}, u32[]{:S(2)}) collective-permute-start(f32[2,8,1152]{2,1,0:T(8,128)S(1)} %add.29), channel_id=1, source_target_pairs={{0,8},{4,12},{8,0},{12,4},{16,24},{20,28},{24,16},{28,20},{1,9},{5... | collective-permute-start | bytes 221192 | tf_op jit(solution)/shard_map/ppermute | solution.py:519
  52.4 7.4 %collective-permute-start.2 = (f32[2,8,1152]{2,1,0:T(8,128)S(1)}, f32[2,8,1152]{2,1,0:T(8,128)S(1)}, u32[]{:S(2)}, u32[]{:S(2)}) collective-permute-start(f32[2,8,1152]{2,1,0:T(8,128)S(1)} %add.29), channel_id=1, source_target_pairs={{0,16},{4,20},{8,24},{12,28},{16,0},{20,4},{24,8},{28,12},{1,17},{... | collective-permute-start | bytes 221192 | tf_op jit(solution)/shard_map/ppermute | solution.py:519
  53.6 6.2 %collective-permute-start.3 = (f32[2,8,1152]{2,1,0:T(8,128)S(1)}, f32[2,8,1152]{2,1,0:T(8,128)S(1)}, u32[]{:S(2)}, u32[]{:S(2)}) collective-permute-start(f32[2,8,1152]{2,1,0:T(8,128)S(1)} %add.29), channel_id=1, source_target_pairs={{0,24},{4,28},{8,16},{12,20},{16,8},{20,12},{24,0},{28,4},{1,25},{... | collective-permute-start | bytes 221192 | tf_op jit(solution)/shard_map/ppermute | solution.py:519
  59.9 22.1 %copy-start.9 = (s32[2,64]{1,0:T(2,128)}, s32[2,64]{1,0:T(2,128)S(1)}, u32[]{:S(2)}) copy-start(s32[2,64]{1,0:T(2,128)S(1)} %collective-permute-done.5.flag_ref) | copy-start | bytes 1540
  59.9 30.3 %collective-permute-start.9 = (bf16[64,8,1024]{2,1,0:T(8,128)(2,1)}, bf16[64,8,1024]{2,1,0:T(8,128)(2,1)}, u32[]{:S(2)}, u32[]{:S(2)}) collective-permute-start(bf16[64,8,1024]{2,1,0:T(8,128)(2,1)} %get-tuple-element.49), channel_id=1, source_target_pairs={{0,28},{1,5},{2,30},{3,7},{4,0},{5,9},{6,2},{7,11},{8,4},{9,13},{1... | collective-permute-start | bytes 3145736 | tf_op jit(solution)/shard_map/ppermute | solution.py:585
  61.1 3.8 %collective-permute-start.6 = (f32[2,8,1152]{2,1,0:T(8,128)S(1)}, f32[2,8,1152]{2,1,0:T(8,128)S(1)}, u32[]{:S(2)}, u32[]{:S(2)}) collective-permute-start(f32[2,8,1152]{2,1,0:T(8,128)S(1)} %add_add_fusion.rest_0_), channel_id=1, source_target_pairs={{0,1},{1,0},{2,3},{3,2},{4,5},{5,4},{6,7},{7,6},{8,9},{9,8},{10,11... | collective-permute-start | bytes 221192 | tf_op jit(solution)/shard_map/ppermute | solution.py:584
  65.0 17.0 %copy-start.1 = (f32[2,8,1152]{2,1,0:T(8,128)}, f32[2,8,1152]{2,1,0:T(8,128)S(1)}, u32[]{:S(2)}) copy-start(f32[2,8,1152]{2,1,0:T(8,128)S(1)} %collective-permute-done.6.rest_1_.rest_3_) | copy-start | bytes 221188
  65.0 17.0 %collective-permute-start.7 = (bf16[24,8,1024]{2,1,0:T(8,128)(2,1)}, bf16[24,8,1024]{2,1,0:T(8,128)(2,1)S(1)}, u32[]{:S(2)}, u32[]{:S(2)}) collective-permute-start(bf16[24,8,1024]{2,1,0:T(8,128)(2,1)} %get-tuple-element.48), channel_id=1, source_target_pairs={{0,1},{1,0},{2,3},{3,2},{4,5},{5,4},{6,7},{7,6},{8,9},{9,8},{10,11... | collective-permute-start | bytes 1179656 | tf_op jit(solution)/shard_map/ppermute | solution.py:589
  66.2 34.4 %collective-permute-start.8 = (bf16[64,8,1024]{2,1,0:T(8,128)(2,1)}, bf16[64,8,1024]{2,1,0:T(8,128)(2,1)}, u32[]{:S(2)}, u32[]{:S(2)}) collective-permute-start(bf16[64,8,1024]{2,1,0:T(8,128)(2,1)} %get-tuple-element.49), channel_id=1, source_target_pairs={{0,1},{1,0},{2,3},{3,2},{4,5},{5,4},{6,7},{7,6},{8,9},{9,8},{10,11... | collective-permute-start | bytes 3145736 | tf_op jit(solution)/shard_map/ppermute | solution.py:590
  66.5 15.9 %collective-permute-start.10 = (bf16[40,8,1024]{2,1,0:T(8,128)(2,1)}, bf16[40,8,1024]{2,1,0:T(8,128)(2,1)}, u32[]{:S(2)}, u32[]{:S(2)}) collective-permute-start(bf16[40,8,1024]{2,1,0:T(8,128)(2,1)} %collective-permute-done.4.rest_0_), channel_id=1, source_target_pairs={{0,28},{1,5},{2,30},{3,7},{4,0},{5,9},{6,2},{7,11},{8,4},{9,13},{1... | collective-permute-start | bytes 1966088 | tf_op jit(solution)/shard_map/ppermute | solution.py:591
  82.0 18.6 %copy-start = (bf16[24,8,1024]{2,1,0:T(8,128)(2,1)}, bf16[24,8,1024]{2,1,0:T(8,128)(2,1)S(1)}, u32[]{:S(2)}) copy-start(bf16[24,8,1024]{2,1,0:T(8,128)(2,1)S(1)} %collective-permute-done.7.rest_1_) | copy-start | bytes 1179652
  82.0 8.2 %collective-permute-start.11 = (bf16[24,8,1024]{2,1,0:T(8,128)(2,1)S(1)}, bf16[24,8,1024]{2,1,0:T(8,128)(2,1)S(1)}, u32[]{:S(2)}, u32[]{:S(2)}) collective-permute-start(bf16[24,8,1024]{2,1,0:T(8,128)(2,1)S(1)} %collective-permute-done.7.rest_1_), channel_id=1, source_target_pairs={{0,28},{1,5},{2,30},{3,7},{4,0},{5,9},{6,2},{7,11},{8,4},{9,13},{1... | collective-permute-start | bytes 1179656 | tf_op jit(solution)/shard_map/ppermute | solution.py:597
  129.2 30.9 %collective-permute-start.13 = (bf16[64,32,128]{2,1,0:T(8,128)(2,1)}, bf16[64,32,128]{2,1,0:T(8,128)(2,1)S(1)}, u32[]{:S(2)}, u32[]{:S(2)}) collective-permute-start(bf16[64,32,128]{2,1,0:T(8,128)(2,1)} %get-tuple-element.64), channel_id=1, source_target_pairs={{0,2},{1,31},{2,0},{3,29},{4,6},{5,3},{6,4},{7,1},{8,10},{9,7},{10... | collective-permute-start | bytes 1572872 | tf_op jit(solution)/shard_map/ppermute | solution.py:626
  129.2 30.9 %collective-permute-start.12 = (bf16[64,32,128]{2,1,0:T(8,128)(2,1)}, bf16[64,32,128]{2,1,0:T(8,128)(2,1)S(1)}, u32[]{:S(2)}, u32[]{:S(2)}) collective-permute-start(bf16[64,32,128]{2,1,0:T(8,128)(2,1)} %get-tuple-element.63), channel_id=1, source_target_pairs={{0,0},{1,29},{2,2},{3,31},{4,4},{5,1},{6,6},{7,3},{8,8},{9,5},{10,... | collective-permute-start | bytes 1572872 | tf_op jit(solution)/shard_map/ppermute | solution.py:626
  130.9 42.5 %collective-permute-start.15 = (bf16[64,32,128]{2,1,0:T(8,128)(2,1)}, bf16[64,32,128]{2,1,0:T(8,128)(2,1)S(1)}, u32[]{:S(2)}, u32[]{:S(2)}) collective-permute-start(bf16[64,32,128]{2,1,0:T(8,128)(2,1)} %get-tuple-element.66), channel_id=1, source_target_pairs={{0,3},{1,30},{2,1},{3,28},{4,7},{5,2},{6,5},{7,0},{8,11},{9,6},{10... | collective-permute-start | bytes 1572872 | tf_op jit(solution)/shard_map/ppermute | solution.py:626
  130.9 42.5 %collective-permute-start.14 = (bf16[64,32,128]{2,1,0:T(8,128)(2,1)}, bf16[64,32,128]{2,1,0:T(8,128)(2,1)S(1)}, u32[]{:S(2)}, u32[]{:S(2)}) collective-permute-start(bf16[64,32,128]{2,1,0:T(8,128)(2,1)} %get-tuple-element.65), channel_id=1, source_target_pairs={{0,1},{1,28},{2,3},{3,30},{4,5},{5,0},{6,7},{7,2},{8,9},{9,4},{10,... | collective-permute-start | bytes 1572872 | tf_op jit(solution)/shard_map/ppermute | solution.py:626
  (2 other events, 9.4 us)

commit v11 on v10

--- a/solution.py
+++ b/solution.py
@@ -39,46 +39,50 @@
     return window.astype(np.float32), waves.astype(np.float32), cast(segment), cast(lag)
 
 
-def section_sums(odd_ref, dead_ref, sec_ref, x_ref, whole_ref, out_ref, half_ref, tail_ref, sem):
-    chans, wins, ns = x_ref.shape
-    first = pl.program_id(0) * chans
-    width, length = half_ref.shape[0], tail_ref.shape[0]
+def section_sums(odd_ref, dead_ref, sec_ref, x_hbm, out_ref, half_hbm, tail_hbm, x, in_sem, sem):
+    chans, wins, ns = x.shape
+    width, length = half_hbm.shape[0], tail_hbm.shape[0]
     odd = odd_ref[0]
-    copies = [
-        pltpu.make_async_copy(whole_ref.at[pl.ds(odd * width, width)], half_ref, sem.at[0]),
+    part = chans // STEPS
+    arriving = [
         pltpu.make_async_copy(
-            whole_ref.at[pl.ds((2 - odd) * width - length, length)], tail_ref, sem.at[1]
+            x_hbm.at[pl.ds(n * part, part)], x.at[pl.ds(n * part, part)], in_sem.at[n]
+        )
+        for n in range(STEPS)
+    ]
+    for copy in arriving:
+        copy.start()
+    leaving = [
+        pltpu.make_async_copy(x.at[pl.ds(odd * width, width)], half_hbm, sem.at[0]),
+        pltpu.make_async_copy(
+            x.at[pl.ds((2 - odd) * width - length, length)], tail_hbm, sem.at[1]
         ),
     ]
 
-    @pl.when(pl.program_id(0) == 0)
-    def _():
-        out_ref[...] = jnp.zeros_like(out_ref)
-        for copy in copies:
-            copy.start()
-
     def body(c, carry):
-        value = x_ref[c].astype(F32)
-        live = 1 - dead_ref[first + c]
+        value = x[c].astype(F32)
+        live = 1 - dead_ref[c]
         sums, counts = carry
-        weights = [jnp.where(sec_ref[first + c] == s, live, 0).astype(F32) for s in range(NSEC)]
+        weights = [jnp.where(sec_ref[c] == s, live, 0).astype(F32) for s in range(NSEC)]
         return (
             tuple(sums[s] + weights[s] * value for s in range(NSEC)),
             tuple(counts[s] + weights[s] for s in range(NSEC)),
         )
 
     zero = jnp.zeros((wins, ns), F32)
-    sums, counts = lax.fori_loop(
-        0, chans, body, ((zero,) * NSEC, (jnp.float32(0),) * NSEC), unroll=8
-    )
+    carry = ((zero,) * NSEC, (jnp.float32(0),) * NSEC)
+    for n, copy in enumerate(arriving):
+        copy.wait()
+        if n == STEPS - 1:
+            for out in leaving:
+                out.start()
+        carry = lax.fori_loop(n * part, (n + 1) * part, body, carry, unroll=8)
+    sums, counts = carry
     for s in range(NSEC):
-        out_ref[s, :, :ns] += sums[s]
-        out_ref[s, :, ns:] += jnp.zeros((wins, LANE), F32) + counts[s]
-
-    @pl.when(pl.program_id(0) == pl.num_programs(0) - 1)
-    def _():
-        for copy in copies:
-            copy.wait()
+        out_ref[s, :, :ns] = sums[s]
+        out_ref[s, :, ns:] = jnp.zeros((wins, LANE), F32) + counts[s]
+    for out in leaving:
+        out.wait()
 
 
 def circulant_kernel(filter_ref, out_ref):
@@ -560,23 +564,24 @@
         lax.dynamic_slice_in_dim(flags, odd * width, width, 1), both, halo_pairs
     )
     smem = pl.BlockSpec(memory_space=pltpu.SMEM)
-    steps = 4
     anywhere = pl.BlockSpec(memory_space=pl.ANY)
     sums, own_half, tail = pl.pallas_call(
         section_sums,
-        grid=(steps,),
         out_shape=[
             jax.ShapeDtypeStruct((NSEC, wins, ns + LANE), F32),
             jax.ShapeDtypeStruct((width, wins, ns), BF16),
             jax.ShapeDtypeStruct((width - head, wins, ns), BF16),
         ],
-        in_specs=[smem] * 3
-        + [pl.BlockSpec((chans // steps, wins, ns), lambda i: (i, 0, 0)), anywhere],
-        out_specs=[pl.BlockSpec((NSEC, wins, ns + LANE), lambda i: (0, 0, 0)), anywhere, anywhere],
-        scratch_shapes=[pltpu.SemaphoreType.DMA((2,))],
+        in_specs=[smem] * 3 + [anywhere],
+        out_specs=[pl.BlockSpec(memory_space=pltpu.VMEM), anywhere, anywhere],
+        scratch_shapes=[
+            pltpu.VMEM(samples.shape, BF16),
+            pltpu.SemaphoreType.DMA((STEPS,)),
+            pltpu.SemaphoreType.DMA((2,)),
+        ],
         compiler_params=pltpu.CompilerParams(vmem_limit_bytes=VMEM),
         cost_estimate=pl.CostEstimate(flops=1, bytes_accessed=1, transcendentals=0),
-    )(odd[None], dead_flags, section_ids, samples, samples)
+    )(odd[None], dead_flags, section_ids, samples)
     total, their_head = add_over(sums, "fibre", their_head)
     total, halo_flags, own_half, conv = lax.optimization_barrier(
         (total, halo_flags, own_half, conv)

time: 176 us -> 135 us (0.77)
  Pallas kernels: 101 us -> 58.4 us
    pallas_call x1, Pallas kernels: 46.5 us -> 4.12 us  [shards(): pl.pallas_call(section_sums, out_shape=[jax.ShapeDtypeStruct((NSEC, wins,...]
  transfers between devices with their start and end apart: 16 -> 16, of which waited for: 6 -> 5; matrix products, arithmetic and copies ran while one was open for 2% -> 3% of each run, Pallas kernels for 41% -> 22%
where the time goes in v11:
time: 135 us; the launch traced here: 134 us
  Pallas kernels  58.4 us (43%)
  waiting for transfers between devices  51.9 us (38%)
  starting transfers between devices  15.7 us (12%)
  other arithmetic  5.13 us (4%)
  local copies, waits for them, and re-layouts  2.62 us (2%)
    ppermute x4, waiting for transfers between devices, shards(): arrived.append(lax.ppermute(found[d], both, pairs).astype(F32))  40.4 us
    pallas_call x1, Pallas kernels, stacks(): pl.pallas_call(functools.partial(stack_kernel, places, scale, shares), ou...  28.5 us
    pallas_call x2, Pallas kernels, segments(): pl.pallas_call(functools.partial(segments_kernel, places, wanted, len(tot...  23.2 us
    ppermute x1, waiting for transfers between devices, shards(): halo_tail = lax.ppermute(forward, both, halo_pairs)  8.07 us
    ppermute x4, starting transfers between devices, shards(): arrived.append(lax.ppermute(found[d], both, pairs).astype(F32))  4.58 us
    pallas_call x1, Pallas kernels, shards(): pl.pallas_call(section_sums, out_shape=[jax.ShapeDtypeStruct((NSEC, wins,...  4.12 us
    ppermute x4, starting transfers between devices, add_over(): lax.ppermute(value, axis, [(i, i ^ s) for i in range(count)])  3.73 us
  transfers between devices with their start and end apart: 16, of which 5 were waited for; matrix products, arithmetic and copies ran while one was open for 3% of the time, Pallas kernels for 22%

profile of v11, /device:TPU:19, one launch (start us, length us, event | category | flops | bytes accessed | tf_op | source)
XLA Modules:
  0.0 133.9 jit_solution(1992562396398856175)
XLA Ops:
  0.0 1.2 constant_dynamic-slice_fusion.1
  1.2 1.4 %collective-permute-start.4 = (bf16[40,8,1024]{2,1,0:T(8,128)(2,1)S(1)}, bf16[40,8,1024]{2,1,0:T(8,128)(2,1)}, u32[]{:S(2)}, u32[]{:S(2)}) collective-permute-start(bf16[40,8,1024]{2,1,0:T(8,128)(2,1)S(1)} %constant_dynamic-slice_fusion.1), channel_id=1, source_target_pairs={{0,1},{1,0},{2,3},{3,2},{4,5},{5,4},{6,7},{7,6},{8,9},{9,8},{10,11... | collective-permute-start | bytes 1966088 | tf_op jit(solution)/shard_map/ppermute | solution.py:559
  2.5 4.1 %shard_map.82 = (f32[2,8,1152]{2,1,0:T(8,128)}, bf16[64,8,1024]{2,1,0:T(8,128)(2,1)}, bf16[24,8,1024]{2,1,0:T(8,128)(2,1)}) custom-call(s32[1]{0:T(128)} %bitcast.1.odd_ref, s32[128]{0:T(128)} %dead_ref.1, s32[128]{0:T(128)} %sec_ref.1, bf16[128,8,1024]{2,1,0:T(8,128)(2,1)} %rest_1_.1), custom_call_target="tpu_custom_call" | custom-call | flops 1 | bytes 1 | tf_op jit(solution)/shard_map/pallas_call | solution.py:568
  6.7 1.0 collective-permute-start
  7.8 1.0 collective-permute-done
  8.8 0.9 add.29
  10.0 1.2 collective-permute-start.2
  11.3 1.2 collective-permute-start.3
  12.4 2.4 %multiply_reduce_fusion = f32[1024]{0:T(1024)} fusion(f32[512,1024]{1,0:T(8,128)} %constant.33.clone, f32[512]{0:T(512)S(1)} %copy-done.5), kind=kLoop, calls=%fused_computation.1 | loop fusion | flops 1047552 | bytes 2103296 | tf_op jit(solution)/shard_map/reduce_sum | solution.py:542
  14.8 2.6 %shard_map.83.rest_3_.rest_6_.rest_5_ = bf16[1024,1024]{1,0:T(8,128)(2,1)} custom-call(f32[1,1024]{1,0:T(1,128)} %bitcast.5), custom_call_target="tpu_custom_call" | custom-call | flops 1 | bytes 1 | tf_op jit(solution)/shard_map/pallas_call | solution.py:543
  17.5 1.2 collective-permute-start.9
  18.8 2.2 %collective-permute-start.6 = (f32[2,8,1152]{2,1,0:T(8,128)S(1)}, f32[2,8,1152]{2,1,0:T(8,128)S(1)}, u32[]{:S(2)}, u32[]{:S(2)}) collective-permute-start(f32[2,8,1152]{2,1,0:T(8,128)S(1)} %add_add_fusion.rest_0_), channel_id=1, source_target_pairs={{0,1},{1,0},{2,3},{3,2},{4,5},{5,4},{6,7},{7,6},{8,9},{9,8},{10,11... | collective-permute-start | bytes 221192 | tf_op jit(solution)/shard_map/ppermute | solution.py:589
  21.0 2.4 %collective-permute-done.6.rest_1_.rest_3_ = f32[2,8,1152]{2,1,0:T(8,128)S(1)} collective-permute-done((f32[2,8,1152]{2,1,0:T(8,128)S(1)}, f32[2,8,1152]{2,1,0:T(8,128)S(1)}, u32[]{:S(2)}, u32[]{:S(2)}) %collective-permute-start.6) | collective-permute-done | bytes 73760 | tf_op jit(solution)/shard_map/ppermute | solution.py:589
  23.4 1.4 %collective-permute-start.7 = (bf16[24,8,1024]{2,1,0:T(8,128)(2,1)}, bf16[24,8,1024]{2,1,0:T(8,128)(2,1)S(1)}, u32[]{:S(2)}, u32[]{:S(2)}) collective-permute-start(bf16[24,8,1024]{2,1,0:T(8,128)(2,1)} %get-tuple-element.48), channel_id=1, source_target_pairs={{0,1},{1,0},{2,3},{3,2},{4,5},{5,4},{6,7},{7,6},{8,9},{9,8},{10,11... | collective-permute-start | bytes 1179656 | tf_op jit(solution)/shard_map/ppermute | solution.py:594
  24.9 0.9 collective-permute-start.10
  26.5 13.5 %shard_map.84 = (bf16[128,1,128,128]{3,2,1,0:T(8,128)(2,1)}, bf16[128,128,128]{2,1,0:T(8,128)(2,1)}) custom-call(s32[1]{0:T(128)} %bitcast.1.odd_ref, s32[2,128]{1,0:T(2,128)} %copy-done.3, f32[2,8,1152]{2,1,0:T(8,128)} %copy-done.2, bf16[128,8,1024]{2,1,0:T(8,128)(2,1)} %rest_1_.1, f32[8,1024]{1,0:T(8,128)} %jit_solution_.3.rest_2_.rest_5_.rest_4_, ...), custom_call_target="tpu_custom_call" | custom-call | flops 3758096384 | bytes 16777216 | tf_op jit(solution)/shard_map/pallas_call | solution.py:332
  40.1 8.1 %collective-permute-done.11.rest_4_ = bf16[24,8,1024]{2,1,0:T(8,128)(2,1)S(1)} collective-permute-done((bf16[24,8,1024]{2,1,0:T(8,128)(2,1)S(1)}, bf16[24,8,1024]{2,1,0:T(8,128)(2,1)S(1)}, u32[]{:S(2)}, u32[]{:S(2)}) %collective-permute-start.11) | collective-permute-done | bytes 393248 | tf_op jit(solution)/shard_map/ppermute | solution.py:602
  48.9 9.7 %shard_map.85 = (bf16[128,2,128,128]{3,2,1,0:T(8,128)(2,1)}, bf16[128,128,128]{2,1,0:T(8,128)(2,1)}) custom-call(s32[1]{0:T(128)} %bitcast.1.odd_ref, s32[2,64]{1,0:T(2,128)} %copy-done.9, f32[2,8,1152]{2,1,0:T(8,128)} %copy-done.2, f32[2,8,1152]{2,1,0:T(8,128)} %copy-done.1, bf16[64,8,1024]{2,1,0:T(8,128)(2,1)} %collective-permute-done.9.rest_2_, ...), custom_call_target="tpu_custom_call" | custom-call | flops 3758096384 | bytes 16777216 | tf_op jit(solution)/shard_map/pallas_call | solution.py:332
  58.6 28.5 %shard_map.86 = (bf16[64,32,128]{2,1,0:T(8,128)(2,1)}, bf16[64,32,128]{2,1,0:T(8,128)(2,1)}, bf16[64,32,128]{2,1,0:T(8,128)(2,1)}, bf16[64,32,128]{2,1,0:T(8,128)(2,1)}) custom-call(s32[1]{0:T(128)} %bitcast.me_ref, s32[2,128]{1,0:T(2,128)} %copy-done.3, bf16[40,8,1024]{2,1,0:T(8,128)(2,1)} %collective-permute-done.4.rest_0_, bf16[24,8,1024]{2,1,0:T(8,128)(2,1)} %copy-done, ...), custom_call_target="tpu_custom_call" | custom-call | flops 4294967296 | bytes 20971520 | tf_op jit(solution)/shard_map/pallas_call | solution.py:492
  87.2 1.7 %collective-permute-start.12 = (bf16[64,32,128]{2,1,0:T(8,128)(2,1)}, bf16[64,32,128]{2,1,0:T(8,128)(2,1)S(1)}, u32[]{:S(2)}, u32[]{:S(2)}) collective-permute-start(bf16[64,32,128]{2,1,0:T(8,128)(2,1)} %get-tuple-element.63), channel_id=1, source_target_pairs={{0,0},{1,29},{2,2},{3,31},{4,4},{5,1},{6,6},{7,3},{8,8},{9,5},{10,... | collective-permute-start | bytes 1572872 | tf_op jit(solution)/shard_map/ppermute | solution.py:631
  88.9 2.8 %collective-permute-start.14 = (bf16[64,32,128]{2,1,0:T(8,128)(2,1)}, bf16[64,32,128]{2,1,0:T(8,128)(2,1)S(1)}, u32[]{:S(2)}, u32[]{:S(2)}) collective-permute-start(bf16[64,32,128]{2,1,0:T(8,128)(2,1)} %get-tuple-element.65), channel_id=1, source_target_pairs={{0,1},{1,28},{2,3},{3,30},{4,5},{5,0},{6,7},{7,2},{8,9},{9,4},{10,... | collective-permute-start | bytes 1572872 | tf_op jit(solution)/shard_map/ppermute | solution.py:631
  91.7 27.0 %collective-permute-done.13 = bf16[64,32,128]{2,1,0:T(8,128)(2,1)S(1)} collective-permute-done((bf16[64,32,128]{2,1,0:T(8,128)(2,1)}, bf16[64,32,128]{2,1,0:T(8,128)(2,1)S(1)}, u32[]{:S(2)}, u32[]{:S(2)}) %collective-permute-start.13) | collective-permute-done | bytes 524320 | tf_op jit(solution)/shard_map/ppermute | solution.py:631
  118.7 13.4 %collective-permute-done.15 = bf16[64,32,128]{2,1,0:T(8,128)(2,1)S(1)} collective-permute-done((bf16[64,32,128]{2,1,0:T(8,128)(2,1)}, bf16[64,32,128]{2,1,0:T(8,128)(2,1)S(1)}, u32[]{:S(2)}, u32[]{:S(2)}) %collective-permute-start.15) | collective-permute-done | bytes 524320 | tf_op jit(solution)/shard_map/ppermute | solution.py:631
  132.4 1.5 %pad_maximum_fusion = f32[128,32,128]{2,1,0:T(8,128)} fusion(f32[64,32,128]{2,1,0:T(8,128)S(1)} %get-tuple-element.68, f32[64,32,128]{2,1,0:T(8,128)S(1)} %get-tuple-element.67), kind=kLoop, calls=%fused_computation | loop fusion | flops 524288 | bytes 4194304 | tf_op jit(solution)/shard_map/concatenate | solution.py:634
  (42 shorter events, 2.5 us)
Async XLA Ops:
  0.0 7.7 %copy-start.6 = (s32[128]{0:T(128)S(1)}, s32[128]{0:T(128)}, u32[]{:S(2)}) copy-start(s32[128]{0:T(128)} %sec_ref.1) | copy-start | bytes 1540
  0.0 12.4 %copy-start.5 = (f32[512]{0:T(512)S(1)}, f32[512]{0:T(512)}, u32[]{:S(2)}) copy-start(f32[512]{0:T(512)} %param.9) | copy-start | bytes 6148
  1.2 16.3 %collective-permute-start.4 = (bf16[40,8,1024]{2,1,0:T(8,128)(2,1)S(1)}, bf16[40,8,1024]{2,1,0:T(8,128)(2,1)}, u32[]{:S(2)}, u32[]{:S(2)}) collective-permute-start(bf16[40,8,1024]{2,1,0:T(8,128)(2,1)S(1)} %constant_dynamic-slice_fusion.1), channel_id=1, source_target_pairs={{0,1},{1,0},{2,3},{3,2},{4,5},{5,4},{6,7},{7,6},{8,9},{9,8},{10,11... | collective-permute-start | bytes 1966088 | tf_op jit(solution)/shard_map/ppermute | solution.py:559
  6.7 2.1 %collective-permute-start = (f32[2,8,1152]{2,1,0:T(8,128)}, f32[2,8,1152]{2,1,0:T(8,128)S(1)}, u32[]{:S(2)}, u32[]{:S(2)}) collective-permute-start(f32[2,8,1152]{2,1,0:T(8,128)} %get-tuple-element.36), channel_id=1, source_target_pairs={{0,4},{4,0},{8,12},{12,8},{16,20},{20,16},{24,28},{28,24},{1,5},{5... | collective-permute-start | bytes 221192 | tf_op jit(solution)/shard_map/ppermute | solution.py:523
  7.7 9.7 %copy-start.3 = (s32[2,128]{1,0:T(2,128)}, s32[2,128]{1,0:T(2,128)S(1)}, u32[]{:S(2)}) copy-start(s32[2,128]{1,0:T(2,128)S(1)} %pad_add_fusion.flag_ref) | copy-start | bytes 3076
  7.8 9.7 %collective-permute-start.5 = (s32[2,64]{1,0:T(2,128)S(1)}, s32[2,64]{1,0:T(2,128)S(1)}, u32[]{:S(2)}, u32[]{:S(2)}) collective-permute-start(s32[2,64]{1,0:T(2,128)S(1)} %constant_dynamic-slice_fusion), channel_id=1, source_target_pairs={{0,28},{1,5},{2,30},{3,7},{4,0},{5,9},{6,2},{7,11},{8,4},{9,13},{1... | collective-permute-start | bytes 1544 | tf_op jit(solution)/shard_map/ppermute | solution.py:563
  9.7 16.1 %copy-start.4 = (f32[1024]{0:T(1024)S(1)}, f32[1024]{0:T(1024)}, u32[]{:S(2)}) copy-start(f32[1024]{0:T(1024)} %constant.36.clone) | copy-start | bytes 12292
  9.7 7.7 %collective-permute-start.1 = (f32[2,8,1152]{2,1,0:T(8,128)S(1)}, f32[2,8,1152]{2,1,0:T(8,128)S(1)}, u32[]{:S(2)}, u32[]{:S(2)}) collective-permute-start(f32[2,8,1152]{2,1,0:T(8,128)S(1)} %add.29), channel_id=1, source_target_pairs={{0,8},{4,12},{8,0},{12,4},{16,24},{20,28},{24,16},{28,20},{1,9},{5... | collective-permute-start | bytes 221192 | tf_op jit(solution)/shard_map/ppermute | solution.py:523
  10.0 7.4 %collective-permute-start.2 = (f32[2,8,1152]{2,1,0:T(8,128)S(1)}, f32[2,8,1152]{2,1,0:T(8,128)S(1)}, u32[]{:S(2)}, u32[]{:S(2)}) collective-permute-start(f32[2,8,1152]{2,1,0:T(8,128)S(1)} %add.29), channel_id=1, source_target_pairs={{0,16},{4,20},{8,24},{12,28},{16,0},{20,4},{24,8},{28,12},{1,17},{... | collective-permute-start | bytes 221192 | tf_op jit(solution)/shard_map/ppermute | solution.py:523
  11.3 6.2 %collective-permute-start.3 = (f32[2,8,1152]{2,1,0:T(8,128)S(1)}, f32[2,8,1152]{2,1,0:T(8,128)S(1)}, u32[]{:S(2)}, u32[]{:S(2)}) collective-permute-start(f32[2,8,1152]{2,1,0:T(8,128)S(1)} %add.29), channel_id=1, source_target_pairs={{0,24},{4,28},{8,16},{12,20},{16,8},{20,12},{24,0},{28,4},{1,25},{... | collective-permute-start | bytes 221192 | tf_op jit(solution)/shard_map/ppermute | solution.py:523
  17.5 8.9 %copy-start.2 = (f32[2,8,1152]{2,1,0:T(8,128)}, f32[2,8,1152]{2,1,0:T(8,128)S(1)}, u32[]{:S(2)}) copy-start(f32[2,8,1152]{2,1,0:T(8,128)S(1)} %add_add_fusion.rest_0_) | copy-start | bytes 221188
  17.5 22.4 %copy-start.9 = (s32[2,64]{1,0:T(2,128)}, s32[2,64]{1,0:T(2,128)S(1)}, u32[]{:S(2)}) copy-start(s32[2,64]{1,0:T(2,128)S(1)} %collective-permute-done.5.flag_ref) | copy-start | bytes 1540
  17.5 30.6 %collective-permute-start.9 = (bf16[64,8,1024]{2,1,0:T(8,128)(2,1)}, bf16[64,8,1024]{2,1,0:T(8,128)(2,1)}, u32[]{:S(2)}, u32[]{:S(2)}) collective-permute-start(bf16[64,8,1024]{2,1,0:T(8,128)(2,1)} %get-tuple-element.49), channel_id=1, source_target_pairs={{0,28},{1,5},{2,30},{3,7},{4,0},{5,9},{6,2},{7,11},{8,4},{9,13},{1... | collective-permute-start | bytes 3145736 | tf_op jit(solution)/shard_map/ppermute | solution.py:590
  18.8 4.6 %collective-permute-start.6 = (f32[2,8,1152]{2,1,0:T(8,128)S(1)}, f32[2,8,1152]{2,1,0:T(8,128)S(1)}, u32[]{:S(2)}, u32[]{:S(2)}) collective-permute-start(f32[2,8,1152]{2,1,0:T(8,128)S(1)} %add_add_fusion.rest_0_), channel_id=1, source_target_pairs={{0,1},{1,0},{2,3},{3,2},{4,5},{5,4},{6,7},{7,6},{8,9},{9,8},{10,11... | collective-permute-start | bytes 221192 | tf_op jit(solution)/shard_map/ppermute | solution.py:589
  23.4 16.5 %copy-start.1 = (f32[2,8,1152]{2,1,0:T(8,128)}, f32[2,8,1152]{2,1,0:T(8,128)S(1)}, u32[]{:S(2)}) copy-start(f32[2,8,1152]{2,1,0:T(8,128)S(1)} %collective-permute-done.6.rest_1_.rest_3_) | copy-start | bytes 221188
  23.4 16.5 %collective-permute-start.7 = (bf16[24,8,1024]{2,1,0:T(8,128)(2,1)}, bf16[24,8,1024]{2,1,0:T(8,128)(2,1)S(1)}, u32[]{:S(2)}, u32[]{:S(2)}) collective-permute-start(bf16[24,8,1024]{2,1,0:T(8,128)(2,1)} %get-tuple-element.48), channel_id=1, source_target_pairs={{0,1},{1,0},{2,3},{3,2},{4,5},{5,4},{6,7},{7,6},{8,9},{9,8},{10,11... | collective-permute-start | bytes 1179656 | tf_op jit(solution)/shard_map/ppermute | solution.py:594
  24.8 33.7 %collective-permute-start.8 = (bf16[64,8,1024]{2,1,0:T(8,128)(2,1)}, bf16[64,8,1024]{2,1,0:T(8,128)(2,1)}, u32[]{:S(2)}, u32[]{:S(2)}) collective-permute-start(bf16[64,8,1024]{2,1,0:T(8,128)(2,1)} %get-tuple-element.49), channel_id=1, source_target_pairs={{0,1},{1,0},{2,3},{3,2},{4,5},{5,4},{6,7},{7,6},{8,9},{9,8},{10,11... | collective-permute-start | bytes 3145736 | tf_op jit(solution)/shard_map/ppermute | solution.py:595
  24.9 15.2 %collective-permute-start.10 = (bf16[40,8,1024]{2,1,0:T(8,128)(2,1)}, bf16[40,8,1024]{2,1,0:T(8,128)(2,1)}, u32[]{:S(2)}, u32[]{:S(2)}) collective-permute-start(bf16[40,8,1024]{2,1,0:T(8,128)(2,1)} %collective-permute-done.4.rest_0_), channel_id=1, source_target_pairs={{0,28},{1,5},{2,30},{3,7},{4,0},{5,9},{6,2},{7,11},{8,4},{9,13},{1... | collective-permute-start | bytes 1966088 | tf_op jit(solution)/shard_map/ppermute | solution.py:596
  40.0 18.6 %copy-start = (bf16[24,8,1024]{2,1,0:T(8,128)(2,1)}, bf16[24,8,1024]{2,1,0:T(8,128)(2,1)S(1)}, u32[]{:S(2)}) copy-start(bf16[24,8,1024]{2,1,0:T(8,128)(2,1)S(1)} %collective-permute-done.7.rest_1_) | copy-start | bytes 1179652
  40.0 8.2 %collective-permute-start.11 = (bf16[24,8,1024]{2,1,0:T(8,128)(2,1)S(1)}, bf16[24,8,1024]{2,1,0:T(8,128)(2,1)S(1)}, u32[]{:S(2)}, u32[]{:S(2)}) collective-permute-start(bf16[24,8,1024]{2,1,0:T(8,128)(2,1)S(1)} %collective-permute-done.7.rest_1_), channel_id=1, source_target_pairs={{0,28},{1,5},{2,30},{3,7},{4,0},{5,9},{6,2},{7,11},{8,4},{9,13},{1... | collective-permute-start | bytes 1179656 | tf_op jit(solution)/shard_map/ppermute | solution.py:602
  87.1 31.6 %collective-permute-start.13 = (bf16[64,32,128]{2,1,0:T(8,128)(2,1)}, bf16[64,32,128]{2,1,0:T(8,128)(2,1)S(1)}, u32[]{:S(2)}, u32[]{:S(2)}) collective-permute-start(bf16[64,32,128]{2,1,0:T(8,128)(2,1)} %get-tuple-element.64), channel_id=1, source_target_pairs={{0,2},{1,31},{2,0},{3,29},{4,6},{5,3},{6,4},{7,1},{8,10},{9,7},{10... | collective-permute-start | bytes 1572872 | tf_op jit(solution)/shard_map/ppermute | solution.py:631
  87.2 31.5 %collective-permute-start.12 = (bf16[64,32,128]{2,1,0:T(8,128)(2,1)}, bf16[64,32,128]{2,1,0:T(8,128)(2,1)S(1)}, u32[]{:S(2)}, u32[]{:S(2)}) collective-permute-start(bf16[64,32,128]{2,1,0:T(8,128)(2,1)} %get-tuple-element.63), channel_id=1, source_target_pairs={{0,0},{1,29},{2,2},{3,31},{4,4},{5,1},{6,6},{7,3},{8,8},{9,5},{10,... | collective-permute-start | bytes 1572872 | tf_op jit(solution)/shard_map/ppermute | solution.py:631
  88.9 43.1 %collective-permute-start.15 = (bf16[64,32,128]{2,1,0:T(8,128)(2,1)}, bf16[64,32,128]{2,1,0:T(8,128)(2,1)S(1)}, u32[]{:S(2)}, u32[]{:S(2)}) collective-permute-start(bf16[64,32,128]{2,1,0:T(8,128)(2,1)} %get-tuple-element.66), channel_id=1, source_target_pairs={{0,3},{1,30},{2,1},{3,28},{4,7},{5,2},{6,5},{7,0},{8,11},{9,6},{10... | collective-permute-start | bytes 1572872 | tf_op jit(solution)/shard_map/ppermute | solution.py:631
  88.9 43.1 %collective-permute-start.14 = (bf16[64,32,128]{2,1,0:T(8,128)(2,1)}, bf16[64,32,128]{2,1,0:T(8,128)(2,1)S(1)}, u32[]{:S(2)}, u32[]{:S(2)}) collective-permute-start(bf16[64,32,128]{2,1,0:T(8,128)(2,1)} %get-tuple-element.65), channel_id=1, source_target_pairs={{0,1},{1,28},{2,3},{3,30},{4,5},{5,0},{6,7},{7,2},{8,9},{9,4},{10,... | collective-permute-start | bytes 1572872 | tf_op jit(solution)/shard_map/ppermute | solution.py:631
  (2 other events, 8.4 us)

commit v12 on v11

--- a/solution.py
+++ b/solution.py
@@ -92,8 +92,8 @@
         out_ref[t : t + 16, :] = pltpu.roll(block, t, 1, stride=1, stride_axis=0).astype(BF16)
 
 
-def segment_factors(places, want, repeat, odd, flag_ref, tot, x, hann, conv, seg, work, copied, emit):
-    common, clean, mass, square, rows, series, series_a, stage = work
+def segment_factors(places, odd, flag_ref, tot, x, hann, conv, seg, work, copied, first=None):
+    common, clean, mass, square, rows, series_all, stage = work
     _, wins, ns = x[0].shape
     chans = sum(piece.shape[0] for piece in x)
     pitch = wins + 1
@@ -102,23 +102,22 @@
     blocks = ns // half
     jw = blocks * wins
     jpitch = jw + 1
-    held = flag_ref.shape[1]
     for copy in copied["first"]:
         copy.wait()
     for g in range(len(tot)):
         for s in range(NSEC):
             common[g * NSEC + s] = tot[g][s, :, :ns] / jnp.maximum(tot[g][s, :, ns : ns + 1], 1.0)
     sign = 1.0 - 2.0 * (lax.broadcasted_iota(jnp.int32, (chans, LANE), 1) % 2).astype(F32)
-    lower = lax.broadcasted_iota(jnp.int32, (1, LANE), 1) < LANE // 2
-
-    for number, (group, even_base, odd_base) in enumerate(places):
+
+    for number, (group, base, flags) in enumerate(places):
         piece = x[number]
         length = piece.shape[0]
-        base = even_base + odd * (odd_base - even_base)
+        base = base[0] + odd * (base[1] - base[0])
+        flags = flags[0] + odd * (flags[1] - flags[0])
 
         def clean_channel(c, _):
             at = base + c
-            flag = lax.rem(at, held)
+            flag = flags + c
             live = (1 - flag_ref[0, flag]).astype(F32)
             value = (piece[c].astype(F32) - common[group * NSEC + flag_ref[1, flag]]) * (
                 hann[...] * live
@@ -139,7 +138,8 @@
     for copy in copied["tables"]:
         copy.wait()
 
-    def some_windows(step, _):
+    for step in range(wins // TOGETHER):
+        series = series_all.at[step]
         for i in range(TOGETHER):
             window = pl.ds(step * TOGETHER + i, chans, stride=pitch)
             total = mass[window, :]
@@ -173,26 +173,13 @@
             )
             place(1, j, b)
 
-        @pl.when(want)
-        def _():
-            source = series
-            if repeat:
-                source = series_a
-                for i in range(TOGETHER):
-                    value = series[:, i * chans : (i + 1) * chans]
-                    turned = jnp.concatenate(
-                        [value[:, chans // 2 :], value[:, : chans // 2]], axis=1
-                    )
-                    series_a[:, i * chans : (i + 1) * chans] = jnp.where(lower, value, turned)
+        if first is not None:
+            source = first(step, series)
             for j in range(blocks):
                 a = jnp.dot(
                     seg[...], source[j * half : j * half + size, :], preferred_element_type=F32
                 )
                 place(0, j, a)
-
-        return 0
-
-    lax.fori_loop(0, wins // TOGETHER, some_windows, 0)
 
     def factor(which, k, turn=False):
         real, imag = [
@@ -203,20 +190,14 @@
         return jnp.concatenate([real.astype(BF16), imag.astype(BF16)], axis=0)
 
     def first_factor(k, put):
-        if repeat:
-            put(0, slice(None), jnp.where(lower, factor(0, k), factor(0, k, True)).T)
-        else:
-            width = chans // 2
-            for part in range(2):
-                value = factor(0, k, part == 1).T
-                for group in range(2):
-                    put(
-                        group,
-                        slice(part * width, (part + 1) * width),
-                        value[group * width : (group + 1) * width],
-                    )
-
-    emit(want, first_factor, lambda k: factor(1, k))
+        width = chans // 2
+        for part in range(2):
+            value = factor(0, k, part == 1).T
+            rows_at = slice(part * width, (part + 1) * width)
+            put(1, rows_at, value[:width])
+            put(0, rows_at, value[width:])
+
+    return first_factor, lambda k: factor(1, k)
 
 
 def work_shapes(groups, chans, wins, ns):
@@ -228,19 +209,37 @@
         pltpu.VMEM((chans * (wins + 1), LANE), F32),
         pltpu.VMEM((chans * (wins + 1), LANE), F32),
         pltpu.VMEM((TOGETHER * chans, ns), BF16),
-        pltpu.VMEM((ns + half, TOGETHER * chans), BF16),
-        pltpu.VMEM((ns + half, TOGETHER * chans), BF16),
+        pltpu.VMEM((wins // TOGETHER, ns + half, TOGETHER * chans), BF16),
         pltpu.VMEM((2, rows, chans), F32),
     ]
 
 
-def input_copies(first, x, tables_in, sem):
+class Choice:
+    def __init__(self, odd, sources, target, sem):
+        self.options = [
+            (odd == side, pltpu.make_async_copy(source, target, sem))
+            for side, source in enumerate(sources)
+        ]
+
+    def start(self):
+        for here, copy in self.options:
+            pl.when(here)(copy.start)
+
+    def wait(self):
+        for here, copy in self.options:
+            pl.when(here)(copy.wait)
+
+
+def input_copies(odd, first, x, tables_in, sem):
     copied = {"first": [], "x": [], "tables": []}
     used = 0
 
     def copy(source, target):
         nonlocal used
-        made = pltpu.make_async_copy(source, target, sem.at[used])
+        if isinstance(source, tuple):
+            made = Choice(odd, source, target, sem.at[used])
+        else:
+            made = pltpu.make_async_copy(source, target, sem.at[used])
         made.start()
         used += 1
         return made
@@ -249,205 +248,243 @@
     for source, target in x:
         parts = max(target.shape[0] // PART, 1)
         part = target.shape[0] // parts
+        rows = [pl.ds(n * part, part) for n in range(parts)]
         copied["x"].append(
             [
-                copy(source.at[pl.ds(n * part, part)], target.at[pl.ds(n * part, part)])
-                for n in range(parts)
+                copy(
+                    tuple(option.at[here] for option in source)
+                    if isinstance(source, tuple)
+                    else source.at[here],
+                    target.at[here],
+                )
+                for here in rows
             ]
         )
     copied["tables"] = [copy(*pair) for pair in tables_in]
     return copied
 
 
-def segments_kernel(places, wanted, groups, odd_ref, flag_ref, *rest):
-    count = len(places)
-    tot_hbm, rest = rest[:groups], rest[groups:]
-    x_hbm, rest = rest[:count], rest[count:]
-    hann_hbm, conv_hbm, seg_hbm, a_hbm, b_hbm = rest[:5]
-    tot, rest = rest[5 : 5 + groups], rest[5 + groups :]
-    x, rest = rest[:count], rest[count:]
-    hann, conv, seg = rest[:3]
-    work, (a_out, b_out, in_sem, out_sem) = rest[3:-4], rest[-4:]
+def own_kernel(places, odd_ref, flag_ref, *rest):
+    tot_hbm, x_hbm, hann_hbm, conv_hbm, seg_hbm, b_hbm, p_hbm = rest[:7]
+    tot, x, hann, conv, seg = rest[7:12]
+    work, (b_out, in_sem, out_sem, p_sem) = rest[12:-4], rest[-4:]
+    odd = odd_ref[0]
     copied = input_copies(
-        list(zip(tot_hbm, tot)) + [(hann_hbm, hann)],
-        list(zip(x_hbm, x)),
+        odd,
+        [(tot_hbm, tot), (hann_hbm, hann)],
+        [(x_hbm, x)],
         [(conv_hbm, conv), (seg_hbm, seg)],
         in_sem,
     )
-    bins = b_out.shape[0]
-    step = bins // STEPS
-
-    def emit(want, first_factor, second_factor):
-        def first(k, _):
-            def put(group, rows, value):
-                a_out[k, group, rows] = value
-
-            first_factor(k, put)
+    _, second = segment_factors(
+        places, odd, flag_ref, [tot], [x], hann, conv, seg, work, copied
+    )
+
+    def put_second(k, stage):
+        stage[k] = second(k)
+
+    kept = pltpu.make_async_copy(work[-2], p_hbm, p_sem)
+    kept.start()
+    send_factor(put_second, b_out, b_hbm, out_sem)
+    kept.wait()
+
+
+def send_factor(factor, stage, target, sem):
+    step = stage.shape[0] // STEPS
+    copies = []
+    for n in range(STEPS):
+        part = pl.ds(n * step, step)
+
+        def one_bin(k, _):
+            factor(k, stage)
             return 0
 
-        def second(k, _):
-            b_out[k] = second_factor(k)
+        lax.fori_loop(n * step, (n + 1) * step, one_bin, 0, unroll=8)
+        copies.append(pltpu.make_async_copy(stage.at[part], target.at[part], sem.at[n]))
+        copies[-1].start()
+    for copy in copies:
+        copy.wait()
+
+
+def second_kernel(places, odd_ref, flag_ref, *rest):
+    tot_hbm, (even_hbm, odd_hbm), rest = rest[:2], (rest[2:4], rest[4:6]), rest[6:]
+    halo_hbm, hann_hbm, conv_hbm, seg_hbm, p_hbm, a_hbm, b_hbm = rest[:7]
+    tot, x, rest = rest[7:9], rest[9:12], rest[12:]
+    hann, conv, seg, own, mixed, a_out, b_out = rest[:7]
+    work, (in_sem, p_sem, out_sem) = rest[7:-3], rest[-3:]
+    odd = odd_ref[0]
+    copied = input_copies(
+        odd,
+        list(zip(tot_hbm, tot)) + [(hann_hbm, hann)],
+        list(zip(zip(even_hbm, odd_hbm), x)) + [(halo_hbm, x[2])],
+        [(conv_hbm, conv), (seg_hbm, seg)],
+        in_sem,
+    )
+    kept = pltpu.make_async_copy(p_hbm, own, p_sem)
+    kept.start()
+    copied["tables"].append(kept)
+    chans = b_out.shape[2]
+    lane = lax.broadcasted_iota(jnp.int32, (1, chans), 1)
+
+    def first(step, series):
+        @pl.when(odd == 1)
+        def _():
+            mixed[...] = series[...]
+
+        @pl.when(odd == 0)
+        def _():
+            for i in range(TOGETHER):
+                columns = slice(i * chans, (i + 1) * chans)
+                value = own[step, :, columns]
+                turned = jnp.concatenate([value[:, chans // 2 :], value[:, : chans // 2]], axis=1)
+                mixed[:, columns] = jnp.where(lane < chans // 2, series[:, columns], turned)
+
+        return mixed
+
+    first_factor, second_factor = segment_factors(
+        places, odd, flag_ref, tot, x, hann, conv, seg, work, copied, first
+    )
+
+    def both_factors(k, stage):
+        def put(group, rows, value):
+            a_out[k, group, rows] = value
+
+        first_factor(k, put)
+        stage[k] = second_factor(k)
+
+    step = b_out.shape[0] // STEPS
+    copies = []
+    for n in range(STEPS):
+        part = pl.ds(n * step, step)
+
+        def one_bin(k, _):
+            both_factors(k, b_out)
             return 0
 
-        def send(n, source, target):
-            part = pl.ds(n % STEPS * step, step)
-            return pltpu.make_async_copy(source.at[part], target.at[part], out_sem.at[n])
-
-        @pl.when(want)
-        def _():
-            for n in range(STEPS):
-                lax.fori_loop(n * step, (n + 1) * step, first, 0, unroll=8)
-                send(n, a_out, a_hbm).start()
-
-        for n in range(STEPS):
-            lax.fori_loop(n * step, (n + 1) * step, second, 0, unroll=8)
-            send(STEPS + n, b_out, b_hbm).start()
-
-        @pl.when(want)
-        def _():
-            for n in range(STEPS):
-                send(n, a_out, a_hbm).wait()
-
-        for n in range(STEPS):
-            send(STEPS + n, b_out, b_hbm).wait()
-
-    odd = odd_ref[0]
-    segment_factors(
-        *(places, odd == wanted, wanted == 0, odd, flag_ref),
-        *(tot, x, hann, conv, seg, work, copied, emit),
-    )
-
-
-def segments(places, wanted, odd, flags, totals, pieces, hann, conv, seg):
-    chans = sum(x.shape[0] for x in pieces)
+        lax.fori_loop(n * step, (n + 1) * step, one_bin, 0, unroll=8)
+        for m, (source, target) in enumerate(((a_out, a_hbm), (b_out, b_hbm))):
+            copies.append(
+                pltpu.make_async_copy(source.at[part], target.at[part], out_sem.at[2 * n + m])
+            )
+            copies[-1].start()
+    for copy in copies:
+        copy.wait()
+
+
+def segments(places, side, flags, totals, pieces, series, hann, conv, seg):
+    chans = LANE
     _, wins, ns = pieces[0].shape
     size = seg.shape[0]
     half = size // 2
     depth = ns // half * wins * 2
     smem = pl.BlockSpec(memory_space=pltpu.SMEM)
     anywhere = pl.BlockSpec(memory_space=pl.ANY)
+    b_shape = jax.ShapeDtypeStruct((half, depth, chans), BF16)
+    p_shape = jax.ShapeDtypeStruct((wins // TOGETHER, ns + half, TOGETHER * chans), BF16)
+    a_shape = jax.ShapeDtypeStruct((half, 2, chans, depth), BF16)
+    scratch = lambda *values: [pltpu.VMEM(value.shape, value.dtype) for value in values]
     operands = list(totals) + list(pieces) + [hann, conv, seg]
-    a_shape = jax.ShapeDtypeStruct((half, 2 if wanted else 1, chans, depth), BF16)
-    b_shape = jax.ShapeDtypeStruct((half, depth, chans), BF16)
+    count = len(operands) + chans // PART
+    if series is None:
+        kernel, out = own_kernel, [b_shape, p_shape]
+        held = scratch(*operands)
+        last = scratch(b_shape) + [
+            pltpu.SemaphoreType.DMA((count,)),
+            pltpu.SemaphoreType.DMA((STEPS,)),
+            pltpu.SemaphoreType.DMA,
+        ]
+    else:
+        kernel, out = second_kernel, [a_shape, b_shape]
+        held = scratch(*totals, pieces[0], pieces[1], pieces[4], hann, conv, seg, series)
+        held += [pltpu.VMEM(p_shape.shape[1:], BF16)] + scratch(a_shape, b_shape)
+        last = [
+            pltpu.SemaphoreType.DMA((count,)),
+            pltpu.SemaphoreType.DMA,
+            pltpu.SemaphoreType.DMA((2 * STEPS,)),
+        ]
+        operands.append(series)
     return pl.pallas_call(
-        functools.partial(segments_kernel, places, wanted, len(totals)),
-        out_shape=[a_shape, b_shape],
+        functools.partial(kernel, places),
+        out_shape=out,
         in_specs=[smem] * 2 + [anywhere] * len(operands),
         out_specs=[anywhere] * 2,
-        scratch_shapes=[pltpu.VMEM(value.shape, value.dtype) for value in operands]
-        + work_shapes(len(totals), chans, wins, ns)
-        + [
-            pltpu.VMEM(a_shape.shape, BF16),
-            pltpu.VMEM(b_shape.shape, BF16),
-            pltpu.SemaphoreType.DMA((len(operands) + chans // PART,)),
-            pltpu.SemaphoreType.DMA((2 * STEPS,)),
-        ],
+        scratch_shapes=held + work_shapes(len(totals), chans, wins, ns) + last,
         compiler_params=pltpu.CompilerParams(vmem_limit_bytes=VMEM),
         cost_estimate=pl.CostEstimate(
             flops=2 * wins * chans * ns * (ns + 3 * size),
             bytes_accessed=16 * 1024 * 1024,
             transcendentals=0,
         ),
-    )(odd, flags, *operands)
+    )(side, flags, *operands)
 
 
 def stack_kernel(places, scale, shares, me_ref, flag_ref, *rest):
-    count = len(places)
-    x_hbm, rest = rest[:count], rest[count:]
+    even_hbm, odd_hbm, late_hbm, rest = rest[:2], rest[2:4], rest[4], rest[5:]
     tot_hbm, hann_hbm, conv_hbm, seg_hbm, lag_hbm = rest[:5]
-    left_hbm, rest = rest[5:9], rest[9:]
+    a_hbm, b0_hbm, b2_hbm, rest = *rest[5:8], rest[8:]
     outs, rest = rest[:shares], rest[shares:]
-    x, rest = rest[:count], rest[count:]
-    tot, hann, conv, seg, lag = rest[:5]
-    (a, b0, bh), rest = rest[5:8], rest[8:]
-    work, (b1, one, in_sem, late_sem) = rest[:-4], rest[-4:]
+    x, rest = rest[:3], rest[3:]
+    tot, hann, conv, seg, lag, a, b0, b2 = rest[:8]
+    work, (b3, one, in_sem, late_sem) = rest[8:-4], rest[-4:]
     me = me_ref[0]
     odd = lax.rem(me, 2)
     copied = input_copies(
+        odd,
         [(tot_hbm, tot), (hann_hbm, hann)],
-        list(zip(x_hbm, x)),
+        list(zip(zip(even_hbm, odd_hbm), x)) + [(late_hbm, x[2])],
         [(conv_hbm, conv), (seg_hbm, seg), (lag_hbm, lag)],
         in_sem,
     )
-    a0_hbm, ah_hbm, b0_hbm, bh_hbm = left_hbm
-    own_a = pltpu.make_async_copy(a0_hbm.at[:, 0], a.at[:, 0], late_sem.at[0])
-    halo_a = pltpu.make_async_copy(ah_hbm, a, late_sem.at[0])
     late = [
-        pltpu.make_async_copy(b0_hbm, b0, late_sem.at[1]),
-        pltpu.make_async_copy(bh_hbm, bh, late_sem.at[2]),
+        pltpu.make_async_copy(source, target, late_sem.at[n])
+        for n, (source, target) in enumerate(((b0_hbm, b0), (b2_hbm, b2), (a_hbm, a)))
     ]
     for copy in late:
         copy.start()
-
-    @pl.when(odd == 0)
-    def _():
-        own_a.start()
-
-    @pl.when(odd == 1)
-    def _():
-        halo_a.start()
-
     bins, depth, chans = b0.shape
     width = chans // 2
     nfr = lag.shape[1]
     pitch = nfr + 1
     cross = work[-1]
 
-    def emit(want, first_factor, second_factor):
-        def first(k, _):
-            def put(group, rows, value):
-                a[k, 1, rows] = value
-
-            first_factor(k, put)
-            return 0
-
-        def second(k, _):
-            b1[k] = second_factor(k)
-            return 0
-
-        @pl.when(want)
-        def _():
-            lax.fori_loop(0, bins, first, 0, unroll=8)
-
-        lax.fori_loop(0, bins, second, 0, unroll=8)
-
-    segment_factors(
-        *(places, odd == 0, True, odd, flag_ref),
-        *([tot], x, hann, conv, seg, work, copied, emit),
-    )
+    _, second_factor = segment_factors(
+        places, odd, flag_ref, [tot], x, hann, conv, seg, work, copied
+    )
+
+    def second(k, _):
+        b3[k] = second_factor(k)
+        return 0
+
+    lax.fori_loop(0, bins, second, 0, unroll=8)
     for copy in late:
         copy.wait()
 
-    @pl.when(odd == 0)
-    def _():
-        own_a.wait()
-
-    @pl.when(odd == 1)
-    def _():
-        halo_a.wait()
-
     lane = lax.broadcasted_iota(jnp.int32, (1, chans), 1)
-    keep = [jnp.where((lane < width) == (g == 0), 1.0, 0.0).astype(BF16) for g in range(2)]
-
-    def one_bin(k, _):
-        halo = bh[k]
-        right = jnp.concatenate(
-            [
-                jnp.concatenate([b0[k], halo * keep[0]], axis=1),
-                jnp.concatenate([b1[k], halo * keep[1]], axis=1),
-            ],
-            axis=0,
-        )
-        left = jnp.concatenate([a[k, 0], a[k, 1]], axis=1)
-        value = jnp.dot(left, right, preferred_element_type=F32)
-        for p in range(2):
-            for t in range(2):
-                cross[t, pl.ds(2 * k + p, width, stride=pitch), :] = value[
-                    p * width : (p + 1) * width, t * chans : (t + 1) * chans
-                ]
-        return 0
-
-    lax.fori_loop(0, bins, one_bin, 0, unroll=8)
+    low, high = [jnp.where((lane < width) == (g == 0), 1.0, 0.0).astype(BF16) for g in range(2)]
+
+    def bins_with(near, far):
+        def one_bin(k, _):
+            inner = near[k] * low + b3[k] * high if near is not b3 else b3[k]
+            right = jnp.concatenate(
+                [
+                    jnp.concatenate([b0[k], b2[k] * high], axis=1),
+                    jnp.concatenate([inner, far[k] * low], axis=1),
+                ],
+                axis=0,
+            )
+            left = jnp.concatenate([a[k, 0], a[k, 1]], axis=1)
+            value = jnp.dot(left, right, preferred_element_type=F32)
+            for p in range(2):
+                for t in range(2):
+                    cross[t, pl.ds(2 * k + p, width, stride=pitch), :] = value[
+                        p * width : (p + 1) * width, t * chans : (t + 1) * chans
+                    ]
+            return 0
+
+        lax.fori_loop(0, bins, one_bin, 0, unroll=8)
+
+    pl.when(odd == 0)(lambda: bins_with(b2, b3))
+    pl.when(odd == 1)(lambda: bins_with(b3, b2))
 
     row = lax.broadcasted_iota(jnp.int32, one.shape[1:], 0)
     column = lax.broadcasted_iota(jnp.int32, one.shape[1:], 1)
@@ -480,7 +517,7 @@
     lax.fori_loop(0, width, one_channel, 0, unroll=4)
 
 
-def stacks(places, shares, scale, me, flags, total, pieces, hann, conv, seg, lag, a0, ah, b0, bh):
+def stacks(places, shares, scale, me, flags, total, pieces, hann, conv, seg, lag, a, b0, b2):
     bins, depth, chans = b0.shape
     width = chans // 2
     _, wins, ns = pieces[0].shape
@@ -488,15 +525,15 @@
     smem = pl.BlockSpec(memory_space=pltpu.SMEM)
     vmem = pl.BlockSpec(memory_space=pltpu.VMEM)
     anywhere = pl.BlockSpec(memory_space=pl.ANY)
-    operands = [*pieces, total, hann, conv, seg, lag, a0, ah, b0, bh]
+    tables_in = [total, hann, conv, seg, lag, a, b0, b2]
+    operands = [*pieces, *tables_in]
+    held = [pieces[0], pieces[1], pieces[4], *tables_in]
     return pl.pallas_call(
         functools.partial(stack_kernel, places, scale, shares),
         out_shape=[jax.ShapeDtypeStruct((width, OFFS // shares, nlag), BF16)] * shares,
         in_specs=[smem] * 2 + [anywhere] * len(operands),
         out_specs=[vmem] * shares,
-        scratch_shapes=[
-            pltpu.VMEM(value.shape, value.dtype) for value in operands if value is not a0
-        ]
+        scratch_shapes=[pltpu.VMEM(value.shape, value.dtype) for value in held]
         + work_shapes(1, chans, wins, ns)
         + [
             pltpu.VMEM(b0.shape, BF16),
@@ -583,11 +620,10 @@
         cost_estimate=pl.CostEstimate(flops=1, bytes_accessed=1, transcendentals=0),
     )(odd[None], dead_flags, section_ids, samples)
     total, their_head = add_over(sums, "fibre", their_head)
-    total, halo_flags, own_half, conv = lax.optimization_barrier(
-        (total, halo_flags, own_half, conv)
-    )
+    halo_source, conv = lax.optimization_barrier((own_half, conv))
+    halo = lax.ppermute(halo_source, both, halo_pairs)
+    total, halo_flags, conv = lax.optimization_barrier((total, halo_flags, conv))
     their_total = lax.ppermute(total, "tm", swap)
-    halo = lax.ppermute(own_half, both, halo_pairs)
     ready = (total, their_total, their_head, own_half, tail, flags, hann, conv, seg, lag)
     ready = lax.optimization_barrier(ready)
     total, their_total, their_head, own_half, tail, flags, hann, conv, seg, lag = ready
@@ -597,29 +633,38 @@
 
     side = odd[None]
     parts = (hann, conv, seg)
-    a0, b0 = segments(((0, 0, 0),), 0, side, flags, (total,), (samples,), *parts)
+    every = jnp.concatenate([flags, halo_flags], axis=1)
+    b0, series = segments(((0, (0, 0), (0, 0)),), side, flags, (total,), (samples,), None, *parts)
     b0, forward = lax.optimization_barrier((b0, their_tail))
     halo_tail = lax.ppermute(forward, both, halo_pairs)
-    ah, bh = segments(
-        ((0, 0, 0), (1, width, width), (1, width + head, width + head)),
-        1,
+    a, b2 = segments(
+        (
+            (1, (0, 0), (0, chans)),
+            (1, (head, head), (head, chans + head)),
+            (0, (width, width), (chans, chans)),
+        ),
         side,
-        halo_flags,
+        every,
         (total, their_total),
-        (halo, halo_head, halo_tail),
+        (their_head, their_tail, halo_head, halo_tail, halo),
+        series,
         *parts,
     )
     scale = 2.0 / ns / LAGS / math.sqrt(nf * wins * groups)
     found = stacks(
-        ((0, 0, width), (0, head, width + head), (0, width, 0)),
+        (
+            (0, (0, width), (chans, width)),
+            (0, (head, width + head), (chans + head, width + head)),
+            (0, (width, 0), (width, 0)),
+        ),
         groups,
         scale,
         me[None],
-        flags,
+        every,
         their_total,
-        (their_head, their_tail, their_second),
+        (halo_head, halo_tail, their_head, their_tail, their_second),
         *(hann, conv, seg, lag),
-        *(a0, ah, b0, bh),
+        *(a, b0, b2),
     )
     arrived = []
     for d in range(groups):

time: 135 us -> 135 us (level)
  waiting for transfers between devices: 51.9 us -> 56.1 us
  Pallas kernels: 58.4 us -> 54.7 us
    pallas_call x1, Pallas kernels: 28.5 us -> 23.1 us  [stacks(): pl.pallas_call(functools.partial(stack_kernel, places, scale, shares), ou...]
    ppermute x4, waiting for transfers between devices: 40.4 us -> 44.1 us  [shards(): arrived.append(lax.ppermute(found[d], both, pairs).astype(F32))]
    ppermute x1, waiting for transfers between devices: 0.02 us -> 1.86 us  [shards(): halo_head = lax.ppermute(their_head, both, halo_pairs)]
    ppermute x1, starting transfers between devices: 0.05 us -> 1.84 us  [shards(): their_second = lax.ppermute(own_half, 'tm', swap)]
    pallas_call x2, Pallas kernels: 23.2 us -> 24.8 us  [segments(): pl.pallas_call(functools.partial(kernel, places), out_shape=out, in_specs...]
    ppermute x1, waiting for transfers between devices: 8.07 us -> 6.49 us  [shards(): halo_tail = lax.ppermute(forward, both, halo_pairs)]
    ppermute x4, starting transfers between devices: 4.58 us -> 3.14 us  [shards(): arrived.append(lax.ppermute(found[d], both, pairs).astype(F32))]
  transfers between devices with their start and end apart: 16 -> 16, of which waited for: 5 -> 6; matrix products, arithmetic and copies ran while one was open for 3% -> 4% of each run, Pallas kernels for 22% -> 23%
where the time goes in v12:
time: 135 us
  waiting for transfers between devices  56.1 us (42%)
  Pallas kernels  54.7 us (41%)
  starting transfers between devices  14.6 us (11%)
  other arithmetic  6.06 us (4%)
  local copies, waits for them, and re-layouts  3.34 us (2%)
    ppermute x4, waiting for transfers between devices, shards(): arrived.append(lax.ppermute(found[d], both, pairs).astype(F32))  44.1 us
    pallas_call x2, Pallas kernels, segments(): pl.pallas_call(functools.partial(kernel, places), out_shape=out, in_specs...  24.8 us
    pallas_call x1, Pallas kernels, stacks(): pl.pallas_call(functools.partial(stack_kernel, places, scale, shares), ou...  23.1 us
    ppermute x1, waiting for transfers between devices, shards(): halo_tail = lax.ppermute(forward, both, halo_pairs)  6.49 us
    pallas_call x1, Pallas kernels, shards(): pl.pallas_call(section_sums, out_shape=[jax.ShapeDtypeStruct((NSEC, wins,...  4.12 us
    ppermute x4, starting transfers between devices, add_over(): lax.ppermute(value, axis, [(i, i ^ s) for i in range(count)])  3.73 us
    ppermute x4, starting transfers between devices, shards(): arrived.append(lax.ppermute(found[d], both, pairs).astype(F32))  3.14 us
  transfers between devices with their start and end apart: 16, of which 6 were waited for; matrix products, arithmetic and copies ran while one was open for 4% of the time, Pallas kernels for 23%

profile of v12, /device:TPU:19, one launch (start us, length us, event | category | flops | bytes accessed | tf_op | source)
XLA Modules:
  0.0 135.0 jit_solution(1539596475534585372)
XLA Ops:
  0.0 2.0 %constant_dynamic-slice_fusion.1 = bf16[40,8,1024]{2,1,0:T(8,128)(2,1)} fusion(bf16[128,8,1024]{2,1,0:T(8,128)(2,1)} %rest_1_.1, s32[]{:T(128)S(6)} %select_n.27), kind=kLoop, calls=%fused_computation.11 | loop fusion | bytes 1310724 | tf_op jit(solution)/shard_map/dynamic_slice | solution.py:597
  2.0 1.3 collective-permute-start.4
  3.3 4.1 %shard_map.82 = (f32[2,8,1152]{2,1,0:T(8,128)}, bf16[64,8,1024]{2,1,0:T(8,128)(2,1)}, bf16[24,8,1024]{2,1,0:T(8,128)(2,1)}) custom-call(s32[1]{0:T(128)} %bitcast.1.odd_ref, s32[128]{0:T(128)} %dead_ref.1, s32[128]{0:T(128)} %sec_ref.1, bf16[128,8,1024]{2,1,0:T(8,128)(2,1)} %rest_1_.1), custom_call_target="tpu_custom_call" | custom-call | flops 1 | bytes 1 | tf_op jit(solution)/shard_map/pallas_call | solution.py:605
  7.4 1.0 collective-permute-start
  8.6 1.0 collective-permute-done
  10.8 1.2 collective-permute-start.2
  12.1 1.2 collective-permute-start.3
  13.2 2.4 %multiply_reduce_fusion = f32[1024]{0:T(1024)} fusion(f32[512,1024]{1,0:T(8,128)} %constant.33.clone, f32[512]{0:T(512)S(1)} %copy-done.8), kind=kLoop, calls=%fused_computation.1 | loop fusion | flops 1047552 | bytes 2103296 | tf_op jit(solution)/shard_map/reduce_sum | solution.py:579
  15.6 2.6 %shard_map.83.rest_3_.rest_8_.rest_7_ = bf16[1024,1024]{1,0:T(8,128)(2,1)} custom-call(f32[1,1024]{1,0:T(1,128)} %bitcast.5), custom_call_target="tpu_custom_call" | custom-call | flops 1 | bytes 1 | tf_op jit(solution)/shard_map/pallas_call | solution.py:580
  18.2 1.2 collective-permute-start.11
  21.0 1.3 collective-permute-start.6
  22.4 2.6 %collective-permute-done.6.rest_1_.rest_5_ = f32[2,8,1152]{2,1,0:T(8,128)S(1)} collective-permute-done((f32[2,8,1152]{2,1,0:T(8,128)S(1)}, f32[2,8,1152]{2,1,0:T(8,128)S(1)}, u32[]{:S(2)}, u32[]{:S(2)}) %collective-permute-start.6) | collective-permute-done | bytes 73760 | tf_op jit(solution)/shard_map/ppermute | solution.py:626
  25.0 1.6 %collective-permute-start.8 = (bf16[24,8,1024]{2,1,0:T(8,128)(2,1)}, bf16[24,8,1024]{2,1,0:T(8,128)(2,1)}, u32[]{:S(2)}, u32[]{:S(2)}) collective-permute-start(bf16[24,8,1024]{2,1,0:T(8,128)(2,1)} %get-tuple-element.55), channel_id=1, source_target_pairs={{0,1},{1,0},{2,3},{3,2},{4,5},{5,4},{6,7},{7,6},{8,9},{9,8},{10,11... | collective-permute-start | bytes 1179656 | tf_op jit(solution)/shard_map/ppermute | solution.py:630
  26.9 1.8 %collective-permute-start.10 = (bf16[64,8,1024]{2,1,0:T(8,128)(2,1)}, bf16[64,8,1024]{2,1,0:T(8,128)(2,1)}, u32[]{:S(2)}, u32[]{:S(2)}) collective-permute-start(bf16[64,8,1024]{2,1,0:T(8,128)(2,1)} %get-tuple-element.60), channel_id=1, source_target_pairs={{0,1},{1,0},{2,3},{3,2},{4,5},{5,4},{6,7},{7,6},{8,9},{9,8},{10,11... | collective-permute-start | bytes 3145736 | tf_op jit(solution)/shard_map/ppermute | solution.py:631
  29.4 9.3 %shard_map.84 = (bf16[128,128,128]{2,1,0:T(8,128)(2,1)}, bf16[2,1152,512]{2,1,0:T(8,128)(2,1)}) custom-call(s32[1]{0:T(128)} %bitcast.1.odd_ref, s32[2,128]{1,0:T(2,128)} %copy-done.4, f32[2,8,1152]{2,1,0:T(8,128)} %copy-done.2, bf16[128,8,1024]{2,1,0:T(8,128)(2,1)} %rest_1_.1, f32[8,1024]{1,0:T(8,128)} %jit_solution_.3.rest_2_.rest_7_.rest_6_, ...), custom_call_target="tpu_custom_call" | custom-call | flops 3758096384 | bytes 16777216 | tf_op jit(solution)/shard_map/pallas_call | solution.py:406
  38.8 1.9 %collective-permute-done.7.rest_4_.rest_0_ = bf16[40,8,1024]{2,1,0:T(8,128)(2,1)} collective-permute-done((bf16[40,8,1024]{2,1,0:T(8,128)(2,1)S(1)}, bf16[40,8,1024]{2,1,0:T(8,128)(2,1)}, u32[]{:S(2)}, u32[]{:S(2)}) %collective-permute-start.7) | collective-permute-done | bytes 655392 | tf_op jit(solution)/shard_map/ppermute | solution.py:632
  40.7 6.5 %collective-permute-done.9.rest_5_.rest_1_ = bf16[24,8,1024]{2,1,0:T(8,128)(2,1)} collective-permute-done((bf16[24,8,1024]{2,1,0:T(8,128)(2,1)}, bf16[24,8,1024]{2,1,0:T(8,128)(2,1)}, u32[]{:S(2)}, u32[]{:S(2)}) %collective-permute-start.9) | collective-permute-done | bytes 393248 | tf_op jit(solution)/shard_map/ppermute | solution.py:639
  47.2 15.6 %shard_map.85 = (bf16[128,2,128,128]{3,2,1,0:T(8,128)(2,1)}, bf16[128,128,128]{2,1,0:T(8,128)(2,1)}) custom-call(s32[1]{0:T(128)} %bitcast.1.odd_ref, s32[2,192]{1,0:T(2,128)} %copy-done.6, f32[2,8,1152]{2,1,0:T(8,128)} %copy-done.2, f32[2,8,1152]{2,1,0:T(8,128)} %copy-done.1, bf16[40,8,1024]{2,1,0:T(8,128)(2,1)} %copy-done, ...), custom_call_target="tpu_custom_call" | custom-call | flops 3758096384 | bytes 16777216 | tf_op jit(solution)/shard_map/pallas_call | solution.py:406
  62.7 23.1 %shard_map.86 = (bf16[64,32,128]{2,1,0:T(8,128)(2,1)}, bf16[64,32,128]{2,1,0:T(8,128)(2,1)}, bf16[64,32,128]{2,1,0:T(8,128)(2,1)}, bf16[64,32,128]{2,1,0:T(8,128)(2,1)}) custom-call(s32[1]{0:T(128)} %bitcast.me_ref, s32[2,192]{1,0:T(2,128)} %copy-done.6, bf16[40,8,1024]{2,1,0:T(8,128)(2,1)} %collective-permute-done.7.rest_4_.rest_0_, ...), custom_call_target="tpu_custom_call" | custom-call | flops 4294967296 | bytes 20971520 | tf_op jit(solution)/shard_map/pallas_call | solution.py:531
  86.0 1.7 %collective-permute-start.12 = (bf16[64,32,128]{2,1,0:T(8,128)(2,1)}, bf16[64,32,128]{2,1,0:T(8,128)(2,1)S(1)}, u32[]{:S(2)}, u32[]{:S(2)}) collective-permute-start(bf16[64,32,128]{2,1,0:T(8,128)(2,1)} %get-tuple-element.65), channel_id=1, source_target_pairs={{0,0},{1,29},{2,2},{3,31},{4,4},{5,1},{6,6},{7,3},{8,8},{9,5},{10,... | collective-permute-start | bytes 1572872 | tf_op jit(solution)/shard_map/ppermute | solution.py:676
  87.7 1.3 collective-permute-start.14
  89.0 29.9 %collective-permute-done.13 = bf16[64,32,128]{2,1,0:T(8,128)(2,1)S(1)} collective-permute-done((bf16[64,32,128]{2,1,0:T(8,128)(2,1)}, bf16[64,32,128]{2,1,0:T(8,128)(2,1)S(1)}, u32[]{:S(2)}, u32[]{:S(2)}) %collective-permute-start.13) | collective-permute-done | bytes 524320 | tf_op jit(solution)/shard_map/ppermute | solution.py:676
  118.9 14.2 %collective-permute-done.15 = bf16[64,32,128]{2,1,0:T(8,128)(2,1)S(1)} collective-permute-done((bf16[64,32,128]{2,1,0:T(8,128)(2,1)}, bf16[64,32,128]{2,1,0:T(8,128)(2,1)S(1)}, u32[]{:S(2)}, u32[]{:S(2)}) %collective-permute-start.15) | collective-permute-done | bytes 524320 | tf_op jit(solution)/shard_map/ppermute | solution.py:676
  133.5 1.5 %pad_maximum_fusion = f32[128,32,128]{2,1,0:T(8,128)} fusion(f32[64,32,128]{2,1,0:T(8,128)S(1)} %get-tuple-element.70, f32[64,32,128]{2,1,0:T(8,128)S(1)} %get-tuple-element.69), kind=kLoop, calls=%fused_computation | loop fusion | flops 524288 | bytes 4194304 | tf_op jit(solution)/shard_map/concatenate | solution.py:679
  (46 shorter events, 4.5 us)
Async XLA Ops:
  0.0 8.5 %copy-start.10 = (s32[128]{0:T(128)S(1)}, s32[128]{0:T(128)}, u32[]{:S(2)}) copy-start(s32[128]{0:T(128)} %dead_ref.1) | copy-start | bytes 1540
  0.0 8.5 %copy-start.9 = (s32[128]{0:T(128)S(1)}, s32[128]{0:T(128)}, u32[]{:S(2)}) copy-start(s32[128]{0:T(128)} %sec_ref.1) | copy-start | bytes 1540
  0.0 13.2 %copy-start.8 = (f32[512]{0:T(512)S(1)}, f32[512]{0:T(512)}, u32[]{:S(2)}) copy-start(f32[512]{0:T(512)} %param.9) | copy-start | bytes 6148
  2.0 18.0 %collective-permute-start.4 = (bf16[40,8,1024]{2,1,0:T(8,128)(2,1)}, bf16[40,8,1024]{2,1,0:T(8,128)(2,1)S(1)}, u32[]{:S(2)}, u32[]{:S(2)}) collective-permute-start(bf16[40,8,1024]{2,1,0:T(8,128)(2,1)} %constant_dynamic-slice_fusion.1), channel_id=1, source_target_pairs={{0,1},{1,0},{2,3},{3,2},{4,5},{5,4},{6,7},{7,6},{8,9},{9,8},{10,11... | collective-permute-start | bytes 1966088 | tf_op jit(solution)/shard_map/ppermute | solution.py:596
  7.4 2.1 %collective-permute-start = (f32[2,8,1152]{2,1,0:T(8,128)}, f32[2,8,1152]{2,1,0:T(8,128)S(1)}, u32[]{:S(2)}, u32[]{:S(2)}) collective-permute-start(f32[2,8,1152]{2,1,0:T(8,128)} %get-tuple-element.37), channel_id=1, source_target_pairs={{0,4},{4,0},{8,12},{12,8},{16,20},{20,16},{24,28},{28,24},{1,5},{5... | collective-permute-start | bytes 221192 | tf_op jit(solution)/shard_map/ppermute | solution.py:560
  8.5 9.7 %copy-start.4 = (s32[2,128]{1,0:T(2,128)}, s32[2,128]{1,0:T(2,128)S(1)}, u32[]{:S(2)}) copy-start(s32[2,128]{1,0:T(2,128)S(1)} %pad_add_fusion.flag_ref) | copy-start | bytes 3076
  8.6 12.4 %collective-permute-start.5 = (s32[2,64]{1,0:T(2,128)S(1)}, s32[2,64]{1,0:T(2,128)S(1)}, u32[]{:S(2)}, u32[]{:S(2)}) collective-permute-start(s32[2,64]{1,0:T(2,128)S(1)} %constant_dynamic-slice_fusion), channel_id=1, source_target_pairs={{0,28},{1,5},{2,30},{3,7},{4,0},{5,9},{6,2},{7,11},{8,4},{9,13},{1... | collective-permute-start | bytes 1544 | tf_op jit(solution)/shard_map/ppermute | solution.py:600
  10.5 18.3 %copy-start.7 = (f32[1024]{0:T(1024)S(1)}, f32[1024]{0:T(1024)}, u32[]{:S(2)}) copy-start(f32[1024]{0:T(1024)} %constant.36.clone) | copy-start | bytes 12292
  10.5 7.7 %collective-permute-start.1 = (f32[2,8,1152]{2,1,0:T(8,128)S(1)}, f32[2,8,1152]{2,1,0:T(8,128)S(1)}, u32[]{:S(2)}, u32[]{:S(2)}) collective-permute-start(f32[2,8,1152]{2,1,0:T(8,128)S(1)} %add.29), channel_id=1, source_target_pairs={{0,8},{4,12},{8,0},{12,4},{16,24},{20,28},{24,16},{28,20},{1,9},{5... | collective-permute-start | bytes 221192 | tf_op jit(solution)/shard_map/ppermute | solution.py:560
  10.8 8.6 %collective-permute-start.2 = (f32[2,8,1152]{2,1,0:T(8,128)S(1)}, f32[2,8,1152]{2,1,0:T(8,128)S(1)}, u32[]{:S(2)}, u32[]{:S(2)}) collective-permute-start(f32[2,8,1152]{2,1,0:T(8,128)S(1)} %add.29), channel_id=1, source_target_pairs={{0,16},{4,20},{8,24},{12,28},{16,0},{20,4},{24,8},{28,12},{1,17},{... | collective-permute-start | bytes 221192 | tf_op jit(solution)/shard_map/ppermute | solution.py:560
  12.1 7.4 %collective-permute-start.3 = (f32[2,8,1152]{2,1,0:T(8,128)S(1)}, f32[2,8,1152]{2,1,0:T(8,128)S(1)}, u32[]{:S(2)}, u32[]{:S(2)}) collective-permute-start(f32[2,8,1152]{2,1,0:T(8,128)S(1)} %add.29), channel_id=1, source_target_pairs={{0,24},{4,28},{8,16},{12,20},{16,8},{20,12},{24,0},{28,4},{1,25},{... | collective-permute-start | bytes 221192 | tf_op jit(solution)/shard_map/ppermute | solution.py:560
  18.2 20.6 %collective-permute-start.11 = (bf16[64,8,1024]{2,1,0:T(8,128)(2,1)}, bf16[64,8,1024]{2,1,0:T(8,128)(2,1)}, u32[]{:S(2)}, u32[]{:S(2)}) collective-permute-start(bf16[64,8,1024]{2,1,0:T(8,128)(2,1)} %get-tuple-element.60), channel_id=1, source_target_pairs={{0,28},{1,5},{2,30},{3,7},{4,0},{5,9},{6,2},{7,11},{8,4},{9,13},{1... | collective-permute-start | bytes 3145736 | tf_op jit(solution)/shard_map/ppermute | solution.py:624
  20.0 18.6 %copy-start = (bf16[40,8,1024]{2,1,0:T(8,128)(2,1)}, bf16[40,8,1024]{2,1,0:T(8,128)(2,1)S(1)}, u32[]{:S(2)}) copy-start(bf16[40,8,1024]{2,1,0:T(8,128)(2,1)S(1)} %collective-permute-done.4.rest_2_) | copy-start | bytes 1966084
  21.0 3.9 %collective-permute-start.6 = (f32[2,8,1152]{2,1,0:T(8,128)S(1)}, f32[2,8,1152]{2,1,0:T(8,128)S(1)}, u32[]{:S(2)}, u32[]{:S(2)}) collective-permute-start(f32[2,8,1152]{2,1,0:T(8,128)S(1)} %add_add_fusion.rest_0_), channel_id=1, source_target_pairs={{0,1},{1,0},{2,3},{3,2},{4,5},{5,4},{6,7},{7,6},{8,9},{9,8},{10,11... | collective-permute-start | bytes 221192 | tf_op jit(solution)/shard_map/ppermute | solution.py:626
  25.0 13.7 %copy-start.1 = (f32[2,8,1152]{2,1,0:T(8,128)}, f32[2,8,1152]{2,1,0:T(8,128)S(1)}, u32[]{:S(2)}) copy-start(f32[2,8,1152]{2,1,0:T(8,128)S(1)} %collective-permute-done.6.rest_1_.rest_5_) | copy-start | bytes 221188
  25.0 13.7 %collective-permute-start.8 = (bf16[24,8,1024]{2,1,0:T(8,128)(2,1)}, bf16[24,8,1024]{2,1,0:T(8,128)(2,1)}, u32[]{:S(2)}, u32[]{:S(2)}) collective-permute-start(bf16[24,8,1024]{2,1,0:T(8,128)(2,1)} %get-tuple-element.55), channel_id=1, source_target_pairs={{0,1},{1,0},{2,3},{3,2},{4,5},{5,4},{6,7},{7,6},{8,9},{9,8},{10,11... | collective-permute-start | bytes 1179656 | tf_op jit(solution)/shard_map/ppermute | solution.py:630
  26.6 14.1 %collective-permute-start.7 = (bf16[40,8,1024]{2,1,0:T(8,128)(2,1)S(1)}, bf16[40,8,1024]{2,1,0:T(8,128)(2,1)}, u32[]{:S(2)}, u32[]{:S(2)}) collective-permute-start(bf16[40,8,1024]{2,1,0:T(8,128)(2,1)S(1)} %collective-permute-done.4.rest_2_), channel_id=1, source_target_pairs={{0,28},{1,5},{2,30},{3,7},{4,0},{5,9},{6,2},{7,11},{8,4},{9,13},{1... | collective-permute-start | bytes 1966088 | tf_op jit(solution)/shard_map/ppermute | solution.py:632
  26.9 35.8 %collective-permute-start.10 = (bf16[64,8,1024]{2,1,0:T(8,128)(2,1)}, bf16[64,8,1024]{2,1,0:T(8,128)(2,1)}, u32[]{:S(2)}, u32[]{:S(2)}) collective-permute-start(bf16[64,8,1024]{2,1,0:T(8,128)(2,1)} %get-tuple-element.60), channel_id=1, source_target_pairs={{0,1},{1,0},{2,3},{3,2},{4,5},{5,4},{6,7},{7,6},{8,9},{9,8},{10,11... | collective-permute-start | bytes 3145736 | tf_op jit(solution)/shard_map/ppermute | solution.py:631
  29.4 9.4 %copy-start.5 = (s32[2,128]{1,0:T(2,128)S(1)}, s32[2,128]{1,0:T(2,128)}, u32[]{:S(2)}) copy-start(s32[2,128]{1,0:T(2,128)} %copy-done.4) | copy-start | bytes 3076
  38.7 8.5 %collective-permute-start.9 = (bf16[24,8,1024]{2,1,0:T(8,128)(2,1)}, bf16[24,8,1024]{2,1,0:T(8,128)(2,1)}, u32[]{:S(2)}, u32[]{:S(2)}) collective-permute-start(bf16[24,8,1024]{2,1,0:T(8,128)(2,1)} %collective-permute-done.8.rest_3_), channel_id=1, source_target_pairs={{0,28},{1,5},{2,30},{3,7},{4,0},{5,9},{6,2},{7,11},{8,4},{9,13},{1... | collective-permute-start | bytes 1179656 | tf_op jit(solution)/shard_map/ppermute | solution.py:639
  85.9 33.0 %collective-permute-start.13 = (bf16[64,32,128]{2,1,0:T(8,128)(2,1)}, bf16[64,32,128]{2,1,0:T(8,128)(2,1)S(1)}, u32[]{:S(2)}, u32[]{:S(2)}) collective-permute-start(bf16[64,32,128]{2,1,0:T(8,128)(2,1)} %get-tuple-element.66), channel_id=1, source_target_pairs={{0,2},{1,31},{2,0},{3,29},{4,6},{5,3},{6,4},{7,1},{8,10},{9,7},{10... | collective-permute-start | bytes 1572872 | tf_op jit(solution)/shard_map/ppermute | solution.py:676
  86.0 32.9 %collective-permute-start.12 = (bf16[64,32,128]{2,1,0:T(8,128)(2,1)}, bf16[64,32,128]{2,1,0:T(8,128)(2,1)S(1)}, u32[]{:S(2)}, u32[]{:S(2)}) collective-permute-start(bf16[64,32,128]{2,1,0:T(8,128)(2,1)} %get-tuple-element.65), channel_id=1, source_target_pairs={{0,0},{1,29},{2,2},{3,31},{4,4},{5,1},{6,6},{7,3},{8,8},{9,5},{10,... | collective-permute-start | bytes 1572872 | tf_op jit(solution)/shard_map/ppermute | solution.py:676
  87.7 45.5 %collective-permute-start.15 = (bf16[64,32,128]{2,1,0:T(8,128)(2,1)}, bf16[64,32,128]{2,1,0:T(8,128)(2,1)S(1)}, u32[]{:S(2)}, u32[]{:S(2)}) collective-permute-start(bf16[64,32,128]{2,1,0:T(8,128)(2,1)} %get-tuple-element.68), channel_id=1, source_target_pairs={{0,3},{1,30},{2,1},{3,28},{4,7},{5,2},{6,5},{7,0},{8,11},{9,6},{10... | collective-permute-start | bytes 1572872 | tf_op jit(solution)/shard_map/ppermute | solution.py:676
  87.7 45.5 %collective-permute-start.14 = (bf16[64,32,128]{2,1,0:T(8,128)(2,1)}, bf16[64,32,128]{2,1,0:T(8,128)(2,1)S(1)}, u32[]{:S(2)}, u32[]{:S(2)}) collective-permute-start(bf16[64,32,128]{2,1,0:T(8,128)(2,1)} %get-tuple-element.67), channel_id=1, source_target_pairs={{0,1},{1,28},{2,3},{3,30},{4,5},{5,0},{6,7},{7,2},{8,9},{9,4},{10,... | collective-permute-start | bytes 1572872 | tf_op jit(solution)/shard_map/ppermute | solution.py:676
  (3 other events, 17.4 us)

commit v13 on v12

--- a/solution.py
+++ b/solution.py
@@ -115,7 +115,7 @@
         base = base[0] + odd * (base[1] - base[0])
         flags = flags[0] + odd * (flags[1] - flags[0])
 
-        def clean_channel(c, _):
+        def clean_channel(c):
             at = base + c
             flag = flags + c
             live = (1 - flag_ref[0, flag]).astype(F32)
@@ -128,13 +128,12 @@
             square[row, :] = sum([tile * tile for tile in tiles[1:]], tiles[0] * tiles[0])
             for t, tile in enumerate(tiles):
                 clean[t, row, :] = tile
-            return 0
 
         parts = copied["x"][number]
         part = length // len(parts)
         for n, copy in enumerate(parts):
             copy.wait()
-            lax.fori_loop(n * part, (n + 1) * part, clean_channel, 0, unroll=8)
+            repeat(n * part, (n + 1) * part, clean_channel, 4)
     for copy in copied["tables"]:
         copy.wait()
 
@@ -214,6 +213,15 @@
     ]
 
 
+def repeat(start, stop, body, together):
+    def step(n, _):
+        for i in range(together):
+            body(start + n * together + i)
+        return 0
+
+    lax.fori_loop(0, (stop - start) // together, step, 0)
+
+
 class Choice:
     def __init__(self, odd, sources, target, sem):
         self.options = [
@@ -295,11 +303,7 @@
     for n in range(STEPS):
         part = pl.ds(n * step, step)
 
-        def one_bin(k, _):
-            factor(k, stage)
-            return 0
-
-        lax.fori_loop(n * step, (n + 1) * step, one_bin, 0, unroll=8)
+        repeat(n * step, (n + 1) * step, lambda k: factor(k, stage), 4)
         copies.append(pltpu.make_async_copy(stage.at[part], target.at[part], sem.at[n]))
         copies[-1].start()
     for copy in copies:
@@ -357,11 +361,7 @@
     for n in range(STEPS):
         part = pl.ds(n * step, step)
 
-        def one_bin(k, _):
-            both_factors(k, b_out)
-            return 0
-
-        lax.fori_loop(n * step, (n + 1) * step, one_bin, 0, unroll=8)
+        repeat(n * step, (n + 1) * step, lambda k: both_factors(k, b_out), 4)
         for m, (source, target) in enumerate(((a_out, a_hbm), (b_out, b_hbm))):
             copies.append(
                 pltpu.make_async_copy(source.at[part], target.at[part], out_sem.at[2 * n + m])
@@ -451,11 +451,10 @@
         places, odd, flag_ref, [tot], x, hann, conv, seg, work, copied
     )
 
-    def second(k, _):
+    def second(k):
         b3[k] = second_factor(k)
-        return 0
-
-    lax.fori_loop(0, bins, second, 0, unroll=8)
+
+    repeat(0, bins, second, 4)
     for copy in late:
         copy.wait()
 
@@ -463,7 +462,7 @@
     low, high = [jnp.where((lane < width) == (g == 0), 1.0, 0.0).astype(BF16) for g in range(2)]
 
     def bins_with(near, far):
-        def one_bin(k, _):
+        def one_bin(k):
             inner = near[k] * low + b3[k] * high if near is not b3 else b3[k]
             right = jnp.concatenate(
                 [
@@ -479,9 +478,8 @@
                     cross[t, pl.ds(2 * k + p, width, stride=pitch), :] = value[
                         p * width : (p + 1) * width, t * chans : (t + 1) * chans
                     ]
-            return 0
-
-        lax.fori_loop(0, bins, one_bin, 0, unroll=8)
+
+        repeat(0, bins, one_bin, 4)
 
     pl.when(odd == 0)(lambda: bins_with(b2, b3))
     pl.when(odd == 1)(lambda: bins_with(b3, b2))
@@ -496,7 +494,7 @@
         one[t] = jnp.where(found, 1.0, 0.0)
     share = OFFS // shares
 
-    def one_channel(c, _):
+    def one_channel(c):
         value = jnp.concatenate(
             [cross[t, pl.ds(c * pitch, nfr), :] for t in range(2)], axis=1
         ).astype(BF16)
@@ -512,9 +510,8 @@
         band = lax.dot_general(pick, lagged.astype(BF16), NT, preferred_element_type=F32)
         for d, out in enumerate(outs):
             out[c] = band[d * share : (d + 1) * share, :].astype(BF16)
-        return 0
-
-    lax.fori_loop(0, width, one_channel, 0, unroll=4)
+
+    repeat(0, width, one_channel, 4)
 
 
 def stacks(places, shares, scale, me, flags, total, pieces, hann, conv, seg, lag, a, b0, b2):
@@ -575,7 +572,7 @@
     odd = me % 2
     window, waves, seg, lag = tables(ns, nf)
     waves, seg, lag = jnp.asarray(waves), jnp.asarray(seg), jnp.asarray(lag)
-    hann = jnp.asarray(np.broadcast_to(window[None, :], (wins, ns)))
+    hann = jnp.asarray(window[None, :])
     response = jnp.sum(band_gain[:, None] * waves, axis=0, keepdims=True)
     conv = pl.pallas_call(
         circulant_kernel,
@@ -622,13 +619,15 @@
     total, their_head = add_over(sums, "fibre", their_head)
     halo_source, conv = lax.optimization_barrier((own_half, conv))
     halo = lax.ppermute(halo_source, both, halo_pairs)
-    total, halo_flags, conv = lax.optimization_barrier((total, halo_flags, conv))
+    total, halo_flags, conv, own_half, tail = lax.optimization_barrier(
+        (total, halo_flags, conv, own_half, tail)
+    )
     their_total = lax.ppermute(total, "tm", swap)
-    ready = (total, their_total, their_head, own_half, tail, flags, hann, conv, seg, lag)
-    ready = lax.optimization_barrier(ready)
-    total, their_total, their_head, own_half, tail, flags, hann, conv, seg, lag = ready
     their_tail = lax.ppermute(tail, "tm", swap)
     their_second = lax.ppermute(own_half, "tm", swap)
+    ready = (total, their_total, their_head, flags, hann, conv, seg, lag)
+    ready = lax.optimization_barrier(ready)
+    total, their_total, their_head, flags, hann, conv, seg, lag = ready
     halo_head = lax.ppermute(their_head, both, halo_pairs)
 
     side = odd[None]
@@ -666,14 +665,20 @@
         *(hann, conv, seg, lag),
         *(a, b0, b2),
     )
-    arrived = []
-    for d in range(groups):
+    arrived = {}
+    found = list(found)
+    for d in reversed(range(groups)):
+        if d == 1 and groups > 2:
+            found[0], found[1], arrived[2] = lax.optimization_barrier(
+                (found[0], found[1], arrived[2])
+            )
         pairs = [
             (b * groups + z, (b - z % 2) % blocks * groups + (z ^ d))
             for b in range(blocks)
             for z in range(groups)
         ]
-        arrived.append(lax.ppermute(found[d], both, pairs).astype(F32))
+        arrived[d] = lax.ppermute(found[d], both, pairs)
+    arrived = [arrived[d].astype(F32) for d in range(groups)]
     same = sum(arrived[2::2], arrived[0])
     other = sum(arrived[3::2], arrived[1])
     return jnp.concatenate(

time: 135 us -> 142 us (1.052)
  Pallas kernels: 54.7 us -> 57.8 us
  starting transfers between devices: 14.6 us -> 17.3 us
  waiting for transfers between devices: 56.1 us -> 58.4 us
  local copies, waits for them, and re-layouts: 3.34 us -> 1.89 us
    ppermute x4, starting transfers between devices: 3.14 us -> 6.47 us  [shards(): arrived[d] = lax.ppermute(found[d], both, pairs)]
    ppermute x4, waiting for transfers between devices: 44.1 us -> 47.2 us  [shards(): arrived[d] = lax.ppermute(found[d], both, pairs)]
    ppermute x1, waiting for transfers between devices: 1.86 us -> 4.74 us  [shards(): halo_head = lax.ppermute(their_head, both, halo_pairs)]
    pallas_call x1, Pallas kernels: 23.1 us -> 25.8 us  [stacks(): pl.pallas_call(functools.partial(stack_kernel, places, scale, shares), ou...]
    ppermute x1, waiting for transfers between devices: 6.49 us -> 4.32 us  [shards(): halo_tail = lax.ppermute(forward, both, halo_pairs)]
    ppermute x1, waiting for transfers between devices: 2.62 us -> 1.15 us  [shards(): their_total = lax.ppermute(total, 'tm', swap)]
  transfers between devices with their start and end apart: 16 -> 16, of which waited for: 6 -> 7; matrix products, arithmetic and copies ran while one was open for 4% -> 3% of each run, Pallas kernels for 23% -> 23%
where the time goes in v13:
time: 142 us
  waiting for transfers between devices  58.4 us (41%)
  Pallas kernels  57.8 us (41%)
  starting transfers between devices  17.3 us (12%)
  other arithmetic  6.02 us (4%)
  local copies, waits for them, and re-layouts  1.89 us (1%)
    ppermute x4, waiting for transfers between devices, shards(): arrived[d] = lax.ppermute(found[d], both, pairs)  47.2 us
    pallas_call x1, Pallas kernels, stacks(): pl.pallas_call(functools.partial(stack_kernel, places, scale, shares), ou...  25.8 us
    pallas_call x2, Pallas kernels, segments(): pl.pallas_call(functools.partial(kernel, places), out_shape=out, in_specs...  25.3 us
    ppermute x4, starting transfers between devices, shards(): arrived[d] = lax.ppermute(found[d], both, pairs)  6.47 us
    ppermute x1, waiting for transfers between devices, shards(): halo_head = lax.ppermute(their_head, both, halo_pairs)  4.74 us
    ppermute x1, waiting for transfers between devices, shards(): halo_tail = lax.ppermute(forward, both, halo_pairs)  4.32 us
    pallas_call x1, Pallas kernels, shards(): pl.pallas_call(section_sums, out_shape=[jax.ShapeDtypeStruct((NSEC, wins,...  4.11 us
    ppermute x4, starting transfers between devices, add_over(): lax.ppermute(value, axis, [(i, i ^ s) for i in range(count)])  3.73 us
  transfers between devices with their start and end apart: 16, of which 7 were waited for; matrix products, arithmetic and copies ran while one was open for 3% of the time, Pallas kernels for 23%

profile of v13, /device:TPU:19, one launch (start us, length us, event | category | flops | bytes accessed | tf_op | source)
XLA Modules:
  0.0 141.6 jit_solution(18320994747320030762)
XLA Ops:
  0.0 1.2 constant_dynamic-slice_fusion.1
  1.2 1.4 collective-permute-start.4
  2.5 4.1 %shard_map.82 = (f32[2,8,1152]{2,1,0:T(8,128)}, bf16[64,8,1024]{2,1,0:T(8,128)(2,1)}, bf16[24,8,1024]{2,1,0:T(8,128)(2,1)}) custom-call(s32[1]{0:T(128)} %bitcast.1.odd_ref, s32[128]{0:T(128)} %dead_ref.1, s32[128]{0:T(128)} %sec_ref.1, bf16[128,8,1024]{2,1,0:T(8,128)(2,1)} %rest_1_.1), custom_call_target="tpu_custom_call" | custom-call | flops 1 | bytes 1 | tf_op jit(solution)/shard_map/pallas_call | solution.py:602
  6.7 1.0 collective-permute-start
  7.8 1.0 collective-permute-done
  10.0 1.2 collective-permute-start.2
  11.3 1.2 collective-permute-start.3
  12.4 2.4 %multiply_reduce_fusion = f32[1024]{0:T(1024)} fusion(f32[512,1024]{1,0:T(8,128)} %constant.33.clone, f32[512]{0:T(512)S(1)} %copy-done.7), kind=kLoop, calls=%fused_computation.1 | loop fusion | flops 1047552 | bytes 2103296 | tf_op jit(solution)/shard_map/reduce_sum | solution.py:576
  14.8 2.6 %shard_map.83.rest_3_.rest_8_.rest_7_ = bf16[1024,1024]{1,0:T(8,128)(2,1)} custom-call(f32[1,1024]{1,0:T(1,128)} %bitcast.5), custom_call_target="tpu_custom_call" | custom-call | flops 1 | bytes 1 | tf_op jit(solution)/shard_map/pallas_call | solution.py:577
  17.4 1.2 collective-permute-start.11
  20.2 1.3 collective-permute-start.6
  21.7 1.3 collective-permute-start.10
  23.0 1.1 collective-permute-done.6.rest_1_.rest_5_
  25.1 9.1 %shard_map.84 = (bf16[128,128,128]{2,1,0:T(8,128)(2,1)}, bf16[2,1152,512]{2,1,0:T(8,128)(2,1)}) custom-call(s32[1]{0:T(128)} %bitcast.1.odd_ref, s32[2,128]{1,0:T(2,128)} %copy-done.4, f32[2,8,1152]{2,1,0:T(8,128)} %copy-done.2, bf16[128,8,1024]{2,1,0:T(8,128)(2,1)} %rest_1_.1, f32[1,1024]{1,0:T(1,128)} %constant.36.clone.rest_2_.rest_7_.rest_6_, ...), custom_call_target="tpu_custom_call" | custom-call | flops 3758096384 | bytes 16777216 | tf_op jit(solution)/shard_map/pallas_call | solution.py:406
  35.0 4.7 %collective-permute-done.7.rest_4_.rest_0_ = bf16[40,8,1024]{2,1,0:T(8,128)(2,1)S(1)} collective-permute-done((bf16[40,8,1024]{2,1,0:T(8,128)(2,1)}, bf16[40,8,1024]{2,1,0:T(8,128)(2,1)S(1)}, u32[]{:S(2)}, u32[]{:S(2)}) %collective-permute-start.7) | collective-permute-done | bytes 655392 | tf_op jit(solution)/shard_map/ppermute | solution.py:631
  39.8 4.3 %collective-permute-done.9.rest_5_.rest_1_ = bf16[24,8,1024]{2,1,0:T(8,128)(2,1)} collective-permute-done((bf16[24,8,1024]{2,1,0:T(8,128)(2,1)}, bf16[24,8,1024]{2,1,0:T(8,128)(2,1)}, u32[]{:S(2)}, u32[]{:S(2)}) %collective-permute-start.9) | collective-permute-done | bytes 393248 | tf_op jit(solution)/shard_map/ppermute | solution.py:638
  44.1 16.2 %shard_map.85 = (bf16[128,2,128,128]{3,2,1,0:T(8,128)(2,1)}, bf16[128,128,128]{2,1,0:T(8,128)(2,1)}) custom-call(s32[1]{0:T(128)} %bitcast.1.odd_ref, s32[2,192]{1,0:T(2,128)} %copy-done.6, f32[2,8,1152]{2,1,0:T(8,128)} %copy-done.2, f32[2,8,1152]{2,1,0:T(8,128)} %copy-done.1, bf16[40,8,1024]{2,1,0:T(8,128)(2,1)} %collective-permute-done.4.rest_2_, ...), custom_call_target="tpu_custom_call" | custom-call | flops 3758096384 | bytes 16777216 | tf_op jit(solution)/shard_map/pallas_call | solution.py:406
  60.3 25.8 %shard_map.86 = (bf16[64,32,128]{2,1,0:T(8,128)(2,1)}, bf16[64,32,128]{2,1,0:T(8,128)(2,1)}, bf16[64,32,128]{2,1,0:T(8,128)(2,1)}, bf16[64,32,128]{2,1,0:T(8,128)(2,1)}) custom-call(s32[1]{0:T(128)} %bitcast.me_ref, s32[2,192]{1,0:T(2,128)} %copy-done.6, bf16[40,8,1024]{2,1,0:T(8,128)(2,1)} %copy-done, ...), custom_call_target="tpu_custom_call" | custom-call | flops 4294967296 | bytes 20971520 | tf_op jit(solution)/shard_map/pallas_call | solution.py:528
  87.1 33.2 %collective-permute-done.12 = bf16[64,32,128]{2,1,0:T(8,128)(2,1)S(1)} collective-permute-done((bf16[64,32,128]{2,1,0:T(8,128)(2,1)}, bf16[64,32,128]{2,1,0:T(8,128)(2,1)S(1)}, u32[]{:S(2)}, u32[]{:S(2)}) %collective-permute-start.12) | collective-permute-done | bytes 524320 | tf_op jit(solution)/shard_map/ppermute | solution.py:680
  120.4 1.7 %collective-permute-start.13 = (bf16[64,32,128]{2,1,0:T(8,128)(2,1)}, bf16[64,32,128]{2,1,0:T(8,128)(2,1)S(1)}, u32[]{:S(2)}, u32[]{:S(2)}) collective-permute-start(bf16[64,32,128]{2,1,0:T(8,128)(2,1)} %get-tuple-element.71), channel_id=1, source_target_pairs={{0,0},{1,29},{2,2},{3,31},{4,4},{5,1},{6,6},{7,3},{8,8},{9,5},{10,... | collective-permute-start | bytes 1572872 | tf_op jit(solution)/shard_map/ppermute | solution.py:680
  122.1 3.7 %collective-permute-start.14 = (bf16[64,32,128]{2,1,0:T(8,128)(2,1)}, bf16[64,32,128]{2,1,0:T(8,128)(2,1)S(1)}, u32[]{:S(2)}, u32[]{:S(2)}) collective-permute-start(bf16[64,32,128]{2,1,0:T(8,128)(2,1)} %get-tuple-element.73), channel_id=1, source_target_pairs={{0,1},{1,28},{2,3},{3,30},{4,5},{5,0},{6,7},{7,2},{8,9},{9,4},{10,... | collective-permute-start | bytes 1572872 | tf_op jit(solution)/shard_map/ppermute | solution.py:680
  125.8 8.1 %collective-permute-done.15 = bf16[64,32,128]{2,1,0:T(8,128)(2,1)S(1)} collective-permute-done((bf16[64,32,128]{2,1,0:T(8,128)(2,1)}, bf16[64,32,128]{2,1,0:T(8,128)(2,1)S(1)}, u32[]{:S(2)}, u32[]{:S(2)}) %collective-permute-start.15) | collective-permute-done | bytes 524320 | tf_op jit(solution)/shard_map/ppermute | solution.py:680
  133.9 5.9 %collective-permute-done.14 = bf16[64,32,128]{2,1,0:T(8,128)(2,1)S(1)} collective-permute-done((bf16[64,32,128]{2,1,0:T(8,128)(2,1)}, bf16[64,32,128]{2,1,0:T(8,128)(2,1)S(1)}, u32[]{:S(2)}, u32[]{:S(2)}) %collective-permute-start.14) | collective-permute-done | bytes 524320 | tf_op jit(solution)/shard_map/ppermute | solution.py:680
  140.1 1.5 %pad_maximum_fusion = f32[128,32,128]{2,1,0:T(8,128)} fusion(f32[64,32,128]{2,1,0:T(8,128)S(1)} %get-tuple-element.76, f32[64,32,128]{2,1,0:T(8,128)S(1)} %get-tuple-element.75), kind=kLoop, calls=%fused_computation | loop fusion | flops 524288 | bytes 4194304 | tf_op jit(solution)/shard_map/concatenate | solution.py:684
  (43 shorter events, 6.2 us)
Async XLA Ops:
  0.0 7.7 %copy-start.9 = (s32[128]{0:T(128)S(1)}, s32[128]{0:T(128)}, u32[]{:S(2)}) copy-start(s32[128]{0:T(128)} %dead_ref.1) | copy-start | bytes 1540
  0.0 7.7 %copy-start.8 = (s32[128]{0:T(128)S(1)}, s32[128]{0:T(128)}, u32[]{:S(2)}) copy-start(s32[128]{0:T(128)} %sec_ref.1) | copy-start | bytes 1540
  0.0 12.4 %copy-start.7 = (f32[512]{0:T(512)S(1)}, f32[512]{0:T(512)}, u32[]{:S(2)}) copy-start(f32[512]{0:T(512)} %param.9) | copy-start | bytes 6148
  1.2 18.1 %collective-permute-start.4 = (bf16[40,8,1024]{2,1,0:T(8,128)(2,1)S(1)}, bf16[40,8,1024]{2,1,0:T(8,128)(2,1)}, u32[]{:S(2)}, u32[]{:S(2)}) collective-permute-start(bf16[40,8,1024]{2,1,0:T(8,128)(2,1)S(1)} %constant_dynamic-slice_fusion.1), channel_id=1, source_target_pairs={{0,1},{1,0},{2,3},{3,2},{4,5},{5,4},{6,7},{7,6},{8,9},{9,8},{10,11... | collective-permute-start | bytes 1966088 | tf_op jit(solution)/shard_map/ppermute | solution.py:593
  6.7 2.1 %collective-permute-start = (f32[2,8,1152]{2,1,0:T(8,128)}, f32[2,8,1152]{2,1,0:T(8,128)S(1)}, u32[]{:S(2)}, u32[]{:S(2)}) collective-permute-start(f32[2,8,1152]{2,1,0:T(8,128)} %get-tuple-element.40), channel_id=1, source_target_pairs={{0,4},{4,0},{8,12},{12,8},{16,20},{20,16},{24,28},{28,24},{1,5},{5... | collective-permute-start | bytes 221192 | tf_op jit(solution)/shard_map/ppermute | solution.py:557
  7.7 9.7 %copy-start.4 = (s32[2,128]{1,0:T(2,128)}, s32[2,128]{1,0:T(2,128)S(1)}, u32[]{:S(2)}) copy-start(s32[2,128]{1,0:T(2,128)S(1)} %pad_add_fusion.flag_ref) | copy-start | bytes 3076
  7.8 12.4 %collective-permute-start.5 = (s32[2,64]{1,0:T(2,128)S(1)}, s32[2,64]{1,0:T(2,128)S(1)}, u32[]{:S(2)}, u32[]{:S(2)}) collective-permute-start(s32[2,64]{1,0:T(2,128)S(1)} %constant_dynamic-slice_fusion), channel_id=1, source_target_pairs={{0,28},{1,5},{2,30},{3,7},{4,0},{5,9},{6,2},{7,11},{8,4},{9,13},{1... | collective-permute-start | bytes 1544 | tf_op jit(solution)/shard_map/ppermute | solution.py:597
  9.7 7.7 %collective-permute-start.1 = (f32[2,8,1152]{2,1,0:T(8,128)S(1)}, f32[2,8,1152]{2,1,0:T(8,128)S(1)}, u32[]{:S(2)}, u32[]{:S(2)}) collective-permute-start(f32[2,8,1152]{2,1,0:T(8,128)S(1)} %add.29), channel_id=1, source_target_pairs={{0,8},{4,12},{8,0},{12,4},{16,24},{20,28},{24,16},{28,20},{1,9},{5... | collective-permute-start | bytes 221192 | tf_op jit(solution)/shard_map/ppermute | solution.py:557
  10.0 8.6 %collective-permute-start.2 = (f32[2,8,1152]{2,1,0:T(8,128)S(1)}, f32[2,8,1152]{2,1,0:T(8,128)S(1)}, u32[]{:S(2)}, u32[]{:S(2)}) collective-permute-start(f32[2,8,1152]{2,1,0:T(8,128)S(1)} %add.29), channel_id=1, source_target_pairs={{0,16},{4,20},{8,24},{12,28},{16,0},{20,4},{24,8},{28,12},{1,17},{... | collective-permute-start | bytes 221192 | tf_op jit(solution)/shard_map/ppermute | solution.py:557
  11.3 7.4 %collective-permute-start.3 = (f32[2,8,1152]{2,1,0:T(8,128)S(1)}, f32[2,8,1152]{2,1,0:T(8,128)S(1)}, u32[]{:S(2)}, u32[]{:S(2)}) collective-permute-start(f32[2,8,1152]{2,1,0:T(8,128)S(1)} %add.29), channel_id=1, source_target_pairs={{0,24},{4,28},{8,16},{12,20},{16,8},{20,12},{24,0},{28,4},{1,25},{... | collective-permute-start | bytes 221192 | tf_op jit(solution)/shard_map/ppermute | solution.py:557
  17.4 17.6 %collective-permute-start.11 = (bf16[64,8,1024]{2,1,0:T(8,128)(2,1)}, bf16[64,8,1024]{2,1,0:T(8,128)(2,1)}, u32[]{:S(2)}, u32[]{:S(2)}) collective-permute-start(bf16[64,8,1024]{2,1,0:T(8,128)(2,1)} %get-tuple-element.63), channel_id=1, source_target_pairs={{0,28},{1,5},{2,30},{3,7},{4,0},{5,9},{6,2},{7,11},{8,4},{9,13},{1... | collective-permute-start | bytes 3145736 | tf_op jit(solution)/shard_map/ppermute | solution.py:621
  20.2 4.9 %copy-start.2 = (f32[2,8,1152]{2,1,0:T(8,128)}, f32[2,8,1152]{2,1,0:T(8,128)S(1)}, u32[]{:S(2)}) copy-start(f32[2,8,1152]{2,1,0:T(8,128)S(1)} %add_add_fusion.rest_0_) | copy-start | bytes 221188
  20.2 14.8 %copy-start.5 = (s32[2,128]{1,0:T(2,128)S(1)}, s32[2,128]{1,0:T(2,128)}, u32[]{:S(2)}) copy-start(s32[2,128]{1,0:T(2,128)} %copy-done.4) | copy-start | bytes 3076
  20.2 3.9 %collective-permute-start.6 = (f32[2,8,1152]{2,1,0:T(8,128)S(1)}, f32[2,8,1152]{2,1,0:T(8,128)S(1)}, u32[]{:S(2)}, u32[]{:S(2)}) collective-permute-start(f32[2,8,1152]{2,1,0:T(8,128)S(1)} %add_add_fusion.rest_0_), channel_id=1, source_target_pairs={{0,1},{1,0},{2,3},{3,2},{4,5},{5,4},{6,7},{7,6},{8,9},{9,8},{10,11... | collective-permute-start | bytes 221192 | tf_op jit(solution)/shard_map/ppermute | solution.py:625
  21.5 12.7 %collective-permute-start.8 = (bf16[24,8,1024]{2,1,0:T(8,128)(2,1)}, bf16[24,8,1024]{2,1,0:T(8,128)(2,1)}, u32[]{:S(2)}, u32[]{:S(2)}) collective-permute-start(bf16[24,8,1024]{2,1,0:T(8,128)(2,1)} %get-tuple-element.58), channel_id=1, source_target_pairs={{0,1},{1,0},{2,3},{3,2},{4,5},{5,4},{6,7},{7,6},{8,9},{9,8},{10,11... | collective-permute-start | bytes 1179656 | tf_op jit(solution)/shard_map/ppermute | solution.py:626
  21.7 38.6 %collective-permute-start.10 = (bf16[64,8,1024]{2,1,0:T(8,128)(2,1)}, bf16[64,8,1024]{2,1,0:T(8,128)(2,1)}, u32[]{:S(2)}, u32[]{:S(2)}) collective-permute-start(bf16[64,8,1024]{2,1,0:T(8,128)(2,1)} %get-tuple-element.63), channel_id=1, source_target_pairs={{0,1},{1,0},{2,3},{3,2},{4,5},{5,4},{6,7},{7,6},{8,9},{9,8},{10,11... | collective-permute-start | bytes 3145736 | tf_op jit(solution)/shard_map/ppermute | solution.py:627
  24.1 10.1 %copy-start.1 = (f32[2,8,1152]{2,1,0:T(8,128)}, f32[2,8,1152]{2,1,0:T(8,128)S(1)}, u32[]{:S(2)}) copy-start(f32[2,8,1152]{2,1,0:T(8,128)S(1)} %collective-permute-done.6.rest_1_.rest_5_) | copy-start | bytes 221188
  24.2 15.6 %collective-permute-start.7 = (bf16[40,8,1024]{2,1,0:T(8,128)(2,1)}, bf16[40,8,1024]{2,1,0:T(8,128)(2,1)S(1)}, u32[]{:S(2)}, u32[]{:S(2)}) collective-permute-start(bf16[40,8,1024]{2,1,0:T(8,128)(2,1)} %collective-permute-done.4.rest_2_), channel_id=1, source_target_pairs={{0,28},{1,5},{2,30},{3,7},{4,0},{5,9},{6,2},{7,11},{8,4},{9,13},{1... | collective-permute-start | bytes 1966088 | tf_op jit(solution)/shard_map/ppermute | solution.py:631
  34.2 9.9 %collective-permute-start.9 = (bf16[24,8,1024]{2,1,0:T(8,128)(2,1)}, bf16[24,8,1024]{2,1,0:T(8,128)(2,1)}, u32[]{:S(2)}, u32[]{:S(2)}) collective-permute-start(bf16[24,8,1024]{2,1,0:T(8,128)(2,1)} %collective-permute-done.8.rest_3_), channel_id=1, source_target_pairs={{0,28},{1,5},{2,30},{3,7},{4,0},{5,9},{6,2},{7,11},{8,4},{9,13},{1... | collective-permute-start | bytes 1179656 | tf_op jit(solution)/shard_map/ppermute | solution.py:638
  35.0 9.1 %copy-start.6 = (s32[2,192]{1,0:T(2,128)}, s32[2,192]{1,0:T(2,128)S(1)}, u32[]{:S(2)}) copy-start(s32[2,192]{1,0:T(2,128)S(1)} %constant_dynamic-update-slice_fusion.flag_ref) | copy-start | bytes 4612
  86.1 34.3 %collective-permute-start.12 = (bf16[64,32,128]{2,1,0:T(8,128)(2,1)}, bf16[64,32,128]{2,1,0:T(8,128)(2,1)S(1)}, u32[]{:S(2)}, u32[]{:S(2)}) collective-permute-start(bf16[64,32,128]{2,1,0:T(8,128)(2,1)} %get-tuple-element.70), channel_id=1, source_target_pairs={{0,2},{1,31},{2,0},{3,29},{4,6},{5,3},{6,4},{7,1},{8,10},{9,7},{10... | collective-permute-start | bytes 1572872 | tf_op jit(solution)/shard_map/ppermute | solution.py:680
  86.2 47.7 %collective-permute-start.15 = (bf16[64,32,128]{2,1,0:T(8,128)(2,1)}, bf16[64,32,128]{2,1,0:T(8,128)(2,1)S(1)}, u32[]{:S(2)}, u32[]{:S(2)}) collective-permute-start(bf16[64,32,128]{2,1,0:T(8,128)(2,1)} %get-tuple-element.74), channel_id=1, source_target_pairs={{0,3},{1,30},{2,1},{3,28},{4,7},{5,2},{6,5},{7,0},{8,11},{9,6},{10... | collective-permute-start | bytes 1572872 | tf_op jit(solution)/shard_map/ppermute | solution.py:680
  120.4 13.5 %collective-permute-start.13 = (bf16[64,32,128]{2,1,0:T(8,128)(2,1)}, bf16[64,32,128]{2,1,0:T(8,128)(2,1)S(1)}, u32[]{:S(2)}, u32[]{:S(2)}) collective-permute-start(bf16[64,32,128]{2,1,0:T(8,128)(2,1)} %get-tuple-element.71), channel_id=1, source_target_pairs={{0,0},{1,29},{2,2},{3,31},{4,4},{5,1},{6,6},{7,3},{8,8},{9,5},{10,... | collective-permute-start | bytes 1572872 | tf_op jit(solution)/shard_map/ppermute | solution.py:680
  122.1 17.7 %collective-permute-start.14 = (bf16[64,32,128]{2,1,0:T(8,128)(2,1)}, bf16[64,32,128]{2,1,0:T(8,128)(2,1)S(1)}, u32[]{:S(2)}, u32[]{:S(2)}) collective-permute-start(bf16[64,32,128]{2,1,0:T(8,128)(2,1)} %get-tuple-element.73), channel_id=1, source_target_pairs={{0,1},{1,28},{2,3},{3,30},{4,5},{5,0},{6,7},{7,2},{8,9},{9,4},{10,... | collective-permute-start | bytes 1572872 | tf_op jit(solution)/shard_map/ppermute | solution.py:680
  (2 other events, 4.9 us)

commit v14 on v13

--- a/solution.py
+++ b/solution.py
@@ -133,7 +133,7 @@
         part = length // len(parts)
         for n, copy in enumerate(parts):
             copy.wait()
-            repeat(n * part, (n + 1) * part, clean_channel, 4)
+            repeat(n * part, (n + 1) * part, clean_channel, 8)
     for copy in copied["tables"]:
         copy.wait()
 
@@ -215,11 +215,10 @@
 
 def repeat(start, stop, body, together):
     def step(n, _):
-        for i in range(together):
-            body(start + n * together + i)
+        body(n)
         return 0
 
-    lax.fori_loop(0, (stop - start) // together, step, 0)
+    lax.fori_loop(start, stop, step, 0, unroll=math.gcd(together, stop - start))
 
 
 class Choice:
@@ -303,7 +302,7 @@
     for n in range(STEPS):
         part = pl.ds(n * step, step)
 
-        repeat(n * step, (n + 1) * step, lambda k: factor(k, stage), 4)
+        repeat(n * step, (n + 1) * step, lambda k: factor(k, stage), 16)
         copies.append(pltpu.make_async_copy(stage.at[part], target.at[part], sem.at[n]))
         copies[-1].start()
     for copy in copies:
@@ -361,7 +360,7 @@
     for n in range(STEPS):
         part = pl.ds(n * step, step)
 
-        repeat(n * step, (n + 1) * step, lambda k: both_factors(k, b_out), 4)
+        repeat(n * step, (n + 1) * step, lambda k: both_factors(k, b_out), 16)
         for m, (source, target) in enumerate(((a_out, a_hbm), (b_out, b_hbm))):
             copies.append(
                 pltpu.make_async_copy(source.at[part], target.at[part], out_sem.at[2 * n + m])
@@ -454,7 +453,7 @@
     def second(k):
         b3[k] = second_factor(k)
 
-    repeat(0, bins, second, 4)
+    repeat(0, bins, second, 16)
     for copy in late:
         copy.wait()
 
@@ -479,7 +478,7 @@
                         p * width : (p + 1) * width, t * chans : (t + 1) * chans
                     ]
 
-        repeat(0, bins, one_bin, 4)
+        repeat(0, bins, one_bin, 16)
 
     pl.when(odd == 0)(lambda: bins_with(b2, b3))
     pl.when(odd == 1)(lambda: bins_with(b3, b2))
@@ -511,7 +510,7 @@
         for d, out in enumerate(outs):
             out[c] = band[d * share : (d + 1) * share, :].astype(BF16)
 
-    repeat(0, width, one_channel, 4)
+    repeat(0, width, one_channel, 8)
 
 
 def stacks(places, shares, scale, me, flags, total, pieces, hann, conv, seg, lag, a, b0, b2):
@@ -666,12 +665,7 @@
         *(a, b0, b2),
     )
     arrived = {}
-    found = list(found)
     for d in reversed(range(groups)):
-        if d == 1 and groups > 2:
-            found[0], found[1], arrived[2] = lax.optimization_barrier(
-                (found[0], found[1], arrived[2])
-            )
         pairs = [
             (b * groups + z, (b - z % 2) % blocks * groups + (z ^ d))
             for b in range(blocks)

time: 142 us -> 129 us (0.908)
  Pallas kernels: 57.8 us -> 50.8 us
  waiting for transfers between devices: 58.4 us -> 55 us
  starting transfers between devices: 17.3 us -> 14.7 us
    pallas_call x1, Pallas kernels: 25.8 us -> 19.5 us  [stacks(): pl.pallas_call(functools.partial(stack_kernel, places, scale, shares), ou...]
    ppermute x4, waiting for transfers between devices: 47.2 us -> 43.8 us  [shards(): arrived[d] = lax.ppermute(found[d], both, pairs)]
    ppermute x4, starting transfers between devices: 6.47 us -> 3.84 us  [shards(): arrived[d] = lax.ppermute(found[d], both, pairs)]
  transfers between devices with their start and end apart: 16 -> 16, of which waited for: 7 -> 6; matrix products, arithmetic and copies ran while one was open for 3% -> 3% of each run, Pallas kernels for 23% -> 24%
where the time goes in v14:
time: 129 us
  waiting for transfers between devices  55 us (43%)
  Pallas kernels  50.8 us (39%)
  starting transfers between devices  14.7 us (11%)
  other arithmetic  6.02 us (5%)
  local copies, waits for them, and re-layouts  1.89 us (1%)
    ppermute x4, waiting for transfers between devices, shards(): arrived[d] = lax.ppermute(found[d], both, pairs)  43.8 us
    pallas_call x2, Pallas kernels, segments(): pl.pallas_call(functools.partial(kernel, places), out_shape=out, in_specs...  24.6 us
    pallas_call x1, Pallas kernels, stacks(): pl.pallas_call(functools.partial(stack_kernel, places, scale, shares), ou...  19.5 us
    ppermute x1, waiting for transfers between devices, shards(): halo_head = lax.ppermute(their_head, both, halo_pairs)  4.75 us
    ppermute x1, waiting for transfers between devices, shards(): halo_tail = lax.ppermute(forward, both, halo_pairs)  4.32 us
    pallas_call x1, Pallas kernels, shards(): pl.pallas_call(section_sums, out_shape=[jax.ShapeDtypeStruct((NSEC, wins,...  4.11 us
    ppermute x4, starting transfers between devices, shards(): arrived[d] = lax.ppermute(found[d], both, pairs)  3.84 us
    ppermute x4, starting transfers between devices, add_over(): lax.ppermute(value, axis, [(i, i ^ s) for i in range(count)])  3.73 us
  transfers between devices with their start and end apart: 16, of which 6 were waited for; matrix products, arithmetic and copies ran while one was open for 3% of the time, Pallas kernels for 24%

profile of v14, /device:TPU:19, one launch (start us, length us, event | category | flops | bytes accessed | tf_op | source)
XLA Modules:
  0.0 128.6 jit_solution(3795376833323785041)
XLA Ops:
  0.0 1.2 constant_dynamic-slice_fusion.1
  1.2 1.4 %collective-permute-start.4 = (bf16[40,8,1024]{2,1,0:T(8,128)(2,1)S(1)}, bf16[40,8,1024]{2,1,0:T(8,128)(2,1)}, u32[]{:S(2)}, u32[]{:S(2)}) collective-permute-start(bf16[40,8,1024]{2,1,0:T(8,128)(2,1)S(1)} %constant_dynamic-slice_fusion.1), channel_id=1, source_target_pairs={{0,1},{1,0},{2,3},{3,2},{4,5},{5,4},{6,7},{7,6},{8,9},{9,8},{10,11... | collective-permute-start | bytes 1966088 | tf_op jit(solution)/shard_map/ppermute | solution.py:592
  2.5 4.1 %shard_map.82 = (f32[2,8,1152]{2,1,0:T(8,128)}, bf16[64,8,1024]{2,1,0:T(8,128)(2,1)}, bf16[24,8,1024]{2,1,0:T(8,128)(2,1)}) custom-call(s32[1]{0:T(128)} %bitcast.1.odd_ref, s32[128]{0:T(128)} %dead_ref.1, s32[128]{0:T(128)} %sec_ref.1, bf16[128,8,1024]{2,1,0:T(8,128)(2,1)} %rest_1_.1), custom_call_target="tpu_custom_call" | custom-call | flops 1 | bytes 1 | tf_op jit(solution)/shard_map/pallas_call | solution.py:601
  6.7 1.0 collective-permute-start
  7.8 1.0 collective-permute-done
  10.0 1.2 collective-permute-start.2
  11.3 1.2 collective-permute-start.3
  12.4 2.4 %multiply_reduce_fusion = f32[1024]{0:T(1024)} fusion(f32[512,1024]{1,0:T(8,128)} %constant.33.clone, f32[512]{0:T(512)S(1)} %copy-done.7), kind=kLoop, calls=%fused_computation.1 | loop fusion | flops 1047552 | bytes 2103296 | tf_op jit(solution)/shard_map/reduce_sum | solution.py:575
  14.8 2.6 %shard_map.83.rest_3_.rest_8_.rest_7_ = bf16[1024,1024]{1,0:T(8,128)(2,1)} custom-call(f32[1,1024]{1,0:T(1,128)} %bitcast.5), custom_call_target="tpu_custom_call" | custom-call | flops 1 | bytes 1 | tf_op jit(solution)/shard_map/pallas_call | solution.py:576
  17.4 1.2 collective-permute-start.11
  19.3 0.9 add_add_fusion.rest_0_
  20.2 1.3 %collective-permute-start.6 = (f32[2,8,1152]{2,1,0:T(8,128)S(1)}, f32[2,8,1152]{2,1,0:T(8,128)S(1)}, u32[]{:S(2)}, u32[]{:S(2)}) collective-permute-start(f32[2,8,1152]{2,1,0:T(8,128)S(1)} %add_add_fusion.rest_0_), channel_id=1, source_target_pairs={{0,1},{1,0},{2,3},{3,2},{4,5},{5,4},{6,7},{7,6},{8,9},{9,8},{10,11... | collective-permute-start | bytes 221192 | tf_op jit(solution)/shard_map/ppermute | solution.py:624
  21.7 1.3 collective-permute-start.10
  23.0 1.1 collective-permute-done.6.rest_1_.rest_5_
  25.1 9.1 %shard_map.84 = (bf16[128,128,128]{2,1,0:T(8,128)(2,1)}, bf16[2,1152,512]{2,1,0:T(8,128)(2,1)}) custom-call(s32[1]{0:T(128)} %bitcast.1.odd_ref, s32[2,128]{1,0:T(2,128)} %copy-done.4, f32[2,8,1152]{2,1,0:T(8,128)} %copy-done.2, bf16[128,8,1024]{2,1,0:T(8,128)(2,1)} %rest_1_.1, f32[1,1024]{1,0:T(1,128)} %constant.36.clone.rest_2_.rest_7_.rest_6_, ...), custom_call_target="tpu_custom_call" | custom-call | flops 3758096384 | bytes 16777216 | tf_op jit(solution)/shard_map/pallas_call | solution.py:405
  35.0 4.7 %collective-permute-done.7.rest_4_.rest_0_ = bf16[40,8,1024]{2,1,0:T(8,128)(2,1)S(1)} collective-permute-done((bf16[40,8,1024]{2,1,0:T(8,128)(2,1)}, bf16[40,8,1024]{2,1,0:T(8,128)(2,1)S(1)}, u32[]{:S(2)}, u32[]{:S(2)}) %collective-permute-start.7) | collective-permute-done | bytes 655392 | tf_op jit(solution)/shard_map/ppermute | solution.py:630
  39.8 4.3 %collective-permute-done.9.rest_5_.rest_1_ = bf16[24,8,1024]{2,1,0:T(8,128)(2,1)} collective-permute-done((bf16[24,8,1024]{2,1,0:T(8,128)(2,1)}, bf16[24,8,1024]{2,1,0:T(8,128)(2,1)}, u32[]{:S(2)}, u32[]{:S(2)}) %collective-permute-start.9) | collective-permute-done | bytes 393248 | tf_op jit(solution)/shard_map/ppermute | solution.py:637
  44.1 15.5 %shard_map.85 = (bf16[128,2,128,128]{3,2,1,0:T(8,128)(2,1)}, bf16[128,128,128]{2,1,0:T(8,128)(2,1)}) custom-call(s32[1]{0:T(128)} %bitcast.1.odd_ref, s32[2,192]{1,0:T(2,128)} %copy-done.6, f32[2,8,1152]{2,1,0:T(8,128)} %copy-done.2, f32[2,8,1152]{2,1,0:T(8,128)} %copy-done.1, bf16[40,8,1024]{2,1,0:T(8,128)(2,1)} %collective-permute-done.4.rest_2_, ...), custom_call_target="tpu_custom_call" | custom-call | flops 3758096384 | bytes 16777216 | tf_op jit(solution)/shard_map/pallas_call | solution.py:405
  59.6 19.5 %shard_map.86 = (bf16[64,32,128]{2,1,0:T(8,128)(2,1)}, bf16[64,32,128]{2,1,0:T(8,128)(2,1)}, bf16[64,32,128]{2,1,0:T(8,128)(2,1)}, bf16[64,32,128]{2,1,0:T(8,128)(2,1)}) custom-call(s32[1]{0:T(128)} %bitcast.me_ref, s32[2,192]{1,0:T(2,128)} %copy-done.6, bf16[40,8,1024]{2,1,0:T(8,128)(2,1)} %copy-done, ...), custom_call_target="tpu_custom_call" | custom-call | flops 4294967296 | bytes 20971520 | tf_op jit(solution)/shard_map/pallas_call | solution.py:527
  79.2 1.7 %collective-permute-start.12 = (bf16[64,32,128]{2,1,0:T(8,128)(2,1)}, bf16[64,32,128]{2,1,0:T(8,128)(2,1)S(1)}, u32[]{:S(2)}, u32[]{:S(2)}) collective-permute-start(bf16[64,32,128]{2,1,0:T(8,128)(2,1)} %get-tuple-element.65), channel_id=1, source_target_pairs={{0,0},{1,29},{2,2},{3,31},{4,4},{5,1},{6,6},{7,3},{8,8},{9,5},{10,... | collective-permute-start | bytes 1572872 | tf_op jit(solution)/shard_map/ppermute | solution.py:674
  80.9 1.1 collective-permute-start.15
  82.9 30.4 %collective-permute-done.13 = bf16[64,32,128]{2,1,0:T(8,128)(2,1)S(1)} collective-permute-done((bf16[64,32,128]{2,1,0:T(8,128)(2,1)}, bf16[64,32,128]{2,1,0:T(8,128)(2,1)S(1)}, u32[]{:S(2)}, u32[]{:S(2)}) %collective-permute-start.13) | collective-permute-done | bytes 524320 | tf_op jit(solution)/shard_map/ppermute | solution.py:674
  113.3 13.4 %collective-permute-done.15 = bf16[64,32,128]{2,1,0:T(8,128)(2,1)S(1)} collective-permute-done((bf16[64,32,128]{2,1,0:T(8,128)(2,1)}, bf16[64,32,128]{2,1,0:T(8,128)(2,1)S(1)}, u32[]{:S(2)}, u32[]{:S(2)}) %collective-permute-start.15) | collective-permute-done | bytes 524320 | tf_op jit(solution)/shard_map/ppermute | solution.py:674
  127.1 1.5 %pad_maximum_fusion = f32[128,32,128]{2,1,0:T(8,128)} fusion(f32[64,32,128]{2,1,0:T(8,128)S(1)} %get-tuple-element.70, f32[64,32,128]{2,1,0:T(8,128)S(1)} %get-tuple-element.69), kind=kLoop, calls=%fused_computation | loop fusion | flops 524288 | bytes 4194304 | tf_op jit(solution)/shard_map/concatenate | solution.py:678
  (43 shorter events, 5.3 us)
Async XLA Ops:
  0.0 7.7 %copy-start.9 = (s32[128]{0:T(128)S(1)}, s32[128]{0:T(128)}, u32[]{:S(2)}) copy-start(s32[128]{0:T(128)} %dead_ref.1) | copy-start | bytes 1540
  0.0 7.7 %copy-start.8 = (s32[128]{0:T(128)S(1)}, s32[128]{0:T(128)}, u32[]{:S(2)}) copy-start(s32[128]{0:T(128)} %sec_ref.1) | copy-start | bytes 1540
  0.0 12.4 %copy-start.7 = (f32[512]{0:T(512)S(1)}, f32[512]{0:T(512)}, u32[]{:S(2)}) copy-start(f32[512]{0:T(512)} %param.9) | copy-start | bytes 6148
  1.2 18.1 %collective-permute-start.4 = (bf16[40,8,1024]{2,1,0:T(8,128)(2,1)S(1)}, bf16[40,8,1024]{2,1,0:T(8,128)(2,1)}, u32[]{:S(2)}, u32[]{:S(2)}) collective-permute-start(bf16[40,8,1024]{2,1,0:T(8,128)(2,1)S(1)} %constant_dynamic-slice_fusion.1), channel_id=1, source_target_pairs={{0,1},{1,0},{2,3},{3,2},{4,5},{5,4},{6,7},{7,6},{8,9},{9,8},{10,11... | collective-permute-start | bytes 1966088 | tf_op jit(solution)/shard_map/ppermute | solution.py:592
  6.7 2.1 %collective-permute-start = (f32[2,8,1152]{2,1,0:T(8,128)}, f32[2,8,1152]{2,1,0:T(8,128)S(1)}, u32[]{:S(2)}, u32[]{:S(2)}) collective-permute-start(f32[2,8,1152]{2,1,0:T(8,128)} %get-tuple-element.37), channel_id=1, source_target_pairs={{0,4},{4,0},{8,12},{12,8},{16,20},{20,16},{24,28},{28,24},{1,5},{5... | collective-permute-start | bytes 221192 | tf_op jit(solution)/shard_map/ppermute | solution.py:556
  7.7 9.7 %copy-start.4 = (s32[2,128]{1,0:T(2,128)}, s32[2,128]{1,0:T(2,128)S(1)}, u32[]{:S(2)}) copy-start(s32[2,128]{1,0:T(2,128)S(1)} %pad_add_fusion.flag_ref) | copy-start | bytes 3076
  7.8 12.4 %collective-permute-start.5 = (s32[2,64]{1,0:T(2,128)S(1)}, s32[2,64]{1,0:T(2,128)S(1)}, u32[]{:S(2)}, u32[]{:S(2)}) collective-permute-start(s32[2,64]{1,0:T(2,128)S(1)} %constant_dynamic-slice_fusion), channel_id=1, source_target_pairs={{0,28},{1,5},{2,30},{3,7},{4,0},{5,9},{6,2},{7,11},{8,4},{9,13},{1... | collective-permute-start | bytes 1544 | tf_op jit(solution)/shard_map/ppermute | solution.py:596
  9.7 7.7 %collective-permute-start.1 = (f32[2,8,1152]{2,1,0:T(8,128)S(1)}, f32[2,8,1152]{2,1,0:T(8,128)S(1)}, u32[]{:S(2)}, u32[]{:S(2)}) collective-permute-start(f32[2,8,1152]{2,1,0:T(8,128)S(1)} %add.29), channel_id=1, source_target_pairs={{0,8},{4,12},{8,0},{12,4},{16,24},{20,28},{24,16},{28,20},{1,9},{5... | collective-permute-start | bytes 221192 | tf_op jit(solution)/shard_map/ppermute | solution.py:556
  10.0 8.6 %collective-permute-start.2 = (f32[2,8,1152]{2,1,0:T(8,128)S(1)}, f32[2,8,1152]{2,1,0:T(8,128)S(1)}, u32[]{:S(2)}, u32[]{:S(2)}) collective-permute-start(f32[2,8,1152]{2,1,0:T(8,128)S(1)} %add.29), channel_id=1, source_target_pairs={{0,16},{4,20},{8,24},{12,28},{16,0},{20,4},{24,8},{28,12},{1,17},{... | collective-permute-start | bytes 221192 | tf_op jit(solution)/shard_map/ppermute | solution.py:556
  11.3 7.4 %collective-permute-start.3 = (f32[2,8,1152]{2,1,0:T(8,128)S(1)}, f32[2,8,1152]{2,1,0:T(8,128)S(1)}, u32[]{:S(2)}, u32[]{:S(2)}) collective-permute-start(f32[2,8,1152]{2,1,0:T(8,128)S(1)} %add.29), channel_id=1, source_target_pairs={{0,24},{4,28},{8,16},{12,20},{16,8},{20,12},{24,0},{28,4},{1,25},{... | collective-permute-start | bytes 221192 | tf_op jit(solution)/shard_map/ppermute | solution.py:556
  17.4 17.6 %collective-permute-start.11 = (bf16[64,8,1024]{2,1,0:T(8,128)(2,1)}, bf16[64,8,1024]{2,1,0:T(8,128)(2,1)}, u32[]{:S(2)}, u32[]{:S(2)}) collective-permute-start(bf16[64,8,1024]{2,1,0:T(8,128)(2,1)} %get-tuple-element.60), channel_id=1, source_target_pairs={{0,28},{1,5},{2,30},{3,7},{4,0},{5,9},{6,2},{7,11},{8,4},{9,13},{1... | collective-permute-start | bytes 3145736 | tf_op jit(solution)/shard_map/ppermute | solution.py:620
  20.2 4.9 %copy-start.2 = (f32[2,8,1152]{2,1,0:T(8,128)}, f32[2,8,1152]{2,1,0:T(8,128)S(1)}, u32[]{:S(2)}) copy-start(f32[2,8,1152]{2,1,0:T(8,128)S(1)} %add_add_fusion.rest_0_) | copy-start | bytes 221188
  20.2 14.8 %copy-start.5 = (s32[2,128]{1,0:T(2,128)S(1)}, s32[2,128]{1,0:T(2,128)}, u32[]{:S(2)}) copy-start(s32[2,128]{1,0:T(2,128)} %copy-done.4) | copy-start | bytes 3076
  20.2 3.9 %collective-permute-start.6 = (f32[2,8,1152]{2,1,0:T(8,128)S(1)}, f32[2,8,1152]{2,1,0:T(8,128)S(1)}, u32[]{:S(2)}, u32[]{:S(2)}) collective-permute-start(f32[2,8,1152]{2,1,0:T(8,128)S(1)} %add_add_fusion.rest_0_), channel_id=1, source_target_pairs={{0,1},{1,0},{2,3},{3,2},{4,5},{5,4},{6,7},{7,6},{8,9},{9,8},{10,11... | collective-permute-start | bytes 221192 | tf_op jit(solution)/shard_map/ppermute | solution.py:624
  21.5 12.7 %collective-permute-start.8 = (bf16[24,8,1024]{2,1,0:T(8,128)(2,1)}, bf16[24,8,1024]{2,1,0:T(8,128)(2,1)}, u32[]{:S(2)}, u32[]{:S(2)}) collective-permute-start(bf16[24,8,1024]{2,1,0:T(8,128)(2,1)} %get-tuple-element.55), channel_id=1, source_target_pairs={{0,1},{1,0},{2,3},{3,2},{4,5},{5,4},{6,7},{7,6},{8,9},{9,8},{10,11... | collective-permute-start | bytes 1179656 | tf_op jit(solution)/shard_map/ppermute | solution.py:625
  21.7 37.9 %collective-permute-start.10 = (bf16[64,8,1024]{2,1,0:T(8,128)(2,1)}, bf16[64,8,1024]{2,1,0:T(8,128)(2,1)}, u32[]{:S(2)}, u32[]{:S(2)}) collective-permute-start(bf16[64,8,1024]{2,1,0:T(8,128)(2,1)} %get-tuple-element.60), channel_id=1, source_target_pairs={{0,1},{1,0},{2,3},{3,2},{4,5},{5,4},{6,7},{7,6},{8,9},{9,8},{10,11... | collective-permute-start | bytes 3145736 | tf_op jit(solution)/shard_map/ppermute | solution.py:626
  24.1 10.0 %copy-start.1 = (f32[2,8,1152]{2,1,0:T(8,128)}, f32[2,8,1152]{2,1,0:T(8,128)S(1)}, u32[]{:S(2)}) copy-start(f32[2,8,1152]{2,1,0:T(8,128)S(1)} %collective-permute-done.6.rest_1_.rest_5_) | copy-start | bytes 221188
  24.2 15.6 %collective-permute-start.7 = (bf16[40,8,1024]{2,1,0:T(8,128)(2,1)}, bf16[40,8,1024]{2,1,0:T(8,128)(2,1)S(1)}, u32[]{:S(2)}, u32[]{:S(2)}) collective-permute-start(bf16[40,8,1024]{2,1,0:T(8,128)(2,1)} %collective-permute-done.4.rest_2_), channel_id=1, source_target_pairs={{0,28},{1,5},{2,30},{3,7},{4,0},{5,9},{6,2},{7,11},{8,4},{9,13},{1... | collective-permute-start | bytes 1966088 | tf_op jit(solution)/shard_map/ppermute | solution.py:630
  34.2 9.9 %collective-permute-start.9 = (bf16[24,8,1024]{2,1,0:T(8,128)(2,1)}, bf16[24,8,1024]{2,1,0:T(8,128)(2,1)}, u32[]{:S(2)}, u32[]{:S(2)}) collective-permute-start(bf16[24,8,1024]{2,1,0:T(8,128)(2,1)} %collective-permute-done.8.rest_3_), channel_id=1, source_target_pairs={{0,28},{1,5},{2,30},{3,7},{4,0},{5,9},{6,2},{7,11},{8,4},{9,13},{1... | collective-permute-start | bytes 1179656 | tf_op jit(solution)/shard_map/ppermute | solution.py:637
  35.0 9.1 %copy-start.6 = (s32[2,192]{1,0:T(2,128)}, s32[2,192]{1,0:T(2,128)S(1)}, u32[]{:S(2)}) copy-start(s32[2,192]{1,0:T(2,128)S(1)} %constant_dynamic-update-slice_fusion.flag_ref) | copy-start | bytes 4612
  79.1 34.2 %collective-permute-start.13 = (bf16[64,32,128]{2,1,0:T(8,128)(2,1)}, bf16[64,32,128]{2,1,0:T(8,128)(2,1)S(1)}, u32[]{:S(2)}, u32[]{:S(2)}) collective-permute-start(bf16[64,32,128]{2,1,0:T(8,128)(2,1)} %get-tuple-element.66), channel_id=1, source_target_pairs={{0,2},{1,31},{2,0},{3,29},{4,6},{5,3},{6,4},{7,1},{8,10},{9,7},{10... | collective-permute-start | bytes 1572872 | tf_op jit(solution)/shard_map/ppermute | solution.py:674
  79.2 34.1 %collective-permute-start.12 = (bf16[64,32,128]{2,1,0:T(8,128)(2,1)}, bf16[64,32,128]{2,1,0:T(8,128)(2,1)S(1)}, u32[]{:S(2)}, u32[]{:S(2)}) collective-permute-start(bf16[64,32,128]{2,1,0:T(8,128)(2,1)} %get-tuple-element.65), channel_id=1, source_target_pairs={{0,0},{1,29},{2,2},{3,31},{4,4},{5,1},{6,6},{7,3},{8,8},{9,5},{10,... | collective-permute-start | bytes 1572872 | tf_op jit(solution)/shard_map/ppermute | solution.py:674
  80.9 45.9 %collective-permute-start.15 = (bf16[64,32,128]{2,1,0:T(8,128)(2,1)}, bf16[64,32,128]{2,1,0:T(8,128)(2,1)S(1)}, u32[]{:S(2)}, u32[]{:S(2)}) collective-permute-start(bf16[64,32,128]{2,1,0:T(8,128)(2,1)} %get-tuple-element.68), channel_id=1, source_target_pairs={{0,3},{1,30},{2,1},{3,28},{4,7},{5,2},{6,5},{7,0},{8,11},{9,6},{10... | collective-permute-start | bytes 1572872 | tf_op jit(solution)/shard_map/ppermute | solution.py:674
  82.0 44.7 %collective-permute-start.14 = (bf16[64,32,128]{2,1,0:T(8,128)(2,1)}, bf16[64,32,128]{2,1,0:T(8,128)(2,1)S(1)}, u32[]{:S(2)}, u32[]{:S(2)}) collective-permute-start(bf16[64,32,128]{2,1,0:T(8,128)(2,1)} %get-tuple-element.67), channel_id=1, source_target_pairs={{0,1},{1,28},{2,3},{3,30},{4,5},{5,0},{6,7},{7,2},{8,9},{9,4},{10,... | collective-permute-start | bytes 1572872 | tf_op jit(solution)/shard_map/ppermute | solution.py:674
  (2 other events, 4.9 us)

commit v15 on v14

--- a/solution.py
+++ b/solution.py
@@ -87,7 +87,7 @@
 
 def circulant_kernel(filter_ref, out_ref):
     ns = filter_ref.shape[1]
-    for t in range(0, ns, 16):
+    for t in range(0, TILE, 16):
         block = jnp.broadcast_to(filter_ref[...], (16, ns))
         out_ref[t : t + 16, :] = pltpu.roll(block, t, 1, stride=1, stride_axis=0).astype(BF16)
 
@@ -152,8 +152,9 @@
                     clean[t, window, :] * level
                 ).astype(BF16)
         for t in range(0, ns, TILE):
+            turned = jnp.concatenate([conv[:, ns - t :], conv[:, : ns - t]], axis=1) if t else conv[...]
             series[half // 2 + t : half // 2 + t + TILE, :] = lax.dot_general(
-                conv[t : t + TILE, :], rows[...], NT, preferred_element_type=F32
+                turned, rows[...], NT, preferred_element_type=F32
             ).astype(BF16)
         series[: half // 2, :] = series[ns : ns + half // 2, :]
         series[ns + half // 2 :, :] = series[half // 2 : half, :]
@@ -180,23 +181,20 @@
                 )
                 place(0, j, a)
 
-    def factor(which, k, turn=False):
-        real, imag = [
-            stage[which, pl.ds((2 * k + part) * jpitch, jw), :] for part in range(2)
+    def parts(which, k):
+        return [
+            stage[which, pl.ds((2 * k + part) * jpitch, jw), :].astype(BF16) for part in range(2)
         ]
-        if turn:
-            real, imag = imag, -real
-        return jnp.concatenate([real.astype(BF16), imag.astype(BF16)], axis=0)
-
-    def first_factor(k, put):
-        width = chans // 2
-        for part in range(2):
-            value = factor(0, k, part == 1).T
-            rows_at = slice(part * width, (part + 1) * width)
-            put(1, rows_at, value[:width])
-            put(0, rows_at, value[width:])
-
-    return first_factor, lambda k: factor(1, k)
+
+    lower = lax.broadcasted_iota(jnp.int32, (1, chans), 1) < chans // 2
+
+    def first_factor(k):
+        real, imag = parts(0, k)
+        return jnp.concatenate(
+            [jnp.where(lower, imag, real), jnp.where(lower, real, imag)], axis=0
+        ).T
+
+    return first_factor, lambda k: jnp.concatenate(parts(1, k), axis=0)
 
 
 def work_shapes(groups, chans, wins, ns):
@@ -302,7 +300,7 @@
     for n in range(STEPS):
         part = pl.ds(n * step, step)
 
-        repeat(n * step, (n + 1) * step, lambda k: factor(k, stage), 16)
+        repeat(n * step, (n + 1) * step, lambda k: factor(k, stage), 32)
         copies.append(pltpu.make_async_copy(stage.at[part], target.at[part], sem.at[n]))
         copies[-1].start()
     for copy in copies:
@@ -349,10 +347,10 @@
     )
 
     def both_factors(k, stage):
-        def put(group, rows, value):
-            a_out[k, group, rows] = value
-
-        first_factor(k, put)
+        value = first_factor(k)
+        width = value.shape[0] // 2
+        a_out[k, 1] = value[:width]
+        a_out[k, 0] = value[width:]
         stage[k] = second_factor(k)
 
     step = b_out.shape[0] // STEPS
@@ -380,7 +378,7 @@
     anywhere = pl.BlockSpec(memory_space=pl.ANY)
     b_shape = jax.ShapeDtypeStruct((half, depth, chans), BF16)
     p_shape = jax.ShapeDtypeStruct((wins // TOGETHER, ns + half, TOGETHER * chans), BF16)
-    a_shape = jax.ShapeDtypeStruct((half, 2, chans, depth), BF16)
+    a_shape = jax.ShapeDtypeStruct((half, 2, chans // 2, depth), BF16)
     scratch = lambda *values: [pltpu.VMEM(value.shape, value.dtype) for value in values]
     operands = list(totals) + list(pieces) + [hann, conv, seg]
     count = len(operands) + chans // PART
@@ -453,24 +451,32 @@
     def second(k):
         b3[k] = second_factor(k)
 
-    repeat(0, bins, second, 16)
+    repeat(0, bins, second, 32)
     for copy in late:
         copy.wait()
 
     lane = lax.broadcasted_iota(jnp.int32, (1, chans), 1)
     low, high = [jnp.where((lane < width) == (g == 0), 1.0, 0.0).astype(BF16) for g in range(2)]
+
+    lower = lane < width
 
     def bins_with(near, far):
         def one_bin(k):
             inner = near[k] * low + b3[k] * high if near is not b3 else b3[k]
-            right = jnp.concatenate(
+            own = jnp.concatenate([b0[k], b2[k] * high], axis=1)
+            theirs = jnp.concatenate([inner, far[k] * low], axis=1)
+            part = depth // 2
+            right = jnp.concatenate([own[:part], theirs[:part], theirs[part:], own[part:]], axis=0)
+            real = jnp.where(lower, a[k, 0], a[k, 1])
+            imag = jnp.where(lower, a[k, 1], a[k, 0])
+            turn = lambda v: jnp.concatenate([v[:, part:], v[:, :part]], axis=1)
+            left = jnp.concatenate(
                 [
-                    jnp.concatenate([b0[k], b2[k] * high], axis=1),
-                    jnp.concatenate([inner, far[k] * low], axis=1),
+                    jnp.concatenate([real, imag], axis=1),
+                    jnp.concatenate([turn(imag), -turn(real)], axis=1),
                 ],
                 axis=0,
             )
-            left = jnp.concatenate([a[k, 0], a[k, 1]], axis=1)
             value = jnp.dot(left, right, preferred_element_type=F32)
             for p in range(2):
                 for t in range(2):
@@ -478,7 +484,7 @@
                         p * width : (p + 1) * width, t * chans : (t + 1) * chans
                     ]
 
-        repeat(0, bins, one_bin, 16)
+        repeat(0, bins, one_bin, 32)
 
     pl.when(odd == 0)(lambda: bins_with(b2, b3))
     pl.when(odd == 1)(lambda: bins_with(b3, b2))
@@ -510,7 +516,7 @@
         for d, out in enumerate(outs):
             out[c] = band[d * share : (d + 1) * share, :].astype(BF16)
 
-    repeat(0, width, one_channel, 8)
+    repeat(0, width, one_channel, 16)
 
 
 def stacks(places, shares, scale, me, flags, total, pieces, hann, conv, seg, lag, a, b0, b2):
@@ -575,7 +581,7 @@
     response = jnp.sum(band_gain[:, None] * waves, axis=0, keepdims=True)
     conv = pl.pallas_call(
         circulant_kernel,
-        out_shape=jax.ShapeDtypeStruct((ns, ns), BF16),
+        out_shape=jax.ShapeDtypeStruct((TILE, ns), BF16),
         compiler_params=pltpu.CompilerParams(vmem_limit_bytes=VMEM),
         cost_estimate=pl.CostEstimate(flops=1, bytes_accessed=1, transcendentals=0),
     )(response)

time: 129 us -> 124 us (0.961)
  Pallas kernels: 50.8 us -> 45.8 us
    pallas_call x2, Pallas kernels: 24.6 us -> 22.5 us  [segments(): pl.pallas_call(functools.partial(kernel, places), out_shape=out, in_specs...]
    pallas_call x1, Pallas kernels: 19.5 us -> 17.6 us  [stacks(): pl.pallas_call(functools.partial(stack_kernel, places, scale, shares), ou...]
  transfers between devices with their start and end apart: 16 -> 16, of which waited for: 6 -> 6; matrix products, arithmetic and copies ran while one was open for 3% -> 4% of each run, Pallas kernels for 24% -> 23%
where the time goes in v15:
time: 124 us; the launch traced here: 123 us
  waiting for transfers between devices  53.9 us (43%)
  Pallas kernels  45.8 us (37%)
  starting transfers between devices  14.9 us (12%)
  other arithmetic  5.99 us (5%)
  local copies, waits for them, and re-layouts  2.57 us (2%)
    ppermute x4, waiting for transfers between devices, shards(): arrived[d] = lax.ppermute(found[d], both, pairs)  43.5 us
    pallas_call x2, Pallas kernels, segments(): pl.pallas_call(functools.partial(kernel, places), out_shape=out, in_specs...  22.5 us
    pallas_call x1, Pallas kernels, stacks(): pl.pallas_call(functools.partial(stack_kernel, places, scale, shares), ou...  17.6 us
    ppermute x1, waiting for transfers between devices, shards(): halo_tail = lax.ppermute(forward, both, halo_pairs)  4.32 us
    ppermute x1, waiting for transfers between devices, shards(): halo_head = lax.ppermute(their_head, both, halo_pairs)  4.13 us
    pallas_call x1, Pallas kernels, shards(): pl.pallas_call(section_sums, out_shape=[jax.ShapeDtypeStruct((NSEC, wins,...  4.08 us
    ppermute x4, starting transfers between devices, shards(): arrived[d] = lax.ppermute(found[d], both, pairs)  3.84 us
    ppermute x4, starting transfers between devices, add_over(): lax.ppermute(value, axis, [(i, i ^ s) for i in range(count)])  3.73 us
  transfers between devices with their start and end apart: 16, of which 6 were waited for; matrix products, arithmetic and copies ran while one was open for 4% of the time, Pallas kernels for 23%

profile of v15, /device:TPU:19, one launch (start us, length us, event | category | flops | bytes accessed | tf_op | source)
XLA Modules:
  0.0 123.3 jit_solution(4839822113723303238)
XLA Ops:
  0.0 1.2 constant_dynamic-slice_fusion.1
  1.2 1.4 %collective-permute-start.4 = (bf16[40,8,1024]{2,1,0:T(8,128)(2,1)S(1)}, bf16[40,8,1024]{2,1,0:T(8,128)(2,1)}, u32[]{:S(2)}, u32[]{:S(2)}) collective-permute-start(bf16[40,8,1024]{2,1,0:T(8,128)(2,1)S(1)} %constant_dynamic-slice_fusion.1), channel_id=1, source_target_pairs={{0,1},{1,0},{2,3},{3,2},{4,5},{5,4},{6,7},{7,6},{8,9},{9,8},{10,11... | collective-permute-start | bytes 1966088 | tf_op jit(solution)/shard_map/ppermute | solution.py:598
  2.5 4.1 %shard_map.82 = (f32[2,8,1152]{2,1,0:T(8,128)}, bf16[64,8,1024]{2,1,0:T(8,128)(2,1)}, bf16[24,8,1024]{2,1,0:T(8,128)(2,1)}) custom-call(s32[1]{0:T(128)} %bitcast.1.odd_ref, s32[128]{0:T(128)} %dead_ref.1, s32[128]{0:T(128)} %sec_ref.1, bf16[128,8,1024]{2,1,0:T(8,128)(2,1)} %rest_1_.1), custom_call_target="tpu_custom_call" | custom-call | flops 1 | bytes 1 | tf_op jit(solution)/shard_map/pallas_call | solution.py:607
  6.6 1.0 collective-permute-start
  7.8 1.0 collective-permute-done
  10.0 1.2 %collective-permute-start.2 = (f32[2,8,1152]{2,1,0:T(8,128)S(1)}, f32[2,8,1152]{2,1,0:T(8,128)S(1)}, u32[]{:S(2)}, u32[]{:S(2)}) collective-permute-start(f32[2,8,1152]{2,1,0:T(8,128)S(1)} %add.29), channel_id=1, source_target_pairs={{0,16},{4,20},{8,24},{12,28},{16,0},{20,4},{24,8},{28,12},{1,17},{... | collective-permute-start | bytes 221192 | tf_op jit(solution)/shard_map/ppermute | solution.py:562
  11.2 1.2 collective-permute-start.3
  12.4 2.4 %multiply_reduce_fusion = f32[1024]{0:T(1024)} fusion(f32[512,1024]{1,0:T(8,128)} %constant.33.clone, f32[512]{0:T(512)S(1)} %copy-done.6), kind=kLoop, calls=%fused_computation.1 | loop fusion | flops 1047552 | bytes 2103296 | tf_op jit(solution)/shard_map/reduce_sum | solution.py:581
  14.8 1.7 %shard_map.83.rest_3_.rest_8_.rest_7_ = bf16[256,1024]{1,0:T(8,128)(2,1)} custom-call(f32[1,1024]{1,0:T(1,128)} %bitcast.5), custom_call_target="tpu_custom_call" | custom-call | flops 1 | bytes 1 | tf_op jit(solution)/shard_map/pallas_call | solution.py:582
  16.4 1.2 collective-permute-start.11
  18.3 0.9 add_add_fusion.rest_0_
  19.2 1.3 %collective-permute-start.6 = (f32[2,8,1152]{2,1,0:T(8,128)S(1)}, f32[2,8,1152]{2,1,0:T(8,128)S(1)}, u32[]{:S(2)}, u32[]{:S(2)}) collective-permute-start(f32[2,8,1152]{2,1,0:T(8,128)S(1)} %add_add_fusion.rest_0_), channel_id=1, source_target_pairs={{0,1},{1,0},{2,3},{3,2},{4,5},{5,4},{6,7},{7,6},{8,9},{9,8},{10,11... | collective-permute-start | bytes 221192 | tf_op jit(solution)/shard_map/ppermute | solution.py:630
  20.7 1.3 %collective-permute-start.10 = (bf16[64,8,1024]{2,1,0:T(8,128)(2,1)}, bf16[64,8,1024]{2,1,0:T(8,128)(2,1)}, u32[]{:S(2)}, u32[]{:S(2)}) collective-permute-start(bf16[64,8,1024]{2,1,0:T(8,128)(2,1)} %get-tuple-element.60), channel_id=1, source_target_pairs={{0,1},{1,0},{2,3},{3,2},{4,5},{5,4},{6,7},{7,6},{8,9},{9,8},{10,11... | collective-permute-start | bytes 3145736 | tf_op jit(solution)/shard_map/ppermute | solution.py:632
  22.9 1.2 collective-permute-start.7
  24.1 9.1 %shard_map.84 = (bf16[128,128,128]{2,1,0:T(8,128)(2,1)}, bf16[2,1152,512]{2,1,0:T(8,128)(2,1)}) custom-call(s32[1]{0:T(128)} %bitcast.1.odd_ref, s32[2,128]{1,0:T(2,128)} %copy-done.4, f32[2,8,1152]{2,1,0:T(8,128)} %copy-done.2, bf16[128,8,1024]{2,1,0:T(8,128)(2,1)} %rest_1_.1, f32[1,1024]{1,0:T(1,128)} %constant.36.clone.rest_2_.rest_7_.rest_6_, ...), custom_call_target="tpu_custom_call" | custom-call | flops 3758096384 | bytes 16777216 | tf_op jit(solution)/shard_map/pallas_call | solution.py:403
  34.6 4.1 %collective-permute-done.7.rest_4_.rest_0_ = bf16[40,8,1024]{2,1,0:T(8,128)(2,1)S(1)} collective-permute-done((bf16[40,8,1024]{2,1,0:T(8,128)(2,1)}, bf16[40,8,1024]{2,1,0:T(8,128)(2,1)S(1)}, u32[]{:S(2)}, u32[]{:S(2)}) %collective-permute-start.7) | collective-permute-done | bytes 655392 | tf_op jit(solution)/shard_map/ppermute | solution.py:636
  38.8 4.3 %collective-permute-done.9.rest_5_.rest_1_ = bf16[24,8,1024]{2,1,0:T(8,128)(2,1)} collective-permute-done((bf16[24,8,1024]{2,1,0:T(8,128)(2,1)}, bf16[24,8,1024]{2,1,0:T(8,128)(2,1)}, u32[]{:S(2)}, u32[]{:S(2)}) %collective-permute-start.9) | collective-permute-done | bytes 393248 | tf_op jit(solution)/shard_map/ppermute | solution.py:643
  43.1 13.4 %shard_map.85 = (bf16[128,2,64,128]{3,2,1,0:T(8,128)(2,1)}, bf16[128,128,128]{2,1,0:T(8,128)(2,1)}) custom-call(s32[1]{0:T(128)} %bitcast.1.odd_ref, s32[2,192]{1,0:T(2,128)} %copy-done.5, f32[2,8,1152]{2,1,0:T(8,128)} %copy-done.2, f32[2,8,1152]{2,1,0:T(8,128)} %copy-done.1, bf16[40,8,1024]{2,1,0:T(8,128)(2,1)} %collective-permute-done.4.rest_2_, ...), custom_call_target="tpu_custom_call" | custom-call | flops 3758096384 | bytes 16777216 | tf_op jit(solution)/shard_map/pallas_call | solution.py:403
  56.5 17.6 %shard_map.86 = (bf16[64,32,128]{2,1,0:T(8,128)(2,1)}, bf16[64,32,128]{2,1,0:T(8,128)(2,1)}, bf16[64,32,128]{2,1,0:T(8,128)(2,1)}, bf16[64,32,128]{2,1,0:T(8,128)(2,1)}) custom-call(s32[1]{0:T(128)} %bitcast.me_ref, s32[2,192]{1,0:T(2,128)} %copy-done.5, bf16[40,8,1024]{2,1,0:T(8,128)(2,1)} %copy-done, ...), custom_call_target="tpu_custom_call" | custom-call | flops 4294967296 | bytes 20971520 | tf_op jit(solution)/shard_map/pallas_call | solution.py:533
  74.2 1.7 %collective-permute-start.12 = (bf16[64,32,128]{2,1,0:T(8,128)(2,1)}, bf16[64,32,128]{2,1,0:T(8,128)(2,1)S(1)}, u32[]{:S(2)}, u32[]{:S(2)}) collective-permute-start(bf16[64,32,128]{2,1,0:T(8,128)(2,1)} %get-tuple-element.65), channel_id=1, source_target_pairs={{0,0},{1,29},{2,2},{3,31},{4,4},{5,1},{6,6},{7,3},{8,8},{9,5},{10,... | collective-permute-start | bytes 1572872 | tf_op jit(solution)/shard_map/ppermute | solution.py:680
  76.7 1.2 %collective-permute-start.14 = (bf16[64,32,128]{2,1,0:T(8,128)(2,1)}, bf16[64,32,128]{2,1,0:T(8,128)(2,1)S(1)}, u32[]{:S(2)}, u32[]{:S(2)}) collective-permute-start(bf16[64,32,128]{2,1,0:T(8,128)(2,1)} %get-tuple-element.67), channel_id=1, source_target_pairs={{0,1},{1,28},{2,3},{3,30},{4,5},{5,0},{6,7},{7,2},{8,9},{9,4},{10,... | collective-permute-start | bytes 1572872 | tf_op jit(solution)/shard_map/ppermute | solution.py:680
  78.0 30.1 %collective-permute-done.13 = bf16[64,32,128]{2,1,0:T(8,128)(2,1)S(1)} collective-permute-done((bf16[64,32,128]{2,1,0:T(8,128)(2,1)}, bf16[64,32,128]{2,1,0:T(8,128)(2,1)S(1)}, u32[]{:S(2)}, u32[]{:S(2)}) %collective-permute-start.13) | collective-permute-done | bytes 524320 | tf_op jit(solution)/shard_map/ppermute | solution.py:680
  108.0 13.5 %collective-permute-done.15 = bf16[64,32,128]{2,1,0:T(8,128)(2,1)S(1)} collective-permute-done((bf16[64,32,128]{2,1,0:T(8,128)(2,1)}, bf16[64,32,128]{2,1,0:T(8,128)(2,1)S(1)}, u32[]{:S(2)}, u32[]{:S(2)}) %collective-permute-start.15) | collective-permute-done | bytes 524320 | tf_op jit(solution)/shard_map/ppermute | solution.py:680
  121.8 1.5 %pad_maximum_fusion = f32[128,32,128]{2,1,0:T(8,128)} fusion(f32[64,32,128]{2,1,0:T(8,128)S(1)} %get-tuple-element.70, f32[64,32,128]{2,1,0:T(8,128)S(1)} %get-tuple-element.69), kind=kLoop, calls=%fused_computation | loop fusion | flops 524288 | bytes 4194304 | tf_op jit(solution)/shard_map/concatenate | solution.py:684
  (41 shorter events, 5.8 us)
Async XLA Ops:
  0.0 7.7 %copy-start.8 = (s32[128]{0:T(128)S(1)}, s32[128]{0:T(128)}, u32[]{:S(2)}) copy-start(s32[128]{0:T(128)} %dead_ref.1) | copy-start | bytes 1540
  0.0 7.7 %copy-start.7 = (s32[128]{0:T(128)S(1)}, s32[128]{0:T(128)}, u32[]{:S(2)}) copy-start(s32[128]{0:T(128)} %sec_ref.1) | copy-start | bytes 1540
  0.0 12.4 %copy-start.6 = (f32[512]{0:T(512)S(1)}, f32[512]{0:T(512)}, u32[]{:S(2)}) copy-start(f32[512]{0:T(512)} %param.9) | copy-start | bytes 6148
  1.2 17.1 %collective-permute-start.4 = (bf16[40,8,1024]{2,1,0:T(8,128)(2,1)S(1)}, bf16[40,8,1024]{2,1,0:T(8,128)(2,1)}, u32[]{:S(2)}, u32[]{:S(2)}) collective-permute-start(bf16[40,8,1024]{2,1,0:T(8,128)(2,1)S(1)} %constant_dynamic-slice_fusion.1), channel_id=1, source_target_pairs={{0,1},{1,0},{2,3},{3,2},{4,5},{5,4},{6,7},{7,6},{8,9},{9,8},{10,11... | collective-permute-start | bytes 1966088 | tf_op jit(solution)/shard_map/ppermute | solution.py:598
  6.6 2.1 %collective-permute-start = (f32[2,8,1152]{2,1,0:T(8,128)}, f32[2,8,1152]{2,1,0:T(8,128)S(1)}, u32[]{:S(2)}, u32[]{:S(2)}) collective-permute-start(f32[2,8,1152]{2,1,0:T(8,128)} %get-tuple-element.37), channel_id=1, source_target_pairs={{0,4},{4,0},{8,12},{12,8},{16,20},{20,16},{24,28},{28,24},{1,5},{5... | collective-permute-start | bytes 221192 | tf_op jit(solution)/shard_map/ppermute | solution.py:562
  7.7 16.4 %copy-start.4 = (s32[2,128]{1,0:T(2,128)}, s32[2,128]{1,0:T(2,128)S(1)}, u32[]{:S(2)}) copy-start(s32[2,128]{1,0:T(2,128)S(1)} %pad_add_fusion.flag_ref) | copy-start | bytes 3076
  7.8 11.4 %collective-permute-start.5 = (s32[2,64]{1,0:T(2,128)S(1)}, s32[2,64]{1,0:T(2,128)S(1)}, u32[]{:S(2)}, u32[]{:S(2)}) collective-permute-start(s32[2,64]{1,0:T(2,128)S(1)} %constant_dynamic-slice_fusion), channel_id=1, source_target_pairs={{0,28},{1,5},{2,30},{3,7},{4,0},{5,9},{6,2},{7,11},{8,4},{9,13},{1... | collective-permute-start | bytes 1544 | tf_op jit(solution)/shard_map/ppermute | solution.py:602
  9.7 6.7 %collective-permute-start.1 = (f32[2,8,1152]{2,1,0:T(8,128)S(1)}, f32[2,8,1152]{2,1,0:T(8,128)S(1)}, u32[]{:S(2)}, u32[]{:S(2)}) collective-permute-start(f32[2,8,1152]{2,1,0:T(8,128)S(1)} %add.29), channel_id=1, source_target_pairs={{0,8},{4,12},{8,0},{12,4},{16,24},{20,28},{24,16},{28,20},{1,9},{5... | collective-permute-start | bytes 221192 | tf_op jit(solution)/shard_map/ppermute | solution.py:562
  10.0 7.6 %collective-permute-start.2 = (f32[2,8,1152]{2,1,0:T(8,128)S(1)}, f32[2,8,1152]{2,1,0:T(8,128)S(1)}, u32[]{:S(2)}, u32[]{:S(2)}) collective-permute-start(f32[2,8,1152]{2,1,0:T(8,128)S(1)} %add.29), channel_id=1, source_target_pairs={{0,16},{4,20},{8,24},{12,28},{16,0},{20,4},{24,8},{28,12},{1,17},{... | collective-permute-start | bytes 221192 | tf_op jit(solution)/shard_map/ppermute | solution.py:562
  11.2 6.4 %collective-permute-start.3 = (f32[2,8,1152]{2,1,0:T(8,128)S(1)}, f32[2,8,1152]{2,1,0:T(8,128)S(1)}, u32[]{:S(2)}, u32[]{:S(2)}) collective-permute-start(f32[2,8,1152]{2,1,0:T(8,128)S(1)} %add.29), channel_id=1, source_target_pairs={{0,24},{4,28},{8,16},{12,20},{16,8},{20,12},{24,0},{28,4},{1,25},{... | collective-permute-start | bytes 221192 | tf_op jit(solution)/shard_map/ppermute | solution.py:562
  16.4 18.2 %collective-permute-start.11 = (bf16[64,8,1024]{2,1,0:T(8,128)(2,1)}, bf16[64,8,1024]{2,1,0:T(8,128)(2,1)}, u32[]{:S(2)}, u32[]{:S(2)}) collective-permute-start(bf16[64,8,1024]{2,1,0:T(8,128)(2,1)} %get-tuple-element.60), channel_id=1, source_target_pairs={{0,28},{1,5},{2,30},{3,7},{4,0},{5,9},{6,2},{7,11},{8,4},{9,13},{1... | collective-permute-start | bytes 3145736 | tf_op jit(solution)/shard_map/ppermute | solution.py:626
  19.2 4.9 %copy-start.2 = (f32[2,8,1152]{2,1,0:T(8,128)}, f32[2,8,1152]{2,1,0:T(8,128)S(1)}, u32[]{:S(2)}) copy-start(f32[2,8,1152]{2,1,0:T(8,128)S(1)} %add_add_fusion.rest_0_) | copy-start | bytes 221188
  19.2 3.7 %collective-permute-start.6 = (f32[2,8,1152]{2,1,0:T(8,128)S(1)}, f32[2,8,1152]{2,1,0:T(8,128)S(1)}, u32[]{:S(2)}, u32[]{:S(2)}) collective-permute-start(f32[2,8,1152]{2,1,0:T(8,128)S(1)} %add_add_fusion.rest_0_), channel_id=1, source_target_pairs={{0,1},{1,0},{2,3},{3,2},{4,5},{5,4},{6,7},{7,6},{8,9},{9,8},{10,11... | collective-permute-start | bytes 221192 | tf_op jit(solution)/shard_map/ppermute | solution.py:630
  20.5 12.7 %collective-permute-start.8 = (bf16[24,8,1024]{2,1,0:T(8,128)(2,1)}, bf16[24,8,1024]{2,1,0:T(8,128)(2,1)}, u32[]{:S(2)}, u32[]{:S(2)}) collective-permute-start(bf16[24,8,1024]{2,1,0:T(8,128)(2,1)} %get-tuple-element.55), channel_id=1, source_target_pairs={{0,1},{1,0},{2,3},{3,2},{4,5},{5,4},{6,7},{7,6},{8,9},{9,8},{10,11... | collective-permute-start | bytes 1179656 | tf_op jit(solution)/shard_map/ppermute | solution.py:631
  20.7 35.8 %collective-permute-start.10 = (bf16[64,8,1024]{2,1,0:T(8,128)(2,1)}, bf16[64,8,1024]{2,1,0:T(8,128)(2,1)}, u32[]{:S(2)}, u32[]{:S(2)}) collective-permute-start(bf16[64,8,1024]{2,1,0:T(8,128)(2,1)} %get-tuple-element.60), channel_id=1, source_target_pairs={{0,1},{1,0},{2,3},{3,2},{4,5},{5,4},{6,7},{7,6},{8,9},{9,8},{10,11... | collective-permute-start | bytes 3145736 | tf_op jit(solution)/shard_map/ppermute | solution.py:632
  22.9 10.3 %copy-start.1 = (f32[2,8,1152]{2,1,0:T(8,128)}, f32[2,8,1152]{2,1,0:T(8,128)S(1)}, u32[]{:S(2)}) copy-start(f32[2,8,1152]{2,1,0:T(8,128)S(1)} %collective-permute-done.6.rest_1_.rest_5_) | copy-start | bytes 221188
  22.9 15.9 %collective-permute-start.7 = (bf16[40,8,1024]{2,1,0:T(8,128)(2,1)}, bf16[40,8,1024]{2,1,0:T(8,128)(2,1)S(1)}, u32[]{:S(2)}, u32[]{:S(2)}) collective-permute-start(bf16[40,8,1024]{2,1,0:T(8,128)(2,1)} %collective-permute-done.4.rest_2_), channel_id=1, source_target_pairs={{0,28},{1,5},{2,30},{3,7},{4,0},{5,9},{6,2},{7,11},{8,4},{9,13},{1... | collective-permute-start | bytes 1966088 | tf_op jit(solution)/shard_map/ppermute | solution.py:636
  33.2 9.9 %collective-permute-start.9 = (bf16[24,8,1024]{2,1,0:T(8,128)(2,1)}, bf16[24,8,1024]{2,1,0:T(8,128)(2,1)}, u32[]{:S(2)}, u32[]{:S(2)}) collective-permute-start(bf16[24,8,1024]{2,1,0:T(8,128)(2,1)} %collective-permute-done.8.rest_3_), channel_id=1, source_target_pairs={{0,28},{1,5},{2,30},{3,7},{4,0},{5,9},{6,2},{7,11},{8,4},{9,13},{1... | collective-permute-start | bytes 1179656 | tf_op jit(solution)/shard_map/ppermute | solution.py:643
  34.6 8.5 %copy-start.5 = (s32[2,192]{1,0:T(2,128)}, s32[2,192]{1,0:T(2,128)S(1)}, u32[]{:S(2)}) copy-start(s32[2,192]{1,0:T(2,128)S(1)} %constant_dynamic-update-slice_fusion.flag_ref) | copy-start | bytes 4612
  38.8 4.3 %copy-start = (bf16[40,8,1024]{2,1,0:T(8,128)(2,1)}, bf16[40,8,1024]{2,1,0:T(8,128)(2,1)S(1)}, u32[]{:S(2)}) copy-start(bf16[40,8,1024]{2,1,0:T(8,128)(2,1)S(1)} %collective-permute-done.7.rest_4_.rest_0_) | copy-start | bytes 1966084
  74.1 33.9 %collective-permute-start.13 = (bf16[64,32,128]{2,1,0:T(8,128)(2,1)}, bf16[64,32,128]{2,1,0:T(8,128)(2,1)S(1)}, u32[]{:S(2)}, u32[]{:S(2)}) collective-permute-start(bf16[64,32,128]{2,1,0:T(8,128)(2,1)} %get-tuple-element.66), channel_id=1, source_target_pairs={{0,2},{1,31},{2,0},{3,29},{4,6},{5,3},{6,4},{7,1},{8,10},{9,7},{10... | collective-permute-start | bytes 1572872 | tf_op jit(solution)/shard_map/ppermute | solution.py:680
  74.2 33.8 %collective-permute-start.12 = (bf16[64,32,128]{2,1,0:T(8,128)(2,1)}, bf16[64,32,128]{2,1,0:T(8,128)(2,1)S(1)}, u32[]{:S(2)}, u32[]{:S(2)}) collective-permute-start(bf16[64,32,128]{2,1,0:T(8,128)(2,1)} %get-tuple-element.65), channel_id=1, source_target_pairs={{0,0},{1,29},{2,2},{3,31},{4,4},{5,1},{6,6},{7,3},{8,8},{9,5},{10,... | collective-permute-start | bytes 1572872 | tf_op jit(solution)/shard_map/ppermute | solution.py:680
  75.9 45.6 %collective-permute-start.15 = (bf16[64,32,128]{2,1,0:T(8,128)(2,1)}, bf16[64,32,128]{2,1,0:T(8,128)(2,1)S(1)}, u32[]{:S(2)}, u32[]{:S(2)}) collective-permute-start(bf16[64,32,128]{2,1,0:T(8,128)(2,1)} %get-tuple-element.68), channel_id=1, source_target_pairs={{0,3},{1,30},{2,1},{3,28},{4,7},{5,2},{6,5},{7,0},{8,11},{9,6},{10... | collective-permute-start | bytes 1572872 | tf_op jit(solution)/shard_map/ppermute | solution.py:680
  76.7 44.8 %collective-permute-start.14 = (bf16[64,32,128]{2,1,0:T(8,128)(2,1)}, bf16[64,32,128]{2,1,0:T(8,128)(2,1)S(1)}, u32[]{:S(2)}, u32[]{:S(2)}) collective-permute-start(bf16[64,32,128]{2,1,0:T(8,128)(2,1)} %get-tuple-element.67), channel_id=1, source_target_pairs={{0,1},{1,28},{2,3},{3,30},{4,5},{5,0},{6,7},{7,2},{8,9},{9,4},{10,... | collective-permute-start | bytes 1572872 | tf_op jit(solution)/shard_map/ppermute | solution.py:680
  (1 other events, 0.6 us)

commit v16 on v15

--- a/solution.py
+++ b/solution.py
@@ -14,7 +14,7 @@
 LAGS = 128
 NSEC = 2
 LANE = 128
-PART = 16
+PART = 32
 TILE = 256
 STEPS = 4
 TOGETHER = 4
@@ -133,7 +133,7 @@
         part = length // len(parts)
         for n, copy in enumerate(parts):
             copy.wait()
-            repeat(n * part, (n + 1) * part, clean_channel, 8)
+            repeat(n * part, (n + 1) * part, clean_channel, 16)
     for copy in copied["tables"]:
         copy.wait()
 
@@ -432,9 +432,13 @@
         [(conv_hbm, conv), (seg_hbm, seg), (lag_hbm, lag)],
         in_sem,
     )
+    some = b0.shape[0] // STEPS
     late = [
-        pltpu.make_async_copy(source, target, late_sem.at[n])
-        for n, (source, target) in enumerate(((b0_hbm, b0), (b2_hbm, b2), (a_hbm, a)))
+        pltpu.make_async_copy(
+            source.at[pl.ds(n * some, some)], target.at[pl.ds(n * some, some)], late_sem.at[n, m]
+        )
+        for n in range(STEPS)
+        for m, (source, target) in enumerate(((b0_hbm, b0), (b2_hbm, b2), (a_hbm, a)))
     ]
     for copy in late:
         copy.start()
@@ -452,8 +456,6 @@
         b3[k] = second_factor(k)
 
     repeat(0, bins, second, 32)
-    for copy in late:
-        copy.wait()
 
     lane = lax.broadcasted_iota(jnp.int32, (1, chans), 1)
     low, high = [jnp.where((lane < width) == (g == 0), 1.0, 0.0).astype(BF16) for g in range(2)]
@@ -484,7 +486,10 @@
                         p * width : (p + 1) * width, t * chans : (t + 1) * chans
                     ]
 
-        repeat(0, bins, one_bin, 32)
+        for n in range(STEPS):
+            for copy in late[3 * n : 3 * (n + 1)]:
+                copy.wait()
+            repeat(n * some, (n + 1) * some, one_bin, 32)
 
     pl.when(odd == 0)(lambda: bins_with(b2, b3))
     pl.when(odd == 1)(lambda: bins_with(b3, b2))
@@ -541,7 +546,7 @@
             pltpu.VMEM(b0.shape, BF16),
             pltpu.VMEM((2, chans + width, chans), F32),
             pltpu.SemaphoreType.DMA((8 + chans // PART,)),
-            pltpu.SemaphoreType.DMA((3,)),
+            pltpu.SemaphoreType.DMA((STEPS, 3)),
         ],
         compiler_params=pltpu.CompilerParams(vmem_limit_bytes=VMEM),
         cost_estimate=pl.CostEstimate(
@@ -579,12 +584,6 @@
     waves, seg, lag = jnp.asarray(waves), jnp.asarray(seg), jnp.asarray(lag)
     hann = jnp.asarray(window[None, :])
     response = jnp.sum(band_gain[:, None] * waves, axis=0, keepdims=True)
-    conv = pl.pallas_call(
-        circulant_kernel,
-        out_shape=jax.ShapeDtypeStruct((TILE, ns), BF16),
-        compiler_params=pltpu.CompilerParams(vmem_limit_bytes=VMEM),
-        cost_estimate=pl.CostEstimate(flops=1, bytes_accessed=1, transcendentals=0),
-    )(response)
     swap = [(z, z ^ 1) for z in range(groups)]
     both = ("fibre", "tm")
     halo_pairs = [
@@ -622,11 +621,17 @@
         cost_estimate=pl.CostEstimate(flops=1, bytes_accessed=1, transcendentals=0),
     )(odd[None], dead_flags, section_ids, samples)
     total, their_head = add_over(sums, "fibre", their_head)
-    halo_source, conv = lax.optimization_barrier((own_half, conv))
+    halo_source, halo_flags = lax.optimization_barrier((own_half, halo_flags))
     halo = lax.ppermute(halo_source, both, halo_pairs)
-    total, halo_flags, conv, own_half, tail = lax.optimization_barrier(
-        (total, halo_flags, conv, own_half, tail)
-    )
+    total, response, own_half, tail = lax.optimization_barrier(
+        (total, response, own_half, tail)
+    )
+    conv = pl.pallas_call(
+        circulant_kernel,
+        out_shape=jax.ShapeDtypeStruct((TILE, ns), BF16),
+        compiler_params=pltpu.CompilerParams(vmem_limit_bytes=VMEM),
+        cost_estimate=pl.CostEstimate(flops=1, bytes_accessed=1, transcendentals=0),
+    )(response)
     their_total = lax.ppermute(total, "tm", swap)
     their_tail = lax.ppermute(tail, "tm", swap)
     their_second = lax.ppermute(own_half, "tm", swap)

time: 124 us -> 124 us (level)
  transfers between devices with their start and end apart: 16 -> 16, of which waited for: 6 -> 6; matrix products, arithmetic and copies ran while one was open for 4% -> 3% of each run, Pallas kernels for 23% -> 23%
where the time goes in v16:
time: 124 us; the launch traced here: 123 us
  waiting for transfers between devices  52.8 us (43%)
  Pallas kernels  47 us (38%)
  starting transfers between devices  15.6 us (13%)
  other arithmetic  5.13 us (4%)
  local copies, waits for them, and re-layouts  1.9 us (2%)
    ppermute x4, waiting for transfers between devices, shards(): arrived[d] = lax.ppermute(found[d], both, pairs)  43.1 us
    pallas_call x2, Pallas kernels, segments(): pl.pallas_call(functools.partial(kernel, places), out_shape=out, in_specs...  22.5 us
    pallas_call x1, Pallas kernels, stacks(): pl.pallas_call(functools.partial(stack_kernel, places, scale, shares), ou...  18.8 us
    ppermute x1, waiting for transfers between devices, shards(): halo_tail = lax.ppermute(forward, both, halo_pairs)  4.32 us
    pallas_call x1, Pallas kernels, shards(): pl.pallas_call(section_sums, out_shape=[jax.ShapeDtypeStruct((NSEC, wins,...  4.12 us
    ppermute x4, starting transfers between devices, shards(): arrived[d] = lax.ppermute(found[d], both, pairs)  3.99 us
    ppermute x4, starting transfers between devices, add_over(): lax.ppermute(value, axis, [(i, i ^ s) for i in range(count)])  3.73 us
    ppermute x1, waiting for transfers between devices, shards(): halo_head = lax.ppermute(their_head, both, halo_pairs)  3.46 us
  transfers between devices with their start and end apart: 16, of which 6 were waited for; matrix products, arithmetic and copies ran while one was open for 3% of the time, Pallas kernels for 23%

profile of v16, /device:TPU:19, one launch (start us, length us, event | category | flops | bytes accessed | tf_op | source)
XLA Modules:
  0.0 122.6 jit_solution(29417840136642520)
XLA Ops:
  0.0 1.2 constant_dynamic-slice_fusion.1
  1.2 1.4 %collective-permute-start.4 = (bf16[40,8,1024]{2,1,0:T(8,128)(2,1)S(1)}, bf16[40,8,1024]{2,1,0:T(8,128)(2,1)}, u32[]{:S(2)}, u32[]{:S(2)}) collective-permute-start(bf16[40,8,1024]{2,1,0:T(8,128)(2,1)S(1)} %constant_dynamic-slice_fusion.1), channel_id=1, source_target_pairs={{0,1},{1,0},{2,3},{3,2},{4,5},{5,4},{6,7},{7,6},{8,9},{9,8},{10,11... | collective-permute-start | bytes 1966088 | tf_op jit(solution)/shard_map/ppermute | solution.py:597
  2.5 4.1 %shard_map.82 = (f32[2,8,1152]{2,1,0:T(8,128)}, bf16[64,8,1024]{2,1,0:T(8,128)(2,1)}, bf16[24,8,1024]{2,1,0:T(8,128)(2,1)}) custom-call(s32[1]{0:T(128)} %bitcast.1.odd_ref, s32[128]{0:T(128)} %dead_ref.1, s32[128]{0:T(128)} %sec_ref.1, bf16[128,8,1024]{2,1,0:T(8,128)(2,1)} %rest_1_.1), custom_call_target="tpu_custom_call" | custom-call | flops 1 | bytes 1 | tf_op jit(solution)/shard_map/pallas_call | solution.py:606
  6.7 1.0 collective-permute-start
  7.8 1.0 collective-permute-done
  10.0 1.2 %collective-permute-start.2 = (f32[2,8,1152]{2,1,0:T(8,128)S(1)}, f32[2,8,1152]{2,1,0:T(8,128)S(1)}, u32[]{:S(2)}, u32[]{:S(2)}) collective-permute-start(f32[2,8,1152]{2,1,0:T(8,128)S(1)} %add.29), channel_id=1, source_target_pairs={{0,16},{4,20},{8,24},{12,28},{16,0},{20,4},{24,8},{28,12},{1,17},{... | collective-permute-start | bytes 221192 | tf_op jit(solution)/shard_map/ppermute | solution.py:567
  11.3 1.2 collective-permute-start.3
  12.4 2.4 %multiply_reduce_fusion = f32[1024]{0:T(1024)} fusion(f32[512,1024]{1,0:T(8,128)} %constant.33.clone, f32[512]{0:T(512)S(1)} %copy-done.5), kind=kLoop, calls=%fused_computation.1 | loop fusion | flops 1047552 | bytes 2103296 | tf_op jit(solution)/shard_map/reduce_sum | solution.py:586
  14.8 1.2 collective-permute-start.11
  16.0 0.9 collective-permute-done.4.rest_2_
  17.0 1.4 %collective-permute-start.5 = (f32[2,8,1152]{2,1,0:T(8,128)S(1)}, f32[2,8,1152]{2,1,0:T(8,128)S(1)}, u32[]{:S(2)}, u32[]{:S(2)}) collective-permute-start(f32[2,8,1152]{2,1,0:T(8,128)S(1)} %add_add_fusion.rest_0_), channel_id=1, source_target_pairs={{0,1},{1,0},{2,3},{3,2},{4,5},{5,4},{6,7},{7,6},{8,9},{9,8},{10,11... | collective-permute-start | bytes 221192 | tf_op jit(solution)/shard_map/ppermute | solution.py:635
  18.5 1.7 %shard_map.83.rest_3_.rest_8_.rest_7_ = bf16[256,1024]{1,0:T(8,128)(2,1)} custom-call(f32[1,1024]{1,0:T(1,128)} %bitcast.5), custom_call_target="tpu_custom_call" | custom-call | flops 1 | bytes 1 | tf_op jit(solution)/shard_map/pallas_call | solution.py:629
  20.2 1.3 %collective-permute-start.10 = (bf16[64,8,1024]{2,1,0:T(8,128)(2,1)}, bf16[64,8,1024]{2,1,0:T(8,128)(2,1)}, u32[]{:S(2)}, u32[]{:S(2)}) collective-permute-start(bf16[64,8,1024]{2,1,0:T(8,128)(2,1)} %get-tuple-element.58), channel_id=1, source_target_pairs={{0,1},{1,0},{2,3},{3,2},{4,5},{5,4},{6,7},{7,6},{8,9},{9,8},{10,11... | collective-permute-start | bytes 3145736 | tf_op jit(solution)/shard_map/ppermute | solution.py:637
  21.5 2.4 %collective-permute-start.7 = (bf16[40,8,1024]{2,1,0:T(8,128)(2,1)}, bf16[40,8,1024]{2,1,0:T(8,128)(2,1)S(1)}, u32[]{:S(2)}, u32[]{:S(2)}) collective-permute-start(bf16[40,8,1024]{2,1,0:T(8,128)(2,1)} %collective-permute-done.4.rest_2_), channel_id=1, source_target_pairs={{0,28},{1,5},{2,30},{3,7},{4,0},{5,9},{6,2},{7,11},{8,4},{9,13},{1... | collective-permute-start | bytes 1966088 | tf_op jit(solution)/shard_map/ppermute | solution.py:641
  23.9 9.1 %shard_map.84 = (bf16[128,128,128]{2,1,0:T(8,128)(2,1)}, bf16[2,1152,512]{2,1,0:T(8,128)(2,1)}) custom-call(s32[1]{0:T(128)} %bitcast.1.odd_ref, s32[2,128]{1,0:T(2,128)} %copy-done.3, f32[2,8,1152]{2,1,0:T(8,128)} %copy-done.2, bf16[128,8,1024]{2,1,0:T(8,128)(2,1)} %rest_1_.1, f32[1,1024]{1,0:T(1,128)} %constant.36.clone.rest_2_.rest_7_.rest_6_, ...), custom_call_target="tpu_custom_call" | custom-call | flops 3758096384 | bytes 16777216 | tf_op jit(solution)/shard_map/pallas_call | solution.py:403
  33.7 3.5 %collective-permute-done.7.rest_4_.rest_0_ = bf16[40,8,1024]{2,1,0:T(8,128)(2,1)S(1)} collective-permute-done((bf16[40,8,1024]{2,1,0:T(8,128)(2,1)}, bf16[40,8,1024]{2,1,0:T(8,128)(2,1)S(1)}, u32[]{:S(2)}, u32[]{:S(2)}) %collective-permute-start.7) | collective-permute-done | bytes 655392 | tf_op jit(solution)/shard_map/ppermute | solution.py:641
  37.2 4.3 %collective-permute-done.9.rest_5_.rest_1_ = bf16[24,8,1024]{2,1,0:T(8,128)(2,1)} collective-permute-done((bf16[24,8,1024]{2,1,0:T(8,128)(2,1)}, bf16[24,8,1024]{2,1,0:T(8,128)(2,1)}, u32[]{:S(2)}, u32[]{:S(2)}) %collective-permute-start.9) | collective-permute-done | bytes 393248 | tf_op jit(solution)/shard_map/ppermute | solution.py:648
  41.5 13.4 %shard_map.85 = (bf16[128,2,64,128]{3,2,1,0:T(8,128)(2,1)}, bf16[128,128,128]{2,1,0:T(8,128)(2,1)}) custom-call(s32[1]{0:T(128)} %bitcast.1.odd_ref, s32[2,192]{1,0:T(2,128)} %copy-done.4, f32[2,8,1152]{2,1,0:T(8,128)} %copy-done.2, f32[2,8,1152]{2,1,0:T(8,128)} %copy-done.1, bf16[40,8,1024]{2,1,0:T(8,128)(2,1)} %collective-permute-done.4.rest_2_, ...), custom_call_target="tpu_custom_call" | custom-call | flops 3758096384 | bytes 16777216 | tf_op jit(solution)/shard_map/pallas_call | solution.py:403
  54.9 18.8 %shard_map.86 = (bf16[64,32,128]{2,1,0:T(8,128)(2,1)}, bf16[64,32,128]{2,1,0:T(8,128)(2,1)}, bf16[64,32,128]{2,1,0:T(8,128)(2,1)}, bf16[64,32,128]{2,1,0:T(8,128)(2,1)}) custom-call(s32[1]{0:T(128)} %bitcast.me_ref, s32[2,192]{1,0:T(2,128)} %copy-done.4, bf16[40,8,1024]{2,1,0:T(8,128)(2,1)} %copy-done, ...), custom_call_target="tpu_custom_call" | custom-call | flops 4294967296 | bytes 20971520 | tf_op jit(solution)/shard_map/pallas_call | solution.py:538
  73.8 1.7 %collective-permute-start.12 = (bf16[64,32,128]{2,1,0:T(8,128)(2,1)}, bf16[64,32,128]{2,1,0:T(8,128)(2,1)S(1)}, u32[]{:S(2)}, u32[]{:S(2)}) collective-permute-start(bf16[64,32,128]{2,1,0:T(8,128)(2,1)} %get-tuple-element.63), channel_id=1, source_target_pairs={{0,0},{1,29},{2,2},{3,31},{4,4},{5,1},{6,6},{7,3},{8,8},{9,5},{10,... | collective-permute-start | bytes 1572872 | tf_op jit(solution)/shard_map/ppermute | solution.py:685
  76.2 1.4 %collective-permute-start.14 = (bf16[64,32,128]{2,1,0:T(8,128)(2,1)}, bf16[64,32,128]{2,1,0:T(8,128)(2,1)S(1)}, u32[]{:S(2)}, u32[]{:S(2)}) collective-permute-start(bf16[64,32,128]{2,1,0:T(8,128)(2,1)} %get-tuple-element.65), channel_id=1, source_target_pairs={{0,1},{1,28},{2,3},{3,30},{4,5},{5,0},{6,7},{7,2},{8,9},{9,4},{10,... | collective-permute-start | bytes 1572872 | tf_op jit(solution)/shard_map/ppermute | solution.py:685
  77.7 29.8 %collective-permute-done.13 = bf16[64,32,128]{2,1,0:T(8,128)(2,1)S(1)} collective-permute-done((bf16[64,32,128]{2,1,0:T(8,128)(2,1)}, bf16[64,32,128]{2,1,0:T(8,128)(2,1)S(1)}, u32[]{:S(2)}, u32[]{:S(2)}) %collective-permute-start.13) | collective-permute-done | bytes 524320 | tf_op jit(solution)/shard_map/ppermute | solution.py:685
  107.5 13.3 %collective-permute-done.15 = bf16[64,32,128]{2,1,0:T(8,128)(2,1)S(1)} collective-permute-done((bf16[64,32,128]{2,1,0:T(8,128)(2,1)}, bf16[64,32,128]{2,1,0:T(8,128)(2,1)S(1)}, u32[]{:S(2)}, u32[]{:S(2)}) %collective-permute-start.15) | collective-permute-done | bytes 524320 | tf_op jit(solution)/shard_map/ppermute | solution.py:685
  121.1 1.5 %pad_maximum_fusion = f32[128,32,128]{2,1,0:T(8,128)} fusion(f32[64,32,128]{2,1,0:T(8,128)S(1)} %get-tuple-element.68, f32[64,32,128]{2,1,0:T(8,128)S(1)} %get-tuple-element.67), kind=kLoop, calls=%fused_computation | loop fusion | flops 524288 | bytes 4194304 | tf_op jit(solution)/shard_map/concatenate | solution.py:689
  (39 shorter events, 3.5 us)
Async XLA Ops:
  0.0 7.7 %copy-start.7 = (s32[128]{0:T(128)S(1)}, s32[128]{0:T(128)}, u32[]{:S(2)}) copy-start(s32[128]{0:T(128)} %dead_ref.1) | copy-start | bytes 1540
  0.0 7.7 %copy-start.6 = (s32[128]{0:T(128)S(1)}, s32[128]{0:T(128)}, u32[]{:S(2)}) copy-start(s32[128]{0:T(128)} %sec_ref.1) | copy-start | bytes 1540
  0.0 12.4 %copy-start.5 = (f32[512]{0:T(512)S(1)}, f32[512]{0:T(512)}, u32[]{:S(2)}) copy-start(f32[512]{0:T(512)} %param.9) | copy-start | bytes 6148
  1.2 15.8 %collective-permute-start.4 = (bf16[40,8,1024]{2,1,0:T(8,128)(2,1)S(1)}, bf16[40,8,1024]{2,1,0:T(8,128)(2,1)}, u32[]{:S(2)}, u32[]{:S(2)}) collective-permute-start(bf16[40,8,1024]{2,1,0:T(8,128)(2,1)S(1)} %constant_dynamic-slice_fusion.1), channel_id=1, source_target_pairs={{0,1},{1,0},{2,3},{3,2},{4,5},{5,4},{6,7},{7,6},{8,9},{9,8},{10,11... | collective-permute-start | bytes 1966088 | tf_op jit(solution)/shard_map/ppermute | solution.py:597
  6.7 2.1 %collective-permute-start = (f32[2,8,1152]{2,1,0:T(8,128)}, f32[2,8,1152]{2,1,0:T(8,128)S(1)}, u32[]{:S(2)}, u32[]{:S(2)}) collective-permute-start(f32[2,8,1152]{2,1,0:T(8,128)} %get-tuple-element.36), channel_id=1, source_target_pairs={{0,4},{4,0},{8,12},{12,8},{16,20},{20,16},{24,28},{28,24},{1,5},{5... | collective-permute-start | bytes 221192 | tf_op jit(solution)/shard_map/ppermute | solution.py:567
  7.7 16.2 %copy-start.3 = (s32[2,128]{1,0:T(2,128)}, s32[2,128]{1,0:T(2,128)S(1)}, u32[]{:S(2)}) copy-start(s32[2,128]{1,0:T(2,128)S(1)} %pad_add_fusion.flag_ref) | copy-start | bytes 3076
  7.8 7.0 %collective-permute-start.6 = (s32[2,64]{1,0:T(2,128)S(1)}, s32[2,64]{1,0:T(2,128)S(1)}, u32[]{:S(2)}, u32[]{:S(2)}) collective-permute-start(s32[2,64]{1,0:T(2,128)S(1)} %constant_dynamic-slice_fusion), channel_id=1, source_target_pairs={{0,28},{1,5},{2,30},{3,7},{4,0},{5,9},{6,2},{7,11},{8,4},{9,13},{1... | collective-permute-start | bytes 1544 | tf_op jit(solution)/shard_map/ppermute | solution.py:601
  9.7 6.3 %collective-permute-start.1 = (f32[2,8,1152]{2,1,0:T(8,128)S(1)}, f32[2,8,1152]{2,1,0:T(8,128)S(1)}, u32[]{:S(2)}, u32[]{:S(2)}) collective-permute-start(f32[2,8,1152]{2,1,0:T(8,128)S(1)} %add.29), channel_id=1, source_target_pairs={{0,8},{4,12},{8,0},{12,4},{16,24},{20,28},{24,16},{28,20},{1,9},{5... | collective-permute-start | bytes 221192 | tf_op jit(solution)/shard_map/ppermute | solution.py:567
  10.0 6.0 %collective-permute-start.2 = (f32[2,8,1152]{2,1,0:T(8,128)S(1)}, f32[2,8,1152]{2,1,0:T(8,128)S(1)}, u32[]{:S(2)}, u32[]{:S(2)}) collective-permute-start(f32[2,8,1152]{2,1,0:T(8,128)S(1)} %add.29), channel_id=1, source_target_pairs={{0,16},{4,20},{8,24},{12,28},{16,0},{20,4},{24,8},{28,12},{1,17},{... | collective-permute-start | bytes 221192 | tf_op jit(solution)/shard_map/ppermute | solution.py:567
  11.3 4.8 %collective-permute-start.3 = (f32[2,8,1152]{2,1,0:T(8,128)S(1)}, f32[2,8,1152]{2,1,0:T(8,128)S(1)}, u32[]{:S(2)}, u32[]{:S(2)}) collective-permute-start(f32[2,8,1152]{2,1,0:T(8,128)S(1)} %add.29), channel_id=1, source_target_pairs={{0,24},{4,28},{8,16},{12,20},{16,8},{20,12},{24,0},{28,4},{1,25},{... | collective-permute-start | bytes 221192 | tf_op jit(solution)/shard_map/ppermute | solution.py:567
  14.8 18.9 %collective-permute-start.11 = (bf16[64,8,1024]{2,1,0:T(8,128)(2,1)}, bf16[64,8,1024]{2,1,0:T(8,128)(2,1)}, u32[]{:S(2)}, u32[]{:S(2)}) collective-permute-start(bf16[64,8,1024]{2,1,0:T(8,128)(2,1)} %get-tuple-element.58), channel_id=1, source_target_pairs={{0,28},{1,5},{2,30},{3,7},{4,0},{5,9},{6,2},{7,11},{8,4},{9,13},{1... | collective-permute-start | bytes 3145736 | tf_op jit(solution)/shard_map/ppermute | solution.py:625
  17.0 6.9 %copy-start.2 = (f32[2,8,1152]{2,1,0:T(8,128)}, f32[2,8,1152]{2,1,0:T(8,128)S(1)}, u32[]{:S(2)}) copy-start(f32[2,8,1152]{2,1,0:T(8,128)S(1)} %add_add_fusion.rest_0_) | copy-start | bytes 221188
  17.0 4.5 %collective-permute-start.5 = (f32[2,8,1152]{2,1,0:T(8,128)S(1)}, f32[2,8,1152]{2,1,0:T(8,128)S(1)}, u32[]{:S(2)}, u32[]{:S(2)}) collective-permute-start(f32[2,8,1152]{2,1,0:T(8,128)S(1)} %add_add_fusion.rest_0_), channel_id=1, source_target_pairs={{0,1},{1,0},{2,3},{3,2},{4,5},{5,4},{6,7},{7,6},{8,9},{9,8},{10,11... | collective-permute-start | bytes 221192 | tf_op jit(solution)/shard_map/ppermute | solution.py:635
  18.3 14.6 %collective-permute-start.8 = (bf16[24,8,1024]{2,1,0:T(8,128)(2,1)}, bf16[24,8,1024]{2,1,0:T(8,128)(2,1)}, u32[]{:S(2)}, u32[]{:S(2)}) collective-permute-start(bf16[24,8,1024]{2,1,0:T(8,128)(2,1)} %get-tuple-element.53), channel_id=1, source_target_pairs={{0,1},{1,0},{2,3},{3,2},{4,5},{5,4},{6,7},{7,6},{8,9},{9,8},{10,11... | collective-permute-start | bytes 1179656 | tf_op jit(solution)/shard_map/ppermute | solution.py:636
  20.2 34.7 %collective-permute-start.10 = (bf16[64,8,1024]{2,1,0:T(8,128)(2,1)}, bf16[64,8,1024]{2,1,0:T(8,128)(2,1)}, u32[]{:S(2)}, u32[]{:S(2)}) collective-permute-start(bf16[64,8,1024]{2,1,0:T(8,128)(2,1)} %get-tuple-element.58), channel_id=1, source_target_pairs={{0,1},{1,0},{2,3},{3,2},{4,5},{5,4},{6,7},{7,6},{8,9},{9,8},{10,11... | collective-permute-start | bytes 3145736 | tf_op jit(solution)/shard_map/ppermute | solution.py:637
  21.5 11.5 %copy-start.1 = (f32[2,8,1152]{2,1,0:T(8,128)}, f32[2,8,1152]{2,1,0:T(8,128)S(1)}, u32[]{:S(2)}) copy-start(f32[2,8,1152]{2,1,0:T(8,128)S(1)} %collective-permute-done.5.rest_1_.rest_5_) | copy-start | bytes 221188
  21.5 15.7 %collective-permute-start.7 = (bf16[40,8,1024]{2,1,0:T(8,128)(2,1)}, bf16[40,8,1024]{2,1,0:T(8,128)(2,1)S(1)}, u32[]{:S(2)}, u32[]{:S(2)}) collective-permute-start(bf16[40,8,1024]{2,1,0:T(8,128)(2,1)} %collective-permute-done.4.rest_2_), channel_id=1, source_target_pairs={{0,28},{1,5},{2,30},{3,7},{4,0},{5,9},{6,2},{7,11},{8,4},{9,13},{1... | collective-permute-start | bytes 1966088 | tf_op jit(solution)/shard_map/ppermute | solution.py:641
  33.0 8.5 %collective-permute-start.9 = (bf16[24,8,1024]{2,1,0:T(8,128)(2,1)}, bf16[24,8,1024]{2,1,0:T(8,128)(2,1)}, u32[]{:S(2)}, u32[]{:S(2)}) collective-permute-start(bf16[24,8,1024]{2,1,0:T(8,128)(2,1)} %collective-permute-done.8.rest_3_), channel_id=1, source_target_pairs={{0,28},{1,5},{2,30},{3,7},{4,0},{5,9},{6,2},{7,11},{8,4},{9,13},{1... | collective-permute-start | bytes 1179656 | tf_op jit(solution)/shard_map/ppermute | solution.py:648
  33.7 7.8 %copy-start.4 = (s32[2,192]{1,0:T(2,128)}, s32[2,192]{1,0:T(2,128)S(1)}, u32[]{:S(2)}) copy-start(s32[2,192]{1,0:T(2,128)S(1)} %constant_dynamic-update-slice_fusion.flag_ref) | copy-start | bytes 4612
  37.2 4.3 %copy-start = (bf16[40,8,1024]{2,1,0:T(8,128)(2,1)}, bf16[40,8,1024]{2,1,0:T(8,128)(2,1)S(1)}, u32[]{:S(2)}) copy-start(bf16[40,8,1024]{2,1,0:T(8,128)(2,1)S(1)} %collective-permute-done.7.rest_4_.rest_0_) | copy-start | bytes 1966084
  73.7 33.8 %collective-permute-start.13 = (bf16[64,32,128]{2,1,0:T(8,128)(2,1)}, bf16[64,32,128]{2,1,0:T(8,128)(2,1)S(1)}, u32[]{:S(2)}, u32[]{:S(2)}) collective-permute-start(bf16[64,32,128]{2,1,0:T(8,128)(2,1)} %get-tuple-element.64), channel_id=1, source_target_pairs={{0,2},{1,31},{2,0},{3,29},{4,6},{5,3},{6,4},{7,1},{8,10},{9,7},{10... | collective-permute-start | bytes 1572872 | tf_op jit(solution)/shard_map/ppermute | solution.py:685
  73.8 33.7 %collective-permute-start.12 = (bf16[64,32,128]{2,1,0:T(8,128)(2,1)}, bf16[64,32,128]{2,1,0:T(8,128)(2,1)S(1)}, u32[]{:S(2)}, u32[]{:S(2)}) collective-permute-start(bf16[64,32,128]{2,1,0:T(8,128)(2,1)} %get-tuple-element.63), channel_id=1, source_target_pairs={{0,0},{1,29},{2,2},{3,31},{4,4},{5,1},{6,6},{7,3},{8,8},{9,5},{10,... | collective-permute-start | bytes 1572872 | tf_op jit(solution)/shard_map/ppermute | solution.py:685
  75.5 45.3 %collective-permute-start.15 = (bf16[64,32,128]{2,1,0:T(8,128)(2,1)}, bf16[64,32,128]{2,1,0:T(8,128)(2,1)S(1)}, u32[]{:S(2)}, u32[]{:S(2)}) collective-permute-start(bf16[64,32,128]{2,1,0:T(8,128)(2,1)} %get-tuple-element.66), channel_id=1, source_target_pairs={{0,3},{1,30},{2,1},{3,28},{4,7},{5,2},{6,5},{7,0},{8,11},{9,6},{10... | collective-permute-start | bytes 1572872 | tf_op jit(solution)/shard_map/ppermute | solution.py:685
  76.2 44.6 %collective-permute-start.14 = (bf16[64,32,128]{2,1,0:T(8,128)(2,1)}, bf16[64,32,128]{2,1,0:T(8,128)(2,1)S(1)}, u32[]{:S(2)}, u32[]{:S(2)}) collective-permute-start(bf16[64,32,128]{2,1,0:T(8,128)(2,1)} %get-tuple-element.65), channel_id=1, source_target_pairs={{0,1},{1,28},{2,3},{3,30},{4,5},{5,0},{6,7},{7,2},{8,9},{9,4},{10,... | collective-permute-start | bytes 1572872 | tf_op jit(solution)/shard_map/ppermute | solution.py:685

commit v17 on v16

--- a/solution.py
+++ b/solution.py
@@ -415,51 +415,14 @@
     )(side, flags, *operands)
 
 
-def stack_kernel(places, scale, shares, me_ref, flag_ref, *rest):
-    even_hbm, odd_hbm, late_hbm, rest = rest[:2], rest[2:4], rest[4], rest[5:]
-    tot_hbm, hann_hbm, conv_hbm, seg_hbm, lag_hbm = rest[:5]
-    a_hbm, b0_hbm, b2_hbm, rest = *rest[5:8], rest[8:]
-    outs, rest = rest[:shares], rest[shares:]
-    x, rest = rest[:3], rest[3:]
-    tot, hann, conv, seg, lag, a, b0, b2 = rest[:8]
-    work, (b3, one, in_sem, late_sem) = rest[8:-4], rest[-4:]
-    me = me_ref[0]
-    odd = lax.rem(me, 2)
-    copied = input_copies(
-        odd,
-        [(tot_hbm, tot), (hann_hbm, hann)],
-        list(zip(zip(even_hbm, odd_hbm), x)) + [(late_hbm, x[2])],
-        [(conv_hbm, conv), (seg_hbm, seg), (lag_hbm, lag)],
-        in_sem,
-    )
-    some = b0.shape[0] // STEPS
-    late = [
-        pltpu.make_async_copy(
-            source.at[pl.ds(n * some, some)], target.at[pl.ds(n * some, some)], late_sem.at[n, m]
-        )
-        for n in range(STEPS)
-        for m, (source, target) in enumerate(((b0_hbm, b0), (b2_hbm, b2), (a_hbm, a)))
-    ]
-    for copy in late:
-        copy.start()
-    bins, depth, chans = b0.shape
+def correlate(first, count, scale, shares, me, a, b0, b2, b3, lag, cross, one, outs, bins_loop):
+    depth, chans = b0.shape[1:]
     width = chans // 2
     nfr = lag.shape[1]
     pitch = nfr + 1
-    cross = work[-1]
-
-    _, second_factor = segment_factors(
-        places, odd, flag_ref, [tot], x, hann, conv, seg, work, copied
-    )
-
-    def second(k):
-        b3[k] = second_factor(k)
-
-    repeat(0, bins, second, 32)
-
+    odd = lax.rem(me, 2)
     lane = lax.broadcasted_iota(jnp.int32, (1, chans), 1)
     low, high = [jnp.where((lane < width) == (g == 0), 1.0, 0.0).astype(BF16) for g in range(2)]
-
     lower = lane < width
 
     def bins_with(near, far):
@@ -482,14 +445,11 @@
             value = jnp.dot(left, right, preferred_element_type=F32)
             for p in range(2):
                 for t in range(2):
-                    cross[t, pl.ds(2 * k + p, width, stride=pitch), :] = value[
-                        p * width : (p + 1) * width, t * chans : (t + 1) * chans
+                    cross[t, pl.ds(2 * k + p, count, stride=pitch), :] = value[
+                        p * count : (p + 1) * count, t * chans : (t + 1) * chans
                     ]
 
-        for n in range(STEPS):
-            for copy in late[3 * n : 3 * (n + 1)]:
-                copy.wait()
-            repeat(n * some, (n + 1) * some, one_bin, 32)
+        bins_loop(one_bin)
 
     pl.when(odd == 0)(lambda: bins_with(b2, b3))
     pl.when(odd == 1)(lambda: bins_with(b3, b2))
@@ -508,7 +468,7 @@
         value = jnp.concatenate(
             [cross[t, pl.ds(c * pitch, nfr), :] for t in range(2)], axis=1
         ).astype(BF16)
-        starts = [c + 1 + share * (me ^ d) for d in range(shares)]
+        starts = [first + c + 1 + share * (me ^ d) for d in range(shares)]
         pick = jnp.concatenate(
             [
                 jnp.concatenate([one[t, pl.ds(start, share), :] for start in starts], axis=0)
@@ -521,40 +481,151 @@
         for d, out in enumerate(outs):
             out[c] = band[d * share : (d + 1) * share, :].astype(BF16)
 
-    repeat(0, width, one_channel, 16)
+    repeat(0, count, one_channel, 16)
+
+
+def last_kernel(places, scale, shares, me_ref, flag_ref, *rest):
+    even_hbm, odd_hbm, late_hbm, rest = rest[:2], rest[2:4], rest[4], rest[5:]
+    tot_hbm, hann_hbm, conv_hbm, seg_hbm, lag_hbm = rest[:5]
+    a_hbm, b0_hbm, b2_hbm, rest = *rest[5:8], rest[8:]
+    outs, b3_hbm, rest = rest[:shares], rest[shares], rest[shares + 1 :]
+    x, rest = rest[:3], rest[3:]
+    tot, hann, conv, seg, lag, b0, b2 = rest[:7]
+    work, (a, b3, one, in_sem, late_sem, out_sem) = rest[7:-6], rest[-6:]
+    me = me_ref[0]
+    odd = lax.rem(me, 2)
+    copied = input_copies(
+        odd,
+        [(tot_hbm, tot), (hann_hbm, hann)],
+        list(zip(zip(even_hbm, odd_hbm), x)) + [(late_hbm, x[2])],
+        [(conv_hbm, conv), (seg_hbm, seg), (lag_hbm, lag)],
+        in_sem,
+    )
+    count = a.shape[2]
+    late = [
+        pltpu.make_async_copy(source, target, late_sem.at[n])
+        for n, (source, target) in enumerate(
+            ((b0_hbm, b0), (b2_hbm, b2), (a_hbm.at[:, :, pl.ds(0, count)], a))
+        )
+    ]
+    for copy in late:
+        copy.start()
+    _, second_factor = segment_factors(
+        places, odd, flag_ref, [tot], x, hann, conv, seg, work, copied
+    )
+    bins = b3.shape[0]
+
+    def second(k):
+        b3[k] = second_factor(k)
+
+    repeat(0, bins, second, 32)
+    kept = pltpu.make_async_copy(b3, b3_hbm, out_sem)
+    kept.start()
+    for copy in late:
+        copy.wait()
+    correlate(
+        *(0, count, scale, shares, me, a, b0, b2, b3, lag, work[-1], one, outs),
+        lambda one_bin: repeat(0, bins, one_bin, 32),
+    )
+    kept.wait()
+
+
+def rest_kernel(first, scale, shares, me_ref, *rest):
+    lag_hbm, a_hbm, b0_hbm, b2_hbm, b3_hbm = rest[:5]
+    outs, rest = rest[5 : 5 + shares], rest[5 + shares :]
+    lag, a, b0, b2, b3, cross, one, lag_sem, sem = rest
+    bins, count = b0.shape[0], a.shape[2]
+    some = bins // STEPS
+
+    def factors(n):
+        part = pl.ds(n * some, some)
+        return [
+            pltpu.make_async_copy(source, target, sem.at[n, m])
+            for m, (source, target) in enumerate(
+                (
+                    (b0_hbm.at[part], b0.at[part]),
+                    (b2_hbm.at[part], b2.at[part]),
+                    (b3_hbm.at[part], b3.at[part]),
+                    (a_hbm.at[part, :, pl.ds(first, count)], a.at[part]),
+                )
+            )
+        ]
+
+    for n in range(STEPS):
+        for copy in factors(n):
+            copy.start()
+    table = pltpu.make_async_copy(lag_hbm, lag, lag_sem)
+    table.start()
+    table.wait()
+
+    def bins_loop(one_bin):
+        def part(n, _):
+            for copy in factors(n):
+                copy.wait()
+            repeat(0, some, lambda k: one_bin(n * some + k), some)
+            return 0
+
+        lax.fori_loop(0, STEPS, part, 0)
+
+    correlate(first, count, scale, shares, me_ref[0], a, b0, b2, b3, lag, cross, one, outs, bins_loop)
 
 
 def stacks(places, shares, scale, me, flags, total, pieces, hann, conv, seg, lag, a, b0, b2):
     bins, depth, chans = b0.shape
     width = chans // 2
+    count = width // 2
     _, wins, ns = pieces[0].shape
     nlag, nfr = lag.shape
     smem = pl.BlockSpec(memory_space=pltpu.SMEM)
     vmem = pl.BlockSpec(memory_space=pltpu.VMEM)
     anywhere = pl.BlockSpec(memory_space=pl.ANY)
-    tables_in = [total, hann, conv, seg, lag, a, b0, b2]
-    operands = [*pieces, *tables_in]
-    held = [pieces[0], pieces[1], pieces[4], *tables_in]
-    return pl.pallas_call(
-        functools.partial(stack_kernel, places, scale, shares),
-        out_shape=[jax.ShapeDtypeStruct((width, OFFS // shares, nlag), BF16)] * shares,
+    out = [jax.ShapeDtypeStruct((count, OFFS // shares, nlag), BF16)] * shares
+    operands = [*pieces, total, hann, conv, seg, lag, a, b0, b2]
+    held = [pieces[0], pieces[1], pieces[4], total, hann, conv, seg, lag, b0, b2]
+    some_a = pltpu.VMEM((bins, 2, count, depth), BF16)
+    one = pltpu.VMEM((2, chans + width, chans), F32)
+    params = pltpu.CompilerParams(vmem_limit_bytes=VMEM)
+    cost = pl.CostEstimate(
+        flops=2 * count * bins * 4 * (2 * depth * chans + 2 * OFFS * chans),
+        bytes_accessed=20 * 1024 * 1024,
+        transcendentals=0,
+    )
+    *head, b3 = pl.pallas_call(
+        functools.partial(last_kernel, places, scale, shares),
+        out_shape=out + [jax.ShapeDtypeStruct(b0.shape, BF16)],
         in_specs=[smem] * 2 + [anywhere] * len(operands),
-        out_specs=[vmem] * shares,
+        out_specs=[vmem] * shares + [anywhere],
         scratch_shapes=[pltpu.VMEM(value.shape, value.dtype) for value in held]
         + work_shapes(1, chans, wins, ns)
         + [
+            some_a,
             pltpu.VMEM(b0.shape, BF16),
-            pltpu.VMEM((2, chans + width, chans), F32),
+            one,
             pltpu.SemaphoreType.DMA((8 + chans // PART,)),
-            pltpu.SemaphoreType.DMA((STEPS, 3)),
+            pltpu.SemaphoreType.DMA((3,)),
+            pltpu.SemaphoreType.DMA,
         ],
-        compiler_params=pltpu.CompilerParams(vmem_limit_bytes=VMEM),
-        cost_estimate=pl.CostEstimate(
-            flops=2 * width * bins * 4 * (2 * depth * chans + 2 * OFFS * chans),
-            bytes_accessed=20 * 1024 * 1024,
-            transcendentals=0,
-        ),
+        compiler_params=params,
+        cost_estimate=cost,
     )(me, flags, *operands)
+    tail = pl.pallas_call(
+        functools.partial(rest_kernel, count, scale, shares),
+        out_shape=out,
+        in_specs=[smem] + [anywhere] * 5,
+        out_specs=[vmem] * shares,
+        scratch_shapes=[
+            pltpu.VMEM(lag.shape, BF16),
+            some_a,
+            *[pltpu.VMEM(b0.shape, BF16)] * 3,
+            pltpu.VMEM((2, count * (nfr + 1), chans), F32),
+            one,
+            pltpu.SemaphoreType.DMA,
+            pltpu.SemaphoreType.DMA((STEPS, 4)),
+        ],
+        compiler_params=params,
+        cost_estimate=cost,
+    )(me, lag, a, b0, b2, b3)
+    return head, tail
 
 
 def add_over(value, axis, beside):
@@ -675,20 +746,22 @@
         *(hann, conv, seg, lag),
         *(a, b0, b2),
     )
-    arrived = {}
-    for d in reversed(range(groups)):
-        pairs = [
-            (b * groups + z, (b - z % 2) % blocks * groups + (z ^ d))
-            for b in range(blocks)
-            for z in range(groups)
-        ]
-        arrived[d] = lax.ppermute(found[d], both, pairs)
-    arrived = [arrived[d].astype(F32) for d in range(groups)]
-    same = sum(arrived[2::2], arrived[0])
-    other = sum(arrived[3::2], arrived[1])
-    return jnp.concatenate(
-        [jnp.where(odd == 0, same, other), jnp.where(odd == 0, other, same)], axis=0
-    )
+    lower, upper = [], []
+    for part in found:
+        arrived = {}
+        for d in reversed(range(groups)):
+            pairs = [
+                (b * groups + z, (b - z % 2) % blocks * groups + (z ^ d))
+                for b in range(blocks)
+                for z in range(groups)
+            ]
+            arrived[d] = lax.ppermute(part[d], both, pairs)
+        arrived = [arrived[d].astype(F32) for d in range(groups)]
+        same = sum(arrived[2::2], arrived[0])
+        other = sum(arrived[3::2], arrived[1])
+        lower.append(jnp.where(odd == 0, same, other))
+        upper.append(jnp.where(odd == 0, other, same))
+    return jnp.concatenate(lower + upper, axis=0)
 
 
 def solution(mesh):

time: 124 us -> 122 us (0.984); the launches traced: 123 us -> 122 us
  waiting for transfers between devices: 52.8 us -> 35.4 us
  starting transfers between devices: 15.6 us -> 23.7 us
  Pallas kernels: 47 us -> 54.6 us
    ppermute x4 -> x8, waiting for transfers between devices: 43.1 us -> 25.8 us  [shards(): arrived[d] = lax.ppermute(part[d], both, pairs)]
    ppermute x4 -> x8, starting transfers between devices: 3.99 us -> 12.1 us  [shards(): arrived[d] = lax.ppermute(part[d], both, pairs)]
    pallas_call x1 -> x2, Pallas kernels: 18.8 us -> 26.3 us  [the longest x1 15.1 us: stacks(): pl.pallas_call(functools.partial(last_kernel, places, scale, shares), out...]
  transfers between devices with their start and end apart: 16 -> 20, of which waited for: 6 -> 8; matrix products, arithmetic and copies ran while one was open for 3% -> 4% of each run, Pallas kernels for 23% -> 32%
where the time goes in v17:
time: 122 us
  Pallas kernels  54.6 us (45%)
  waiting for transfers between devices  35.4 us (29%)
  starting transfers between devices  23.7 us (19%)
  other arithmetic  6.08 us (5%)
  local copies, waits for them, and re-layouts  1.93 us (2%)
    ppermute x8, waiting for transfers between devices, shards(): arrived[d] = lax.ppermute(part[d], both, pairs)  25.8 us
    pallas_call x2, Pallas kernels, segments(): pl.pallas_call(functools.partial(kernel, places), out_shape=out, in_specs...  22.5 us
    pallas_call x1, Pallas kernels, stacks(): pl.pallas_call(functools.partial(last_kernel, places, scale, shares), out...  15.1 us
    ppermute x8, starting transfers between devices, shards(): arrived[d] = lax.ppermute(part[d], both, pairs)  12.1 us
    pallas_call x1, Pallas kernels, stacks(): pl.pallas_call(functools.partial(rest_kernel, count, scale, shares), out_...  11.2 us
    ppermute x1, waiting for transfers between devices, shards(): halo_tail = lax.ppermute(forward, both, halo_pairs)  4.34 us
    pallas_call x1, Pallas kernels, shards(): pl.pallas_call(section_sums, out_shape=[jax.ShapeDtypeStruct((NSEC, wins,...  4.1 us
    ppermute x4, starting transfers between devices, add_over(): lax.ppermute(value, axis, [(i, i ^ s) for i in range(count)])  3.73 us
  transfers between devices with their start and end apart: 20, of which 8 were waited for; matrix products, arithmetic and copies ran while one was open for 4% of the time, Pallas kernels for 32%

profile of v17, /device:TPU:19, one launch (start us, length us, event | category | flops | bytes accessed | tf_op | source)
XLA Modules:
  0.0 122.0 jit_solution(16008854280216448775)
XLA Ops:
  1.2 1.4 %collective-permute-start.4 = (bf16[40,8,1024]{2,1,0:T(8,128)(2,1)S(1)}, bf16[40,8,1024]{2,1,0:T(8,128)(2,1)}, u32[]{:S(2)}, u32[]{:S(2)}) collective-permute-start(bf16[40,8,1024]{2,1,0:T(8,128)(2,1)S(1)} %constant_dynamic-slice_fusion.1), channel_id=1, source_target_pairs={{0,1},{1,0},{2,3},{3,2},{4,5},{5,4},{6,7},{7,6},{8,9},{9,8},{10,11... | collective-permute-start | bytes 1966088 | tf_op jit(solution)/shard_map/ppermute | solution.py:668
  2.5 4.1 %shard_map.82 = (f32[2,8,1152]{2,1,0:T(8,128)}, bf16[64,8,1024]{2,1,0:T(8,128)(2,1)}, bf16[24,8,1024]{2,1,0:T(8,128)(2,1)}) custom-call(s32[1]{0:T(128)} %bitcast.1.odd_ref, s32[128]{0:T(128)} %dead_ref.1, s32[128]{0:T(128)} %sec_ref.1, bf16[128,8,1024]{2,1,0:T(8,128)(2,1)} %rest_1_.1), custom_call_target="tpu_custom_call" | custom-call | flops 1 | bytes 1 | tf_op jit(solution)/shard_map/pallas_call | solution.py:677
  9.7 1.3 %collective-permute-start.3 = (f32[2,8,1152]{2,1,0:T(8,128)S(1)}, f32[2,8,1152]{2,1,0:T(8,128)S(1)}, u32[]{:S(2)}, u32[]{:S(2)}) collective-permute-start(f32[2,8,1152]{2,1,0:T(8,128)S(1)} %add.35), channel_id=1, source_target_pairs={{0,24},{4,28},{8,16},{12,20},{16,8},{20,12},{24,0},{28,4},{1,25},{... | collective-permute-start | bytes 221192 | tf_op jit(solution)/shard_map/ppermute | solution.py:638
  11.2 1.2 collective-permute-start.1
  12.4 2.4 %multiply_reduce_fusion = f32[1024]{0:T(1024)} fusion(f32[512,1024]{1,0:T(8,128)} %constant.33.clone, f32[512]{0:T(512)S(1)} %copy-done.5), kind=kLoop, calls=%fused_computation.1 | loop fusion | flops 1047552 | bytes 2103296 | tf_op jit(solution)/shard_map/reduce_sum | solution.py:657
  14.8 1.2 collective-permute-start.11
  17.0 1.4 %collective-permute-start.5 = (f32[2,8,1152]{2,1,0:T(8,128)S(1)}, f32[2,8,1152]{2,1,0:T(8,128)S(1)}, u32[]{:S(2)}, u32[]{:S(2)}) collective-permute-start(f32[2,8,1152]{2,1,0:T(8,128)S(1)} %add_add_fusion.rest_0_), channel_id=1, source_target_pairs={{0,1},{1,0},{2,3},{3,2},{4,5},{5,4},{6,7},{7,6},{8,9},{9,8},{10,11... | collective-permute-start | bytes 221192 | tf_op jit(solution)/shard_map/ppermute | solution.py:706
  18.5 1.7 %shard_map.83.rest_3_.rest_8_.rest_7_ = bf16[256,1024]{1,0:T(8,128)(2,1)} custom-call(f32[1,1024]{1,0:T(1,128)} %bitcast.5), custom_call_target="tpu_custom_call" | custom-call | flops 1 | bytes 1 | tf_op jit(solution)/shard_map/pallas_call | solution.py:700
  20.2 1.3 %collective-permute-start.10 = (bf16[64,8,1024]{2,1,0:T(8,128)(2,1)}, bf16[64,8,1024]{2,1,0:T(8,128)(2,1)}, u32[]{:S(2)}, u32[]{:S(2)}) collective-permute-start(bf16[64,8,1024]{2,1,0:T(8,128)(2,1)} %get-tuple-element.60), channel_id=1, source_target_pairs={{0,1},{1,0},{2,3},{3,2},{4,5},{5,4},{6,7},{7,6},{8,9},{9,8},{10,11... | collective-permute-start | bytes 3145736 | tf_op jit(solution)/shard_map/ppermute | solution.py:708
  21.5 2.4 %collective-permute-start.7 = (bf16[40,8,1024]{2,1,0:T(8,128)(2,1)}, bf16[40,8,1024]{2,1,0:T(8,128)(2,1)S(1)}, u32[]{:S(2)}, u32[]{:S(2)}) collective-permute-start(bf16[40,8,1024]{2,1,0:T(8,128)(2,1)} %collective-permute-done.4.rest_2_), channel_id=1, source_target_pairs={{0,28},{1,5},{2,30},{3,7},{4,0},{5,9},{6,2},{7,11},{8,4},{9,13},{1... | collective-permute-start | bytes 1966088 | tf_op jit(solution)/shard_map/ppermute | solution.py:712
  23.9 9.1 %shard_map.84 = (bf16[128,128,128]{2,1,0:T(8,128)(2,1)}, bf16[2,1152,512]{2,1,0:T(8,128)(2,1)}) custom-call(s32[1]{0:T(128)} %bitcast.1.odd_ref, s32[2,128]{1,0:T(2,128)} %copy-done.3, f32[2,8,1152]{2,1,0:T(8,128)} %copy-done.2, bf16[128,8,1024]{2,1,0:T(8,128)(2,1)} %rest_1_.1, f32[1,1024]{1,0:T(1,128)} %constant.36.clone.rest_2_.rest_7_.rest_6_, ...), custom_call_target="tpu_custom_call" | custom-call | flops 3758096384 | bytes 16777216 | tf_op jit(solution)/shard_map/pallas_call | solution.py:403
  33.8 3.4 %collective-permute-done.7.rest_4_.rest_0_ = bf16[40,8,1024]{2,1,0:T(8,128)(2,1)S(1)} collective-permute-done((bf16[40,8,1024]{2,1,0:T(8,128)(2,1)}, bf16[40,8,1024]{2,1,0:T(8,128)(2,1)S(1)}, u32[]{:S(2)}, u32[]{:S(2)}) %collective-permute-start.7) | collective-permute-done | bytes 655392 | tf_op jit(solution)/shard_map/ppermute | solution.py:712
  37.2 4.3 %collective-permute-done.9.rest_5_.rest_1_ = bf16[24,8,1024]{2,1,0:T(8,128)(2,1)} collective-permute-done((bf16[24,8,1024]{2,1,0:T(8,128)(2,1)}, bf16[24,8,1024]{2,1,0:T(8,128)(2,1)}, u32[]{:S(2)}, u32[]{:S(2)}) %collective-permute-start.9) | collective-permute-done | bytes 393248 | tf_op jit(solution)/shard_map/ppermute | solution.py:719
  41.5 13.4 %shard_map.85 = (bf16[128,2,64,128]{3,2,1,0:T(8,128)(2,1)}, bf16[128,128,128]{2,1,0:T(8,128)(2,1)}) custom-call(s32[1]{0:T(128)} %bitcast.1.odd_ref, s32[2,192]{1,0:T(2,128)} %copy-done.4, f32[2,8,1152]{2,1,0:T(8,128)} %copy-done.2, f32[2,8,1152]{2,1,0:T(8,128)} %copy-done.1, bf16[40,8,1024]{2,1,0:T(8,128)(2,1)} %collective-permute-done.4.rest_2_, ...), custom_call_target="tpu_custom_call" | custom-call | flops 3758096384 | bytes 16777216 | tf_op jit(solution)/shard_map/pallas_call | solution.py:403
  54.9 15.1 %shard_map.86 = (bf16[32,32,128]{2,1,0:T(8,128)(2,1)}, bf16[32,32,128]{2,1,0:T(8,128)(2,1)}, bf16[32,32,128]{2,1,0:T(8,128)(2,1)}, bf16[32,32,128]{2,1,0:T(8,128)(2,1)}, bf16[128,128,128]{2,1,0:T(8,128)(2,1)}) custom-call(s32[1]{0:T(128)} %bitcast.me_ref, s32[2,192]{1,0:T(2,128)} %copy-done.4, bf16[40,8,1024]{2,1,0:T(8,128)(2,1)} %copy-done, ...), custom_call_target="tpu_custom_call" | custom-call | flops 2147483648 | bytes 20971520 | tf_op jit(solution)/shard_map/pallas_call | solution.py:593
  70.1 1.6 %collective-permute-start.12 = (bf16[32,32,128]{2,1,0:T(8,128)(2,1)}, bf16[32,32,128]{2,1,0:T(8,128)(2,1)S(1)}, u32[]{:S(2)}, u32[]{:S(2)}) collective-permute-start(bf16[32,32,128]{2,1,0:T(8,128)(2,1)} %get-tuple-element.68), channel_id=1, source_target_pairs={{0,0},{1,29},{2,2},{3,31},{4,4},{5,1},{6,6},{7,3},{8,8},{9,5},{10,... | collective-permute-start | bytes 786440 | tf_op jit(solution)/shard_map/ppermute | solution.py:758
  73.2 11.2 %shard_map.87 = (bf16[32,32,128]{2,1,0:T(8,128)(2,1)}, bf16[32,32,128]{2,1,0:T(8,128)(2,1)}, bf16[32,32,128]{2,1,0:T(8,128)(2,1)}, bf16[32,32,128]{2,1,0:T(8,128)(2,1)}) custom-call(s32[1]{0:T(128)} %bitcast.me_ref, bf16[128,256]{1,0:T(8,128)(2,1)} %constant.35.clone.rest_9_.rest_0_, bf16[128,2,64,128]{3,2,1,0:T(8,128)(2,1)} %get-tuple-element.65.rest_10_.rest_1_, ...), custom_call_target="tpu_custom_call" | custom-call | flops 2147483648 | bytes 20971520 | tf_op jit(solution)/shard_map/pallas_call | solution.py:611
  84.4 1.6 %collective-permute-start.16 = (bf16[32,32,128]{2,1,0:T(8,128)(2,1)}, bf16[32,32,128]{2,1,0:T(8,128)(2,1)S(1)}, u32[]{:S(2)}, u32[]{:S(2)}) collective-permute-start(bf16[32,32,128]{2,1,0:T(8,128)(2,1)} %get-tuple-element.73), channel_id=1, source_target_pairs={{0,0},{1,29},{2,2},{3,31},{4,4},{5,1},{6,6},{7,3},{8,8},{9,5},{10,... | collective-permute-start | bytes 786440 | tf_op jit(solution)/shard_map/ppermute | solution.py:758
  87.2 4.1 %collective-permute-start.18 = (bf16[32,32,128]{2,1,0:T(8,128)(2,1)}, bf16[32,32,128]{2,1,0:T(8,128)(2,1)S(1)}, u32[]{:S(2)}, u32[]{:S(2)}) collective-permute-start(bf16[32,32,128]{2,1,0:T(8,128)(2,1)} %get-tuple-element.75), channel_id=1, source_target_pairs={{0,1},{1,28},{2,3},{3,30},{4,5},{5,0},{6,7},{7,2},{8,9},{9,4},{10,... | collective-permute-start | bytes 786440 | tf_op jit(solution)/shard_map/ppermute | solution.py:758
  91.3 2.1 %collective-permute-start.19 = (bf16[32,32,128]{2,1,0:T(8,128)(2,1)}, bf16[32,32,128]{2,1,0:T(8,128)(2,1)S(1)}, u32[]{:S(2)}, u32[]{:S(2)}) collective-permute-start(bf16[32,32,128]{2,1,0:T(8,128)(2,1)} %get-tuple-element.76), channel_id=1, source_target_pairs={{0,3},{1,30},{2,1},{3,28},{4,7},{5,2},{6,5},{7,0},{8,11},{9,6},{10... | collective-permute-start | bytes 786440 | tf_op jit(solution)/shard_map/ppermute | solution.py:758
  93.4 11.6 %collective-permute-done.15 = bf16[32,32,128]{2,1,0:T(8,128)(2,1)} collective-permute-done((bf16[32,32,128]{2,1,0:T(8,128)(2,1)}, bf16[32,32,128]{2,1,0:T(8,128)(2,1)}, u32[]{:S(2)}, u32[]{:S(2)}) %collective-permute-start.15) | collective-permute-done | bytes 262176 | tf_op jit(solution)/shard_map/ppermute | solution.py:758
  106.1 5.8 %collective-permute-done.17 = bf16[32,32,128]{2,1,0:T(8,128)(2,1)S(1)} collective-permute-done((bf16[32,32,128]{2,1,0:T(8,128)(2,1)}, bf16[32,32,128]{2,1,0:T(8,128)(2,1)S(1)}, u32[]{:S(2)}, u32[]{:S(2)}) %collective-permute-start.17) | collective-permute-done | bytes 262176 | tf_op jit(solution)/shard_map/ppermute | solution.py:758
  111.9 8.4 %collective-permute-done.19 = bf16[32,32,128]{2,1,0:T(8,128)(2,1)S(1)} collective-permute-done((bf16[32,32,128]{2,1,0:T(8,128)(2,1)}, bf16[32,32,128]{2,1,0:T(8,128)(2,1)S(1)}, u32[]{:S(2)}, u32[]{:S(2)}) %collective-permute-start.19) | collective-permute-done | bytes 262176 | tf_op jit(solution)/shard_map/ppermute | solution.py:758
  120.5 1.5 %pad_maximum_fusion = f32[128,32,128]{2,1,0:T(8,128)} fusion(f32[32,32,128]{2,1,0:T(8,128)S(1)} %get-tuple-element.80, f32[32,32,128]{2,1,0:T(8,128)S(1)} %get-tuple-element.78, f32[32,32,128]{2,1,0:T(8,128)S(1)} %get-tuple-element.79, f32[32,32,128]{2,1,0:T(8,128)S(1)} %get-tuple-element.77), kind=kLoop, calls=%fused_computation | loop fusion | flops 1572864 | bytes 4194304 | tf_op jit(solution)/shard_map/concatenate | solution.py:764
  (49 shorter events, 10.4 us)
Async XLA Ops:
  0.0 12.4 %copy-start.5 = (f32[512]{0:T(512)S(1)}, f32[512]{0:T(512)}, u32[]{:S(2)}) copy-start(f32[512]{0:T(512)} %param.9) | copy-start | bytes 6148
  1.2 15.8 %collective-permute-start.4 = (bf16[40,8,1024]{2,1,0:T(8,128)(2,1)S(1)}, bf16[40,8,1024]{2,1,0:T(8,128)(2,1)}, u32[]{:S(2)}, u32[]{:S(2)}) collective-permute-start(bf16[40,8,1024]{2,1,0:T(8,128)(2,1)S(1)} %constant_dynamic-slice_fusion.1), channel_id=1, source_target_pairs={{0,1},{1,0},{2,3},{3,2},{4,5},{5,4},{6,7},{7,6},{8,9},{9,8},{10,11... | collective-permute-start | bytes 1966088 | tf_op jit(solution)/shard_map/ppermute | solution.py:668
  6.6 2.1 %collective-permute-start = (f32[2,8,1152]{2,1,0:T(8,128)}, f32[2,8,1152]{2,1,0:T(8,128)S(1)}, u32[]{:S(2)}, u32[]{:S(2)}) collective-permute-start(f32[2,8,1152]{2,1,0:T(8,128)} %get-tuple-element.41), channel_id=1, source_target_pairs={{0,4},{4,0},{8,12},{12,8},{16,20},{20,16},{24,28},{28,24},{1,5},{5... | collective-permute-start | bytes 221192 | tf_op jit(solution)/shard_map/ppermute | solution.py:638
  7.7 16.2 %copy-start.3 = (s32[2,128]{1,0:T(2,128)}, s32[2,128]{1,0:T(2,128)S(1)}, u32[]{:S(2)}) copy-start(s32[2,128]{1,0:T(2,128)S(1)} %pad_add_fusion.flag_ref) | copy-start | bytes 3076
  7.8 7.0 %collective-permute-start.6 = (s32[2,64]{1,0:T(2,128)S(1)}, s32[2,64]{1,0:T(2,128)S(1)}, u32[]{:S(2)}, u32[]{:S(2)}) collective-permute-start(s32[2,64]{1,0:T(2,128)S(1)} %constant_dynamic-slice_fusion), channel_id=1, source_target_pairs={{0,28},{1,5},{2,30},{3,7},{4,0},{5,9},{6,2},{7,11},{8,4},{9,13},{1... | collective-permute-start | bytes 1544 | tf_op jit(solution)/shard_map/ppermute | solution.py:672
  9.7 6.3 %collective-permute-start.3 = (f32[2,8,1152]{2,1,0:T(8,128)S(1)}, f32[2,8,1152]{2,1,0:T(8,128)S(1)}, u32[]{:S(2)}, u32[]{:S(2)}) collective-permute-start(f32[2,8,1152]{2,1,0:T(8,128)S(1)} %add.35), channel_id=1, source_target_pairs={{0,24},{4,28},{8,16},{12,20},{16,8},{20,12},{24,0},{28,4},{1,25},{... | collective-permute-start | bytes 221192 | tf_op jit(solution)/shard_map/ppermute | solution.py:638
  11.0 5.6 %collective-permute-start.2 = (f32[2,8,1152]{2,1,0:T(8,128)S(1)}, f32[2,8,1152]{2,1,0:T(8,128)S(1)}, u32[]{:S(2)}, u32[]{:S(2)}) collective-permute-start(f32[2,8,1152]{2,1,0:T(8,128)S(1)} %add.35), channel_id=1, source_target_pairs={{0,16},{4,20},{8,24},{12,28},{16,0},{20,4},{24,8},{28,12},{1,17},{... | collective-permute-start | bytes 221192 | tf_op jit(solution)/shard_map/ppermute | solution.py:638
  11.2 5.3 %collective-permute-start.1 = (f32[2,8,1152]{2,1,0:T(8,128)S(1)}, f32[2,8,1152]{2,1,0:T(8,128)S(1)}, u32[]{:S(2)}, u32[]{:S(2)}) collective-permute-start(f32[2,8,1152]{2,1,0:T(8,128)S(1)} %add.35), channel_id=1, source_target_pairs={{0,8},{4,12},{8,0},{12,4},{16,24},{20,28},{24,16},{28,20},{1,9},{5... | collective-permute-start | bytes 221192 | tf_op jit(solution)/shard_map/ppermute | solution.py:638
  14.8 19.0 %collective-permute-start.11 = (bf16[64,8,1024]{2,1,0:T(8,128)(2,1)}, bf16[64,8,1024]{2,1,0:T(8,128)(2,1)}, u32[]{:S(2)}, u32[]{:S(2)}) collective-permute-start(bf16[64,8,1024]{2,1,0:T(8,128)(2,1)} %get-tuple-element.60), channel_id=1, source_target_pairs={{0,28},{1,5},{2,30},{3,7},{4,0},{5,9},{6,2},{7,11},{8,4},{9,13},{1... | collective-permute-start | bytes 3145736 | tf_op jit(solution)/shard_map/ppermute | solution.py:696
  17.0 4.5 %collective-permute-start.5 = (f32[2,8,1152]{2,1,0:T(8,128)S(1)}, f32[2,8,1152]{2,1,0:T(8,128)S(1)}, u32[]{:S(2)}, u32[]{:S(2)}) collective-permute-start(f32[2,8,1152]{2,1,0:T(8,128)S(1)} %add_add_fusion.rest_0_), channel_id=1, source_target_pairs={{0,1},{1,0},{2,3},{3,2},{4,5},{5,4},{6,7},{7,6},{8,9},{9,8},{10,11... | collective-permute-start | bytes 221192 | tf_op jit(solution)/shard_map/ppermute | solution.py:706
  18.3 14.7 %collective-permute-start.8 = (bf16[24,8,1024]{2,1,0:T(8,128)(2,1)}, bf16[24,8,1024]{2,1,0:T(8,128)(2,1)}, u32[]{:S(2)}, u32[]{:S(2)}) collective-permute-start(bf16[24,8,1024]{2,1,0:T(8,128)(2,1)} %get-tuple-element.58), channel_id=1, source_target_pairs={{0,1},{1,0},{2,3},{3,2},{4,5},{5,4},{6,7},{7,6},{8,9},{9,8},{10,11... | collective-permute-start | bytes 1179656 | tf_op jit(solution)/shard_map/ppermute | solution.py:707
  20.2 34.7 %collective-permute-start.10 = (bf16[64,8,1024]{2,1,0:T(8,128)(2,1)}, bf16[64,8,1024]{2,1,0:T(8,128)(2,1)}, u32[]{:S(2)}, u32[]{:S(2)}) collective-permute-start(bf16[64,8,1024]{2,1,0:T(8,128)(2,1)} %get-tuple-element.60), channel_id=1, source_target_pairs={{0,1},{1,0},{2,3},{3,2},{4,5},{5,4},{6,7},{7,6},{8,9},{9,8},{10,11... | collective-permute-start | bytes 3145736 | tf_op jit(solution)/shard_map/ppermute | solution.py:708
  21.5 11.5 %copy-start.1 = (f32[2,8,1152]{2,1,0:T(8,128)}, f32[2,8,1152]{2,1,0:T(8,128)S(1)}, u32[]{:S(2)}) copy-start(f32[2,8,1152]{2,1,0:T(8,128)S(1)} %collective-permute-done.5.rest_1_.rest_5_) | copy-start | bytes 221188
  21.5 15.6 %collective-permute-start.7 = (bf16[40,8,1024]{2,1,0:T(8,128)(2,1)}, bf16[40,8,1024]{2,1,0:T(8,128)(2,1)S(1)}, u32[]{:S(2)}, u32[]{:S(2)}) collective-permute-start(bf16[40,8,1024]{2,1,0:T(8,128)(2,1)} %collective-permute-done.4.rest_2_), channel_id=1, source_target_pairs={{0,28},{1,5},{2,30},{3,7},{4,0},{5,9},{6,2},{7,11},{8,4},{9,13},{1... | collective-permute-start | bytes 1966088 | tf_op jit(solution)/shard_map/ppermute | solution.py:712
  33.0 8.5 %collective-permute-start.9 = (bf16[24,8,1024]{2,1,0:T(8,128)(2,1)}, bf16[24,8,1024]{2,1,0:T(8,128)(2,1)}, u32[]{:S(2)}, u32[]{:S(2)}) collective-permute-start(bf16[24,8,1024]{2,1,0:T(8,128)(2,1)} %collective-permute-done.8.rest_3_), channel_id=1, source_target_pairs={{0,28},{1,5},{2,30},{3,7},{4,0},{5,9},{6,2},{7,11},{8,4},{9,13},{1... | collective-permute-start | bytes 1179656 | tf_op jit(solution)/shard_map/ppermute | solution.py:719
  33.8 7.7 %copy-start.4 = (s32[2,192]{1,0:T(2,128)}, s32[2,192]{1,0:T(2,128)S(1)}, u32[]{:S(2)}) copy-start(s32[2,192]{1,0:T(2,128)S(1)} %constant_dynamic-update-slice_fusion.flag_ref) | copy-start | bytes 4612
  70.1 16.0 %collective-permute-start.12 = (bf16[32,32,128]{2,1,0:T(8,128)(2,1)}, bf16[32,32,128]{2,1,0:T(8,128)(2,1)S(1)}, u32[]{:S(2)}, u32[]{:S(2)}) collective-permute-start(bf16[32,32,128]{2,1,0:T(8,128)(2,1)} %get-tuple-element.68), channel_id=1, source_target_pairs={{0,0},{1,29},{2,2},{3,31},{4,4},{5,1},{6,6},{7,3},{8,8},{9,5},{10,... | collective-permute-start | bytes 786440 | tf_op jit(solution)/shard_map/ppermute | solution.py:758
  71.7 15.6 %collective-permute-start.13 = (bf16[32,32,128]{2,1,0:T(8,128)(2,1)}, bf16[32,32,128]{2,1,0:T(8,128)(2,1)S(1)}, u32[]{:S(2)}, u32[]{:S(2)}) collective-permute-start(bf16[32,32,128]{2,1,0:T(8,128)(2,1)} %get-tuple-element.69), channel_id=1, source_target_pairs={{0,2},{1,31},{2,0},{3,29},{4,6},{5,3},{6,4},{7,1},{8,10},{9,7},{10... | collective-permute-start | bytes 786440 | tf_op jit(solution)/shard_map/ppermute | solution.py:758
  71.7 19.6 %collective-permute-start.14 = (bf16[32,32,128]{2,1,0:T(8,128)(2,1)}, bf16[32,32,128]{2,1,0:T(8,128)(2,1)S(1)}, u32[]{:S(2)}, u32[]{:S(2)}) collective-permute-start(bf16[32,32,128]{2,1,0:T(8,128)(2,1)} %get-tuple-element.70), channel_id=1, source_target_pairs={{0,1},{1,28},{2,3},{3,30},{4,5},{5,0},{6,7},{7,2},{8,9},{9,4},{10,... | collective-permute-start | bytes 786440 | tf_op jit(solution)/shard_map/ppermute | solution.py:758
  72.2 32.7 %collective-permute-start.15 = (bf16[32,32,128]{2,1,0:T(8,128)(2,1)}, bf16[32,32,128]{2,1,0:T(8,128)(2,1)}, u32[]{:S(2)}, u32[]{:S(2)}) collective-permute-start(bf16[32,32,128]{2,1,0:T(8,128)(2,1)} %get-tuple-element.71), channel_id=1, source_target_pairs={{0,3},{1,30},{2,1},{3,28},{4,7},{5,2},{6,5},{7,0},{8,11},{9,6},{10... | collective-permute-start | bytes 786440 | tf_op jit(solution)/shard_map/ppermute | solution.py:758
  84.4 21.6 %collective-permute-start.16 = (bf16[32,32,128]{2,1,0:T(8,128)(2,1)}, bf16[32,32,128]{2,1,0:T(8,128)(2,1)S(1)}, u32[]{:S(2)}, u32[]{:S(2)}) collective-permute-start(bf16[32,32,128]{2,1,0:T(8,128)(2,1)} %get-tuple-element.73), channel_id=1, source_target_pairs={{0,0},{1,29},{2,2},{3,31},{4,4},{5,1},{6,6},{7,3},{8,8},{9,5},{10,... | collective-permute-start | bytes 786440 | tf_op jit(solution)/shard_map/ppermute | solution.py:758
  86.0 25.9 %collective-permute-start.17 = (bf16[32,32,128]{2,1,0:T(8,128)(2,1)}, bf16[32,32,128]{2,1,0:T(8,128)(2,1)S(1)}, u32[]{:S(2)}, u32[]{:S(2)}) collective-permute-start(bf16[32,32,128]{2,1,0:T(8,128)(2,1)} %get-tuple-element.74), channel_id=1, source_target_pairs={{0,2},{1,31},{2,0},{3,29},{4,6},{5,3},{6,4},{7,1},{8,10},{9,7},{10... | collective-permute-start | bytes 786440 | tf_op jit(solution)/shard_map/ppermute | solution.py:758
  87.2 24.7 %collective-permute-start.18 = (bf16[32,32,128]{2,1,0:T(8,128)(2,1)}, bf16[32,32,128]{2,1,0:T(8,128)(2,1)S(1)}, u32[]{:S(2)}, u32[]{:S(2)}) collective-permute-start(bf16[32,32,128]{2,1,0:T(8,128)(2,1)} %get-tuple-element.75), channel_id=1, source_target_pairs={{0,1},{1,28},{2,3},{3,30},{4,5},{5,0},{6,7},{7,2},{8,9},{9,4},{10,... | collective-permute-start | bytes 786440 | tf_op jit(solution)/shard_map/ppermute | solution.py:758
  91.3 29.0 %collective-permute-start.19 = (bf16[32,32,128]{2,1,0:T(8,128)(2,1)}, bf16[32,32,128]{2,1,0:T(8,128)(2,1)S(1)}, u32[]{:S(2)}, u32[]{:S(2)}) collective-permute-start(bf16[32,32,128]{2,1,0:T(8,128)(2,1)} %get-tuple-element.76), channel_id=1, source_target_pairs={{0,3},{1,30},{2,1},{3,28},{4,7},{5,2},{6,5},{7,0},{8,11},{9,6},{10... | collective-permute-start | bytes 786440 | tf_op jit(solution)/shard_map/ppermute | solution.py:758
  (4 other events, 26.6 us)

commit v18 on v17

--- a/solution.py
+++ b/solution.py
@@ -17,6 +17,7 @@
 PART = 32
 TILE = 256
 STEPS = 4
+SENDS = 8
 TOGETHER = 4
 VMEM = 63 * 1024 * 1024
 NT = (((1,), (1,)), ((), ()))
@@ -92,7 +93,7 @@
         out_ref[t : t + 16, :] = pltpu.roll(block, t, 1, stride=1, stride_axis=0).astype(BF16)
 
 
-def segment_factors(places, odd, flag_ref, tot, x, hann, conv, seg, work, copied, first=None):
+def segment_factors(places, odd, flag_ref, tot, x, hann, conv, seg, work, copied, first=None, save=None):
     common, clean, mass, square, rows, series_all, stage = work
     _, wins, ns = x[0].shape
     chans = sum(piece.shape[0] for piece in x)
@@ -158,6 +159,8 @@
             ).astype(BF16)
         series[: half // 2, :] = series[ns : ns + half // 2, :]
         series[ns + half // 2 :, :] = series[half // 2 : half, :]
+        if save is not None:
+            save(step)
 
         def place(which, j, value):
             for i in range(TOGETHER):
@@ -281,23 +284,27 @@
         [(conv_hbm, conv), (seg_hbm, seg)],
         in_sem,
     )
+    kept = [
+        pltpu.make_async_copy(work[-2].at[step], p_hbm.at[step], p_sem.at[step])
+        for step in range(p_hbm.shape[0])
+    ]
     _, second = segment_factors(
-        places, odd, flag_ref, [tot], [x], hann, conv, seg, work, copied
+        *(places, odd, flag_ref, [tot], [x], hann, conv, seg, work, copied),
+        save=lambda step: kept[step].start(),
     )
 
     def put_second(k, stage):
         stage[k] = second(k)
 
-    kept = pltpu.make_async_copy(work[-2], p_hbm, p_sem)
-    kept.start()
     send_factor(put_second, b_out, b_hbm, out_sem)
-    kept.wait()
+    for copy in kept:
+        copy.wait()
 
 
 def send_factor(factor, stage, target, sem):
-    step = stage.shape[0] // STEPS
+    step = stage.shape[0] // SENDS
     copies = []
-    for n in range(STEPS):
+    for n in range(SENDS):
         part = pl.ds(n * step, step)
 
         repeat(n * step, (n + 1) * step, lambda k: factor(k, stage), 32)
@@ -353,9 +360,9 @@
         a_out[k, 0] = value[width:]
         stage[k] = second_factor(k)
 
-    step = b_out.shape[0] // STEPS
+    step = b_out.shape[0] // SENDS
     copies = []
-    for n in range(STEPS):
+    for n in range(SENDS):
         part = pl.ds(n * step, step)
 
         repeat(n * step, (n + 1) * step, lambda k: both_factors(k, b_out), 16)
@@ -387,8 +394,8 @@
         held = scratch(*operands)
         last = scratch(b_shape) + [
             pltpu.SemaphoreType.DMA((count,)),
-            pltpu.SemaphoreType.DMA((STEPS,)),
-            pltpu.SemaphoreType.DMA,
+            pltpu.SemaphoreType.DMA((SENDS,)),
+            pltpu.SemaphoreType.DMA((wins // TOGETHER,)),
         ]
     else:
         kernel, out = second_kernel, [a_shape, b_shape]
@@ -397,7 +404,7 @@
         last = [
             pltpu.SemaphoreType.DMA((count,)),
             pltpu.SemaphoreType.DMA,
-            pltpu.SemaphoreType.DMA((2 * STEPS,)),
+            pltpu.SemaphoreType.DMA((2 * SENDS,)),
         ]
         operands.append(series)
     return pl.pallas_call(

time: 122 us -> 122 us (level)
  no operation moved by 1% of the time
where the time goes in v18:
time: 122 us
  Pallas kernels  54.4 us (45%)
  waiting for transfers between devices  35.5 us (29%)
  starting transfers between devices  23.7 us (19%)
  other arithmetic  6.08 us (5%)
  local copies, waits for them, and re-layouts  1.93 us (2%)
    ppermute x8, waiting for transfers between devices, shards(): arrived[d] = lax.ppermute(part[d], both, pairs)  25.8 us
    pallas_call x2, Pallas kernels, segments(): pl.pallas_call(functools.partial(kernel, places), out_shape=out, in_specs...  22.3 us
    pallas_call x1, Pallas kernels, stacks(): pl.pallas_call(functools.partial(last_kernel, places, scale, shares), out...  15.2 us
    ppermute x8, starting transfers between devices, shards(): arrived[d] = lax.ppermute(part[d], both, pairs)  12.1 us
    pallas_call x1, Pallas kernels, stacks(): pl.pallas_call(functools.partial(rest_kernel, count, scale, shares), out_...  11.2 us
    ppermute x1, waiting for transfers between devices, shards(): halo_tail = lax.ppermute(forward, both, halo_pairs)  4.33 us
    pallas_call x1, Pallas kernels, shards(): pl.pallas_call(section_sums, out_shape=[jax.ShapeDtypeStruct((NSEC, wins,...  4.1 us
    ppermute x4, starting transfers between devices, add_over(): lax.ppermute(value, axis, [(i, i ^ s) for i in range(count)])  3.73 us
  transfers between devices with their start and end apart: 20, of which 8 were waited for; matrix products, arithmetic and copies ran while one was open for 4% of the time, Pallas kernels for 32%

profile of v18, /device:TPU:19, one launch (start us, length us, event | category | flops | bytes accessed | tf_op | source)
XLA Modules:
  0.0 121.8 jit_solution(7457748611977376591)
XLA Ops:
  1.2 1.4 %collective-permute-start.4 = (bf16[40,8,1024]{2,1,0:T(8,128)(2,1)S(1)}, bf16[40,8,1024]{2,1,0:T(8,128)(2,1)}, u32[]{:S(2)}, u32[]{:S(2)}) collective-permute-start(bf16[40,8,1024]{2,1,0:T(8,128)(2,1)S(1)} %constant_dynamic-slice_fusion.1), channel_id=1, source_target_pairs={{0,1},{1,0},{2,3},{3,2},{4,5},{5,4},{6,7},{7,6},{8,9},{9,8},{10,11... | collective-permute-start | bytes 1966088 | tf_op jit(solution)/shard_map/ppermute | solution.py:675
  2.5 4.1 %shard_map.82 = (f32[2,8,1152]{2,1,0:T(8,128)}, bf16[64,8,1024]{2,1,0:T(8,128)(2,1)}, bf16[24,8,1024]{2,1,0:T(8,128)(2,1)}) custom-call(s32[1]{0:T(128)} %bitcast.1.odd_ref, s32[128]{0:T(128)} %dead_ref.1, s32[128]{0:T(128)} %sec_ref.1, bf16[128,8,1024]{2,1,0:T(8,128)(2,1)} %rest_1_.1), custom_call_target="tpu_custom_call" | custom-call | flops 1 | bytes 1 | tf_op jit(solution)/shard_map/pallas_call | solution.py:684
  9.7 1.3 %collective-permute-start.3 = (f32[2,8,1152]{2,1,0:T(8,128)S(1)}, f32[2,8,1152]{2,1,0:T(8,128)S(1)}, u32[]{:S(2)}, u32[]{:S(2)}) collective-permute-start(f32[2,8,1152]{2,1,0:T(8,128)S(1)} %add.35), channel_id=1, source_target_pairs={{0,24},{4,28},{8,16},{12,20},{16,8},{20,12},{24,0},{28,4},{1,25},{... | collective-permute-start | bytes 221192 | tf_op jit(solution)/shard_map/ppermute | solution.py:645
  11.2 1.2 collective-permute-start.1
  12.4 2.4 %multiply_reduce_fusion = f32[1024]{0:T(1024)} fusion(f32[512,1024]{1,0:T(8,128)} %constant.33.clone, f32[512]{0:T(512)S(1)} %copy-done.5), kind=kLoop, calls=%fused_computation.1 | loop fusion | flops 1047552 | bytes 2103296 | tf_op jit(solution)/shard_map/reduce_sum | solution.py:664
  14.8 1.2 collective-permute-start.11
  17.0 1.4 %collective-permute-start.5 = (f32[2,8,1152]{2,1,0:T(8,128)S(1)}, f32[2,8,1152]{2,1,0:T(8,128)S(1)}, u32[]{:S(2)}, u32[]{:S(2)}) collective-permute-start(f32[2,8,1152]{2,1,0:T(8,128)S(1)} %add_add_fusion.rest_0_), channel_id=1, source_target_pairs={{0,1},{1,0},{2,3},{3,2},{4,5},{5,4},{6,7},{7,6},{8,9},{9,8},{10,11... | collective-permute-start | bytes 221192 | tf_op jit(solution)/shard_map/ppermute | solution.py:713
  18.5 1.7 %shard_map.83.rest_3_.rest_8_.rest_7_ = bf16[256,1024]{1,0:T(8,128)(2,1)} custom-call(f32[1,1024]{1,0:T(1,128)} %bitcast.5), custom_call_target="tpu_custom_call" | custom-call | flops 1 | bytes 1 | tf_op jit(solution)/shard_map/pallas_call | solution.py:707
  20.2 1.3 %collective-permute-start.10 = (bf16[64,8,1024]{2,1,0:T(8,128)(2,1)}, bf16[64,8,1024]{2,1,0:T(8,128)(2,1)}, u32[]{:S(2)}, u32[]{:S(2)}) collective-permute-start(bf16[64,8,1024]{2,1,0:T(8,128)(2,1)} %get-tuple-element.60), channel_id=1, source_target_pairs={{0,1},{1,0},{2,3},{3,2},{4,5},{5,4},{6,7},{7,6},{8,9},{9,8},{10,11... | collective-permute-start | bytes 3145736 | tf_op jit(solution)/shard_map/ppermute | solution.py:715
  21.5 2.4 %collective-permute-start.7 = (bf16[40,8,1024]{2,1,0:T(8,128)(2,1)}, bf16[40,8,1024]{2,1,0:T(8,128)(2,1)S(1)}, u32[]{:S(2)}, u32[]{:S(2)}) collective-permute-start(bf16[40,8,1024]{2,1,0:T(8,128)(2,1)} %collective-permute-done.4.rest_2_), channel_id=1, source_target_pairs={{0,28},{1,5},{2,30},{3,7},{4,0},{5,9},{6,2},{7,11},{8,4},{9,13},{1... | collective-permute-start | bytes 1966088 | tf_op jit(solution)/shard_map/ppermute | solution.py:719
  23.9 9.1 %shard_map.84 = (bf16[128,128,128]{2,1,0:T(8,128)(2,1)}, bf16[2,1152,512]{2,1,0:T(8,128)(2,1)}) custom-call(s32[1]{0:T(128)} %bitcast.1.odd_ref, s32[2,128]{1,0:T(2,128)} %copy-done.3, f32[2,8,1152]{2,1,0:T(8,128)} %copy-done.2, bf16[128,8,1024]{2,1,0:T(8,128)(2,1)} %rest_1_.1, f32[1,1024]{1,0:T(1,128)} %constant.36.clone.rest_2_.rest_7_.rest_6_, ...), custom_call_target="tpu_custom_call" | custom-call | flops 3758096384 | bytes 16777216 | tf_op jit(solution)/shard_map/pallas_call | solution.py:410
  33.8 3.4 %collective-permute-done.7.rest_4_.rest_0_ = bf16[40,8,1024]{2,1,0:T(8,128)(2,1)S(1)} collective-permute-done((bf16[40,8,1024]{2,1,0:T(8,128)(2,1)}, bf16[40,8,1024]{2,1,0:T(8,128)(2,1)S(1)}, u32[]{:S(2)}, u32[]{:S(2)}) %collective-permute-start.7) | collective-permute-done | bytes 655392 | tf_op jit(solution)/shard_map/ppermute | solution.py:719
  37.2 4.3 %collective-permute-done.9.rest_5_.rest_1_ = bf16[24,8,1024]{2,1,0:T(8,128)(2,1)} collective-permute-done((bf16[24,8,1024]{2,1,0:T(8,128)(2,1)}, bf16[24,8,1024]{2,1,0:T(8,128)(2,1)}, u32[]{:S(2)}, u32[]{:S(2)}) %collective-permute-start.9) | collective-permute-done | bytes 393248 | tf_op jit(solution)/shard_map/ppermute | solution.py:726
  41.5 13.2 %shard_map.85 = (bf16[128,2,64,128]{3,2,1,0:T(8,128)(2,1)}, bf16[128,128,128]{2,1,0:T(8,128)(2,1)}) custom-call(s32[1]{0:T(128)} %bitcast.1.odd_ref, s32[2,192]{1,0:T(2,128)} %copy-done.4, f32[2,8,1152]{2,1,0:T(8,128)} %copy-done.2, f32[2,8,1152]{2,1,0:T(8,128)} %copy-done.1, bf16[40,8,1024]{2,1,0:T(8,128)(2,1)} %collective-permute-done.4.rest_2_, ...), custom_call_target="tpu_custom_call" | custom-call | flops 3758096384 | bytes 16777216 | tf_op jit(solution)/shard_map/pallas_call | solution.py:410
  54.7 15.2 %shard_map.86 = (bf16[32,32,128]{2,1,0:T(8,128)(2,1)}, bf16[32,32,128]{2,1,0:T(8,128)(2,1)}, bf16[32,32,128]{2,1,0:T(8,128)(2,1)}, bf16[32,32,128]{2,1,0:T(8,128)(2,1)}, bf16[128,128,128]{2,1,0:T(8,128)(2,1)}) custom-call(s32[1]{0:T(128)} %bitcast.me_ref, s32[2,192]{1,0:T(2,128)} %copy-done.4, bf16[40,8,1024]{2,1,0:T(8,128)(2,1)} %copy-done, ...), custom_call_target="tpu_custom_call" | custom-call | flops 2147483648 | bytes 20971520 | tf_op jit(solution)/shard_map/pallas_call | solution.py:600
  69.8 1.6 %collective-permute-start.12 = (bf16[32,32,128]{2,1,0:T(8,128)(2,1)}, bf16[32,32,128]{2,1,0:T(8,128)(2,1)S(1)}, u32[]{:S(2)}, u32[]{:S(2)}) collective-permute-start(bf16[32,32,128]{2,1,0:T(8,128)(2,1)} %get-tuple-element.68), channel_id=1, source_target_pairs={{0,0},{1,29},{2,2},{3,31},{4,4},{5,1},{6,6},{7,3},{8,8},{9,5},{10,... | collective-permute-start | bytes 786440 | tf_op jit(solution)/shard_map/ppermute | solution.py:765
  73.0 11.2 %shard_map.87 = (bf16[32,32,128]{2,1,0:T(8,128)(2,1)}, bf16[32,32,128]{2,1,0:T(8,128)(2,1)}, bf16[32,32,128]{2,1,0:T(8,128)(2,1)}, bf16[32,32,128]{2,1,0:T(8,128)(2,1)}) custom-call(s32[1]{0:T(128)} %bitcast.me_ref, bf16[128,256]{1,0:T(8,128)(2,1)} %constant.35.clone.rest_9_.rest_0_, bf16[128,2,64,128]{3,2,1,0:T(8,128)(2,1)} %get-tuple-element.65.rest_10_.rest_1_, ...), custom_call_target="tpu_custom_call" | custom-call | flops 2147483648 | bytes 20971520 | tf_op jit(solution)/shard_map/pallas_call | solution.py:618
  84.2 1.6 %collective-permute-start.16 = (bf16[32,32,128]{2,1,0:T(8,128)(2,1)}, bf16[32,32,128]{2,1,0:T(8,128)(2,1)S(1)}, u32[]{:S(2)}, u32[]{:S(2)}) collective-permute-start(bf16[32,32,128]{2,1,0:T(8,128)(2,1)} %get-tuple-element.73), channel_id=1, source_target_pairs={{0,0},{1,29},{2,2},{3,31},{4,4},{5,1},{6,6},{7,3},{8,8},{9,5},{10,... | collective-permute-start | bytes 786440 | tf_op jit(solution)/shard_map/ppermute | solution.py:765
  87.0 4.1 %collective-permute-start.18 = (bf16[32,32,128]{2,1,0:T(8,128)(2,1)}, bf16[32,32,128]{2,1,0:T(8,128)(2,1)S(1)}, u32[]{:S(2)}, u32[]{:S(2)}) collective-permute-start(bf16[32,32,128]{2,1,0:T(8,128)(2,1)} %get-tuple-element.75), channel_id=1, source_target_pairs={{0,1},{1,28},{2,3},{3,30},{4,5},{5,0},{6,7},{7,2},{8,9},{9,4},{10,... | collective-permute-start | bytes 786440 | tf_op jit(solution)/shard_map/ppermute | solution.py:765
  91.1 2.1 %collective-permute-start.19 = (bf16[32,32,128]{2,1,0:T(8,128)(2,1)}, bf16[32,32,128]{2,1,0:T(8,128)(2,1)S(1)}, u32[]{:S(2)}, u32[]{:S(2)}) collective-permute-start(bf16[32,32,128]{2,1,0:T(8,128)(2,1)} %get-tuple-element.76), channel_id=1, source_target_pairs={{0,3},{1,30},{2,1},{3,28},{4,7},{5,2},{6,5},{7,0},{8,11},{9,6},{10... | collective-permute-start | bytes 786440 | tf_op jit(solution)/shard_map/ppermute | solution.py:765
  93.2 11.6 %collective-permute-done.15 = bf16[32,32,128]{2,1,0:T(8,128)(2,1)} collective-permute-done((bf16[32,32,128]{2,1,0:T(8,128)(2,1)}, bf16[32,32,128]{2,1,0:T(8,128)(2,1)}, u32[]{:S(2)}, u32[]{:S(2)}) %collective-permute-start.15) | collective-permute-done | bytes 262176 | tf_op jit(solution)/shard_map/ppermute | solution.py:765
  105.9 5.7 %collective-permute-done.17 = bf16[32,32,128]{2,1,0:T(8,128)(2,1)S(1)} collective-permute-done((bf16[32,32,128]{2,1,0:T(8,128)(2,1)}, bf16[32,32,128]{2,1,0:T(8,128)(2,1)S(1)}, u32[]{:S(2)}, u32[]{:S(2)}) %collective-permute-start.17) | collective-permute-done | bytes 262176 | tf_op jit(solution)/shard_map/ppermute | solution.py:765
  111.7 8.4 %collective-permute-done.19 = bf16[32,32,128]{2,1,0:T(8,128)(2,1)S(1)} collective-permute-done((bf16[32,32,128]{2,1,0:T(8,128)(2,1)}, bf16[32,32,128]{2,1,0:T(8,128)(2,1)S(1)}, u32[]{:S(2)}, u32[]{:S(2)}) %collective-permute-start.19) | collective-permute-done | bytes 262176 | tf_op jit(solution)/shard_map/ppermute | solution.py:765
  120.3 1.5 %pad_maximum_fusion = f32[128,32,128]{2,1,0:T(8,128)} fusion(f32[32,32,128]{2,1,0:T(8,128)S(1)} %get-tuple-element.80, f32[32,32,128]{2,1,0:T(8,128)S(1)} %get-tuple-element.78, f32[32,32,128]{2,1,0:T(8,128)S(1)} %get-tuple-element.79, f32[32,32,128]{2,1,0:T(8,128)S(1)} %get-tuple-element.77), kind=kLoop, calls=%fused_computation | loop fusion | flops 1572864 | bytes 4194304 | tf_op jit(solution)/shard_map/concatenate | solution.py:771
  (49 shorter events, 10.4 us)
Async XLA Ops:
  0.0 12.4 %copy-start.5 = (f32[512]{0:T(512)S(1)}, f32[512]{0:T(512)}, u32[]{:S(2)}) copy-start(f32[512]{0:T(512)} %param.9) | copy-start | bytes 6148
  1.2 15.8 %collective-permute-start.4 = (bf16[40,8,1024]{2,1,0:T(8,128)(2,1)S(1)}, bf16[40,8,1024]{2,1,0:T(8,128)(2,1)}, u32[]{:S(2)}, u32[]{:S(2)}) collective-permute-start(bf16[40,8,1024]{2,1,0:T(8,128)(2,1)S(1)} %constant_dynamic-slice_fusion.1), channel_id=1, source_target_pairs={{0,1},{1,0},{2,3},{3,2},{4,5},{5,4},{6,7},{7,6},{8,9},{9,8},{10,11... | collective-permute-start | bytes 1966088 | tf_op jit(solution)/shard_map/ppermute | solution.py:675
  6.6 2.1 %collective-permute-start = (f32[2,8,1152]{2,1,0:T(8,128)}, f32[2,8,1152]{2,1,0:T(8,128)S(1)}, u32[]{:S(2)}, u32[]{:S(2)}) collective-permute-start(f32[2,8,1152]{2,1,0:T(8,128)} %get-tuple-element.41), channel_id=1, source_target_pairs={{0,4},{4,0},{8,12},{12,8},{16,20},{20,16},{24,28},{28,24},{1,5},{5... | collective-permute-start | bytes 221192 | tf_op jit(solution)/shard_map/ppermute | solution.py:645
  7.7 16.2 %copy-start.3 = (s32[2,128]{1,0:T(2,128)}, s32[2,128]{1,0:T(2,128)S(1)}, u32[]{:S(2)}) copy-start(s32[2,128]{1,0:T(2,128)S(1)} %pad_add_fusion.flag_ref) | copy-start | bytes 3076
  7.8 7.0 %collective-permute-start.6 = (s32[2,64]{1,0:T(2,128)S(1)}, s32[2,64]{1,0:T(2,128)S(1)}, u32[]{:S(2)}, u32[]{:S(2)}) collective-permute-start(s32[2,64]{1,0:T(2,128)S(1)} %constant_dynamic-slice_fusion), channel_id=1, source_target_pairs={{0,28},{1,5},{2,30},{3,7},{4,0},{5,9},{6,2},{7,11},{8,4},{9,13},{1... | collective-permute-start | bytes 1544 | tf_op jit(solution)/shard_map/ppermute | solution.py:679
  9.7 6.3 %collective-permute-start.3 = (f32[2,8,1152]{2,1,0:T(8,128)S(1)}, f32[2,8,1152]{2,1,0:T(8,128)S(1)}, u32[]{:S(2)}, u32[]{:S(2)}) collective-permute-start(f32[2,8,1152]{2,1,0:T(8,128)S(1)} %add.35), channel_id=1, source_target_pairs={{0,24},{4,28},{8,16},{12,20},{16,8},{20,12},{24,0},{28,4},{1,25},{... | collective-permute-start | bytes 221192 | tf_op jit(solution)/shard_map/ppermute | solution.py:645
  11.0 5.6 %collective-permute-start.2 = (f32[2,8,1152]{2,1,0:T(8,128)S(1)}, f32[2,8,1152]{2,1,0:T(8,128)S(1)}, u32[]{:S(2)}, u32[]{:S(2)}) collective-permute-start(f32[2,8,1152]{2,1,0:T(8,128)S(1)} %add.35), channel_id=1, source_target_pairs={{0,16},{4,20},{8,24},{12,28},{16,0},{20,4},{24,8},{28,12},{1,17},{... | collective-permute-start | bytes 221192 | tf_op jit(solution)/shard_map/ppermute | solution.py:645
  11.2 5.3 %collective-permute-start.1 = (f32[2,8,1152]{2,1,0:T(8,128)S(1)}, f32[2,8,1152]{2,1,0:T(8,128)S(1)}, u32[]{:S(2)}, u32[]{:S(2)}) collective-permute-start(f32[2,8,1152]{2,1,0:T(8,128)S(1)} %add.35), channel_id=1, source_target_pairs={{0,8},{4,12},{8,0},{12,4},{16,24},{20,28},{24,16},{28,20},{1,9},{5... | collective-permute-start | bytes 221192 | tf_op jit(solution)/shard_map/ppermute | solution.py:645
  14.8 19.0 %collective-permute-start.11 = (bf16[64,8,1024]{2,1,0:T(8,128)(2,1)}, bf16[64,8,1024]{2,1,0:T(8,128)(2,1)}, u32[]{:S(2)}, u32[]{:S(2)}) collective-permute-start(bf16[64,8,1024]{2,1,0:T(8,128)(2,1)} %get-tuple-element.60), channel_id=1, source_target_pairs={{0,28},{1,5},{2,30},{3,7},{4,0},{5,9},{6,2},{7,11},{8,4},{9,13},{1... | collective-permute-start | bytes 3145736 | tf_op jit(solution)/shard_map/ppermute | solution.py:703
  17.0 4.5 %collective-permute-start.5 = (f32[2,8,1152]{2,1,0:T(8,128)S(1)}, f32[2,8,1152]{2,1,0:T(8,128)S(1)}, u32[]{:S(2)}, u32[]{:S(2)}) collective-permute-start(f32[2,8,1152]{2,1,0:T(8,128)S(1)} %add_add_fusion.rest_0_), channel_id=1, source_target_pairs={{0,1},{1,0},{2,3},{3,2},{4,5},{5,4},{6,7},{7,6},{8,9},{9,8},{10,11... | collective-permute-start | bytes 221192 | tf_op jit(solution)/shard_map/ppermute | solution.py:713
  18.3 14.7 %collective-permute-start.8 = (bf16[24,8,1024]{2,1,0:T(8,128)(2,1)}, bf16[24,8,1024]{2,1,0:T(8,128)(2,1)}, u32[]{:S(2)}, u32[]{:S(2)}) collective-permute-start(bf16[24,8,1024]{2,1,0:T(8,128)(2,1)} %get-tuple-element.58), channel_id=1, source_target_pairs={{0,1},{1,0},{2,3},{3,2},{4,5},{5,4},{6,7},{7,6},{8,9},{9,8},{10,11... | collective-permute-start | bytes 1179656 | tf_op jit(solution)/shard_map/ppermute | solution.py:714
  20.2 34.5 %collective-permute-start.10 = (bf16[64,8,1024]{2,1,0:T(8,128)(2,1)}, bf16[64,8,1024]{2,1,0:T(8,128)(2,1)}, u32[]{:S(2)}, u32[]{:S(2)}) collective-permute-start(bf16[64,8,1024]{2,1,0:T(8,128)(2,1)} %get-tuple-element.60), channel_id=1, source_target_pairs={{0,1},{1,0},{2,3},{3,2},{4,5},{5,4},{6,7},{7,6},{8,9},{9,8},{10,11... | collective-permute-start | bytes 3145736 | tf_op jit(solution)/shard_map/ppermute | solution.py:715
  21.5 11.5 %copy-start.1 = (f32[2,8,1152]{2,1,0:T(8,128)}, f32[2,8,1152]{2,1,0:T(8,128)S(1)}, u32[]{:S(2)}) copy-start(f32[2,8,1152]{2,1,0:T(8,128)S(1)} %collective-permute-done.5.rest_1_.rest_5_) | copy-start | bytes 221188
  21.5 15.6 %collective-permute-start.7 = (bf16[40,8,1024]{2,1,0:T(8,128)(2,1)}, bf16[40,8,1024]{2,1,0:T(8,128)(2,1)S(1)}, u32[]{:S(2)}, u32[]{:S(2)}) collective-permute-start(bf16[40,8,1024]{2,1,0:T(8,128)(2,1)} %collective-permute-done.4.rest_2_), channel_id=1, source_target_pairs={{0,28},{1,5},{2,30},{3,7},{4,0},{5,9},{6,2},{7,11},{8,4},{9,13},{1... | collective-permute-start | bytes 1966088 | tf_op jit(solution)/shard_map/ppermute | solution.py:719
  33.0 8.5 %collective-permute-start.9 = (bf16[24,8,1024]{2,1,0:T(8,128)(2,1)}, bf16[24,8,1024]{2,1,0:T(8,128)(2,1)}, u32[]{:S(2)}, u32[]{:S(2)}) collective-permute-start(bf16[24,8,1024]{2,1,0:T(8,128)(2,1)} %collective-permute-done.8.rest_3_), channel_id=1, source_target_pairs={{0,28},{1,5},{2,30},{3,7},{4,0},{5,9},{6,2},{7,11},{8,4},{9,13},{1... | collective-permute-start | bytes 1179656 | tf_op jit(solution)/shard_map/ppermute | solution.py:726
  33.8 7.7 %copy-start.4 = (s32[2,192]{1,0:T(2,128)}, s32[2,192]{1,0:T(2,128)S(1)}, u32[]{:S(2)}) copy-start(s32[2,192]{1,0:T(2,128)S(1)} %constant_dynamic-update-slice_fusion.flag_ref) | copy-start | bytes 4612
  69.8 16.0 %collective-permute-start.12 = (bf16[32,32,128]{2,1,0:T(8,128)(2,1)}, bf16[32,32,128]{2,1,0:T(8,128)(2,1)S(1)}, u32[]{:S(2)}, u32[]{:S(2)}) collective-permute-start(bf16[32,32,128]{2,1,0:T(8,128)(2,1)} %get-tuple-element.68), channel_id=1, source_target_pairs={{0,0},{1,29},{2,2},{3,31},{4,4},{5,1},{6,6},{7,3},{8,8},{9,5},{10,... | collective-permute-start | bytes 786440 | tf_op jit(solution)/shard_map/ppermute | solution.py:765
  71.5 15.6 %collective-permute-start.13 = (bf16[32,32,128]{2,1,0:T(8,128)(2,1)}, bf16[32,32,128]{2,1,0:T(8,128)(2,1)S(1)}, u32[]{:S(2)}, u32[]{:S(2)}) collective-permute-start(bf16[32,32,128]{2,1,0:T(8,128)(2,1)} %get-tuple-element.69), channel_id=1, source_target_pairs={{0,2},{1,31},{2,0},{3,29},{4,6},{5,3},{6,4},{7,1},{8,10},{9,7},{10... | collective-permute-start | bytes 786440 | tf_op jit(solution)/shard_map/ppermute | solution.py:765
  71.5 19.6 %collective-permute-start.14 = (bf16[32,32,128]{2,1,0:T(8,128)(2,1)}, bf16[32,32,128]{2,1,0:T(8,128)(2,1)S(1)}, u32[]{:S(2)}, u32[]{:S(2)}) collective-permute-start(bf16[32,32,128]{2,1,0:T(8,128)(2,1)} %get-tuple-element.70), channel_id=1, source_target_pairs={{0,1},{1,28},{2,3},{3,30},{4,5},{5,0},{6,7},{7,2},{8,9},{9,4},{10,... | collective-permute-start | bytes 786440 | tf_op jit(solution)/shard_map/ppermute | solution.py:765
  72.0 32.8 %collective-permute-start.15 = (bf16[32,32,128]{2,1,0:T(8,128)(2,1)}, bf16[32,32,128]{2,1,0:T(8,128)(2,1)}, u32[]{:S(2)}, u32[]{:S(2)}) collective-permute-start(bf16[32,32,128]{2,1,0:T(8,128)(2,1)} %get-tuple-element.71), channel_id=1, source_target_pairs={{0,3},{1,30},{2,1},{3,28},{4,7},{5,2},{6,5},{7,0},{8,11},{9,6},{10... | collective-permute-start | bytes 786440 | tf_op jit(solution)/shard_map/ppermute | solution.py:765
  84.2 21.7 %collective-permute-start.16 = (bf16[32,32,128]{2,1,0:T(8,128)(2,1)}, bf16[32,32,128]{2,1,0:T(8,128)(2,1)S(1)}, u32[]{:S(2)}, u32[]{:S(2)}) collective-permute-start(bf16[32,32,128]{2,1,0:T(8,128)(2,1)} %get-tuple-element.73), channel_id=1, source_target_pairs={{0,0},{1,29},{2,2},{3,31},{4,4},{5,1},{6,6},{7,3},{8,8},{9,5},{10,... | collective-permute-start | bytes 786440 | tf_op jit(solution)/shard_map/ppermute | solution.py:765
  85.8 25.8 %collective-permute-start.17 = (bf16[32,32,128]{2,1,0:T(8,128)(2,1)}, bf16[32,32,128]{2,1,0:T(8,128)(2,1)S(1)}, u32[]{:S(2)}, u32[]{:S(2)}) collective-permute-start(bf16[32,32,128]{2,1,0:T(8,128)(2,1)} %get-tuple-element.74), channel_id=1, source_target_pairs={{0,2},{1,31},{2,0},{3,29},{4,6},{5,3},{6,4},{7,1},{8,10},{9,7},{10... | collective-permute-start | bytes 786440 | tf_op jit(solution)/shard_map/ppermute | solution.py:765
  87.0 24.6 %collective-permute-start.18 = (bf16[32,32,128]{2,1,0:T(8,128)(2,1)}, bf16[32,32,128]{2,1,0:T(8,128)(2,1)S(1)}, u32[]{:S(2)}, u32[]{:S(2)}) collective-permute-start(bf16[32,32,128]{2,1,0:T(8,128)(2,1)} %get-tuple-element.75), channel_id=1, source_target_pairs={{0,1},{1,28},{2,3},{3,30},{4,5},{5,0},{6,7},{7,2},{8,9},{9,4},{10,... | collective-permute-start | bytes 786440 | tf_op jit(solution)/shard_map/ppermute | solution.py:765
  91.1 29.0 %collective-permute-start.19 = (bf16[32,32,128]{2,1,0:T(8,128)(2,1)}, bf16[32,32,128]{2,1,0:T(8,128)(2,1)S(1)}, u32[]{:S(2)}, u32[]{:S(2)}) collective-permute-start(bf16[32,32,128]{2,1,0:T(8,128)(2,1)} %get-tuple-element.76), channel_id=1, source_target_pairs={{0,3},{1,30},{2,1},{3,28},{4,7},{5,2},{6,5},{7,0},{8,11},{9,6},{10... | collective-permute-start | bytes 786440 | tf_op jit(solution)/shard_map/ppermute | solution.py:765
  (4 other events, 26.6 us)

commit v19 on v17

--- a/solution.py
+++ b/solution.py
@@ -747,20 +747,22 @@
         *(a, b0, b2),
     )
     lower, upper = [], []
+    order = list(range(2, groups)) + [0, 1]
     for part in found:
         arrived = {}
-        for d in reversed(range(groups)):
+        for d in order:
             pairs = [
                 (b * groups + z, (b - z % 2) % blocks * groups + (z ^ d))
                 for b in range(blocks)
                 for z in range(groups)
             ]
             arrived[d] = lax.ppermute(part[d], both, pairs)
-        arrived = [arrived[d].astype(F32) for d in range(groups)]
-        same = sum(arrived[2::2], arrived[0])
-        other = sum(arrived[3::2], arrived[1])
-        lower.append(jnp.where(odd == 0, same, other))
-        upper.append(jnp.where(odd == 0, other, same))
+        for out, sides in ((lower, (0, 1)), (upper, (1, 0))):
+            terms = [
+                jnp.where(odd == 0, arrived[d + sides[0]], arrived[d + sides[1]]).astype(F32)
+                for d in order[::2]
+            ]
+            out.append(sum(terms[1:], terms[0]))
     return jnp.concatenate(lower + upper, axis=0)
 
 

time: 122 us -> 122 us (level); the launches traced: 122 us -> 120 us
  starting transfers between devices: 23.7 us -> 20.4 us
  waiting for transfers between devices: 35.4 us -> 37.2 us
    ppermute x8, starting transfers between devices: 12.1 us -> 8.78 us  [shards(): arrived[d] = lax.ppermute(part[d], both, pairs)]
    ppermute x8, waiting for transfers between devices: 25.8 us -> 27.6 us  [shards(): arrived[d] = lax.ppermute(part[d], both, pairs)]
    add x0 -> x2, other arithmetic: none -> 1.31 us  [shards(): out.append(sum(terms[1:], terms[0]))]
    select_n x2 -> x0, other arithmetic: 1.27 us -> none  [shards(): lower.append(jnp.where(odd == 0, same, other))]
  transfers between devices with their start and end apart: 20 -> 20, of which waited for: 8 -> 9; matrix products, arithmetic and copies ran while one was open for 4% -> 4% of each run, Pallas kernels for 32% -> 33%
where the time goes in v19:
time: 122 us; the launch traced here: 120 us
  Pallas kernels  54.6 us (45%)
  waiting for transfers between devices  37.2 us (30%)
  starting transfers between devices  20.4 us (17%)
  other arithmetic  6.12 us (5%)
  local copies, waits for them, and re-layouts  1.93 us (2%)
    ppermute x8, waiting for transfers between devices, shards(): arrived[d] = lax.ppermute(part[d], both, pairs)  27.6 us
    pallas_call x2, Pallas kernels, segments(): pl.pallas_call(functools.partial(kernel, places), out_shape=out, in_specs...  22.5 us
    pallas_call x1, Pallas kernels, stacks(): pl.pallas_call(functools.partial(last_kernel, places, scale, shares), out...  15.1 us
    pallas_call x1, Pallas kernels, stacks(): pl.pallas_call(functools.partial(rest_kernel, count, scale, shares), out_...  11.2 us
    ppermute x8, starting transfers between devices, shards(): arrived[d] = lax.ppermute(part[d], both, pairs)  8.78 us
    ppermute x1, waiting for transfers between devices, shards(): halo_tail = lax.ppermute(forward, both, halo_pairs)  4.34 us
    pallas_call x1, Pallas kernels, shards(): pl.pallas_call(section_sums, out_shape=[jax.ShapeDtypeStruct((NSEC, wins,...  4.1 us
    ppermute x4, starting transfers between devices, add_over(): lax.ppermute(value, axis, [(i, i ^ s) for i in range(count)])  3.73 us
  transfers between devices with their start and end apart: 20, of which 9 were waited for; matrix products, arithmetic and copies ran while one was open for 4% of the time, Pallas kernels for 33%

profile of v19, /device:TPU:19, one launch (start us, length us, event | category | flops | bytes accessed | tf_op | source)
XLA Modules:
  0.0 120.4 jit_solution(4567148326939914993)
XLA Ops:
  0.0 1.2 constant_dynamic-slice_fusion.1
  1.2 1.4 %collective-permute-start.4 = (bf16[40,8,1024]{2,1,0:T(8,128)(2,1)S(1)}, bf16[40,8,1024]{2,1,0:T(8,128)(2,1)}, u32[]{:S(2)}, u32[]{:S(2)}) collective-permute-start(bf16[40,8,1024]{2,1,0:T(8,128)(2,1)S(1)} %constant_dynamic-slice_fusion.1), channel_id=1, source_target_pairs={{0,1},{1,0},{2,3},{3,2},{4,5},{5,4},{6,7},{7,6},{8,9},{9,8},{10,11... | collective-permute-start | bytes 1966088 | tf_op jit(solution)/shard_map/ppermute | solution.py:668
  2.5 4.1 %shard_map.82 = (f32[2,8,1152]{2,1,0:T(8,128)}, bf16[64,8,1024]{2,1,0:T(8,128)(2,1)}, bf16[24,8,1024]{2,1,0:T(8,128)(2,1)}) custom-call(s32[1]{0:T(128)} %bitcast.1.odd_ref, s32[128]{0:T(128)} %dead_ref.1, s32[128]{0:T(128)} %sec_ref.1, bf16[128,8,1024]{2,1,0:T(8,128)(2,1)} %rest_1_.1), custom_call_target="tpu_custom_call" | custom-call | flops 1 | bytes 1 | tf_op jit(solution)/shard_map/pallas_call | solution.py:677
  9.7 1.3 %collective-permute-start.3 = (f32[2,8,1152]{2,1,0:T(8,128)S(1)}, f32[2,8,1152]{2,1,0:T(8,128)S(1)}, u32[]{:S(2)}, u32[]{:S(2)}) collective-permute-start(f32[2,8,1152]{2,1,0:T(8,128)S(1)} %add.35), channel_id=1, source_target_pairs={{0,24},{4,28},{8,16},{12,20},{16,8},{20,12},{24,0},{28,4},{1,25},{... | collective-permute-start | bytes 221192 | tf_op jit(solution)/shard_map/ppermute | solution.py:638
  11.2 1.2 %collective-permute-start.1 = (f32[2,8,1152]{2,1,0:T(8,128)S(1)}, f32[2,8,1152]{2,1,0:T(8,128)S(1)}, u32[]{:S(2)}, u32[]{:S(2)}) collective-permute-start(f32[2,8,1152]{2,1,0:T(8,128)S(1)} %add.35), channel_id=1, source_target_pairs={{0,8},{4,12},{8,0},{12,4},{16,24},{20,28},{24,16},{28,20},{1,9},{5... | collective-permute-start | bytes 221192 | tf_op jit(solution)/shard_map/ppermute | solution.py:638
  12.4 2.4 %multiply_reduce_fusion = f32[1024]{0:T(1024)} fusion(f32[512,1024]{1,0:T(8,128)} %constant.33.clone, f32[512]{0:T(512)S(1)} %copy-done.5), kind=kLoop, calls=%fused_computation.1 | loop fusion | flops 1047552 | bytes 2103296 | tf_op jit(solution)/shard_map/reduce_sum | solution.py:657
  14.8 1.2 collective-permute-start.11
  17.0 1.4 %collective-permute-start.5 = (f32[2,8,1152]{2,1,0:T(8,128)S(1)}, f32[2,8,1152]{2,1,0:T(8,128)S(1)}, u32[]{:S(2)}, u32[]{:S(2)}) collective-permute-start(f32[2,8,1152]{2,1,0:T(8,128)S(1)} %add_add_fusion.rest_0_), channel_id=1, source_target_pairs={{0,1},{1,0},{2,3},{3,2},{4,5},{5,4},{6,7},{7,6},{8,9},{9,8},{10,11... | collective-permute-start | bytes 221192 | tf_op jit(solution)/shard_map/ppermute | solution.py:706
  18.5 1.7 %shard_map.83.rest_3_.rest_8_.rest_7_ = bf16[256,1024]{1,0:T(8,128)(2,1)} custom-call(f32[1,1024]{1,0:T(1,128)} %bitcast.5), custom_call_target="tpu_custom_call" | custom-call | flops 1 | bytes 1 | tf_op jit(solution)/shard_map/pallas_call | solution.py:700
  20.2 1.3 %collective-permute-start.10 = (bf16[64,8,1024]{2,1,0:T(8,128)(2,1)}, bf16[64,8,1024]{2,1,0:T(8,128)(2,1)}, u32[]{:S(2)}, u32[]{:S(2)}) collective-permute-start(bf16[64,8,1024]{2,1,0:T(8,128)(2,1)} %get-tuple-element.60), channel_id=1, source_target_pairs={{0,1},{1,0},{2,3},{3,2},{4,5},{5,4},{6,7},{7,6},{8,9},{9,8},{10,11... | collective-permute-start | bytes 3145736 | tf_op jit(solution)/shard_map/ppermute | solution.py:708
  21.5 2.4 %collective-permute-start.7 = (bf16[40,8,1024]{2,1,0:T(8,128)(2,1)}, bf16[40,8,1024]{2,1,0:T(8,128)(2,1)S(1)}, u32[]{:S(2)}, u32[]{:S(2)}) collective-permute-start(bf16[40,8,1024]{2,1,0:T(8,128)(2,1)} %collective-permute-done.4.rest_2_), channel_id=1, source_target_pairs={{0,28},{1,5},{2,30},{3,7},{4,0},{5,9},{6,2},{7,11},{8,4},{9,13},{1... | collective-permute-start | bytes 1966088 | tf_op jit(solution)/shard_map/ppermute | solution.py:712
  23.9 9.1 %shard_map.84 = (bf16[128,128,128]{2,1,0:T(8,128)(2,1)}, bf16[2,1152,512]{2,1,0:T(8,128)(2,1)}) custom-call(s32[1]{0:T(128)} %bitcast.1.odd_ref, s32[2,128]{1,0:T(2,128)} %copy-done.3, f32[2,8,1152]{2,1,0:T(8,128)} %copy-done.2, bf16[128,8,1024]{2,1,0:T(8,128)(2,1)} %rest_1_.1, f32[1,1024]{1,0:T(1,128)} %constant.36.clone.rest_2_.rest_7_.rest_6_, ...), custom_call_target="tpu_custom_call" | custom-call | flops 3758096384 | bytes 16777216 | tf_op jit(solution)/shard_map/pallas_call | solution.py:403
  33.8 3.4 %collective-permute-done.7.rest_4_.rest_0_ = bf16[40,8,1024]{2,1,0:T(8,128)(2,1)S(1)} collective-permute-done((bf16[40,8,1024]{2,1,0:T(8,128)(2,1)}, bf16[40,8,1024]{2,1,0:T(8,128)(2,1)S(1)}, u32[]{:S(2)}, u32[]{:S(2)}) %collective-permute-start.7) | collective-permute-done | bytes 655392 | tf_op jit(solution)/shard_map/ppermute | solution.py:712
  37.2 4.3 %collective-permute-done.9.rest_5_.rest_1_ = bf16[24,8,1024]{2,1,0:T(8,128)(2,1)} collective-permute-done((bf16[24,8,1024]{2,1,0:T(8,128)(2,1)}, bf16[24,8,1024]{2,1,0:T(8,128)(2,1)}, u32[]{:S(2)}, u32[]{:S(2)}) %collective-permute-start.9) | collective-permute-done | bytes 393248 | tf_op jit(solution)/shard_map/ppermute | solution.py:719
  41.5 13.4 %shard_map.85 = (bf16[128,2,64,128]{3,2,1,0:T(8,128)(2,1)}, bf16[128,128,128]{2,1,0:T(8,128)(2,1)}) custom-call(s32[1]{0:T(128)} %bitcast.1.odd_ref, s32[2,192]{1,0:T(2,128)} %copy-done.4, f32[2,8,1152]{2,1,0:T(8,128)} %copy-done.2, f32[2,8,1152]{2,1,0:T(8,128)} %copy-done.1, bf16[40,8,1024]{2,1,0:T(8,128)(2,1)} %collective-permute-done.4.rest_2_, ...), custom_call_target="tpu_custom_call" | custom-call | flops 3758096384 | bytes 16777216 | tf_op jit(solution)/shard_map/pallas_call | solution.py:403
  54.9 15.1 %shard_map.86 = (bf16[32,32,128]{2,1,0:T(8,128)(2,1)}, bf16[32,32,128]{2,1,0:T(8,128)(2,1)}, bf16[32,32,128]{2,1,0:T(8,128)(2,1)}, bf16[32,32,128]{2,1,0:T(8,128)(2,1)}, bf16[128,128,128]{2,1,0:T(8,128)(2,1)}) custom-call(s32[1]{0:T(128)} %bitcast.me_ref, s32[2,192]{1,0:T(2,128)} %copy-done.4, bf16[40,8,1024]{2,1,0:T(8,128)(2,1)} %copy-done, ...), custom_call_target="tpu_custom_call" | custom-call | flops 2147483648 | bytes 20971520 | tf_op jit(solution)/shard_map/pallas_call | solution.py:593
  71.3 1.6 %collective-permute-start.14 = (bf16[32,32,128]{2,1,0:T(8,128)(2,1)}, bf16[32,32,128]{2,1,0:T(8,128)(2,1)S(1)}, u32[]{:S(2)}, u32[]{:S(2)}) collective-permute-start(bf16[32,32,128]{2,1,0:T(8,128)(2,1)} %get-tuple-element.70), channel_id=1, source_target_pairs={{0,0},{1,29},{2,2},{3,31},{4,4},{5,1},{6,6},{7,3},{8,8},{9,5},{10,... | collective-permute-start | bytes 786440 | tf_op jit(solution)/shard_map/ppermute | solution.py:759
  72.9 3.0 %collective-permute-start.15 = (bf16[32,32,128]{2,1,0:T(8,128)(2,1)}, bf16[32,32,128]{2,1,0:T(8,128)(2,1)}, u32[]{:S(2)}, u32[]{:S(2)}) collective-permute-start(bf16[32,32,128]{2,1,0:T(8,128)(2,1)} %get-tuple-element.71), channel_id=1, source_target_pairs={{0,1},{1,28},{2,3},{3,30},{4,5},{5,0},{6,7},{7,2},{8,9},{9,4},{10,... | collective-permute-start | bytes 786440 | tf_op jit(solution)/shard_map/ppermute | solution.py:759
  75.9 11.2 %shard_map.87 = (bf16[32,32,128]{2,1,0:T(8,128)(2,1)}, bf16[32,32,128]{2,1,0:T(8,128)(2,1)}, bf16[32,32,128]{2,1,0:T(8,128)(2,1)}, bf16[32,32,128]{2,1,0:T(8,128)(2,1)}) custom-call(s32[1]{0:T(128)} %bitcast.me_ref, bf16[128,256]{1,0:T(8,128)(2,1)} %constant.35.clone.rest_9_.rest_0_, bf16[128,2,64,128]{3,2,1,0:T(8,128)(2,1)} %get-tuple-element.65.rest_10_.rest_1_, ...), custom_call_target="tpu_custom_call" | custom-call | flops 2147483648 | bytes 20971520 | tf_op jit(solution)/shard_map/pallas_call | solution.py:611
  87.7 1.3 %collective-permute-start.17 = (bf16[32,32,128]{2,1,0:T(8,128)(2,1)}, bf16[32,32,128]{2,1,0:T(8,128)(2,1)S(1)}, u32[]{:S(2)}, u32[]{:S(2)}) collective-permute-start(bf16[32,32,128]{2,1,0:T(8,128)(2,1)} %get-tuple-element.74), channel_id=1, source_target_pairs={{0,3},{1,30},{2,1},{3,28},{4,7},{5,2},{6,5},{7,0},{8,11},{9,6},{10... | collective-permute-start | bytes 786440 | tf_op jit(solution)/shard_map/ppermute | solution.py:759
  89.0 18.0 %collective-permute-done.13 = bf16[32,32,128]{2,1,0:T(8,128)(2,1)S(1)} collective-permute-done((bf16[32,32,128]{2,1,0:T(8,128)(2,1)}, bf16[32,32,128]{2,1,0:T(8,128)(2,1)S(1)}, u32[]{:S(2)}, u32[]{:S(2)}) %collective-permute-start.13) | collective-permute-done | bytes 262176 | tf_op jit(solution)/shard_map/ppermute | solution.py:759
  107.0 1.6 %collective-permute-start.18 = (bf16[32,32,128]{2,1,0:T(8,128)(2,1)}, bf16[32,32,128]{2,1,0:T(8,128)(2,1)S(1)}, u32[]{:S(2)}, u32[]{:S(2)}) collective-permute-start(bf16[32,32,128]{2,1,0:T(8,128)(2,1)} %get-tuple-element.75), channel_id=1, source_target_pairs={{0,0},{1,29},{2,2},{3,31},{4,4},{5,1},{6,6},{7,3},{8,8},{9,5},{10,... | collective-permute-start | bytes 786440 | tf_op jit(solution)/shard_map/ppermute | solution.py:759
  110.2 8.6 %collective-permute-done.17 = bf16[32,32,128]{2,1,0:T(8,128)(2,1)S(1)} collective-permute-done((bf16[32,32,128]{2,1,0:T(8,128)(2,1)}, bf16[32,32,128]{2,1,0:T(8,128)(2,1)S(1)}, u32[]{:S(2)}, u32[]{:S(2)}) %collective-permute-start.17) | collective-permute-done | bytes 262176 | tf_op jit(solution)/shard_map/ppermute | solution.py:759
  118.9 1.5 %pad_maximum_fusion = f32[128,32,128]{2,1,0:T(8,128)} fusion(f32[32,32,128]{2,1,0:T(8,128)S(1)} %get-tuple-element.80, f32[32,32,128]{2,1,0:T(8,128)S(1)} %get-tuple-element.78, f32[32,32,128]{2,1,0:T(8,128)S(1)} %get-tuple-element.79, f32[32,32,128]{2,1,0:T(8,128)S(1)} %get-tuple-element.77), kind=kLoop, calls=%fused_computation | loop fusion | flops 1572864 | bytes 4194304 | tf_op jit(solution)/shard_map/concatenate | solution.py:766
  (49 shorter events, 8.7 us)
Async XLA Ops:
  0.0 12.4 %copy-start.5 = (f32[512]{0:T(512)S(1)}, f32[512]{0:T(512)}, u32[]{:S(2)}) copy-start(f32[512]{0:T(512)} %param.9) | copy-start | bytes 6148
  1.2 15.8 %collective-permute-start.4 = (bf16[40,8,1024]{2,1,0:T(8,128)(2,1)S(1)}, bf16[40,8,1024]{2,1,0:T(8,128)(2,1)}, u32[]{:S(2)}, u32[]{:S(2)}) collective-permute-start(bf16[40,8,1024]{2,1,0:T(8,128)(2,1)S(1)} %constant_dynamic-slice_fusion.1), channel_id=1, source_target_pairs={{0,1},{1,0},{2,3},{3,2},{4,5},{5,4},{6,7},{7,6},{8,9},{9,8},{10,11... | collective-permute-start | bytes 1966088 | tf_op jit(solution)/shard_map/ppermute | solution.py:668
  6.6 2.1 %collective-permute-start = (f32[2,8,1152]{2,1,0:T(8,128)}, f32[2,8,1152]{2,1,0:T(8,128)S(1)}, u32[]{:S(2)}, u32[]{:S(2)}) collective-permute-start(f32[2,8,1152]{2,1,0:T(8,128)} %get-tuple-element.41), channel_id=1, source_target_pairs={{0,4},{4,0},{8,12},{12,8},{16,20},{20,16},{24,28},{28,24},{1,5},{5... | collective-permute-start | bytes 221192 | tf_op jit(solution)/shard_map/ppermute | solution.py:638
  7.7 16.2 %copy-start.3 = (s32[2,128]{1,0:T(2,128)}, s32[2,128]{1,0:T(2,128)S(1)}, u32[]{:S(2)}) copy-start(s32[2,128]{1,0:T(2,128)S(1)} %pad_add_fusion.flag_ref) | copy-start | bytes 3076
  7.8 7.0 %collective-permute-start.6 = (s32[2,64]{1,0:T(2,128)S(1)}, s32[2,64]{1,0:T(2,128)S(1)}, u32[]{:S(2)}, u32[]{:S(2)}) collective-permute-start(s32[2,64]{1,0:T(2,128)S(1)} %constant_dynamic-slice_fusion), channel_id=1, source_target_pairs={{0,28},{1,5},{2,30},{3,7},{4,0},{5,9},{6,2},{7,11},{8,4},{9,13},{1... | collective-permute-start | bytes 1544 | tf_op jit(solution)/shard_map/ppermute | solution.py:672
  9.7 6.3 %collective-permute-start.3 = (f32[2,8,1152]{2,1,0:T(8,128)S(1)}, f32[2,8,1152]{2,1,0:T(8,128)S(1)}, u32[]{:S(2)}, u32[]{:S(2)}) collective-permute-start(f32[2,8,1152]{2,1,0:T(8,128)S(1)} %add.35), channel_id=1, source_target_pairs={{0,24},{4,28},{8,16},{12,20},{16,8},{20,12},{24,0},{28,4},{1,25},{... | collective-permute-start | bytes 221192 | tf_op jit(solution)/shard_map/ppermute | solution.py:638
  11.0 5.6 %collective-permute-start.2 = (f32[2,8,1152]{2,1,0:T(8,128)S(1)}, f32[2,8,1152]{2,1,0:T(8,128)S(1)}, u32[]{:S(2)}, u32[]{:S(2)}) collective-permute-start(f32[2,8,1152]{2,1,0:T(8,128)S(1)} %add.35), channel_id=1, source_target_pairs={{0,16},{4,20},{8,24},{12,28},{16,0},{20,4},{24,8},{28,12},{1,17},{... | collective-permute-start | bytes 221192 | tf_op jit(solution)/shard_map/ppermute | solution.py:638
  11.2 5.3 %collective-permute-start.1 = (f32[2,8,1152]{2,1,0:T(8,128)S(1)}, f32[2,8,1152]{2,1,0:T(8,128)S(1)}, u32[]{:S(2)}, u32[]{:S(2)}) collective-permute-start(f32[2,8,1152]{2,1,0:T(8,128)S(1)} %add.35), channel_id=1, source_target_pairs={{0,8},{4,12},{8,0},{12,4},{16,24},{20,28},{24,16},{28,20},{1,9},{5... | collective-permute-start | bytes 221192 | tf_op jit(solution)/shard_map/ppermute | solution.py:638
  14.8 19.0 %collective-permute-start.11 = (bf16[64,8,1024]{2,1,0:T(8,128)(2,1)}, bf16[64,8,1024]{2,1,0:T(8,128)(2,1)}, u32[]{:S(2)}, u32[]{:S(2)}) collective-permute-start(bf16[64,8,1024]{2,1,0:T(8,128)(2,1)} %get-tuple-element.60), channel_id=1, source_target_pairs={{0,28},{1,5},{2,30},{3,7},{4,0},{5,9},{6,2},{7,11},{8,4},{9,13},{1... | collective-permute-start | bytes 3145736 | tf_op jit(solution)/shard_map/ppermute | solution.py:696
  17.0 4.5 %collective-permute-start.5 = (f32[2,8,1152]{2,1,0:T(8,128)S(1)}, f32[2,8,1152]{2,1,0:T(8,128)S(1)}, u32[]{:S(2)}, u32[]{:S(2)}) collective-permute-start(f32[2,8,1152]{2,1,0:T(8,128)S(1)} %add_add_fusion.rest_0_), channel_id=1, source_target_pairs={{0,1},{1,0},{2,3},{3,2},{4,5},{5,4},{6,7},{7,6},{8,9},{9,8},{10,11... | collective-permute-start | bytes 221192 | tf_op jit(solution)/shard_map/ppermute | solution.py:706
  18.3 14.7 %collective-permute-start.8 = (bf16[24,8,1024]{2,1,0:T(8,128)(2,1)}, bf16[24,8,1024]{2,1,0:T(8,128)(2,1)}, u32[]{:S(2)}, u32[]{:S(2)}) collective-permute-start(bf16[24,8,1024]{2,1,0:T(8,128)(2,1)} %get-tuple-element.58), channel_id=1, source_target_pairs={{0,1},{1,0},{2,3},{3,2},{4,5},{5,4},{6,7},{7,6},{8,9},{9,8},{10,11... | collective-permute-start | bytes 1179656 | tf_op jit(solution)/shard_map/ppermute | solution.py:707
  20.2 34.7 %collective-permute-start.10 = (bf16[64,8,1024]{2,1,0:T(8,128)(2,1)}, bf16[64,8,1024]{2,1,0:T(8,128)(2,1)}, u32[]{:S(2)}, u32[]{:S(2)}) collective-permute-start(bf16[64,8,1024]{2,1,0:T(8,128)(2,1)} %get-tuple-element.60), channel_id=1, source_target_pairs={{0,1},{1,0},{2,3},{3,2},{4,5},{5,4},{6,7},{7,6},{8,9},{9,8},{10,11... | collective-permute-start | bytes 3145736 | tf_op jit(solution)/shard_map/ppermute | solution.py:708
  21.5 11.5 %copy-start.1 = (f32[2,8,1152]{2,1,0:T(8,128)}, f32[2,8,1152]{2,1,0:T(8,128)S(1)}, u32[]{:S(2)}) copy-start(f32[2,8,1152]{2,1,0:T(8,128)S(1)} %collective-permute-done.5.rest_1_.rest_5_) | copy-start | bytes 221188
  21.5 15.6 %collective-permute-start.7 = (bf16[40,8,1024]{2,1,0:T(8,128)(2,1)}, bf16[40,8,1024]{2,1,0:T(8,128)(2,1)S(1)}, u32[]{:S(2)}, u32[]{:S(2)}) collective-permute-start(bf16[40,8,1024]{2,1,0:T(8,128)(2,1)} %collective-permute-done.4.rest_2_), channel_id=1, source_target_pairs={{0,28},{1,5},{2,30},{3,7},{4,0},{5,9},{6,2},{7,11},{8,4},{9,13},{1... | collective-permute-start | bytes 1966088 | tf_op jit(solution)/shard_map/ppermute | solution.py:712
  33.0 8.5 %collective-permute-start.9 = (bf16[24,8,1024]{2,1,0:T(8,128)(2,1)}, bf16[24,8,1024]{2,1,0:T(8,128)(2,1)}, u32[]{:S(2)}, u32[]{:S(2)}) collective-permute-start(bf16[24,8,1024]{2,1,0:T(8,128)(2,1)} %collective-permute-done.8.rest_3_), channel_id=1, source_target_pairs={{0,28},{1,5},{2,30},{3,7},{4,0},{5,9},{6,2},{7,11},{8,4},{9,13},{1... | collective-permute-start | bytes 1179656 | tf_op jit(solution)/shard_map/ppermute | solution.py:719
  33.8 7.7 %copy-start.4 = (s32[2,192]{1,0:T(2,128)}, s32[2,192]{1,0:T(2,128)S(1)}, u32[]{:S(2)}) copy-start(s32[2,192]{1,0:T(2,128)S(1)} %constant_dynamic-update-slice_fusion.flag_ref) | copy-start | bytes 4612
  70.1 17.6 %collective-permute-start.12 = (bf16[32,32,128]{2,1,0:T(8,128)(2,1)}, bf16[32,32,128]{2,1,0:T(8,128)(2,1)S(1)}, u32[]{:S(2)}, u32[]{:S(2)}) collective-permute-start(bf16[32,32,128]{2,1,0:T(8,128)(2,1)} %get-tuple-element.68), channel_id=1, source_target_pairs={{0,2},{1,31},{2,0},{3,29},{4,6},{5,3},{6,4},{7,1},{8,10},{9,7},{10... | collective-permute-start | bytes 786440 | tf_op jit(solution)/shard_map/ppermute | solution.py:759
  70.2 36.8 %collective-permute-start.13 = (bf16[32,32,128]{2,1,0:T(8,128)(2,1)}, bf16[32,32,128]{2,1,0:T(8,128)(2,1)S(1)}, u32[]{:S(2)}, u32[]{:S(2)}) collective-permute-start(bf16[32,32,128]{2,1,0:T(8,128)(2,1)} %get-tuple-element.69), channel_id=1, source_target_pairs={{0,3},{1,30},{2,1},{3,28},{4,7},{5,2},{6,5},{7,0},{8,11},{9,6},{10... | collective-permute-start | bytes 786440 | tf_op jit(solution)/shard_map/ppermute | solution.py:759
  71.3 37.3 %collective-permute-start.14 = (bf16[32,32,128]{2,1,0:T(8,128)(2,1)}, bf16[32,32,128]{2,1,0:T(8,128)(2,1)S(1)}, u32[]{:S(2)}, u32[]{:S(2)}) collective-permute-start(bf16[32,32,128]{2,1,0:T(8,128)(2,1)} %get-tuple-element.70), channel_id=1, source_target_pairs={{0,0},{1,29},{2,2},{3,31},{4,4},{5,1},{6,6},{7,3},{8,8},{9,5},{10,... | collective-permute-start | bytes 786440 | tf_op jit(solution)/shard_map/ppermute | solution.py:759
  72.9 35.7 %collective-permute-start.15 = (bf16[32,32,128]{2,1,0:T(8,128)(2,1)}, bf16[32,32,128]{2,1,0:T(8,128)(2,1)}, u32[]{:S(2)}, u32[]{:S(2)}) collective-permute-start(bf16[32,32,128]{2,1,0:T(8,128)(2,1)} %get-tuple-element.71), channel_id=1, source_target_pairs={{0,1},{1,28},{2,3},{3,30},{4,5},{5,0},{6,7},{7,2},{8,9},{9,4},{10,... | collective-permute-start | bytes 786440 | tf_op jit(solution)/shard_map/ppermute | solution.py:759
  87.1 23.0 %collective-permute-start.16 = (bf16[32,32,128]{2,1,0:T(8,128)(2,1)}, bf16[32,32,128]{2,1,0:T(8,128)(2,1)S(1)}, u32[]{:S(2)}, u32[]{:S(2)}) collective-permute-start(bf16[32,32,128]{2,1,0:T(8,128)(2,1)} %get-tuple-element.73), channel_id=1, source_target_pairs={{0,2},{1,31},{2,0},{3,29},{4,6},{5,3},{6,4},{7,1},{8,10},{9,7},{10... | collective-permute-start | bytes 786440 | tf_op jit(solution)/shard_map/ppermute | solution.py:759
  87.7 31.1 %collective-permute-start.17 = (bf16[32,32,128]{2,1,0:T(8,128)(2,1)}, bf16[32,32,128]{2,1,0:T(8,128)(2,1)S(1)}, u32[]{:S(2)}, u32[]{:S(2)}) collective-permute-start(bf16[32,32,128]{2,1,0:T(8,128)(2,1)} %get-tuple-element.74), channel_id=1, source_target_pairs={{0,3},{1,30},{2,1},{3,28},{4,7},{5,2},{6,5},{7,0},{8,11},{9,6},{10... | collective-permute-start | bytes 786440 | tf_op jit(solution)/shard_map/ppermute | solution.py:759
  107.0 11.8 %collective-permute-start.18 = (bf16[32,32,128]{2,1,0:T(8,128)(2,1)}, bf16[32,32,128]{2,1,0:T(8,128)(2,1)S(1)}, u32[]{:S(2)}, u32[]{:S(2)}) collective-permute-start(bf16[32,32,128]{2,1,0:T(8,128)(2,1)} %get-tuple-element.75), channel_id=1, source_target_pairs={{0,0},{1,29},{2,2},{3,31},{4,4},{5,1},{6,6},{7,3},{8,8},{9,5},{10,... | collective-permute-start | bytes 786440 | tf_op jit(solution)/shard_map/ppermute | solution.py:759
  108.6 10.2 %collective-permute-start.19 = (bf16[32,32,128]{2,1,0:T(8,128)(2,1)}, bf16[32,32,128]{2,1,0:T(8,128)(2,1)S(1)}, u32[]{:S(2)}, u32[]{:S(2)}) collective-permute-start(bf16[32,32,128]{2,1,0:T(8,128)(2,1)} %get-tuple-element.76), channel_id=1, source_target_pairs={{0,1},{1,28},{2,3},{3,30},{4,5},{5,0},{6,7},{7,2},{8,9},{9,4},{10,... | collective-permute-start | bytes 786440 | tf_op jit(solution)/shard_map/ppermute | solution.py:759
  (4 other events, 26.6 us)

commit v20 on v19

--- a/solution.py
+++ b/solution.py
@@ -36,7 +36,7 @@
     segment = np.stack([np.cos(turn), -np.sin(turn)], axis=1).reshape(size, size)
     lag = np.stack([np.cos(turn), -np.sin(turn)], axis=1).reshape(size, size)[:, :LAGS].T
     cast = lambda a: a.astype(np.float32).astype(ml_dtypes.bfloat16)
-    return window.astype(np.float32), waves.astype(np.float32), cast(segment), cast(lag)
+    return window.astype(np.float32), cast(waves), cast(segment), cast(lag)
 
 
 def section_sums(odd_ref, dead_ref, sec_ref, x_hbm, out_ref, half_hbm, tail_hbm, x, in_sem, sem):
@@ -654,7 +654,7 @@
     window, waves, seg, lag = tables(ns, nf)
     waves, seg, lag = jnp.asarray(waves), jnp.asarray(seg), jnp.asarray(lag)
     hann = jnp.asarray(window[None, :])
-    response = jnp.sum(band_gain[:, None] * waves, axis=0, keepdims=True)
+    response = jnp.sum(band_gain[:, None] * waves.astype(F32), axis=0, keepdims=True)
     swap = [(z, z ^ 1) for z in range(groups)]
     both = ("fibre", "tm")
     halo_pairs = [

time: 122 us -> 122 us (level)
  no operation moved by 1% of the time
where the time goes in v20:
time: 122 us; the launch traced here: 120 us
  Pallas kernels  54.6 us (45%)
  waiting for transfers between devices  37.2 us (30%)
  starting transfers between devices  20.4 us (17%)
  other arithmetic  6.12 us (5%)
  local copies, waits for them, and re-layouts  1.93 us (2%)
    ppermute x8, waiting for transfers between devices, shards(): arrived[d] = lax.ppermute(part[d], both, pairs)  27.6 us
    pallas_call x2, Pallas kernels, segments(): pl.pallas_call(functools.partial(kernel, places), out_shape=out, in_specs...  22.5 us
    pallas_call x1, Pallas kernels, stacks(): pl.pallas_call(functools.partial(last_kernel, places, scale, shares), out...  15.1 us
    pallas_call x1, Pallas kernels, stacks(): pl.pallas_call(functools.partial(rest_kernel, count, scale, shares), out_...  11.2 us
    ppermute x8, starting transfers between devices, shards(): arrived[d] = lax.ppermute(part[d], both, pairs)  8.78 us
    ppermute x1, waiting for transfers between devices, shards(): halo_tail = lax.ppermute(forward, both, halo_pairs)  4.34 us
    pallas_call x1, Pallas kernels, shards(): pl.pallas_call(section_sums, out_shape=[jax.ShapeDtypeStruct((NSEC, wins,...  4.1 us
    ppermute x4, starting transfers between devices, add_over(): lax.ppermute(value, axis, [(i, i ^ s) for i in range(count)])  3.73 us
  transfers between devices with their start and end apart: 20, of which 9 were waited for; matrix products, arithmetic and copies ran while one was open for 4% of the time, Pallas kernels for 33%

profile of v20, /device:TPU:19, one launch (start us, length us, event | category | flops | bytes accessed | tf_op | source)
XLA Modules:
  0.0 120.4 jit_solution(18148512781938685834)
XLA Ops:
  0.0 1.2 constant_dynamic-slice_fusion.1
  1.2 1.4 %collective-permute-start.4 = (bf16[40,8,1024]{2,1,0:T(8,128)(2,1)S(1)}, bf16[40,8,1024]{2,1,0:T(8,128)(2,1)}, u32[]{:S(2)}, u32[]{:S(2)}) collective-permute-start(bf16[40,8,1024]{2,1,0:T(8,128)(2,1)S(1)} %constant_dynamic-slice_fusion.1), channel_id=1, source_target_pairs={{0,1},{1,0},{2,3},{3,2},{4,5},{5,4},{6,7},{7,6},{8,9},{9,8},{10,11... | collective-permute-start | bytes 1966088 | tf_op jit(solution)/shard_map/ppermute | solution.py:668
  2.5 4.1 %shard_map.82 = (f32[2,8,1152]{2,1,0:T(8,128)}, bf16[64,8,1024]{2,1,0:T(8,128)(2,1)}, bf16[24,8,1024]{2,1,0:T(8,128)(2,1)}) custom-call(s32[1]{0:T(128)} %bitcast.1.odd_ref, s32[128]{0:T(128)} %dead_ref.1, s32[128]{0:T(128)} %sec_ref.1, bf16[128,8,1024]{2,1,0:T(8,128)(2,1)} %rest_1_.1), custom_call_target="tpu_custom_call" | custom-call | flops 1 | bytes 1 | tf_op jit(solution)/shard_map/pallas_call | solution.py:677
  9.7 1.3 %collective-permute-start.3 = (f32[2,8,1152]{2,1,0:T(8,128)S(1)}, f32[2,8,1152]{2,1,0:T(8,128)S(1)}, u32[]{:S(2)}, u32[]{:S(2)}) collective-permute-start(f32[2,8,1152]{2,1,0:T(8,128)S(1)} %add.35), channel_id=1, source_target_pairs={{0,24},{4,28},{8,16},{12,20},{16,8},{20,12},{24,0},{28,4},{1,25},{... | collective-permute-start | bytes 221192 | tf_op jit(solution)/shard_map/ppermute | solution.py:638
  11.2 1.2 %collective-permute-start.1 = (f32[2,8,1152]{2,1,0:T(8,128)S(1)}, f32[2,8,1152]{2,1,0:T(8,128)S(1)}, u32[]{:S(2)}, u32[]{:S(2)}) collective-permute-start(f32[2,8,1152]{2,1,0:T(8,128)S(1)} %add.35), channel_id=1, source_target_pairs={{0,8},{4,12},{8,0},{12,4},{16,24},{20,28},{24,16},{28,20},{1,9},{5... | collective-permute-start | bytes 221192 | tf_op jit(solution)/shard_map/ppermute | solution.py:638
  12.4 2.4 %multiply_reduce_fusion = f32[1024]{0:T(1024)} fusion(f32[512,1024]{1,0:T(8,128)} %constant.37, f32[512]{0:T(512)S(1)} %copy-done.5), kind=kLoop, calls=%fused_computation.1 | loop fusion | flops 1047552 | bytes 2103296 | tf_op jit(solution)/shard_map/reduce_sum | solution.py:657
  14.8 1.2 collective-permute-start.11
  17.0 1.4 %collective-permute-start.5 = (f32[2,8,1152]{2,1,0:T(8,128)S(1)}, f32[2,8,1152]{2,1,0:T(8,128)S(1)}, u32[]{:S(2)}, u32[]{:S(2)}) collective-permute-start(f32[2,8,1152]{2,1,0:T(8,128)S(1)} %add_add_fusion.rest_0_), channel_id=1, source_target_pairs={{0,1},{1,0},{2,3},{3,2},{4,5},{5,4},{6,7},{7,6},{8,9},{9,8},{10,11... | collective-permute-start | bytes 221192 | tf_op jit(solution)/shard_map/ppermute | solution.py:706
  18.5 1.7 %shard_map.83.rest_3_.rest_8_.rest_7_ = bf16[256,1024]{1,0:T(8,128)(2,1)} custom-call(f32[1,1024]{1,0:T(1,128)} %bitcast.5), custom_call_target="tpu_custom_call" | custom-call | flops 1 | bytes 1 | tf_op jit(solution)/shard_map/pallas_call | solution.py:700
  20.2 1.3 %collective-permute-start.10 = (bf16[64,8,1024]{2,1,0:T(8,128)(2,1)}, bf16[64,8,1024]{2,1,0:T(8,128)(2,1)}, u32[]{:S(2)}, u32[]{:S(2)}) collective-permute-start(bf16[64,8,1024]{2,1,0:T(8,128)(2,1)} %get-tuple-element.60), channel_id=1, source_target_pairs={{0,1},{1,0},{2,3},{3,2},{4,5},{5,4},{6,7},{7,6},{8,9},{9,8},{10,11... | collective-permute-start | bytes 3145736 | tf_op jit(solution)/shard_map/ppermute | solution.py:708
  21.5 2.4 %collective-permute-start.7 = (bf16[40,8,1024]{2,1,0:T(8,128)(2,1)}, bf16[40,8,1024]{2,1,0:T(8,128)(2,1)S(1)}, u32[]{:S(2)}, u32[]{:S(2)}) collective-permute-start(bf16[40,8,1024]{2,1,0:T(8,128)(2,1)} %collective-permute-done.4.rest_2_), channel_id=1, source_target_pairs={{0,28},{1,5},{2,30},{3,7},{4,0},{5,9},{6,2},{7,11},{8,4},{9,13},{1... | collective-permute-start | bytes 1966088 | tf_op jit(solution)/shard_map/ppermute | solution.py:712
  23.9 9.1 %shard_map.84 = (bf16[128,128,128]{2,1,0:T(8,128)(2,1)}, bf16[2,1152,512]{2,1,0:T(8,128)(2,1)}) custom-call(s32[1]{0:T(128)} %bitcast.1.odd_ref, s32[2,128]{1,0:T(2,128)} %copy-done.3, f32[2,8,1152]{2,1,0:T(8,128)} %copy-done.2, bf16[128,8,1024]{2,1,0:T(8,128)(2,1)} %rest_1_.1, f32[1,1024]{1,0:T(1,128)} %constant.36.clone.rest_2_.rest_7_.rest_6_, ...), custom_call_target="tpu_custom_call" | custom-call | flops 3758096384 | bytes 16777216 | tf_op jit(solution)/shard_map/pallas_call | solution.py:403
  33.8 3.4 %collective-permute-done.7.rest_4_.rest_0_ = bf16[40,8,1024]{2,1,0:T(8,128)(2,1)S(1)} collective-permute-done((bf16[40,8,1024]{2,1,0:T(8,128)(2,1)}, bf16[40,8,1024]{2,1,0:T(8,128)(2,1)S(1)}, u32[]{:S(2)}, u32[]{:S(2)}) %collective-permute-start.7) | collective-permute-done | bytes 655392 | tf_op jit(solution)/shard_map/ppermute | solution.py:712
  37.2 4.3 %collective-permute-done.9.rest_5_.rest_1_ = bf16[24,8,1024]{2,1,0:T(8,128)(2,1)} collective-permute-done((bf16[24,8,1024]{2,1,0:T(8,128)(2,1)}, bf16[24,8,1024]{2,1,0:T(8,128)(2,1)}, u32[]{:S(2)}, u32[]{:S(2)}) %collective-permute-start.9) | collective-permute-done | bytes 393248 | tf_op jit(solution)/shard_map/ppermute | solution.py:719
  41.5 13.4 %shard_map.85 = (bf16[128,2,64,128]{3,2,1,0:T(8,128)(2,1)}, bf16[128,128,128]{2,1,0:T(8,128)(2,1)}) custom-call(s32[1]{0:T(128)} %bitcast.1.odd_ref, s32[2,192]{1,0:T(2,128)} %copy-done.4, f32[2,8,1152]{2,1,0:T(8,128)} %copy-done.2, f32[2,8,1152]{2,1,0:T(8,128)} %copy-done.1, bf16[40,8,1024]{2,1,0:T(8,128)(2,1)} %collective-permute-done.4.rest_2_, ...), custom_call_target="tpu_custom_call" | custom-call | flops 3758096384 | bytes 16777216 | tf_op jit(solution)/shard_map/pallas_call | solution.py:403
  54.9 15.1 %shard_map.86 = (bf16[32,32,128]{2,1,0:T(8,128)(2,1)}, bf16[32,32,128]{2,1,0:T(8,128)(2,1)}, bf16[32,32,128]{2,1,0:T(8,128)(2,1)}, bf16[32,32,128]{2,1,0:T(8,128)(2,1)}, bf16[128,128,128]{2,1,0:T(8,128)(2,1)}) custom-call(s32[1]{0:T(128)} %bitcast.me_ref, s32[2,192]{1,0:T(2,128)} %copy-done.4, bf16[40,8,1024]{2,1,0:T(8,128)(2,1)} %copy-done, ...), custom_call_target="tpu_custom_call" | custom-call | flops 2147483648 | bytes 20971520 | tf_op jit(solution)/shard_map/pallas_call | solution.py:593
  71.3 1.6 %collective-permute-start.14 = (bf16[32,32,128]{2,1,0:T(8,128)(2,1)}, bf16[32,32,128]{2,1,0:T(8,128)(2,1)S(1)}, u32[]{:S(2)}, u32[]{:S(2)}) collective-permute-start(bf16[32,32,128]{2,1,0:T(8,128)(2,1)} %get-tuple-element.70), channel_id=1, source_target_pairs={{0,0},{1,29},{2,2},{3,31},{4,4},{5,1},{6,6},{7,3},{8,8},{9,5},{10,... | collective-permute-start | bytes 786440 | tf_op jit(solution)/shard_map/ppermute | solution.py:759
  72.9 3.0 %collective-permute-start.15 = (bf16[32,32,128]{2,1,0:T(8,128)(2,1)}, bf16[32,32,128]{2,1,0:T(8,128)(2,1)}, u32[]{:S(2)}, u32[]{:S(2)}) collective-permute-start(bf16[32,32,128]{2,1,0:T(8,128)(2,1)} %get-tuple-element.71), channel_id=1, source_target_pairs={{0,1},{1,28},{2,3},{3,30},{4,5},{5,0},{6,7},{7,2},{8,9},{9,4},{10,... | collective-permute-start | bytes 786440 | tf_op jit(solution)/shard_map/ppermute | solution.py:759
  75.9 11.2 %shard_map.87 = (bf16[32,32,128]{2,1,0:T(8,128)(2,1)}, bf16[32,32,128]{2,1,0:T(8,128)(2,1)}, bf16[32,32,128]{2,1,0:T(8,128)(2,1)}, bf16[32,32,128]{2,1,0:T(8,128)(2,1)}) custom-call(s32[1]{0:T(128)} %bitcast.me_ref, bf16[128,256]{1,0:T(8,128)(2,1)} %constant.35.clone.rest_9_.rest_0_, bf16[128,2,64,128]{3,2,1,0:T(8,128)(2,1)} %get-tuple-element.65.rest_10_.rest_1_, ...), custom_call_target="tpu_custom_call" | custom-call | flops 2147483648 | bytes 20971520 | tf_op jit(solution)/shard_map/pallas_call | solution.py:611
  87.7 1.3 %collective-permute-start.17 = (bf16[32,32,128]{2,1,0:T(8,128)(2,1)}, bf16[32,32,128]{2,1,0:T(8,128)(2,1)S(1)}, u32[]{:S(2)}, u32[]{:S(2)}) collective-permute-start(bf16[32,32,128]{2,1,0:T(8,128)(2,1)} %get-tuple-element.74), channel_id=1, source_target_pairs={{0,3},{1,30},{2,1},{3,28},{4,7},{5,2},{6,5},{7,0},{8,11},{9,6},{10... | collective-permute-start | bytes 786440 | tf_op jit(solution)/shard_map/ppermute | solution.py:759
  89.0 18.0 %collective-permute-done.13 = bf16[32,32,128]{2,1,0:T(8,128)(2,1)S(1)} collective-permute-done((bf16[32,32,128]{2,1,0:T(8,128)(2,1)}, bf16[32,32,128]{2,1,0:T(8,128)(2,1)S(1)}, u32[]{:S(2)}, u32[]{:S(2)}) %collective-permute-start.13) | collective-permute-done | bytes 262176 | tf_op jit(solution)/shard_map/ppermute | solution.py:759
  107.0 1.6 %collective-permute-start.18 = (bf16[32,32,128]{2,1,0:T(8,128)(2,1)}, bf16[32,32,128]{2,1,0:T(8,128)(2,1)S(1)}, u32[]{:S(2)}, u32[]{:S(2)}) collective-permute-start(bf16[32,32,128]{2,1,0:T(8,128)(2,1)} %get-tuple-element.75), channel_id=1, source_target_pairs={{0,0},{1,29},{2,2},{3,31},{4,4},{5,1},{6,6},{7,3},{8,8},{9,5},{10,... | collective-permute-start | bytes 786440 | tf_op jit(solution)/shard_map/ppermute | solution.py:759
  110.2 8.6 %collective-permute-done.17 = bf16[32,32,128]{2,1,0:T(8,128)(2,1)S(1)} collective-permute-done((bf16[32,32,128]{2,1,0:T(8,128)(2,1)}, bf16[32,32,128]{2,1,0:T(8,128)(2,1)S(1)}, u32[]{:S(2)}, u32[]{:S(2)}) %collective-permute-start.17) | collective-permute-done | bytes 262176 | tf_op jit(solution)/shard_map/ppermute | solution.py:759
  118.9 1.5 %pad_maximum_fusion = f32[128,32,128]{2,1,0:T(8,128)} fusion(f32[32,32,128]{2,1,0:T(8,128)S(1)} %get-tuple-element.80, f32[32,32,128]{2,1,0:T(8,128)S(1)} %get-tuple-element.78, f32[32,32,128]{2,1,0:T(8,128)S(1)} %get-tuple-element.79, f32[32,32,128]{2,1,0:T(8,128)S(1)} %get-tuple-element.77), kind=kLoop, calls=%fused_computation | loop fusion | flops 1572864 | bytes 4194304 | tf_op jit(solution)/shard_map/concatenate | solution.py:766
  (49 shorter events, 8.7 us)
Async XLA Ops:
  0.0 12.4 %copy-start.5 = (f32[512]{0:T(512)S(1)}, f32[512]{0:T(512)}, u32[]{:S(2)}) copy-start(f32[512]{0:T(512)} %param.9) | copy-start | bytes 6148
  1.2 15.8 %collective-permute-start.4 = (bf16[40,8,1024]{2,1,0:T(8,128)(2,1)S(1)}, bf16[40,8,1024]{2,1,0:T(8,128)(2,1)}, u32[]{:S(2)}, u32[]{:S(2)}) collective-permute-start(bf16[40,8,1024]{2,1,0:T(8,128)(2,1)S(1)} %constant_dynamic-slice_fusion.1), channel_id=1, source_target_pairs={{0,1},{1,0},{2,3},{3,2},{4,5},{5,4},{6,7},{7,6},{8,9},{9,8},{10,11... | collective-permute-start | bytes 1966088 | tf_op jit(solution)/shard_map/ppermute | solution.py:668
  6.6 2.1 %collective-permute-start = (f32[2,8,1152]{2,1,0:T(8,128)}, f32[2,8,1152]{2,1,0:T(8,128)S(1)}, u32[]{:S(2)}, u32[]{:S(2)}) collective-permute-start(f32[2,8,1152]{2,1,0:T(8,128)} %get-tuple-element.41), channel_id=1, source_target_pairs={{0,4},{4,0},{8,12},{12,8},{16,20},{20,16},{24,28},{28,24},{1,5},{5... | collective-permute-start | bytes 221192 | tf_op jit(solution)/shard_map/ppermute | solution.py:638
  7.7 16.2 %copy-start.3 = (s32[2,128]{1,0:T(2,128)}, s32[2,128]{1,0:T(2,128)S(1)}, u32[]{:S(2)}) copy-start(s32[2,128]{1,0:T(2,128)S(1)} %pad_add_fusion.flag_ref) | copy-start | bytes 3076
  7.8 7.0 %collective-permute-start.6 = (s32[2,64]{1,0:T(2,128)S(1)}, s32[2,64]{1,0:T(2,128)S(1)}, u32[]{:S(2)}, u32[]{:S(2)}) collective-permute-start(s32[2,64]{1,0:T(2,128)S(1)} %constant_dynamic-slice_fusion), channel_id=1, source_target_pairs={{0,28},{1,5},{2,30},{3,7},{4,0},{5,9},{6,2},{7,11},{8,4},{9,13},{1... | collective-permute-start | bytes 1544 | tf_op jit(solution)/shard_map/ppermute | solution.py:672
  9.7 6.3 %collective-permute-start.3 = (f32[2,8,1152]{2,1,0:T(8,128)S(1)}, f32[2,8,1152]{2,1,0:T(8,128)S(1)}, u32[]{:S(2)}, u32[]{:S(2)}) collective-permute-start(f32[2,8,1152]{2,1,0:T(8,128)S(1)} %add.35), channel_id=1, source_target_pairs={{0,24},{4,28},{8,16},{12,20},{16,8},{20,12},{24,0},{28,4},{1,25},{... | collective-permute-start | bytes 221192 | tf_op jit(solution)/shard_map/ppermute | solution.py:638
  11.0 5.6 %collective-permute-start.2 = (f32[2,8,1152]{2,1,0:T(8,128)S(1)}, f32[2,8,1152]{2,1,0:T(8,128)S(1)}, u32[]{:S(2)}, u32[]{:S(2)}) collective-permute-start(f32[2,8,1152]{2,1,0:T(8,128)S(1)} %add.35), channel_id=1, source_target_pairs={{0,16},{4,20},{8,24},{12,28},{16,0},{20,4},{24,8},{28,12},{1,17},{... | collective-permute-start | bytes 221192 | tf_op jit(solution)/shard_map/ppermute | solution.py:638
  11.2 5.3 %collective-permute-start.1 = (f32[2,8,1152]{2,1,0:T(8,128)S(1)}, f32[2,8,1152]{2,1,0:T(8,128)S(1)}, u32[]{:S(2)}, u32[]{:S(2)}) collective-permute-start(f32[2,8,1152]{2,1,0:T(8,128)S(1)} %add.35), channel_id=1, source_target_pairs={{0,8},{4,12},{8,0},{12,4},{16,24},{20,28},{24,16},{28,20},{1,9},{5... | collective-permute-start | bytes 221192 | tf_op jit(solution)/shard_map/ppermute | solution.py:638
  14.8 19.0 %collective-permute-start.11 = (bf16[64,8,1024]{2,1,0:T(8,128)(2,1)}, bf16[64,8,1024]{2,1,0:T(8,128)(2,1)}, u32[]{:S(2)}, u32[]{:S(2)}) collective-permute-start(bf16[64,8,1024]{2,1,0:T(8,128)(2,1)} %get-tuple-element.60), channel_id=1, source_target_pairs={{0,28},{1,5},{2,30},{3,7},{4,0},{5,9},{6,2},{7,11},{8,4},{9,13},{1... | collective-permute-start | bytes 3145736 | tf_op jit(solution)/shard_map/ppermute | solution.py:696
  17.0 4.5 %collective-permute-start.5 = (f32[2,8,1152]{2,1,0:T(8,128)S(1)}, f32[2,8,1152]{2,1,0:T(8,128)S(1)}, u32[]{:S(2)}, u32[]{:S(2)}) collective-permute-start(f32[2,8,1152]{2,1,0:T(8,128)S(1)} %add_add_fusion.rest_0_), channel_id=1, source_target_pairs={{0,1},{1,0},{2,3},{3,2},{4,5},{5,4},{6,7},{7,6},{8,9},{9,8},{10,11... | collective-permute-start | bytes 221192 | tf_op jit(solution)/shard_map/ppermute | solution.py:706
  18.3 14.7 %collective-permute-start.8 = (bf16[24,8,1024]{2,1,0:T(8,128)(2,1)}, bf16[24,8,1024]{2,1,0:T(8,128)(2,1)}, u32[]{:S(2)}, u32[]{:S(2)}) collective-permute-start(bf16[24,8,1024]{2,1,0:T(8,128)(2,1)} %get-tuple-element.58), channel_id=1, source_target_pairs={{0,1},{1,0},{2,3},{3,2},{4,5},{5,4},{6,7},{7,6},{8,9},{9,8},{10,11... | collective-permute-start | bytes 1179656 | tf_op jit(solution)/shard_map/ppermute | solution.py:707
  20.2 34.7 %collective-permute-start.10 = (bf16[64,8,1024]{2,1,0:T(8,128)(2,1)}, bf16[64,8,1024]{2,1,0:T(8,128)(2,1)}, u32[]{:S(2)}, u32[]{:S(2)}) collective-permute-start(bf16[64,8,1024]{2,1,0:T(8,128)(2,1)} %get-tuple-element.60), channel_id=1, source_target_pairs={{0,1},{1,0},{2,3},{3,2},{4,5},{5,4},{6,7},{7,6},{8,9},{9,8},{10,11... | collective-permute-start | bytes 3145736 | tf_op jit(solution)/shard_map/ppermute | solution.py:708
  21.5 11.5 %copy-start.1 = (f32[2,8,1152]{2,1,0:T(8,128)}, f32[2,8,1152]{2,1,0:T(8,128)S(1)}, u32[]{:S(2)}) copy-start(f32[2,8,1152]{2,1,0:T(8,128)S(1)} %collective-permute-done.5.rest_1_.rest_5_) | copy-start | bytes 221188
  21.5 15.6 %collective-permute-start.7 = (bf16[40,8,1024]{2,1,0:T(8,128)(2,1)}, bf16[40,8,1024]{2,1,0:T(8,128)(2,1)S(1)}, u32[]{:S(2)}, u32[]{:S(2)}) collective-permute-start(bf16[40,8,1024]{2,1,0:T(8,128)(2,1)} %collective-permute-done.4.rest_2_), channel_id=1, source_target_pairs={{0,28},{1,5},{2,30},{3,7},{4,0},{5,9},{6,2},{7,11},{8,4},{9,13},{1... | collective-permute-start | bytes 1966088 | tf_op jit(solution)/shard_map/ppermute | solution.py:712
  33.0 8.5 %collective-permute-start.9 = (bf16[24,8,1024]{2,1,0:T(8,128)(2,1)}, bf16[24,8,1024]{2,1,0:T(8,128)(2,1)}, u32[]{:S(2)}, u32[]{:S(2)}) collective-permute-start(bf16[24,8,1024]{2,1,0:T(8,128)(2,1)} %collective-permute-done.8.rest_3_), channel_id=1, source_target_pairs={{0,28},{1,5},{2,30},{3,7},{4,0},{5,9},{6,2},{7,11},{8,4},{9,13},{1... | collective-permute-start | bytes 1179656 | tf_op jit(solution)/shard_map/ppermute | solution.py:719
  33.8 7.7 %copy-start.4 = (s32[2,192]{1,0:T(2,128)}, s32[2,192]{1,0:T(2,128)S(1)}, u32[]{:S(2)}) copy-start(s32[2,192]{1,0:T(2,128)S(1)} %constant_dynamic-update-slice_fusion.flag_ref) | copy-start | bytes 4612
  70.1 17.6 %collective-permute-start.12 = (bf16[32,32,128]{2,1,0:T(8,128)(2,1)}, bf16[32,32,128]{2,1,0:T(8,128)(2,1)S(1)}, u32[]{:S(2)}, u32[]{:S(2)}) collective-permute-start(bf16[32,32,128]{2,1,0:T(8,128)(2,1)} %get-tuple-element.68), channel_id=1, source_target_pairs={{0,2},{1,31},{2,0},{3,29},{4,6},{5,3},{6,4},{7,1},{8,10},{9,7},{10... | collective-permute-start | bytes 786440 | tf_op jit(solution)/shard_map/ppermute | solution.py:759
  70.2 36.8 %collective-permute-start.13 = (bf16[32,32,128]{2,1,0:T(8,128)(2,1)}, bf16[32,32,128]{2,1,0:T(8,128)(2,1)S(1)}, u32[]{:S(2)}, u32[]{:S(2)}) collective-permute-start(bf16[32,32,128]{2,1,0:T(8,128)(2,1)} %get-tuple-element.69), channel_id=1, source_target_pairs={{0,3},{1,30},{2,1},{3,28},{4,7},{5,2},{6,5},{7,0},{8,11},{9,6},{10... | collective-permute-start | bytes 786440 | tf_op jit(solution)/shard_map/ppermute | solution.py:759
  71.3 37.3 %collective-permute-start.14 = (bf16[32,32,128]{2,1,0:T(8,128)(2,1)}, bf16[32,32,128]{2,1,0:T(8,128)(2,1)S(1)}, u32[]{:S(2)}, u32[]{:S(2)}) collective-permute-start(bf16[32,32,128]{2,1,0:T(8,128)(2,1)} %get-tuple-element.70), channel_id=1, source_target_pairs={{0,0},{1,29},{2,2},{3,31},{4,4},{5,1},{6,6},{7,3},{8,8},{9,5},{10,... | collective-permute-start | bytes 786440 | tf_op jit(solution)/shard_map/ppermute | solution.py:759
  72.9 35.7 %collective-permute-start.15 = (bf16[32,32,128]{2,1,0:T(8,128)(2,1)}, bf16[32,32,128]{2,1,0:T(8,128)(2,1)}, u32[]{:S(2)}, u32[]{:S(2)}) collective-permute-start(bf16[32,32,128]{2,1,0:T(8,128)(2,1)} %get-tuple-element.71), channel_id=1, source_target_pairs={{0,1},{1,28},{2,3},{3,30},{4,5},{5,0},{6,7},{7,2},{8,9},{9,4},{10,... | collective-permute-start | bytes 786440 | tf_op jit(solution)/shard_map/ppermute | solution.py:759
  87.1 23.0 %collective-permute-start.16 = (bf16[32,32,128]{2,1,0:T(8,128)(2,1)}, bf16[32,32,128]{2,1,0:T(8,128)(2,1)S(1)}, u32[]{:S(2)}, u32[]{:S(2)}) collective-permute-start(bf16[32,32,128]{2,1,0:T(8,128)(2,1)} %get-tuple-element.73), channel_id=1, source_target_pairs={{0,2},{1,31},{2,0},{3,29},{4,6},{5,3},{6,4},{7,1},{8,10},{9,7},{10... | collective-permute-start | bytes 786440 | tf_op jit(solution)/shard_map/ppermute | solution.py:759
  87.7 31.1 %collective-permute-start.17 = (bf16[32,32,128]{2,1,0:T(8,128)(2,1)}, bf16[32,32,128]{2,1,0:T(8,128)(2,1)S(1)}, u32[]{:S(2)}, u32[]{:S(2)}) collective-permute-start(bf16[32,32,128]{2,1,0:T(8,128)(2,1)} %get-tuple-element.74), channel_id=1, source_target_pairs={{0,3},{1,30},{2,1},{3,28},{4,7},{5,2},{6,5},{7,0},{8,11},{9,6},{10... | collective-permute-start | bytes 786440 | tf_op jit(solution)/shard_map/ppermute | solution.py:759
  107.0 11.8 %collective-permute-start.18 = (bf16[32,32,128]{2,1,0:T(8,128)(2,1)}, bf16[32,32,128]{2,1,0:T(8,128)(2,1)S(1)}, u32[]{:S(2)}, u32[]{:S(2)}) collective-permute-start(bf16[32,32,128]{2,1,0:T(8,128)(2,1)} %get-tuple-element.75), channel_id=1, source_target_pairs={{0,0},{1,29},{2,2},{3,31},{4,4},{5,1},{6,6},{7,3},{8,8},{9,5},{10,... | collective-permute-start | bytes 786440 | tf_op jit(solution)/shard_map/ppermute | solution.py:759
  108.6 10.2 %collective-permute-start.19 = (bf16[32,32,128]{2,1,0:T(8,128)(2,1)}, bf16[32,32,128]{2,1,0:T(8,128)(2,1)S(1)}, u32[]{:S(2)}, u32[]{:S(2)}) collective-permute-start(bf16[32,32,128]{2,1,0:T(8,128)(2,1)} %get-tuple-element.76), channel_id=1, source_target_pairs={{0,1},{1,28},{2,3},{3,30},{4,5},{5,0},{6,7},{7,2},{8,9},{9,4},{10,... | collective-permute-start | bytes 786440 | tf_op jit(solution)/shard_map/ppermute | solution.py:759
  (4 other events, 26.6 us)

commit v21 on v19

--- a/solution.py
+++ b/solution.py
@@ -358,7 +358,7 @@
     for n in range(STEPS):
         part = pl.ds(n * step, step)
 
-        repeat(n * step, (n + 1) * step, lambda k: both_factors(k, b_out), 16)
+        repeat(n * step, (n + 1) * step, lambda k: both_factors(k, b_out), 32)
         for m, (source, target) in enumerate(((a_out, a_hbm), (b_out, b_hbm))):
             copies.append(
                 pltpu.make_async_copy(source.at[part], target.at[part], out_sem.at[2 * n + m])

time: 122 us -> 122 us (level)
  no operation moved by 1% of the time
where the time goes in v21:
time: 122 us; the launch traced here: 120 us
  Pallas kernels  54.5 us (45%)
  waiting for transfers between devices  37.2 us (30%)
  starting transfers between devices  20.4 us (17%)
  other arithmetic  6.12 us (5%)
  local copies, waits for them, and re-layouts  1.93 us (2%)
    ppermute x8, waiting for transfers between devices, shards(): arrived[d] = lax.ppermute(part[d], both, pairs)  27.5 us
    pallas_call x2, Pallas kernels, segments(): pl.pallas_call(functools.partial(kernel, places), out_shape=out, in_specs...  22.4 us
    pallas_call x1, Pallas kernels, stacks(): pl.pallas_call(functools.partial(last_kernel, places, scale, shares), out...  15.2 us
    pallas_call x1, Pallas kernels, stacks(): pl.pallas_call(functools.partial(rest_kernel, count, scale, shares), out_...  11.2 us
    ppermute x8, starting transfers between devices, shards(): arrived[d] = lax.ppermute(part[d], both, pairs)  8.79 us
    ppermute x1, waiting for transfers between devices, shards(): halo_tail = lax.ppermute(forward, both, halo_pairs)  4.34 us
    pallas_call x1, Pallas kernels, shards(): pl.pallas_call(section_sums, out_shape=[jax.ShapeDtypeStruct((NSEC, wins,...  4.1 us
    ppermute x4, starting transfers between devices, add_over(): lax.ppermute(value, axis, [(i, i ^ s) for i in range(count)])  3.73 us
  transfers between devices with their start and end apart: 20, of which 9 were waited for; matrix products, arithmetic and copies ran while one was open for 4% of the time, Pallas kernels for 33%

profile of v21, /device:TPU:19, one launch (start us, length us, event | category | flops | bytes accessed | tf_op | source)
XLA Modules:
  0.0 120.3 jit_solution(989192348752851185)
XLA Ops:
  0.0 1.2 constant_dynamic-slice_fusion.1
  1.2 1.4 %collective-permute-start.4 = (bf16[40,8,1024]{2,1,0:T(8,128)(2,1)S(1)}, bf16[40,8,1024]{2,1,0:T(8,128)(2,1)}, u32[]{:S(2)}, u32[]{:S(2)}) collective-permute-start(bf16[40,8,1024]{2,1,0:T(8,128)(2,1)S(1)} %constant_dynamic-slice_fusion.1), channel_id=1, source_target_pairs={{0,1},{1,0},{2,3},{3,2},{4,5},{5,4},{6,7},{7,6},{8,9},{9,8},{10,11... | collective-permute-start | bytes 1966088 | tf_op jit(solution)/shard_map/ppermute | solution.py:668
  2.5 4.1 %shard_map.82 = (f32[2,8,1152]{2,1,0:T(8,128)}, bf16[64,8,1024]{2,1,0:T(8,128)(2,1)}, bf16[24,8,1024]{2,1,0:T(8,128)(2,1)}) custom-call(s32[1]{0:T(128)} %bitcast.1.odd_ref, s32[128]{0:T(128)} %dead_ref.1, s32[128]{0:T(128)} %sec_ref.1, bf16[128,8,1024]{2,1,0:T(8,128)(2,1)} %rest_1_.1), custom_call_target="tpu_custom_call" | custom-call | flops 1 | bytes 1 | tf_op jit(solution)/shard_map/pallas_call | solution.py:677
  9.7 1.3 %collective-permute-start.3 = (f32[2,8,1152]{2,1,0:T(8,128)S(1)}, f32[2,8,1152]{2,1,0:T(8,128)S(1)}, u32[]{:S(2)}, u32[]{:S(2)}) collective-permute-start(f32[2,8,1152]{2,1,0:T(8,128)S(1)} %add.35), channel_id=1, source_target_pairs={{0,24},{4,28},{8,16},{12,20},{16,8},{20,12},{24,0},{28,4},{1,25},{... | collective-permute-start | bytes 221192 | tf_op jit(solution)/shard_map/ppermute | solution.py:638
  11.2 1.2 %collective-permute-start.1 = (f32[2,8,1152]{2,1,0:T(8,128)S(1)}, f32[2,8,1152]{2,1,0:T(8,128)S(1)}, u32[]{:S(2)}, u32[]{:S(2)}) collective-permute-start(f32[2,8,1152]{2,1,0:T(8,128)S(1)} %add.35), channel_id=1, source_target_pairs={{0,8},{4,12},{8,0},{12,4},{16,24},{20,28},{24,16},{28,20},{1,9},{5... | collective-permute-start | bytes 221192 | tf_op jit(solution)/shard_map/ppermute | solution.py:638
  12.4 2.4 %multiply_reduce_fusion = f32[1024]{0:T(1024)} fusion(f32[512,1024]{1,0:T(8,128)} %constant.33.clone, f32[512]{0:T(512)S(1)} %copy-done.5), kind=kLoop, calls=%fused_computation.1 | loop fusion | flops 1047552 | bytes 2103296 | tf_op jit(solution)/shard_map/reduce_sum | solution.py:657
  14.8 1.2 collective-permute-start.11
  17.0 1.4 %collective-permute-start.5 = (f32[2,8,1152]{2,1,0:T(8,128)S(1)}, f32[2,8,1152]{2,1,0:T(8,128)S(1)}, u32[]{:S(2)}, u32[]{:S(2)}) collective-permute-start(f32[2,8,1152]{2,1,0:T(8,128)S(1)} %add_add_fusion.rest_0_), channel_id=1, source_target_pairs={{0,1},{1,0},{2,3},{3,2},{4,5},{5,4},{6,7},{7,6},{8,9},{9,8},{10,11... | collective-permute-start | bytes 221192 | tf_op jit(solution)/shard_map/ppermute | solution.py:706
  18.5 1.7 %shard_map.83.rest_3_.rest_8_.rest_7_ = bf16[256,1024]{1,0:T(8,128)(2,1)} custom-call(f32[1,1024]{1,0:T(1,128)} %bitcast.5), custom_call_target="tpu_custom_call" | custom-call | flops 1 | bytes 1 | tf_op jit(solution)/shard_map/pallas_call | solution.py:700
  20.2 1.3 %collective-permute-start.10 = (bf16[64,8,1024]{2,1,0:T(8,128)(2,1)}, bf16[64,8,1024]{2,1,0:T(8,128)(2,1)}, u32[]{:S(2)}, u32[]{:S(2)}) collective-permute-start(bf16[64,8,1024]{2,1,0:T(8,128)(2,1)} %get-tuple-element.60), channel_id=1, source_target_pairs={{0,1},{1,0},{2,3},{3,2},{4,5},{5,4},{6,7},{7,6},{8,9},{9,8},{10,11... | collective-permute-start | bytes 3145736 | tf_op jit(solution)/shard_map/ppermute | solution.py:708
  21.5 2.4 %collective-permute-start.7 = (bf16[40,8,1024]{2,1,0:T(8,128)(2,1)}, bf16[40,8,1024]{2,1,0:T(8,128)(2,1)S(1)}, u32[]{:S(2)}, u32[]{:S(2)}) collective-permute-start(bf16[40,8,1024]{2,1,0:T(8,128)(2,1)} %collective-permute-done.4.rest_2_), channel_id=1, source_target_pairs={{0,28},{1,5},{2,30},{3,7},{4,0},{5,9},{6,2},{7,11},{8,4},{9,13},{1... | collective-permute-start | bytes 1966088 | tf_op jit(solution)/shard_map/ppermute | solution.py:712
  23.9 9.1 %shard_map.84 = (bf16[128,128,128]{2,1,0:T(8,128)(2,1)}, bf16[2,1152,512]{2,1,0:T(8,128)(2,1)}) custom-call(s32[1]{0:T(128)} %bitcast.1.odd_ref, s32[2,128]{1,0:T(2,128)} %copy-done.3, f32[2,8,1152]{2,1,0:T(8,128)} %copy-done.2, bf16[128,8,1024]{2,1,0:T(8,128)(2,1)} %rest_1_.1, f32[1,1024]{1,0:T(1,128)} %constant.36.clone.rest_2_.rest_7_.rest_6_, ...), custom_call_target="tpu_custom_call" | custom-call | flops 3758096384 | bytes 16777216 | tf_op jit(solution)/shard_map/pallas_call | solution.py:403
  33.8 3.4 %collective-permute-done.7.rest_4_.rest_0_ = bf16[40,8,1024]{2,1,0:T(8,128)(2,1)S(1)} collective-permute-done((bf16[40,8,1024]{2,1,0:T(8,128)(2,1)}, bf16[40,8,1024]{2,1,0:T(8,128)(2,1)S(1)}, u32[]{:S(2)}, u32[]{:S(2)}) %collective-permute-start.7) | collective-permute-done | bytes 655392 | tf_op jit(solution)/shard_map/ppermute | solution.py:712
  37.2 4.3 %collective-permute-done.9.rest_5_.rest_1_ = bf16[24,8,1024]{2,1,0:T(8,128)(2,1)} collective-permute-done((bf16[24,8,1024]{2,1,0:T(8,128)(2,1)}, bf16[24,8,1024]{2,1,0:T(8,128)(2,1)}, u32[]{:S(2)}, u32[]{:S(2)}) %collective-permute-start.9) | collective-permute-done | bytes 393248 | tf_op jit(solution)/shard_map/ppermute | solution.py:719
  41.5 13.3 %shard_map.85 = (bf16[128,2,64,128]{3,2,1,0:T(8,128)(2,1)}, bf16[128,128,128]{2,1,0:T(8,128)(2,1)}) custom-call(s32[1]{0:T(128)} %bitcast.1.odd_ref, s32[2,192]{1,0:T(2,128)} %copy-done.4, f32[2,8,1152]{2,1,0:T(8,128)} %copy-done.2, f32[2,8,1152]{2,1,0:T(8,128)} %copy-done.1, bf16[40,8,1024]{2,1,0:T(8,128)(2,1)} %collective-permute-done.4.rest_2_, ...), custom_call_target="tpu_custom_call" | custom-call | flops 3758096384 | bytes 16777216 | tf_op jit(solution)/shard_map/pallas_call | solution.py:403
  54.8 15.2 %shard_map.86 = (bf16[32,32,128]{2,1,0:T(8,128)(2,1)}, bf16[32,32,128]{2,1,0:T(8,128)(2,1)}, bf16[32,32,128]{2,1,0:T(8,128)(2,1)}, bf16[32,32,128]{2,1,0:T(8,128)(2,1)}, bf16[128,128,128]{2,1,0:T(8,128)(2,1)}) custom-call(s32[1]{0:T(128)} %bitcast.me_ref, s32[2,192]{1,0:T(2,128)} %copy-done.4, bf16[40,8,1024]{2,1,0:T(8,128)(2,1)} %copy-done, ...), custom_call_target="tpu_custom_call" | custom-call | flops 2147483648 | bytes 20971520 | tf_op jit(solution)/shard_map/pallas_call | solution.py:593
  71.2 1.6 %collective-permute-start.14 = (bf16[32,32,128]{2,1,0:T(8,128)(2,1)}, bf16[32,32,128]{2,1,0:T(8,128)(2,1)S(1)}, u32[]{:S(2)}, u32[]{:S(2)}) collective-permute-start(bf16[32,32,128]{2,1,0:T(8,128)(2,1)} %get-tuple-element.70), channel_id=1, source_target_pairs={{0,0},{1,29},{2,2},{3,31},{4,4},{5,1},{6,6},{7,3},{8,8},{9,5},{10,... | collective-permute-start | bytes 786440 | tf_op jit(solution)/shard_map/ppermute | solution.py:759
  72.8 3.0 %collective-permute-start.15 = (bf16[32,32,128]{2,1,0:T(8,128)(2,1)}, bf16[32,32,128]{2,1,0:T(8,128)(2,1)}, u32[]{:S(2)}, u32[]{:S(2)}) collective-permute-start(bf16[32,32,128]{2,1,0:T(8,128)(2,1)} %get-tuple-element.71), channel_id=1, source_target_pairs={{0,1},{1,28},{2,3},{3,30},{4,5},{5,0},{6,7},{7,2},{8,9},{9,4},{10,... | collective-permute-start | bytes 786440 | tf_op jit(solution)/shard_map/ppermute | solution.py:759
  75.8 11.2 %shard_map.87 = (bf16[32,32,128]{2,1,0:T(8,128)(2,1)}, bf16[32,32,128]{2,1,0:T(8,128)(2,1)}, bf16[32,32,128]{2,1,0:T(8,128)(2,1)}, bf16[32,32,128]{2,1,0:T(8,128)(2,1)}) custom-call(s32[1]{0:T(128)} %bitcast.me_ref, bf16[128,256]{1,0:T(8,128)(2,1)} %constant.35.clone.rest_9_.rest_0_, bf16[128,2,64,128]{3,2,1,0:T(8,128)(2,1)} %get-tuple-element.65.rest_10_.rest_1_, ...), custom_call_target="tpu_custom_call" | custom-call | flops 2147483648 | bytes 20971520 | tf_op jit(solution)/shard_map/pallas_call | solution.py:611
  87.6 1.3 %collective-permute-start.17 = (bf16[32,32,128]{2,1,0:T(8,128)(2,1)}, bf16[32,32,128]{2,1,0:T(8,128)(2,1)S(1)}, u32[]{:S(2)}, u32[]{:S(2)}) collective-permute-start(bf16[32,32,128]{2,1,0:T(8,128)(2,1)} %get-tuple-element.74), channel_id=1, source_target_pairs={{0,3},{1,30},{2,1},{3,28},{4,7},{5,2},{6,5},{7,0},{8,11},{9,6},{10... | collective-permute-start | bytes 786440 | tf_op jit(solution)/shard_map/ppermute | solution.py:759
  88.9 18.0 %collective-permute-done.13 = bf16[32,32,128]{2,1,0:T(8,128)(2,1)S(1)} collective-permute-done((bf16[32,32,128]{2,1,0:T(8,128)(2,1)}, bf16[32,32,128]{2,1,0:T(8,128)(2,1)S(1)}, u32[]{:S(2)}, u32[]{:S(2)}) %collective-permute-start.13) | collective-permute-done | bytes 262176 | tf_op jit(solution)/shard_map/ppermute | solution.py:759
  106.9 1.6 %collective-permute-start.18 = (bf16[32,32,128]{2,1,0:T(8,128)(2,1)}, bf16[32,32,128]{2,1,0:T(8,128)(2,1)S(1)}, u32[]{:S(2)}, u32[]{:S(2)}) collective-permute-start(bf16[32,32,128]{2,1,0:T(8,128)(2,1)} %get-tuple-element.75), channel_id=1, source_target_pairs={{0,0},{1,29},{2,2},{3,31},{4,4},{5,1},{6,6},{7,3},{8,8},{9,5},{10,... | collective-permute-start | bytes 786440 | tf_op jit(solution)/shard_map/ppermute | solution.py:759
  110.0 8.6 %collective-permute-done.17 = bf16[32,32,128]{2,1,0:T(8,128)(2,1)S(1)} collective-permute-done((bf16[32,32,128]{2,1,0:T(8,128)(2,1)}, bf16[32,32,128]{2,1,0:T(8,128)(2,1)S(1)}, u32[]{:S(2)}, u32[]{:S(2)}) %collective-permute-start.17) | collective-permute-done | bytes 262176 | tf_op jit(solution)/shard_map/ppermute | solution.py:759
  118.8 1.5 %pad_maximum_fusion = f32[128,32,128]{2,1,0:T(8,128)} fusion(f32[32,32,128]{2,1,0:T(8,128)S(1)} %get-tuple-element.80, f32[32,32,128]{2,1,0:T(8,128)S(1)} %get-tuple-element.78, f32[32,32,128]{2,1,0:T(8,128)S(1)} %get-tuple-element.79, f32[32,32,128]{2,1,0:T(8,128)S(1)} %get-tuple-element.77), kind=kLoop, calls=%fused_computation | loop fusion | flops 1572864 | bytes 4194304 | tf_op jit(solution)/shard_map/concatenate | solution.py:766
  (49 shorter events, 8.7 us)
Async XLA Ops:
  0.0 12.4 %copy-start.5 = (f32[512]{0:T(512)S(1)}, f32[512]{0:T(512)}, u32[]{:S(2)}) copy-start(f32[512]{0:T(512)} %param.9) | copy-start | bytes 6148
  1.2 15.8 %collective-permute-start.4 = (bf16[40,8,1024]{2,1,0:T(8,128)(2,1)S(1)}, bf16[40,8,1024]{2,1,0:T(8,128)(2,1)}, u32[]{:S(2)}, u32[]{:S(2)}) collective-permute-start(bf16[40,8,1024]{2,1,0:T(8,128)(2,1)S(1)} %constant_dynamic-slice_fusion.1), channel_id=1, source_target_pairs={{0,1},{1,0},{2,3},{3,2},{4,5},{5,4},{6,7},{7,6},{8,9},{9,8},{10,11... | collective-permute-start | bytes 1966088 | tf_op jit(solution)/shard_map/ppermute | solution.py:668
  6.6 2.1 %collective-permute-start = (f32[2,8,1152]{2,1,0:T(8,128)}, f32[2,8,1152]{2,1,0:T(8,128)S(1)}, u32[]{:S(2)}, u32[]{:S(2)}) collective-permute-start(f32[2,8,1152]{2,1,0:T(8,128)} %get-tuple-element.41), channel_id=1, source_target_pairs={{0,4},{4,0},{8,12},{12,8},{16,20},{20,16},{24,28},{28,24},{1,5},{5... | collective-permute-start | bytes 221192 | tf_op jit(solution)/shard_map/ppermute | solution.py:638
  7.7 16.2 %copy-start.3 = (s32[2,128]{1,0:T(2,128)}, s32[2,128]{1,0:T(2,128)S(1)}, u32[]{:S(2)}) copy-start(s32[2,128]{1,0:T(2,128)S(1)} %pad_add_fusion.flag_ref) | copy-start | bytes 3076
  7.8 7.0 %collective-permute-start.6 = (s32[2,64]{1,0:T(2,128)S(1)}, s32[2,64]{1,0:T(2,128)S(1)}, u32[]{:S(2)}, u32[]{:S(2)}) collective-permute-start(s32[2,64]{1,0:T(2,128)S(1)} %constant_dynamic-slice_fusion), channel_id=1, source_target_pairs={{0,28},{1,5},{2,30},{3,7},{4,0},{5,9},{6,2},{7,11},{8,4},{9,13},{1... | collective-permute-start | bytes 1544 | tf_op jit(solution)/shard_map/ppermute | solution.py:672
  9.7 6.3 %collective-permute-start.3 = (f32[2,8,1152]{2,1,0:T(8,128)S(1)}, f32[2,8,1152]{2,1,0:T(8,128)S(1)}, u32[]{:S(2)}, u32[]{:S(2)}) collective-permute-start(f32[2,8,1152]{2,1,0:T(8,128)S(1)} %add.35), channel_id=1, source_target_pairs={{0,24},{4,28},{8,16},{12,20},{16,8},{20,12},{24,0},{28,4},{1,25},{... | collective-permute-start | bytes 221192 | tf_op jit(solution)/shard_map/ppermute | solution.py:638
  11.0 5.6 %collective-permute-start.2 = (f32[2,8,1152]{2,1,0:T(8,128)S(1)}, f32[2,8,1152]{2,1,0:T(8,128)S(1)}, u32[]{:S(2)}, u32[]{:S(2)}) collective-permute-start(f32[2,8,1152]{2,1,0:T(8,128)S(1)} %add.35), channel_id=1, source_target_pairs={{0,16},{4,20},{8,24},{12,28},{16,0},{20,4},{24,8},{28,12},{1,17},{... | collective-permute-start | bytes 221192 | tf_op jit(solution)/shard_map/ppermute | solution.py:638
  11.2 5.3 %collective-permute-start.1 = (f32[2,8,1152]{2,1,0:T(8,128)S(1)}, f32[2,8,1152]{2,1,0:T(8,128)S(1)}, u32[]{:S(2)}, u32[]{:S(2)}) collective-permute-start(f32[2,8,1152]{2,1,0:T(8,128)S(1)} %add.35), channel_id=1, source_target_pairs={{0,8},{4,12},{8,0},{12,4},{16,24},{20,28},{24,16},{28,20},{1,9},{5... | collective-permute-start | bytes 221192 | tf_op jit(solution)/shard_map/ppermute | solution.py:638
  14.8 19.0 %collective-permute-start.11 = (bf16[64,8,1024]{2,1,0:T(8,128)(2,1)}, bf16[64,8,1024]{2,1,0:T(8,128)(2,1)}, u32[]{:S(2)}, u32[]{:S(2)}) collective-permute-start(bf16[64,8,1024]{2,1,0:T(8,128)(2,1)} %get-tuple-element.60), channel_id=1, source_target_pairs={{0,28},{1,5},{2,30},{3,7},{4,0},{5,9},{6,2},{7,11},{8,4},{9,13},{1... | collective-permute-start | bytes 3145736 | tf_op jit(solution)/shard_map/ppermute | solution.py:696
  17.0 4.5 %collective-permute-start.5 = (f32[2,8,1152]{2,1,0:T(8,128)S(1)}, f32[2,8,1152]{2,1,0:T(8,128)S(1)}, u32[]{:S(2)}, u32[]{:S(2)}) collective-permute-start(f32[2,8,1152]{2,1,0:T(8,128)S(1)} %add_add_fusion.rest_0_), channel_id=1, source_target_pairs={{0,1},{1,0},{2,3},{3,2},{4,5},{5,4},{6,7},{7,6},{8,9},{9,8},{10,11... | collective-permute-start | bytes 221192 | tf_op jit(solution)/shard_map/ppermute | solution.py:706
  18.3 14.7 %collective-permute-start.8 = (bf16[24,8,1024]{2,1,0:T(8,128)(2,1)}, bf16[24,8,1024]{2,1,0:T(8,128)(2,1)}, u32[]{:S(2)}, u32[]{:S(2)}) collective-permute-start(bf16[24,8,1024]{2,1,0:T(8,128)(2,1)} %get-tuple-element.58), channel_id=1, source_target_pairs={{0,1},{1,0},{2,3},{3,2},{4,5},{5,4},{6,7},{7,6},{8,9},{9,8},{10,11... | collective-permute-start | bytes 1179656 | tf_op jit(solution)/shard_map/ppermute | solution.py:707
  20.2 34.6 %collective-permute-start.10 = (bf16[64,8,1024]{2,1,0:T(8,128)(2,1)}, bf16[64,8,1024]{2,1,0:T(8,128)(2,1)}, u32[]{:S(2)}, u32[]{:S(2)}) collective-permute-start(bf16[64,8,1024]{2,1,0:T(8,128)(2,1)} %get-tuple-element.60), channel_id=1, source_target_pairs={{0,1},{1,0},{2,3},{3,2},{4,5},{5,4},{6,7},{7,6},{8,9},{9,8},{10,11... | collective-permute-start | bytes 3145736 | tf_op jit(solution)/shard_map/ppermute | solution.py:708
  21.5 11.5 %copy-start.1 = (f32[2,8,1152]{2,1,0:T(8,128)}, f32[2,8,1152]{2,1,0:T(8,128)S(1)}, u32[]{:S(2)}) copy-start(f32[2,8,1152]{2,1,0:T(8,128)S(1)} %collective-permute-done.5.rest_1_.rest_5_) | copy-start | bytes 221188
  21.5 15.6 %collective-permute-start.7 = (bf16[40,8,1024]{2,1,0:T(8,128)(2,1)}, bf16[40,8,1024]{2,1,0:T(8,128)(2,1)S(1)}, u32[]{:S(2)}, u32[]{:S(2)}) collective-permute-start(bf16[40,8,1024]{2,1,0:T(8,128)(2,1)} %collective-permute-done.4.rest_2_), channel_id=1, source_target_pairs={{0,28},{1,5},{2,30},{3,7},{4,0},{5,9},{6,2},{7,11},{8,4},{9,13},{1... | collective-permute-start | bytes 1966088 | tf_op jit(solution)/shard_map/ppermute | solution.py:712
  33.0 8.5 %collective-permute-start.9 = (bf16[24,8,1024]{2,1,0:T(8,128)(2,1)}, bf16[24,8,1024]{2,1,0:T(8,128)(2,1)}, u32[]{:S(2)}, u32[]{:S(2)}) collective-permute-start(bf16[24,8,1024]{2,1,0:T(8,128)(2,1)} %collective-permute-done.8.rest_3_), channel_id=1, source_target_pairs={{0,28},{1,5},{2,30},{3,7},{4,0},{5,9},{6,2},{7,11},{8,4},{9,13},{1... | collective-permute-start | bytes 1179656 | tf_op jit(solution)/shard_map/ppermute | solution.py:719
  33.8 7.7 %copy-start.4 = (s32[2,192]{1,0:T(2,128)}, s32[2,192]{1,0:T(2,128)S(1)}, u32[]{:S(2)}) copy-start(s32[2,192]{1,0:T(2,128)S(1)} %constant_dynamic-update-slice_fusion.flag_ref) | copy-start | bytes 4612
  69.9 17.6 %collective-permute-start.12 = (bf16[32,32,128]{2,1,0:T(8,128)(2,1)}, bf16[32,32,128]{2,1,0:T(8,128)(2,1)S(1)}, u32[]{:S(2)}, u32[]{:S(2)}) collective-permute-start(bf16[32,32,128]{2,1,0:T(8,128)(2,1)} %get-tuple-element.68), channel_id=1, source_target_pairs={{0,2},{1,31},{2,0},{3,29},{4,6},{5,3},{6,4},{7,1},{8,10},{9,7},{10... | collective-permute-start | bytes 786440 | tf_op jit(solution)/shard_map/ppermute | solution.py:759
  70.1 36.8 %collective-permute-start.13 = (bf16[32,32,128]{2,1,0:T(8,128)(2,1)}, bf16[32,32,128]{2,1,0:T(8,128)(2,1)S(1)}, u32[]{:S(2)}, u32[]{:S(2)}) collective-permute-start(bf16[32,32,128]{2,1,0:T(8,128)(2,1)} %get-tuple-element.69), channel_id=1, source_target_pairs={{0,3},{1,30},{2,1},{3,28},{4,7},{5,2},{6,5},{7,0},{8,11},{9,6},{10... | collective-permute-start | bytes 786440 | tf_op jit(solution)/shard_map/ppermute | solution.py:759
  71.2 37.3 %collective-permute-start.14 = (bf16[32,32,128]{2,1,0:T(8,128)(2,1)}, bf16[32,32,128]{2,1,0:T(8,128)(2,1)S(1)}, u32[]{:S(2)}, u32[]{:S(2)}) collective-permute-start(bf16[32,32,128]{2,1,0:T(8,128)(2,1)} %get-tuple-element.70), channel_id=1, source_target_pairs={{0,0},{1,29},{2,2},{3,31},{4,4},{5,1},{6,6},{7,3},{8,8},{9,5},{10,... | collective-permute-start | bytes 786440 | tf_op jit(solution)/shard_map/ppermute | solution.py:759
  72.8 35.7 %collective-permute-start.15 = (bf16[32,32,128]{2,1,0:T(8,128)(2,1)}, bf16[32,32,128]{2,1,0:T(8,128)(2,1)}, u32[]{:S(2)}, u32[]{:S(2)}) collective-permute-start(bf16[32,32,128]{2,1,0:T(8,128)(2,1)} %get-tuple-element.71), channel_id=1, source_target_pairs={{0,1},{1,28},{2,3},{3,30},{4,5},{5,0},{6,7},{7,2},{8,9},{9,4},{10,... | collective-permute-start | bytes 786440 | tf_op jit(solution)/shard_map/ppermute | solution.py:759
  87.0 23.0 %collective-permute-start.16 = (bf16[32,32,128]{2,1,0:T(8,128)(2,1)}, bf16[32,32,128]{2,1,0:T(8,128)(2,1)S(1)}, u32[]{:S(2)}, u32[]{:S(2)}) collective-permute-start(bf16[32,32,128]{2,1,0:T(8,128)(2,1)} %get-tuple-element.73), channel_id=1, source_target_pairs={{0,2},{1,31},{2,0},{3,29},{4,6},{5,3},{6,4},{7,1},{8,10},{9,7},{10... | collective-permute-start | bytes 786440 | tf_op jit(solution)/shard_map/ppermute | solution.py:759
  87.6 31.1 %collective-permute-start.17 = (bf16[32,32,128]{2,1,0:T(8,128)(2,1)}, bf16[32,32,128]{2,1,0:T(8,128)(2,1)S(1)}, u32[]{:S(2)}, u32[]{:S(2)}) collective-permute-start(bf16[32,32,128]{2,1,0:T(8,128)(2,1)} %get-tuple-element.74), channel_id=1, source_target_pairs={{0,3},{1,30},{2,1},{3,28},{4,7},{5,2},{6,5},{7,0},{8,11},{9,6},{10... | collective-permute-start | bytes 786440 | tf_op jit(solution)/shard_map/ppermute | solution.py:759
  106.9 11.8 %collective-permute-start.18 = (bf16[32,32,128]{2,1,0:T(8,128)(2,1)}, bf16[32,32,128]{2,1,0:T(8,128)(2,1)S(1)}, u32[]{:S(2)}, u32[]{:S(2)}) collective-permute-start(bf16[32,32,128]{2,1,0:T(8,128)(2,1)} %get-tuple-element.75), channel_id=1, source_target_pairs={{0,0},{1,29},{2,2},{3,31},{4,4},{5,1},{6,6},{7,3},{8,8},{9,5},{10,... | collective-permute-start | bytes 786440 | tf_op jit(solution)/shard_map/ppermute | solution.py:759
  108.5 10.2 %collective-permute-start.19 = (bf16[32,32,128]{2,1,0:T(8,128)(2,1)}, bf16[32,32,128]{2,1,0:T(8,128)(2,1)S(1)}, u32[]{:S(2)}, u32[]{:S(2)}) collective-permute-start(bf16[32,32,128]{2,1,0:T(8,128)(2,1)} %get-tuple-element.76), channel_id=1, source_target_pairs={{0,1},{1,28},{2,3},{3,30},{4,5},{5,0},{6,7},{7,2},{8,9},{9,4},{10,... | collective-permute-start | bytes 786440 | tf_op jit(solution)/shard_map/ppermute | solution.py:759
  (4 other events, 26.6 us)
